TPU v7x, 32 devices: a whole 2x2x4 slice. The times are simulated.
32 devices in a mesh: groups: 2 (over y), fsdp: 2 (over x), expert: 4 (over z), dp: 2 (over core).
Axes of the slice: x: 2, y: 2, z: 4, core: 2. Of those that a mesh axis runs over, the one named last changes fastest.
Arguments:
- tokens: bfloat16 [2048, 6144], P(('groups', 'fsdp', 'expert', 'dp')), parts along dimension 0, may hold values from -6 to 6
- cotangent: bfloat16 [2048, 6144], P(('groups', 'fsdp', 'expert', 'dp')), parts along dimension 0, may hold values from -6 to 6
- expert_ids: int32 [2048, 2], P(('groups', 'fsdp', 'expert', 'dp')), parts along dimension 0, may hold values from 0 to 3, all different within a row; in each aligned block of 64 rows (0 to 63, 64 to 127, ...) at most 48 rows name the same one
- combine: float32 [2048, 2], P(('groups', 'fsdp', 'expert', 'dp')), parts along dimension 0, may hold values from 0.25 to 1
- gate_weight: bfloat16 [4, 6144, 128], P('expert', ('fsdp', 'dp')), may hold values from -0.078125 to 0.078125
- up_weight: bfloat16 [4, 6144, 128], P('expert', ('fsdp', 'dp')), may hold values from -0.078125 to 0.078125
- down_weight: bfloat16 [4, 6144, 128], P('expert', ('fsdp', 'dp')), may hold values from -0.5 to 0.5
Outputs:
- grad_tokens: bfloat16 [2048, 6144], P(('groups', 'fsdp', 'expert', 'dp')), parts along dimension 0
- grad_down: float32 [8, 6144, 128], P(('groups', 'expert'), ('fsdp', 'dp')), parts along dimension 0
There are 2 independent parts, one for each index of `groups`. A program takes and returns all parts, laid end to end along the dimension named above; an argument that names none is the same for every part. Nothing has to cross between parts.
Inputs may be any that keep to these rules, and one draw needn't show every extreme that they name: `expert_ids`: the 2 ids of a token differ. Within the 64 rows of one device, no expert is named by more than 48 slots, and in every draw some device has an expert named by exactly 48 slots.
All inputs are finite; a program needn't handle non-finite values.
Results may differ from a plain program's by a relative error of at most 0.0065.
Values may be sent and summed in bfloat16 or wider, within the bound.
No kernel may reach another device: no remote copies, remote signals or barrier semaphores. Data moves between devices by JAX's collectives and lax.ppermute only.
A program may use at most 64 MiB of HBM per device.

v0:
```python
import jax
import jax.numpy as jnp
from jax import lax
from jax.sharding import PartitionSpec as P


def silu_slope(pre_gate):
    sigmoid_val = jax.nn.sigmoid(pre_gate)
    return sigmoid_val * (1.0 + pre_gate * (1.0 - sigmoid_val))


def contract_last(left, right):
    return lax.dot_general(
        left, right, (((1,), (1,)), ((), ())), preferred_element_type=jnp.float32
    )


def contract_first(left, right):
    return lax.dot_general(
        left, right, (((0,), (0,)), ((), ())), preferred_element_type=jnp.float32
    )


def per_device(tokens, cotangent, expert_ids, combine, gate_weight, up_weight, down_weight):
    experts = lax.axis_size("expert")
    tok_rows = tokens.shape[0]
    model_width = tokens.shape[1]
    capacity = min(tok_rows, 3 * tok_rows // experts)
    slot_ids = expert_ids.reshape(-1)
    slot_count = slot_ids.shape[0]
    one_hot = (slot_ids[:, None] == jnp.arange(experts, dtype=jnp.int32)[None, :]).astype(jnp.int32)
    slot_rank = jnp.sum((jnp.cumsum(one_hot, axis=0) - 1) * one_hot, axis=1)
    slot_place = slot_ids * capacity + slot_rank
    slot_source = (
        jnp.full((experts * capacity,), -1, jnp.int32)
        .at[slot_place]
        .set(jnp.arange(slot_count, dtype=jnp.int32))
    )
    filled = slot_source >= 0
    safe_source = jnp.maximum(slot_source, 0)
    row_index = safe_source // 2
    slot_weight = jnp.where(filled, combine.reshape(-1)[safe_source], jnp.float32(0.0))
    send_inputs = jnp.where(filled[:, None], tokens[row_index], jnp.zeros((), jnp.bfloat16))
    send_scaled = (slot_weight[:, None] * cotangent[row_index].astype(jnp.float32)).astype(
        jnp.bfloat16
    )
    send_inputs = send_inputs.reshape(experts, capacity, model_width)
    send_scaled = send_scaled.reshape(experts, capacity, model_width)
    got_inputs, got_scaled = (
        lax.all_to_all(send_inputs, "expert", split_axis=0, concat_axis=0, tiled=True),
        lax.all_to_all(send_scaled, "expert", split_axis=0, concat_axis=0, tiled=True),
    )
    inputs = got_inputs.reshape(-1, model_width)
    scaled = got_scaled.reshape(-1, model_width)
    gate_local = gate_weight[0]
    up_local = up_weight[0]
    down_local = down_weight[0]
    gate_full, up_full, down_full = (
        lax.all_gather(gate_local, ("fsdp", "dp"), axis=0, tiled=True),
        lax.all_gather(up_local, ("fsdp", "dp"), axis=0, tiled=True),
        lax.all_gather(down_local, ("fsdp", "dp"), axis=0, tiled=True),
    )
    gate_sum = jnp.dot(inputs, gate_full, preferred_element_type=jnp.float32)
    up_sum = jnp.dot(inputs, up_full, preferred_element_type=jnp.float32)
    hidden_grad = jnp.dot(scaled, down_full, preferred_element_type=jnp.float32)
    activated = jax.nn.silu(gate_sum)
    hidden = (activated * up_sum).astype(jnp.bfloat16)
    gate_grad = (hidden_grad * up_sum * silu_slope(gate_sum)).astype(jnp.bfloat16)
    up_grad = (hidden_grad * activated).astype(jnp.bfloat16)
    back_rows = (contract_last(gate_grad, gate_full) + contract_last(up_grad, up_full)).astype(
        jnp.bfloat16
    )
    returned = lax.all_to_all(
        back_rows.reshape(experts, capacity, model_width),
        "expert",
        split_axis=0,
        concat_axis=0,
        tiled=True,
    )
    picked_rows = returned.reshape(-1, model_width)[slot_place].reshape(tok_rows, 2, model_width)
    grad_tokens = (
        picked_rows[:, 0].astype(jnp.float32) + picked_rows[:, 1].astype(jnp.float32)
    ).astype(jnp.bfloat16)
    grad_down = lax.psum_scatter(
        contract_first(scaled, hidden), ("fsdp", "dp"), scatter_dimension=0, tiled=True
    )
    return (grad_tokens, grad_down[None])


def solution(mesh):
    placed = (
        P(("groups", "fsdp", "expert", "dp"), None),
        P(("groups", "fsdp", "expert", "dp"), None),
        P(("groups", "fsdp", "expert", "dp"), None),
        P(("groups", "fsdp", "expert", "dp"), None),
        P("expert", ("fsdp", "dp"), None),
        P("expert", ("fsdp", "dp"), None),
        P("expert", ("fsdp", "dp"), None),
    )
    return jax.shard_map(
        per_device,
        mesh=mesh,
        in_specs=placed,
        out_specs=(
            P(("groups", "fsdp", "expert", "dp"), None),
            P(("groups", "expert"), ("fsdp", "dp"), None),
        ),
        check_vma=False,
    )
```

profile of v0, /device:TPU:0, one launch (start us, length us, event | category | flops | bytes accessed | tf_op | source)
XLA Modules:
  0.0 214.9 jit_solution(6958805691639000068)
XLA Ops:
  9.6 0.8 copy.16
  11.1 1.0 scatter_custom_fusion
  12.1 1.6 gather_fusion
  13.8 2.0 gather_fusion.2
  15.8 1.6 broadcast_select_fusion
  17.4 6.5 %all-to-all-start.1 = ((bf16[4,48,6144]{2,1,0:T(8,128)(2,1)}), bf16[4,48,6144]{2,1,0:T(8,128)(2,1)}, u32[]{:S(2)}, u32[]{:S(2)}) async-start(bf16[4,48,6144]{2,1,0:T(8,128)(2,1)} %broadcast_select_fusion), calls=%async_computation.1 | async-start | bytes 4718592 | tf_op jit(solution)/shard_map/all_to_all | solution.py:50
  24.7 3.4 %gather_fusion.1 = bf16[192,6144]{1,0:T(8,128)(2,1)} fusion(bf16[64,6144]{1,0:T(8,128)(2,1)S(1)} %copy-done.1, s32[1024]{0:T(1024)S(1)} %get-tuple-element.8), kind=kCustom, calls=%fused_computation.1 | custom fusion | bytes 4719360 | tf_op jit(solution)/shard_map/gather | solution.py:44
  28.1 3.6 %fusion.1 = bf16[4,48,6144]{2,1,0:T(8,128)(2,1)} fusion(bf16[4,48,6144]{2,1,0:T(8,128)(2,1)} %bitcast.38, f32[4,48]{1,0:T(4,128)S(1)} %mul.56), kind=kLoop, calls=%fused_computation.8 | loop fusion | flops 3538944 | bytes 4719360 | tf_op jit(solution)/shard_map/convert_element_type | solution.py:44
  31.8 46.0 %all-to-all-done.1 = bf16[4,48,6144]{2,1,0:T(8,128)(2,1)} async-done(((bf16[4,48,6144]{2,1,0:T(8,128)(2,1)}), bf16[4,48,6144]{2,1,0:T(8,128)(2,1)}, u32[]{:S(2)}, u32[]{:S(2)}) %all-to-all-start.1) | async-done | bytes 2359328 | tf_op jit(solution)/shard_map/all_to_all | solution.py:50
  77.8 3.6 %all-to-all-start = ((bf16[4,48,6144]{2,1,0:T(8,128)(2,1)}), bf16[4,48,6144]{2,1,0:T(8,128)(2,1)S(1)}, u32[]{:S(2)}, u32[]{:S(2)}) async-start(bf16[4,48,6144]{2,1,0:T(8,128)(2,1)} %fusion.1), calls=%async_computation | async-start | bytes 4718592 | tf_op jit(solution)/shard_map/all_to_all | solution.py:51
  82.2 2.9 %fusion.4 = f32[192,128]{1,0:T(8,128)S(1)} fusion(bf16[192,6144]{1,0:T(8,128)(2,1)} %bitcast.6, bf16[1,6144,128]{2,1,0:T(8,128)(2,1)} %all-gather.11.cloned.1.call-done), kind=kOutput, calls=%fused_computation.12 | convolution fusion | flops 301989888 | bytes 4030464 | tf_op jit(solution)/shard_map/dot_general | solution.py:63
  85.1 2.9 %fusion.7 = f32[192,128]{1,0:T(8,128)S(1)} fusion(bf16[192,6144]{1,0:T(8,128)(2,1)} %bitcast.6, bf16[1,6144,128]{2,1,0:T(8,128)(2,1)} %all-gather.9.cloned.1.call-done), kind=kOutput, calls=%fused_computation.15 | convolution fusion | flops 301989888 | bytes 4030464 | tf_op jit(solution)/shard_map/dot_general | solution.py:64
  88.0 16.9 %all-gather.7.cloned.1.call-done = bf16[1,6144,128]{2,1,0:T(8,128)(2,1)} async-done(((bf16[1,1536,128]{2,1,0:T(8,128)(2,1)}), bf16[1,6144,128]{2,1,0:T(8,128)(2,1)}) %all-gather.7.cloned.1.call-update) | async-done | bytes 1572880 | tf_op jit(solution)/shard_map/all_gather | solution.py:61
  104.9 29.8 %all-to-all-done = bf16[4,48,6144]{2,1,0:T(8,128)(2,1)S(1)} async-done(((bf16[4,48,6144]{2,1,0:T(8,128)(2,1)}), bf16[4,48,6144]{2,1,0:T(8,128)(2,1)S(1)}, u32[]{:S(2)}, u32[]{:S(2)}) %all-to-all-start) | async-done | bytes 2359328 | tf_op jit(solution)/shard_map/all_to_all | solution.py:51
  134.7 3.1 %fusion.9 = f32[192,128]{1,0:T(8,128)S(1)} fusion(bf16[192,6144]{1,0:T(8,128)(2,1)S(1)} %bitcast.35, bf16[1,6144,128]{2,1,0:T(8,128)(2,1)} %all-gather.7.cloned.1.call-done), kind=kOutput, calls=%fused_computation.17 | convolution fusion | flops 301989888 | bytes 4030464 | tf_op jit(solution)/shard_map/dot_general | solution.py:65
  137.8 0.8 fusion.2
  139.2 2.2 %fusion = bf16[192,6144]{1,0:T(8,128)(2,1)} fusion(f32[192,6144]{1,0:T(8,128)S(1)} %fusion.2, bf16[1,6144,128]{2,1,0:T(8,128)(2,1)S(1)} %copy-done.4, f32[192,128]{1,0:T(8,128)S(1)} %fusion.9, f32[192,128]{1,0:T(8,128)S(1)} %fusion.4), kind=kOutput, calls=%fused_computation.6 | convolution fusion | flops 304496640 | bytes 8847360 | tf_op jit(solution)/shard_map/dot_general | solution.py:13
  141.4 3.6 %all-to-all-start.2 = ((bf16[4,48,6144]{2,1,0:T(8,128)(2,1)}), bf16[4,48,6144]{2,1,0:T(8,128)(2,1)S(1)}, u32[]{:S(2)}, u32[]{:S(2)}) async-start(bf16[4,48,6144]{2,1,0:T(8,128)(2,1)} %bitcast.37), calls=%async_computation.2 | async-start | bytes 4718592 | tf_op jit(solution)/shard_map/all_to_all | solution.py:73
  145.3 4.4 %fusion.14 = f32[6144,128]{1,0:T(8,128)} fusion(bf16[192,6144]{1,0:T(8,128)(2,1)} %bitcast.36, f32[192,128]{1,0:T(8,128)S(1)} %fusion.7, f32[192,128]{1,0:T(8,128)S(1)} %fusion.4), kind=kOutput, calls=%fused_computation.29 | convolution fusion | flops 302137344 | bytes 5701632 | tf_op jit(solution)/shard_map/dot_general | solution.py:19
  149.7 48.6 %all-to-all-done.2 = bf16[4,48,6144]{2,1,0:T(8,128)(2,1)S(1)} async-done(((bf16[4,48,6144]{2,1,0:T(8,128)(2,1)}), bf16[4,48,6144]{2,1,0:T(8,128)(2,1)S(1)}, u32[]{:S(2)}, u32[]{:S(2)}) %all-to-all-start.2) | async-done | bytes 2359328 | tf_op jit(solution)/shard_map/all_to_all | solution.py:73
  198.3 2.6 %gather_fusion.3 = bf16[128,6144]{1,0:T(8,128)(2,1)} fusion(bf16[192,6144]{1,0:T(8,128)(2,1)S(1)} %bitcast.34, s32[1024]{0:T(1024)S(1)} %pad_clamp_fusion), kind=kCustom, calls=%fused_computation.3 | custom fusion | bytes 3146240 | tf_op jit(solution)/shard_map/gather | solution.py:80
  200.9 3.4 %reshape.79 = bf16[64,2,6144]{2,1,0:T(2,128)(2,1)S(1)} reshape(bf16[128,6144]{1,0:T(8,128)(2,1)} %gather_fusion.3) | data formatting | bytes 3145728 | tf_op jit(solution)/shard_map/reshape | solution.py:80
  204.4 2.2 %fusion.24 = (bf16[64,1,6144]{2,1,0:T(2,128)(2,1)S(1)}, bf16[64,1,6144]{2,1,0:T(2,128)(2,1)S(1)}) fusion(bf16[64,2,6144]{2,1,0:T(2,128)(2,1)S(1)} %reshape.79), kind=kLoop, calls=%fused_computation.48 | loop fusion | bytes 3145728 | tf_op jit(solution)/shard_map/slice | solution.py:82
  206.6 1.7 fusion.11
  (38 shorter events, 5.7 us)
Async XLA Ops:
  7.2 6.6 %copy-start = (bf16[64,6144]{1,0:T(8,128)(2,1)S(1)}, bf16[64,6144]{1,0:T(8,128)(2,1)}, u32[]{:S(2)}) copy-start(bf16[64,6144]{1,0:T(8,128)(2,1)} %param.7) | copy-start | bytes 2359300
  7.2 75.0 %all-gather.11.cloned.1.call-start = ((), (), s32[]{:S(2)}) async-start(), calls=%async_computation.7 | async-start | bytes 1966080 | tf_op jit(solution)/shard_map/all_gather | solution.py:59
  17.4 7.3 %copy-start.1 = (bf16[64,6144]{1,0:T(8,128)(2,1)S(1)}, bf16[64,6144]{1,0:T(8,128)(2,1)}, u32[]{:S(2)}) copy-start(bf16[64,6144]{1,0:T(8,128)(2,1)} %param.8) | copy-start | bytes 2359300
  17.4 60.4 %all-to-all-start.1 = ((bf16[4,48,6144]{2,1,0:T(8,128)(2,1)}), bf16[4,48,6144]{2,1,0:T(8,128)(2,1)}, u32[]{:S(2)}, u32[]{:S(2)}) async-start(bf16[4,48,6144]{2,1,0:T(8,128)(2,1)} %broadcast_select_fusion), calls=%async_computation.1 | async-start | bytes 4718592 | tf_op jit(solution)/shard_map/all_to_all | solution.py:50
  23.9 61.2 %all-gather.9.cloned.1.call-start = ((), (), s32[]{:S(2)}) async-start(), calls=%async_computation.6 | async-start | bytes 1966080 | tf_op jit(solution)/shard_map/all_gather | solution.py:60
  77.8 56.9 %all-to-all-start = ((bf16[4,48,6144]{2,1,0:T(8,128)(2,1)}), bf16[4,48,6144]{2,1,0:T(8,128)(2,1)S(1)}, u32[]{:S(2)}, u32[]{:S(2)}) async-start(bf16[4,48,6144]{2,1,0:T(8,128)(2,1)} %fusion.1), calls=%async_computation | async-start | bytes 4718592 | tf_op jit(solution)/shard_map/all_to_all | solution.py:51
  81.4 23.5 %all-gather.7.cloned.1.call-start = ((), (), s32[]{:S(2)}) async-start(), calls=%async_computation.5 | async-start | bytes 1966080 | tf_op jit(solution)/shard_map/all_gather | solution.py:61
  134.7 3.1 %copy-start.2 = (bf16[4,48,6144]{2,1,0:T(8,128)(2,1)}, bf16[4,48,6144]{2,1,0:T(8,128)(2,1)S(1)}, u32[]{:S(2)}) copy-start(bf16[4,48,6144]{2,1,0:T(8,128)(2,1)S(1)} %all-to-all-done) | copy-start | bytes 7077892
  134.7 3.1 %copy-start.3 = (bf16[1,6144,128]{2,1,0:T(8,128)(2,1)S(1)}, bf16[1,6144,128]{2,1,0:T(8,128)(2,1)}, u32[]{:S(2)}) copy-start(bf16[1,6144,128]{2,1,0:T(8,128)(2,1)} %all-gather.11.cloned.1.call-done) | copy-start | bytes 4718596
  137.8 1.4 copy-start.4
  141.4 56.9 %all-to-all-start.2 = ((bf16[4,48,6144]{2,1,0:T(8,128)(2,1)}), bf16[4,48,6144]{2,1,0:T(8,128)(2,1)S(1)}, u32[]{:S(2)}, u32[]{:S(2)}) async-start(bf16[4,48,6144]{2,1,0:T(8,128)(2,1)} %bitcast.37), calls=%async_computation.2 | async-start | bytes 4718592 | tf_op jit(solution)/shard_map/all_to_all | solution.py:73
  145.0 63.3 %reduce-scatter.2.cloned.1.call-start = ((), (), s32[]{:S(2)}) async-start(), calls=%async_computation.4 | async-start | bytes 3932160 | tf_op jit(solution)/shard_map/reduce_scatter | solution.py:84
Sparse Core Ops, SparseCore 0:
  9.6 22.3 all-gather.10
  33.5 19.6 all-gather.8
  83.8 21.0 all-gather.6
  149.8 39.1 reduce-scatter.1
where the time goes:
time: 215 us
  waiting for transfers between devices  143 us (67%)
  local copies, waits for them, and re-layouts  19.1 us (9%)
  matrix products  16.2 us (8%)
  starting transfers between devices  14 us (7%)
  between operations  13.9 us (6%)
  other arithmetic  8.17 us (4%)
    all_to_all x1, waiting for transfers between devices, per_device(): lax.all_to_all(back_rows.reshape(experts, capacity, model_width), 'expert...  48.6 us
    all_to_all x1, waiting for transfers between devices, per_device(): lax.all_to_all(send_inputs, 'expert', split_axis=0, concat_axis=0, tiled=...  46 us
    all_to_all x1, waiting for transfers between devices, per_device(): lax.all_to_all(send_scaled, 'expert', split_axis=0, concat_axis=0, tiled=...  29.8 us
    all_gather x1, waiting for transfers between devices, per_device(): lax.all_gather(down_local, ('fsdp', 'dp'), axis=0, tiled=True)  16.9 us
    all_to_all x1, starting transfers between devices, per_device(): lax.all_to_all(send_inputs, 'expert', split_axis=0, concat_axis=0, tiled=...  6.45 us
    dot_general x1, matrix products, contract_first(): lax.dot_general(left, right, (((0,), (0,)), ((), ())), preferred_element_...  4.38 us
  transfers between devices with their start and end apart: 7, of which 4 were waited for; matrix products, arithmetic and copies ran while one was open for 17% of the time, Pallas kernels for 0%

commit v1 on v0

v1 whole, which is shorter than its diff:
```python
import jax
import jax.numpy as jnp
from jax import lax
from jax.experimental import pallas as pl
from jax.experimental.pallas import tpu as pltpu
from jax.sharding import PartitionSpec as P

BF = jnp.bfloat16
F32 = jnp.float32
VMEM = pl.BlockSpec(memory_space=pltpu.VMEM)
SMEM = pl.BlockSpec(memory_space=pltpu.SMEM)
SWAP = [(0, 1), (1, 0)]
PARAMS = pltpu.CompilerParams(vmem_limit_bytes=48 * 1024 * 1024)


def call(body, outs, specs, *args):
    return pl.pallas_call(
        body,
        out_shape=outs,
        in_specs=specs,
        out_specs=jax.tree.map(lambda _: VMEM, outs),
        compiler_params=PARAMS,
    )(*args)


def mm(left, right, dims):
    return lax.dot_general(left, right, (dims, ((), ())), preferred_element_type=F32)


def forward_sums(count, width, scal, ids, near_rows, far_rows, *refs):
    out = refs[-1]
    first, second = ids[:, 0:1], ids[:, 1:2]
    total = [None, None]
    for s in range(count):
        near, far = refs[2 * s], refs[2 * s + 1]
        parts = near.shape[0]
        left = jnp.concatenate([near[p] for p in range(parts)], axis=1) if parts > 1 else near[0]
        right = jnp.concatenate([far[p] for p in range(parts)], axis=1) if parts > 1 else far[0]
        value = mm(near_rows[...], left, ((1,), (0,))) + mm(
            far_rows[...], right, ((1,), (0,))
        )
        label = scal[s]
        for k, named in enumerate((first, second)):
            picked = jnp.where(named == label, value, 0.0)
            total[k] = picked if total[k] is None else total[k] + picked
    out[:, :width] = total[0]
    out[:, width:] = total[1]


def down_products(count, scal, ids, scaled_t, hidden, *outs):
    ff = hidden.shape[1] // 2
    for j in range(count):
        label = scal[j]
        rows = jnp.where(ids[:, 0:1] == label, hidden[:, :ff], jnp.zeros((), BF)) + jnp.where(
            ids[:, 1:2] == label, hidden[:, ff:], jnp.zeros((), BF)
        )
        outs[j][...] = mm(scaled_t[...], rows, ((1,), (0,))).astype(outs[j].dtype)


def token_sums(count, scal, ids, grads, *refs):
    near_out, far_out = refs[-2], refs[-1]
    ff = grads.shape[1] // 4
    near_total = far_total = None
    for s in range(count):
        label = scal[s]
        rows = jnp.where(ids[:, 0:1] == label, grads[:, : 2 * ff], jnp.zeros((), BF)) + jnp.where(
            ids[:, 1:2] == label, grads[:, 2 * ff :], jnp.zeros((), BF)
        )
        near, far = refs[2 * s], refs[2 * s + 1]
        near_w = jnp.concatenate([near[0], near[1]], axis=1)
        far_w = jnp.concatenate([far[0], far[1]], axis=1)
        a = mm(rows, near_w, ((1,), (1,)))
        b = mm(rows, far_w, ((1,), (1,)))
        near_total = a if s == 0 else near_total + a
        far_total = b if s == 0 else far_total + b
    near_out[...] = near_total.astype(BF)
    far_out[...] = far_total.astype(BF)


def split3(value):
    high = lax.reduce_precision(value, 8, 7)
    rest = value - high
    middle = lax.reduce_precision(rest, 8, 7)
    low = rest - middle
    return [high.astype(BF), middle.astype(BF), low.astype(BF)]


def gather_slots(block, e, n):
    pp = lax.ppermute
    if n == 4:
        two = pp(block, "expert", [(i, (i + 2) % 4) for i in range(4)])
        right = pp(block, "expert", [(0, 1), (1, 2), (2, 3)])
        left = pp(block, "expert", [(1, 0), (2, 1), (3, 2)])
        ends = pp(two, "expert", [(2, 3), (1, 0)])
        end_label = jnp.where(e == 0, 3, jnp.where(e == 3, 0, -1))
        return [((e + 2) % 4, two), (e - 1, right), (e + 1, left), (end_label, ends)]
    return [
        ((e - k) % n, pp(block, "expert", [(i, (i + k) % n) for i in range(n)])) for k in range(1, n)
    ]


def per_device(tokens, cotangent, expert_ids, combine, gate_weight, up_weight, down_weight):
    n = lax.axis_size("expert")
    nx, nc = lax.axis_size("fsdp"), lax.axis_size("dp")
    g, f, e, d = (lax.axis_index(a) for a in ("groups", "fsdp", "expert", "dp"))
    own, width = tokens.shape
    quarter, ff = gate_weight.shape[1:]
    half = quarter // 2
    pp = lax.ppermute
    small = nx == 2 and nc == 2

    def halves(w):
        return (
            jnp.where(g == 0, w[:, :half], w[:, half:]),
            jnp.where(g == 0, w[:, half:], w[:, :half]),
        )

    near_g, far_g = halves(gate_weight)
    near_u, far_u = halves(up_weight)
    near_d, far_d = halves(down_weight)
    own_gu = (jnp.concatenate([near_g, near_u]), jnp.concatenate([far_g, far_u]))
    gu = gather_slots(own_gu[0], e, n)
    dn = gather_slots(near_d, e, n)
    labels = jnp.stack([e] + [label for label, _ in gu]).astype(jnp.int32)
    gu_refs, dn_refs = list(own_gu), [near_d, far_d]
    for _, block in gu:
        gu_refs += [block, pp(block, "groups", SWAP)]
    for _, block in dn:
        dn_refs += [block, pp(block, "groups", SWAP)]
    count = len(gu) + 1

    extra = jnp.concatenate(
        [expert_ids.astype(F32).astype(BF)]
        + split3(combine)
        + [jnp.zeros((own, 120), BF)],
        axis=1,
    )
    if small:
        wide = width // 2

        def halve(a, at):
            m = a.shape[1] // 2
            return jnp.where(at == 0, a[:, :m], a[:, m:])

        sent = jnp.concatenate([halve(tokens, 1 - f), halve(cotangent, 1 - f), extra], axis=1)
        got = pp(sent, "fsdp", SWAP)
        tok_x = jnp.concatenate([halve(tokens, f), got[:, :wide]])
        cot_x = jnp.concatenate([halve(cotangent, f), got[:, wide : 2 * wide]])
        extra_x = jnp.concatenate([extra, got[:, 2 * wide :]])
        sent = jnp.concatenate([halve(tok_x, 1 - d), halve(cot_x, 1 - d), extra_x], axis=1)
        got = pp(sent, "dp", SWAP)
        tok = jnp.concatenate([halve(tok_x, d), got[:, :quarter]])
        cot = jnp.concatenate([halve(cot_x, d), got[:, quarter : 2 * quarter]])
        info = jnp.concatenate([extra_x, got[:, 2 * quarter :]])
        mine = 2 * own

        def reduce_rows(part):
            total = part[:mine] + pp(part[mine:], "dp", SWAP)
            other = pp(total.astype(BF), "fsdp", SWAP)
            return total + jnp.concatenate([other[own:], other[:own]]).astype(F32)

        def share_rows(rows):
            return jnp.concatenate([rows, pp(rows, "dp", SWAP)])

        mine_info = extra_x
    else:
        plane = nx * nc

        def to_columns(a):
            a = a.reshape(own, plane, quarter).transpose(1, 0, 2)
            return lax.all_to_all(a, ("fsdp", "dp"), 0, 0, tiled=True).reshape(plane * own, quarter)

        tok, cot = to_columns(tokens), to_columns(cotangent)
        info = lax.all_gather(extra, ("fsdp", "dp"), axis=0, tiled=True)

        def reduce_rows(part):
            return lax.psum_scatter(part, ("fsdp", "dp"), scatter_dimension=0, tiled=True)

        def share_rows(rows):
            return lax.all_gather(rows, ("fsdp", "dp"), axis=0, tiled=True)

        mine_info = extra
    ids = info[:, :2].astype(jnp.int32)
    parts = mine_info[:, 2:8].astype(F32)
    weight = (parts[:, 0:2] + parts[:, 2:4]) + parts[:, 4:6]
    weight = jnp.repeat(weight, ff, axis=1).reshape(-1, 2, ff)
    rows = tok.shape[0]
    cot_t = cot.T

    def sums(a, refs, w):
        return call(
            lambda *r: forward_sums(count, w, *r),
            jax.ShapeDtypeStruct((rows, 2 * w), F32),
            [SMEM, VMEM, VMEM, VMEM] + [VMEM] * len(refs),
            labels,
            ids,
            *halves(a),
            *refs,
        )

    first = reduce_rows(sums(tok, gu_refs, 2 * ff)).reshape(-1, 2, 2 * ff)
    gate_sum, up_sum = first[:, :, :ff], first[:, :, ff:]
    sig = jax.nn.sigmoid(gate_sum)
    act = gate_sum * sig
    hidden = (weight * (act * up_sum)).astype(BF).reshape(-1, 2 * ff)
    hidden = share_rows(hidden)
    targets = jnp.stack([(e + k) % n for k in range(n)]).astype(jnp.int32)
    pieces = call(
        lambda *r: down_products(n, *r),
        [jax.ShapeDtypeStruct((quarter, ff), F32 if k == 0 else BF) for k in range(n)],
        [SMEM, VMEM, VMEM, VMEM],
        targets,
        ids,
        cot_t,
        hidden,
    )
    grad_down = pieces[0]
    for k in range(1, n):
        grad_down = grad_down + pp(
            pieces[k], "expert", [(i, (i + k) % n) for i in range(n)]
        ).astype(F32)

    hidden_grad = weight * reduce_rows(sums(cot, dn_refs, ff)).reshape(-1, 2, ff)
    gate_grad = hidden_grad * up_sum * (sig * (1.0 + gate_sum * (1.0 - sig)))
    up_grad = hidden_grad * act
    grads = jnp.concatenate([gate_grad, up_grad], axis=2).astype(BF).reshape(-1, 4 * ff)
    grads = share_rows(grads)
    near, far = call(
        lambda *r: token_sums(count, *r),
        [jax.ShapeDtypeStruct((rows, half), BF)] * 2,
        [SMEM, VMEM, VMEM] + [VMEM] * len(gu_refs),
        labels,
        ids,
        grads,
        *gu_refs,
    )
    back = jnp.where(
        g == 0, jnp.concatenate([near, far], axis=1), jnp.concatenate([far, near], axis=1)
    )
    if small:
        def join(kept, came, at):
            return jnp.where(
                at == 0,
                jnp.concatenate([kept, came], axis=1),
                jnp.concatenate([came, kept], axis=1),
            )

        back = join(back[:mine], pp(back[mine:], "dp", SWAP), d)
        grad_tokens = join(back[:own], pp(back[own:], "fsdp", SWAP), f)
    else:
        back = lax.all_to_all(
            back.reshape(plane, own, quarter), ("fsdp", "dp"), 0, 0, tiled=True
        )
        grad_tokens = back.transpose(1, 0, 2).reshape(own, width)
    return (grad_tokens, grad_down[None])


def solution(mesh):
    rows = P(("groups", "fsdp", "expert", "dp"), None)
    weights = P("expert", ("fsdp", "dp"), None)
    return jax.shard_map(
        per_device,
        mesh=mesh,
        in_specs=(rows, rows, rows, rows, weights, weights, weights),
        out_specs=(rows, P(("groups", "expert"), ("fsdp", "dp"), None)),
        check_vma=False,
    )
```

time: 215 us -> 204 us (0.949)
  the two profiles are of different devices: /device:TPU:0 before, /device:TPU:24 now
where the time goes in v1:
time: 204 us; the launch traced here: 202 us
  waiting for transfers between devices  99.9 us (49%)
  starting transfers between devices  36.2 us (18%)
  local copies, waits for them, and re-layouts  36 us (18%)
  other arithmetic  19.9 us (10%)
  Pallas kernels  9.24 us (5%)
    ppermute x3, waiting for transfers between devices, per_device(): pp(pieces[k], 'expert', [(i, (i + k) % n) for i in range(n)]).astype(F32)  32.8 us
    ppermute x4, waiting for transfers between devices, per_device(): dn_refs += [block, pp(block, 'groups', SWAP)]  30.9 us
    unnamed x71, local copies, waits for them, and re-layouts  16.6 us
    ppermute x1, waiting for transfers between devices, per_device(): got = pp(sent, 'fsdp', SWAP)  13.9 us
    ppermute x2, starting transfers between devices, gather_slots(): left = pp(block, 'expert', [(1, 0), (2, 1), (3, 2)])  13.2 us
    ppermute x2, waiting for transfers between devices, gather_slots(): ends = pp(two, 'expert', [(2, 3), (1, 0)])  11.1 us
    pallas_call x4, Pallas kernels, call(): pl.pallas_call(body, out_shape=outs, in_specs=specs, out_specs=jax.tree.m...  9.24 us
    concatenate x2, local copies, waits for them, and re-layouts, per_device(): jnp.concatenate([halve(tokens, 1 - f), halve(cotangent, 1 - f), extra], a...  7.64 us
  transfers between devices with their start and end apart: 29, of which 13 were waited for; matrix products, arithmetic and copies ran while one was open for 12% of the time, Pallas kernels for 3%

profile of v1, /device:TPU:24, one launch (start us, length us, event | category | flops | bytes accessed | tf_op | source)
XLA Modules:
  0.0 202.5 jit_solution(11640371693000706652)
XLA Ops:
  5.3 2.6 %broadcast_select_fusion = (bf16[64,3072]{0,1:T(8,128)(2,1)S(1)}, bf16[64,3072]{0,1:T(8,128)(2,1)}, bf16[64,3072]{0,1:T(8,128)(2,1)}, bf16[64,3072]{0,1:T(8,128)(2,1)}) fusion(bf16[64,3072]{0,1:T(8,128)(2,1)S(1)} %copy.62, bf16[64,3072]{0,1:T(8,128)(2,1)} %copy.63, pred[]{:T(512)S(6)} %eq.20, pred[]{:T(512)S(6)} %eq.48, bf16[64,3072]{0,1:T(8,128)(2,1)S(1)} %copy.60, ...), kind=kLoop, calls=%fused_computation.17 | loop fusion | flops 786432 | bytes 3145730 | tf_op jit(solution)/shard_map/jit(_where)/select_n | solution.py:143
  8.0 5.8 %concatenate.70 = bf16[64,6272]{0,1:T(8,128)(2,1)S(1)} concatenate(bf16[64,3072]{0,1:T(8,128)(2,1)} %get-tuple-element.56, bf16[64,3072]{0,1:T(8,128)(2,1)} %get-tuple-element.21, bf16[64,2]{0,1:T(2,128)(2,1)S(1)} %convert_convert_fusion, bf16[64,2]{0,1:T(2,128)(2,1)S(1)} %get-tuple-element.55, bf16[64,2]{0,1:T(2,128)(2,1)S(1)} %get-tuple-element.54, ...), dimensions={1} | concatenate | bytes 1605632 | tf_op jit(solution)/shard_map/concatenate | solution.py:145
  13.8 1.8 copy.43
  19.4 2.1 %broadcast_select_fusion.12 = (bf16[1,768,128]{2,1,0:T(8,128)(2,1)}, bf16[1,768,128]{2,1,0:T(8,128)(2,1)}, bf16[1,768,128]{2,1,0:T(8,128)(2,1)}, bf16[1,768,128]{2,1,0:T(8,128)(2,1)}) fusion(pred[]{:T(512)S(6)} %eq.22, bf16[1,1536,128]{2,1,0:T(8,128)(2,1)} %param.12, bf16[1,1536,128]{2,1,0:T(8,128)(2,1)} %param.11), kind=kLoop, calls=%fused_computation.42 | loop fusion | flops 393216 | bytes 1572865 | tf_op jit(solution)/shard_map/jit(_where)/select_n | solution.py:115
  21.5 13.9 %collective-permute-done = bf16[64,6272]{1,0:T(8,128)(2,1)S(1)} collective-permute-done((bf16[64,6272]{1,0:T(8,128)(2,1)}, bf16[64,6272]{1,0:T(8,128)(2,1)S(1)}, u32[]{:S(2)}, u32[]{:S(2)}) %collective-permute-start) | collective-permute-done | bytes 802848 | tf_op jit(solution)/shard_map/ppermute | solution.py:146
  37.2 2.4 %broadcast_select_fusion.4 = (bf16[128,1536]{0,1:T(8,128)(2,1)}, bf16[128,1536]{0,1:T(8,128)(2,1)S(1)}) fusion(pred[]{:T(512)S(6)} %eq.21, bf16[64,3072]{0,1:T(8,128)(2,1)S(1)} %copy.65, bf16[64,3072]{0,1:T(8,128)(2,1)} %get-tuple-element.57), kind=kLoop, calls=%fused_computation.31 | loop fusion | flops 1769472 | bytes 1572865 | tf_op jit(solution)/shard_map/jit(_where)/select_n | solution.py:143
  41.2 1.8 maximum_maximum_fusion
  44.7 4.6 %collective-permute-start.6 = (bf16[1,768,128]{2,1,0:T(8,128)(2,1)S(1)}, bf16[1,768,128]{2,1,0:T(8,128)(2,1)S(1)}, u32[]{:S(2)}, u32[]{:S(2)}) collective-permute-start(bf16[1,768,128]{2,1,0:T(8,128)(2,1)S(1)} %get-tuple-element.43.r_4_), channel_id=1, source_target_pairs={{2,0},{4,2},{6,4},{3,1},{5,3},{7,5},{10,8},{12,10},{14,12},{11,9},... | collective-permute-start | bytes 589832 | tf_op jit(solution)/shard_map/ppermute | solution.py:93
  54.5 2.2 %collective-permute-done.6.r_10_ = bf16[1,768,128]{2,1,0:T(8,128)(2,1)S(1)} collective-permute-done((bf16[1,768,128]{2,1,0:T(8,128)(2,1)S(1)}, bf16[1,768,128]{2,1,0:T(8,128)(2,1)S(1)}, u32[]{:S(2)}, u32[]{:S(2)}) %collective-permute-start.6) | collective-permute-done | bytes 196640 | tf_op jit(solution)/shard_map/ppermute | solution.py:93
  58.0 8.1 %collective-permute-done.8.r_12_ = bf16[1,768,128]{2,1,0:T(8,128)(2,1)} collective-permute-done((bf16[1,768,128]{2,1,0:T(8,128)(2,1)S(1)}, bf16[1,768,128]{2,1,0:T(8,128)(2,1)}, u32[]{:S(2)}, u32[]{:S(2)}) %collective-permute-start.8) | collective-permute-done | bytes 196640 | tf_op jit(solution)/shard_map/ppermute | solution.py:94
  66.1 8.6 %collective-permute-start.16 = (bf16[2,768,128]{2,1,0:T(8,128)(2,1)S(1)}, bf16[2,768,128]{2,1,0:T(8,128)(2,1)S(1)}, u32[]{:S(2)}, u32[]{:S(2)}) collective-permute-start(bf16[2,768,128]{2,1,0:T(8,128)(2,1)S(1)} %pad_maximum_fusion.4.r_4_.r_3_), channel_id=1, source_target_pairs={{2,0},{4,2},{6,4},{3,1},{5,3},{7,5},{10,8},{12,10},{14,12},{11,9},... | collective-permute-start | bytes 1179656 | tf_op jit(solution)/shard_map/ppermute | solution.py:93
  79.9 3.4 %collective-permute-done.5.r_9_ = bf16[1,768,128]{2,1,0:T(8,128)(2,1)S(1)} collective-permute-done((bf16[1,768,128]{2,1,0:T(8,128)(2,1)S(1)}, bf16[1,768,128]{2,1,0:T(8,128)(2,1)S(1)}, u32[]{:S(2)}, u32[]{:S(2)}) %collective-permute-start.5) | collective-permute-done | bytes 196640 | tf_op jit(solution)/shard_map/ppermute | solution.py:129
  87.2 3.0 %collective-permute-done.18.r_12_.r_11_ = bf16[2,768,128]{2,1,0:T(8,128)(2,1)S(1)} collective-permute-done((bf16[2,768,128]{2,1,0:T(8,128)(2,1)S(1)}, bf16[2,768,128]{2,1,0:T(8,128)(2,1)S(1)}, u32[]{:S(2)}, u32[]{:S(2)}) %collective-permute-start.18) | collective-permute-done | bytes 393248 | tf_op jit(solution)/shard_map/ppermute | solution.py:94
  92.3 1.9 fusion.13
  99.8 27.5 %collective-permute-done.9.r_13_ = bf16[1,768,128]{2,1,0:T(8,128)(2,1)S(1)} collective-permute-done((bf16[1,768,128]{2,1,0:T(8,128)(2,1)}, bf16[1,768,128]{2,1,0:T(8,128)(2,1)S(1)}, u32[]{:S(2)}, u32[]{:S(2)}) %collective-permute-start.9) | collective-permute-done | bytes 196640 | tf_op jit(solution)/shard_map/ppermute | solution.py:129
  136.4 2.2 %shard_map.86 = f32[256,256]{1,0:T(8,128)S(1)} custom-call(s32[5]{0:T(128)S(1)} %stack.36.r_0_, s32[256,2]{1,0:T(8,128)S(1)} %copy.57.r_1_, bf16[256,768]{1,0:T(8,128)(2,1)S(1)} %copy.48.r_2_, bf16[256,768]{1,0:T(8,128)(2,1)S(1)} %copy.49.r_3_, bf16[1,768,128]{2,1,0:T(8,128)(2,1)S(1)} %copy-done.2, bf16[1,768,128]{2,1,0:T(8,128)(2,1)S(1)} %copy-done, ...), custom_call_target="tpu_custom_call" | custom-call | tf_op jit(solution)/shard_map/pallas_call | solution.py:17
  141.6 2.6 %shard_map.87 = f32[256,512]{1,0:T(8,128)S(1)} custom-call(s32[5]{0:T(128)S(1)} %stack.36.r_0_, s32[256,2]{1,0:T(8,128)S(1)} %copy.57.r_1_, bf16[256,768]{1,0:T(8,128)(2,1)S(1)} %copy.52.r_2_, bf16[256,768]{1,0:T(8,128)(2,1)S(1)} %copy.53.r_3_, bf16[2,768,128]{2,1,0:T(8,128)(2,1)S(1)} %pad_maximum_fusion.4.r_4_.r_3_, ...), custom_call_target="tpu_custom_call" | custom-call | tf_op jit(solution)/shard_map/pallas_call | solution.py:17
  147.9 2.5 %collective-permute-done.11 = bf16[128,256]{1,0:T(8,128)(2,1)S(1)} collective-permute-done((bf16[128,256]{1,0:T(8,128)(2,1)S(1)}, bf16[128,256]{1,0:T(8,128)(2,1)S(1)}, u32[]{:S(2)}, u32[]{:S(2)}) %collective-permute-start.11) | collective-permute-done | bytes 65568 | tf_op jit(solution)/shard_map/ppermute | solution.py:159
  150.5 2.4 %collective-permute-done.21 = bf16[128,512]{1,0:T(8,128)(2,1)S(1)} collective-permute-done((bf16[128,512]{1,0:T(8,128)(2,1)S(1)}, bf16[128,512]{1,0:T(8,128)(2,1)S(1)}, u32[]{:S(2)}, u32[]{:S(2)}) %collective-permute-start.21) | collective-permute-done | bytes 131104 | tf_op jit(solution)/shard_map/ppermute | solution.py:159
  155.7 2.7 %shard_map.88 = (bf16[256,768]{1,0:T(8,128)(2,1)S(1)}, bf16[256,768]{1,0:T(8,128)(2,1)S(1)}) custom-call(s32[5]{0:T(128)S(1)} %stack.36.r_0_, s32[256,2]{1,0:T(8,128)S(1)} %copy.57.r_1_, bf16[256,512]{1,0:T(8,128)(2,1)S(1)} %pad_maximum_fusion.6.r_2_, bf16[2,768,128]{2,1,0:T(8,128)(2,1)S(1)} %pad_maximum_fusion.4.r_4_.r_3_, ...), custom_call_target="tpu_custom_call" | custom-call | tf_op jit(solution)/shard_map/pallas_call | solution.py:17
  160.5 1.8 shard_map.89
  162.4 3.5 %collective-permute-start.27 = (bf16[1536,128]{1,0:T(8,128)(2,1)S(1)}, bf16[1536,128]{1,0:T(8,128)(2,1)S(1)}, u32[]{:S(2)}, u32[]{:S(2)}) collective-permute-start(bf16[1536,128]{1,0:T(8,128)(2,1)S(1)} %get-tuple-element.12), channel_id=1, source_target_pairs={{0,4},{2,6},{4,0},{6,2},{1,5},{3,7},{5,1},{7,3},{8,12},{10,14},{12... | collective-permute-start | bytes 1179656 | tf_op jit(solution)/shard_map/ppermute | solution.py:219
  167.5 6.4 %collective-permute-done.26 = bf16[1536,128]{1,0:T(8,128)(2,1)S(1)} collective-permute-done((bf16[1536,128]{1,0:T(8,128)(2,1)S(1)}, bf16[1536,128]{1,0:T(8,128)(2,1)S(1)}, u32[]{:S(2)}, u32[]{:S(2)}) %collective-permute-start.26) | collective-permute-done | bytes 393248 | tf_op jit(solution)/shard_map/ppermute | solution.py:219
  173.9 26.5 %collective-permute-done.27 = bf16[1536,128]{1,0:T(8,128)(2,1)S(1)} collective-permute-done((bf16[1536,128]{1,0:T(8,128)(2,1)S(1)}, bf16[1536,128]{1,0:T(8,128)(2,1)S(1)}, u32[]{:S(2)}, u32[]{:S(2)}) %collective-permute-start.27) | collective-permute-done | bytes 393248 | tf_op jit(solution)/shard_map/ppermute | solution.py:219
  (166 shorter events, 61.0 us)
Async XLA Ops:
  15.6 19.8 %collective-permute-start = (bf16[64,6272]{1,0:T(8,128)(2,1)}, bf16[64,6272]{1,0:T(8,128)(2,1)S(1)}, u32[]{:S(2)}, u32[]{:S(2)}) collective-permute-start(bf16[64,6272]{1,0:T(8,128)(2,1)} %copy.43), channel_id=1, source_target_pairs={{0,8},{8,0},{1,9},{9,1},{2,10},{10,2},{3,11},{11,3},{4,12},{12,4},... | collective-permute-start | bytes 2408456 | tf_op jit(solution)/shard_map/ppermute | solution.py:146
  17.8 31.4 %collective-permute-start.2 = (bf16[1,768,128]{2,1,0:T(8,128)(2,1)S(1)}, bf16[1,768,128]{2,1,0:T(8,128)(2,1)S(1)}, u32[]{:S(2)}, u32[]{:S(2)}) collective-permute-start(bf16[1,768,128]{2,1,0:T(8,128)(2,1)S(1)} %get-tuple-element.43.r_4_), channel_id=1, source_target_pairs={{0,4},{2,6},{4,0},{6,2},{1,5},{3,7},{5,1},{7,3},{8,12},{10,14},{12... | collective-permute-start | bytes 589832 | tf_op jit(solution)/shard_map/ppermute | solution.py:91
  43.0 47.8 %collective-permute-start.1 = (bf16[128,3200]{0,1:T(8,128)(2,1)}, bf16[128,3200]{0,1:T(8,128)(2,1)}, u32[]{:S(2)}, u32[]{:S(2)}) collective-permute-start(bf16[128,3200]{0,1:T(8,128)(2,1)} %maximum_maximum_fusion), channel_id=1, source_target_pairs={{0,1},{1,0},{2,3},{3,2},{4,5},{5,4},{6,7},{7,6},{8,9},{9,8},{10,11... | collective-permute-start | bytes 2457608 | tf_op jit(solution)/shard_map/ppermute | solution.py:151
  43.0 31.7 %collective-permute-start.12 = (bf16[2,768,128]{2,1,0:T(8,128)(2,1)S(1)}, bf16[2,768,128]{2,1,0:T(8,128)(2,1)S(1)}, u32[]{:S(2)}, u32[]{:S(2)}) collective-permute-start(bf16[2,768,128]{2,1,0:T(8,128)(2,1)S(1)} %pad_maximum_fusion.4.r_4_.r_3_), channel_id=1, source_target_pairs={{0,4},{2,6},{4,0},{6,2},{1,5},{3,7},{5,1},{7,3},{8,12},{10,14},{12... | collective-permute-start | bytes 1179656 | tf_op jit(solution)/shard_map/ppermute | solution.py:91
  43.4 8.9 %collective-permute-start.4 = (bf16[1,768,128]{2,1,0:T(8,128)(2,1)S(1)}, bf16[1,768,128]{2,1,0:T(8,128)(2,1)S(1)}, u32[]{:S(2)}, u32[]{:S(2)}) collective-permute-start(bf16[1,768,128]{2,1,0:T(8,128)(2,1)S(1)} %get-tuple-element.43.r_4_), channel_id=1, source_target_pairs={{0,2},{2,4},{4,6},{1,3},{3,5},{5,7},{8,10},{10,12},{12,14},{9,11},... | collective-permute-start | bytes 589832 | tf_op jit(solution)/shard_map/ppermute | solution.py:92
  44.7 12.0 %collective-permute-start.6 = (bf16[1,768,128]{2,1,0:T(8,128)(2,1)S(1)}, bf16[1,768,128]{2,1,0:T(8,128)(2,1)S(1)}, u32[]{:S(2)}, u32[]{:S(2)}) collective-permute-start(bf16[1,768,128]{2,1,0:T(8,128)(2,1)S(1)} %get-tuple-element.43.r_4_), channel_id=1, source_target_pairs={{2,0},{4,2},{6,4},{3,1},{5,3},{7,5},{10,8},{12,10},{14,12},{11,9},... | collective-permute-start | bytes 589832 | tf_op jit(solution)/shard_map/ppermute | solution.py:93
  49.3 16.8 %collective-permute-start.8 = (bf16[1,768,128]{2,1,0:T(8,128)(2,1)S(1)}, bf16[1,768,128]{2,1,0:T(8,128)(2,1)}, u32[]{:S(2)}, u32[]{:S(2)}) collective-permute-start(bf16[1,768,128]{2,1,0:T(8,128)(2,1)S(1)} %collective-permute-done.2.r_6_), channel_id=1, source_target_pairs={{4,6},{2,0},{5,7},{3,1},{12,14},{10,8},{13,15},{11,9},{20,22},{18,... | collective-permute-start | bytes 589832 | tf_op jit(solution)/shard_map/ppermute | solution.py:94
  52.3 24.0 %collective-permute-start.3 = (bf16[1,768,128]{2,1,0:T(8,128)(2,1)S(1)}, bf16[1,768,128]{2,1,0:T(8,128)(2,1)S(1)}, u32[]{:S(2)}, u32[]{:S(2)}) collective-permute-start(bf16[1,768,128]{2,1,0:T(8,128)(2,1)S(1)} %collective-permute-done.2.r_6_), channel_id=1, source_target_pairs={{0,16},{16,0},{1,17},{17,1},{2,18},{18,2},{3,19},{19,3},{4,20},{20... | collective-permute-start | bytes 589832 | tf_op jit(solution)/shard_map/ppermute | solution.py:129
  56.7 28.5 %collective-permute-start.14 = (bf16[2,768,128]{2,1,0:T(8,128)(2,1)S(1)}, bf16[2,768,128]{2,1,0:T(8,128)(2,1)S(1)}, u32[]{:S(2)}, u32[]{:S(2)}) collective-permute-start(bf16[2,768,128]{2,1,0:T(8,128)(2,1)S(1)} %pad_maximum_fusion.4.r_4_.r_3_), channel_id=1, source_target_pairs={{0,2},{2,4},{4,6},{1,3},{3,5},{5,7},{8,10},{10,12},{12,14},{9,11},... | collective-permute-start | bytes 1179656 | tf_op jit(solution)/shard_map/ppermute | solution.py:92
  66.1 20.6 %collective-permute-start.16 = (bf16[2,768,128]{2,1,0:T(8,128)(2,1)S(1)}, bf16[2,768,128]{2,1,0:T(8,128)(2,1)S(1)}, u32[]{:S(2)}, u32[]{:S(2)}) collective-permute-start(bf16[2,768,128]{2,1,0:T(8,128)(2,1)S(1)} %pad_maximum_fusion.4.r_4_.r_3_), channel_id=1, source_target_pairs={{2,0},{4,2},{6,4},{3,1},{5,3},{7,5},{10,8},{12,10},{14,12},{11,9},... | collective-permute-start | bytes 1179656 | tf_op jit(solution)/shard_map/ppermute | solution.py:93
  74.7 15.5 %collective-permute-start.18 = (bf16[2,768,128]{2,1,0:T(8,128)(2,1)S(1)}, bf16[2,768,128]{2,1,0:T(8,128)(2,1)S(1)}, u32[]{:S(2)}, u32[]{:S(2)}) collective-permute-start(bf16[2,768,128]{2,1,0:T(8,128)(2,1)S(1)} %collective-permute-done.12.r_6_.r_5_), channel_id=1, source_target_pairs={{4,6},{2,0},{5,7},{3,1},{12,14},{10,8},{13,15},{11,9},{20,22},{18,... | collective-permute-start | bytes 1179656 | tf_op jit(solution)/shard_map/ppermute | solution.py:94
  77.0 6.3 %collective-permute-start.5 = (bf16[1,768,128]{2,1,0:T(8,128)(2,1)S(1)}, bf16[1,768,128]{2,1,0:T(8,128)(2,1)S(1)}, u32[]{:S(2)}, u32[]{:S(2)}) collective-permute-start(bf16[1,768,128]{2,1,0:T(8,128)(2,1)S(1)} %collective-permute-done.4.r_8_), channel_id=1, source_target_pairs={{0,16},{16,0},{1,17},{17,1},{2,18},{18,2},{3,19},{19,3},{4,20},{20... | collective-permute-start | bytes 589832 | tf_op jit(solution)/shard_map/ppermute | solution.py:129
  84.0 10.2 %collective-permute-start.7 = (bf16[1,768,128]{2,1,0:T(8,128)(2,1)S(1)}, bf16[1,768,128]{2,1,0:T(8,128)(2,1)S(1)}, u32[]{:S(2)}, u32[]{:S(2)}) collective-permute-start(bf16[1,768,128]{2,1,0:T(8,128)(2,1)S(1)} %collective-permute-done.6.r_10_), channel_id=1, source_target_pairs={{0,16},{16,0},{1,17},{17,1},{2,18},{18,2},{3,19},{19,3},{4,20},{20... | collective-permute-start | bytes 589832 | tf_op jit(solution)/shard_map/ppermute | solution.py:129
  85.2 56.3 %collective-permute-start.13 = (bf16[2,768,128]{2,1,0:T(8,128)(2,1)S(1)}, bf16[2,768,128]{2,1,0:T(8,128)(2,1)}, u32[]{:S(2)}, u32[]{:S(2)}) collective-permute-start(bf16[2,768,128]{2,1,0:T(8,128)(2,1)S(1)} %collective-permute-done.12.r_6_.r_5_), channel_id=1, source_target_pairs={{0,16},{16,0},{1,17},{17,1},{2,18},{18,2},{3,19},{19,3},{4,20},{20... | collective-permute-start | bytes 1179656 | tf_op jit(solution)/shard_map/ppermute | solution.py:127
  86.7 54.8 %collective-permute-start.15 = (bf16[2,768,128]{2,1,0:T(8,128)(2,1)S(1)}, bf16[2,768,128]{2,1,0:T(8,128)(2,1)}, u32[]{:S(2)}, u32[]{:S(2)}) collective-permute-start(bf16[2,768,128]{2,1,0:T(8,128)(2,1)S(1)} %collective-permute-done.14.r_8_.r_7_), channel_id=1, source_target_pairs={{0,16},{16,0},{1,17},{17,1},{2,18},{18,2},{3,19},{19,3},{4,20},{20... | collective-permute-start | bytes 1179656 | tf_op jit(solution)/shard_map/ppermute | solution.py:127
  90.2 51.3 %collective-permute-start.17 = (bf16[2,768,128]{2,1,0:T(8,128)(2,1)S(1)}, bf16[2,768,128]{2,1,0:T(8,128)(2,1)}, u32[]{:S(2)}, u32[]{:S(2)}) collective-permute-start(bf16[2,768,128]{2,1,0:T(8,128)(2,1)S(1)} %collective-permute-done.16.r_10_.r_9_), channel_id=1, source_target_pairs={{0,16},{16,0},{1,17},{17,1},{2,18},{18,2},{3,19},{19,3},{4,20},{20... | collective-permute-start | bytes 1179656 | tf_op jit(solution)/shard_map/ppermute | solution.py:127
  90.7 50.8 %collective-permute-start.19 = (bf16[2,768,128]{2,1,0:T(8,128)(2,1)S(1)}, bf16[2,768,128]{2,1,0:T(8,128)(2,1)}, u32[]{:S(2)}, u32[]{:S(2)}) collective-permute-start(bf16[2,768,128]{2,1,0:T(8,128)(2,1)S(1)} %collective-permute-done.18.r_12_.r_11_), channel_id=1, source_target_pairs={{0,16},{16,0},{1,17},{17,1},{2,18},{18,2},{3,19},{19,3},{4,20},{20... | collective-permute-start | bytes 1179656 | tf_op jit(solution)/shard_map/ppermute | solution.py:127
  94.2 33.1 %collective-permute-start.9 = (bf16[1,768,128]{2,1,0:T(8,128)(2,1)}, bf16[1,768,128]{2,1,0:T(8,128)(2,1)S(1)}, u32[]{:S(2)}, u32[]{:S(2)}) collective-permute-start(bf16[1,768,128]{2,1,0:T(8,128)(2,1)} %collective-permute-done.8.r_12_), channel_id=1, source_target_pairs={{0,16},{16,0},{1,17},{17,1},{2,18},{18,2},{3,19},{19,3},{4,20},{20... | collective-permute-start | bytes 589832 | tf_op jit(solution)/shard_map/ppermute | solution.py:129
  139.3 5.5 %collective-permute-start.10 = (f32[128,256]{1,0:T(8,128)}, f32[128,256]{1,0:T(8,128)}, u32[]{:S(2)}, u32[]{:S(2)}) collective-permute-start(f32[128,256]{1,0:T(8,128)} %slice.204), channel_id=1, source_target_pairs={{0,1},{1,0},{2,3},{3,2},{4,5},{5,4},{6,7},{7,6},{8,9},{9,8},{10,11... | collective-permute-start | bytes 393224 | tf_op jit(solution)/shard_map/ppermute | solution.py:158
  158.6 7.3 %collective-permute-start.23 = (bf16[128,1536]{1,0:T(8,128)(2,1)S(1)}, bf16[128,1536]{1,0:T(8,128)(2,1)S(1)}, u32[]{:S(2)}, u32[]{:S(2)}) collective-permute-start(bf16[128,1536]{1,0:T(8,128)(2,1)S(1)} %get-tuple-element.29), channel_id=1, source_target_pairs={{0,1},{1,0},{2,3},{3,2},{4,5},{5,4},{6,7},{7,6},{8,9},{9,8},{10,11... | collective-permute-start | bytes 1179656 | tf_op jit(solution)/shard_map/ppermute | solution.py:248
  162.3 11.6 %collective-permute-start.26 = (bf16[1536,128]{1,0:T(8,128)(2,1)S(1)}, bf16[1536,128]{1,0:T(8,128)(2,1)S(1)}, u32[]{:S(2)}, u32[]{:S(2)}) collective-permute-start(bf16[1536,128]{1,0:T(8,128)(2,1)S(1)} %get-tuple-element.11), channel_id=1, source_target_pairs={{0,2},{2,4},{4,6},{6,0},{1,3},{3,5},{5,7},{7,1},{8,10},{10,12},{12... | collective-permute-start | bytes 1179656 | tf_op jit(solution)/shard_map/ppermute | solution.py:219
  162.4 38.0 %collective-permute-start.27 = (bf16[1536,128]{1,0:T(8,128)(2,1)S(1)}, bf16[1536,128]{1,0:T(8,128)(2,1)S(1)}, u32[]{:S(2)}, u32[]{:S(2)}) collective-permute-start(bf16[1536,128]{1,0:T(8,128)(2,1)S(1)} %get-tuple-element.12), channel_id=1, source_target_pairs={{0,4},{2,6},{4,0},{6,2},{1,5},{3,7},{5,1},{7,3},{8,12},{10,14},{12... | collective-permute-start | bytes 1179656 | tf_op jit(solution)/shard_map/ppermute | solution.py:219
  165.9 34.4 %collective-permute-start.28 = (bf16[1536,128]{1,0:T(8,128)(2,1)S(1)}, bf16[1536,128]{1,0:T(8,128)(2,1)S(1)}, u32[]{:S(2)}, u32[]{:S(2)}) collective-permute-start(bf16[1536,128]{1,0:T(8,128)(2,1)S(1)} %get-tuple-element.13), channel_id=1, source_target_pairs={{0,6},{2,0},{4,2},{6,4},{1,7},{3,1},{5,3},{7,5},{8,14},{10,8},{12,... | collective-permute-start | bytes 1179656 | tf_op jit(solution)/shard_map/ppermute | solution.py:219
  166.2 35.2 %collective-permute-start.24 = (bf16[64,3072]{1,0:T(8,128)(2,1)S(1)}, bf16[64,3072]{1,0:T(8,128)(2,1)S(1)}, u32[]{:S(2)}, u32[]{:S(2)}) collective-permute-start(bf16[64,3072]{1,0:T(8,128)(2,1)S(1)} %get-tuple-element.27), channel_id=1, source_target_pairs={{0,8},{8,0},{1,9},{9,1},{2,10},{10,2},{3,11},{11,3},{4,12},{12,4},... | collective-permute-start | bytes 1179656 | tf_op jit(solution)/shard_map/ppermute | solution.py:249
  (38 other events, 185.8 us)

commit v2 on v1

v2 whole, which is shorter than its diff:
```python
import jax
import jax.numpy as jnp
from jax import lax
from jax.experimental import pallas as pl
from jax.experimental.pallas import tpu as pltpu
from jax.sharding import PartitionSpec as P

BF = jnp.bfloat16
F32 = jnp.float32
VMEM = pl.BlockSpec(memory_space=pltpu.VMEM)
SMEM = pl.BlockSpec(memory_space=pltpu.SMEM)
ANY = pl.BlockSpec(memory_space=pl.ANY)
SWAP = [(0, 1), (1, 0)]
PARAMS = pltpu.CompilerParams(vmem_limit_bytes=48 * 1024 * 1024)


def call(body, outs, specs, *args, scratch=(), flops=0, nbytes=0):
    return pl.pallas_call(
        body,
        out_shape=outs,
        in_specs=specs,
        out_specs=jax.tree.map(lambda _: VMEM, outs),
        scratch_shapes=list(scratch),
        compiler_params=PARAMS,
        cost_estimate=pl.CostEstimate(flops=flops, bytes_accessed=nbytes, transcendentals=0),
    )(*args)


def mm(left, right, dims):
    return lax.dot_general(left, right, (dims, ((), ())), preferred_element_type=F32)


def weight_copies(layout, scal, refs, held, sems):
    slots, at, sem = [], 0, 0
    rows = held.shape[1]
    half = rows // 2
    ff = 128
    parts = held.shape[2] // ff
    mine = scal[len(layout)]
    near = pl.ds(pl.multiple_of(mine * half, 16), half)
    far = pl.ds(pl.multiple_of((1 - mine) * half, 16), half)
    for s, kind in enumerate(layout):
        copies = []
        for p in range(parts):
            lanes = pl.ds(p * ff, ff)
            if kind == "parts":
                pairs = [(refs[at + p].at[0], pl.ds(0, rows))]
            elif kind == "full":
                pairs = [(refs[at].at[p], pl.ds(0, rows))]
            else:
                pairs = [(refs[at].at[p], near), (refs[at + 1].at[p], far)]
            for source, where in pairs:
                copies.append(
                    pltpu.make_async_copy(source, held.at[s, where, lanes], sems.at[sem])
                )
                sem += 1
        at += {"parts": parts, "full": 1, "halves": 2}[kind]
        slots.append(copies)
    return slots


def copy_count(layout, parts):
    return sum(parts * (2 if kind == "halves" else 1) for kind in layout)


def pick(ids, label, value, width):
    zero = jnp.zeros((), value.dtype)
    return jnp.where(ids[:, 0:1] == label, value[:, :width], zero) + jnp.where(
        ids[:, 1:2] == label, value[:, width:], zero
    )


def forward_sums(layout, outs, scal, ids, rows, *refs):
    held, sems = refs[-2:]
    results = refs[-2 - outs : -2]
    width = held.shape[2]
    slots = weight_copies(layout, scal, refs, held, sems)
    for copies in slots:
        for c in copies:
            c.start()
    total = [None, None]
    for s, copies in enumerate(slots):
        for c in copies:
            c.wait()
        value = mm(rows[...], held[s], ((1,), (0,)))
        label = scal[s]
        for k in range(2):
            picked = jnp.where(ids[:, k : k + 1] == label, value, 0.0)
            total[k] = picked if total[k] is None else total[k] + picked
    m = results[0].shape[0]
    for j, out in enumerate(results):
        out[:, :width] = total[0][j * m : (j + 1) * m]
        out[:, width:] = total[1][j * m : (j + 1) * m]


def token_sums(layout, outs, scal, ids, grads, *refs):
    held, sems = refs[-2:]
    results = refs[-2 - outs : -2]
    width = held.shape[2]
    slots = weight_copies(layout, scal, refs, held, sems)
    for copies in slots:
        for c in copies:
            c.start()
    total = None
    for s, copies in enumerate(slots):
        for c in copies:
            c.wait()
        value = mm(pick(ids, scal[s], grads, width), held[s], ((1,), (1,)))
        total = value if total is None else total + value
    m = results[0].shape[0]
    for j, out in enumerate(results):
        out[...] = total[j * m : (j + 1) * m].astype(BF)


def down_products(count, scal, ids, scaled_t, hidden, *outs):
    ff = hidden.shape[1] // 2
    for j in range(count):
        rows = pick(ids, scal[j], hidden, ff)
        outs[j][...] = mm(scaled_t[...], rows, ((1,), (0,))).astype(outs[j].dtype)


def whole_sum(part, other):
    if not other:
        return part[...]
    m = part.shape[0] // 2
    o = other[0]
    return part[...] + jnp.concatenate([o[m:, :], o[:m, :]], axis=0).astype(F32)


def slot_weight(info, k):
    low, middle, high = (
        info[:, at + k : at + k + 1].astype(F32) for at in (6, 4, 2)
    )
    return (high + middle) + low


def hidden_step(info, part, *rest):
    other, (sums, hidden) = rest[:-2], rest[-2:]
    total = whole_sum(part, other)
    sums[...] = total
    ff = total.shape[1] // 4
    for k in range(2):
        gate = total[:, 2 * k * ff : (2 * k + 1) * ff]
        up = total[:, (2 * k + 1) * ff : (2 * k + 2) * ff]
        act = gate * jax.nn.sigmoid(gate)
        hidden[:, k * ff : (k + 1) * ff] = (slot_weight(info, k) * (act * up)).astype(BF)


def grad_step(info, sums, part, *rest):
    other, grads = rest[:-1], rest[-1]
    total = whole_sum(part, other)
    ff = total.shape[1] // 2
    for k in range(2):
        gate = sums[:, 2 * k * ff : (2 * k + 1) * ff]
        up = sums[:, (2 * k + 1) * ff : (2 * k + 2) * ff]
        hidden_grad = slot_weight(info, k) * total[:, k * ff : (k + 1) * ff]
        sig = jax.nn.sigmoid(gate)
        slope = sig * (1.0 + gate * (1.0 - sig))
        grads[:, 2 * k * ff : (2 * k + 1) * ff] = (hidden_grad * up * slope).astype(BF)
        grads[:, (2 * k + 1) * ff : (2 * k + 2) * ff] = (hidden_grad * (gate * sig)).astype(BF)


def split3(value):
    high = lax.reduce_precision(value, 8, 7)
    rest = value - high
    middle = lax.reduce_precision(rest, 8, 7)
    low = rest - middle
    return [high.astype(BF), middle.astype(BF), low.astype(BF)]


def after(value, *earlier):
    return lax.optimization_barrier((value, *earlier))[0]


def per_device(tokens, cotangent, expert_ids, combine, gate_weight, up_weight, down_weight):
    n = lax.axis_size("expert")
    nx, nc = lax.axis_size("fsdp"), lax.axis_size("dp")
    g, f, e, d = (lax.axis_index(a) for a in ("groups", "fsdp", "expert", "dp"))
    own, width = tokens.shape
    quarter, ff = gate_weight.shape[1:]
    half = quarter // 2
    pp = lax.ppermute
    small = nx == 2 and nc == 2

    def partner(block, k):
        return pp(block, "expert", [(i, i ^ k) for i in range(n)])

    gu_own = jnp.concatenate([gate_weight, up_weight])
    gu_near = lax.dynamic_slice_in_dim(gu_own, g * half, half, 1)
    dn_near = lax.dynamic_slice_in_dim(down_weight, g * half, half, 1)
    far_ones = list(range(n - 1, 1, -1))
    gu, dn = {}, {}
    for k in far_ones:
        gu[k] = partner(gu_near, k)
    gu[1] = partner(gu_own, 1)
    for k in far_ones:
        dn[k] = partner(after(dn_near, gu[k]), k)
    dn[1] = partner(after(down_weight, gu[1]), 1)
    labels = jnp.stack([e, e ^ 1] + [e ^ k for k in far_ones] + [g]).astype(jnp.int32)
    layout = ["parts", "full"] + ["halves"] * len(far_ones)
    gu_refs, dn_refs = [gate_weight, up_weight, gu[1]], [down_weight, dn[1]]
    for k in far_ones:
        gu_refs += [gu[k], pp(gu[k], "groups", SWAP)]
    for k in far_ones:
        dn_refs += [dn[k], pp(dn[k], "groups", SWAP)]

    tokens = after(tokens, gu_near)
    cotangent = after(cotangent, gu_near)
    extra = jnp.concatenate(
        [expert_ids.astype(F32).astype(BF)]
        + split3(combine)
        + [jnp.zeros((own, 120), BF)],
        axis=1,
    )
    if small:
        mine = 2 * own

        def halve(a, at):
            m = a.shape[1] // 2
            return jnp.where(at == 0, a[:, :m], a[:, m:])

        def spread(a):
            a = jnp.concatenate([halve(a, f), pp(halve(a, 1 - f), "fsdp", SWAP)])
            return jnp.concatenate([halve(a, d), pp(halve(a, 1 - d), "dp", SWAP)])

        tok, cot = spread(tokens), spread(cotangent)
        mine_info = jnp.concatenate([extra, pp(extra, "fsdp", SWAP)])
        info = jnp.concatenate([mine_info, pp(mine_info, "dp", SWAP)])
        blocks = 2

        def reduce_rows(parts):
            total = parts[0] + pp(parts[1], "dp", SWAP)
            return [total, pp(total.astype(BF), "fsdp", SWAP)]

        def share_rows(rows):
            return jnp.concatenate([rows, pp(rows, "dp", SWAP)])

    else:
        plane = nx * nc
        mine = plane * own
        blocks = 1

        def spread(a):
            a = a.reshape(own, plane, quarter).transpose(1, 0, 2)
            return lax.all_to_all(a, ("fsdp", "dp"), 0, 0, tiled=True).reshape(mine, quarter)

        tok, cot = spread(tokens), spread(cotangent)
        mine_info = extra
        info = lax.all_gather(extra, ("fsdp", "dp"), axis=0, tiled=True)

        def reduce_rows(parts):
            return [lax.psum_scatter(parts[0], ("fsdp", "dp"), scatter_dimension=0, tiled=True)]

        def share_rows(rows):
            return lax.all_gather(rows, ("fsdp", "dp"), axis=0, tiled=True)

    ids = info[:, :2].astype(jnp.int32)
    rows = tok.shape[0]
    cot_t = cot.T

    def held(parts):
        return [
            pltpu.VMEM((n, quarter, parts * ff), BF),
            pltpu.SemaphoreType.DMA((copy_count(layout, parts),)),
        ]

    def sums(a, refs, parts):
        return call(
            lambda *r: forward_sums(layout, blocks, *r),
            [jax.ShapeDtypeStruct((mine, 2 * parts * ff), F32)] * blocks,
            [SMEM, VMEM, VMEM] + [ANY] * len(refs),
            labels,
            ids,
            a,
            *refs,
            scratch=held(parts),
            flops=2 * rows * quarter * n * parts * ff,
            nbytes=2 * n * quarter * parts * ff,
        )

    first = reduce_rows(sums(tok, gu_refs, 2))
    m = first[0].shape[0]
    full_sums, hidden = call(
        hidden_step,
        [jax.ShapeDtypeStruct((m, 4 * ff), F32), jax.ShapeDtypeStruct((m, 2 * ff), BF)],
        [VMEM] * (1 + len(first)),
        mine_info,
        *first,
    )
    hidden = share_rows(hidden)
    targets = jnp.stack([e ^ k for k in range(n)]).astype(jnp.int32)
    pieces = call(
        lambda *r: down_products(n, *r),
        [jax.ShapeDtypeStruct((quarter, ff), F32 if k == 0 else BF) for k in range(n)],
        [SMEM, VMEM, VMEM, VMEM],
        targets,
        ids,
        cot_t,
        hidden,
    )
    grad_down = pieces[0]
    for k in range(1, n):
        grad_down = grad_down + partner(pieces[k], k).astype(F32)

    second = reduce_rows(sums(after(cot, *pieces), dn_refs, 1))
    grads = call(
        grad_step,
        jax.ShapeDtypeStruct((m, 4 * ff), BF),
        [VMEM] * (2 + len(second)),
        mine_info,
        full_sums,
        *second,
    )
    grads = share_rows(grads)
    back = call(
        lambda *r: token_sums(layout, blocks, *r),
        [jax.ShapeDtypeStruct((mine, quarter), BF)] * blocks,
        [SMEM, VMEM, VMEM] + [ANY] * len(gu_refs),
        labels,
        ids,
        grads,
        *gu_refs,
        scratch=held(2),
        flops=4 * rows * quarter * n * ff,
        nbytes=4 * n * quarter * ff,
    )
    if small:

        def join(kept, came, at):
            return jnp.where(
                at == 0,
                jnp.concatenate([kept, came], axis=1),
                jnp.concatenate([came, kept], axis=1),
            )

        back = join(back[0], pp(back[1], "dp", SWAP), d)
        grad_tokens = join(back[:own], pp(back[own:], "fsdp", SWAP), f)
    else:
        back = lax.all_to_all(
            back[0].reshape(plane, own, quarter), ("fsdp", "dp"), 0, 0, tiled=True
        )
        grad_tokens = back.transpose(1, 0, 2).reshape(own, width)
    return (grad_tokens, grad_down[None])


def solution(mesh):
    rows = P(("groups", "fsdp", "expert", "dp"), None)
    weights = P("expert", ("fsdp", "dp"), None)
    return jax.shard_map(
        per_device,
        mesh=mesh,
        in_specs=(rows, rows, rows, rows, weights, weights, weights),
        out_specs=(rows, P(("groups", "expert"), ("fsdp", "dp"), None)),
        check_vma=False,
    )
```

time: 204 us -> 142 us (0.70)
  the two profiles are of different devices: /device:TPU:24 before, /device:TPU:0 now
where the time goes in v2:
time: 142 us
  waiting for transfers between devices  85.2 us (60%)
  starting transfers between devices  28.3 us (20%)
  Pallas kernels  12 us (8%)
  other arithmetic  8.46 us (6%)
  local copies, waits for them, and re-layouts  6.69 us (5%)
    ppermute x9, waiting for transfers between devices, partner(): return pp(block, 'expert', [(i, i ^ k) for i in range(n)])  67.2 us
    ppermute x9, starting transfers between devices, partner(): return pp(block, 'expert', [(i, i ^ k) for i in range(n)])  12.5 us
    pallas_call x6, Pallas kernels, call(): pl.pallas_call(body, out_shape=outs, in_specs=specs, out_specs=jax.tree.m...  12 us
    ppermute x1, waiting for transfers between devices, per_device(): mine_info = jnp.concatenate([extra, pp(extra, 'fsdp', SWAP)])  7.83 us
    ppermute x2, waiting for transfers between devices, per_device(): gu_refs += [gu[k], pp(gu[k], 'groups', SWAP)]  4.76 us
    ppermute x2, starting transfers between devices, reduce_rows(): return [total, pp(total.astype(BF), 'fsdp', SWAP)]  3.12 us
    ppermute x2, starting transfers between devices, per_device(): gu_refs += [gu[k], pp(gu[k], 'groups', SWAP)]  3.04 us
    ppermute x2, starting transfers between devices, per_device(): dn_refs += [dn[k], pp(dn[k], 'groups', SWAP)]  3.04 us
  transfers between devices with their start and end apart: 27, of which 11 were waited for; matrix products, arithmetic and copies ran while one was open for 7% of the time, Pallas kernels for 4%

profile of v2, /device:TPU:0, one launch (start us, length us, event | category | flops | bytes accessed | tf_op | source)
XLA Modules:
  0.0 141.7 jit_solution(3752290756789151223)
XLA Ops:
  0.6 1.8 %constant_dynamic-update-slice_fusion.1 = bf16[2,1536,128]{2,1,0:T(8,128)(2,1)} fusion(bf16[1,1536,128]{2,1,0:T(8,128)(2,1)} %r_3_.5), kind=kLoop, calls=%fused_computation.31 | loop fusion | bytes 786432
  4.3 5.1 %collective-permute-start.5 = (bf16[2,768,128]{2,1,0:T(8,128)(2,1)S(1)}, bf16[2,768,128]{2,1,0:T(8,128)(2,1)S(1)}, u32[]{:S(2)}, u32[]{:S(2)}) collective-permute-start(bf16[2,768,128]{2,1,0:T(8,128)(2,1)S(1)} %constant_dynamic-slice_fusion.1), channel_id=1, source_target_pairs={{0,6},{2,4},{4,2},{6,0},{1,7},{3,5},{5,3},{7,1},{8,14},{10,12},{12... | collective-permute-start | bytes 1179656 | tf_op jit(solution)/shard_map/ppermute | solution.py:186
  13.5 7.8 %collective-permute-done = bf16[64,128]{1,0:T(8,128)(2,1)S(1)} collective-permute-done((bf16[64,128]{1,0:T(8,128)(2,1)S(1)}, bf16[64,128]{1,0:T(8,128)(2,1)S(1)}, u32[]{:S(2)}, u32[]{:S(2)}) %collective-permute-start) | collective-permute-done | bytes 16416 | tf_op jit(solution)/shard_map/ppermute | solution.py:227
  22.9 1.5 %collective-permute-start.6 = (bf16[2,768,128]{2,1,0:T(8,128)(2,1)S(1)}, bf16[2,768,128]{2,1,0:T(8,128)(2,1)S(1)}, u32[]{:S(2)}, u32[]{:S(2)}) collective-permute-start(bf16[2,768,128]{2,1,0:T(8,128)(2,1)S(1)} %collective-permute-done.5.r_6_), channel_id=1, source_target_pairs={{0,16},{16,0},{1,17},{17,1},{2,18},{18,2},{3,19},{19,3},{4,20},{20... | collective-permute-start | bytes 1179656 | tf_op jit(solution)/shard_map/ppermute | solution.py:203
  24.4 18.6 %collective-permute-done.7.r_8_ = bf16[2,768,128]{2,1,0:T(8,128)(2,1)S(1)} collective-permute-done((bf16[2,768,128]{2,1,0:T(8,128)(2,1)S(1)}, bf16[2,768,128]{2,1,0:T(8,128)(2,1)S(1)}, u32[]{:S(2)}, u32[]{:S(2)}) %collective-permute-start.7) | collective-permute-done | bytes 393248 | tf_op jit(solution)/shard_map/ppermute | solution.py:186
  43.0 1.5 %collective-permute-start.8 = (bf16[2,768,128]{2,1,0:T(8,128)(2,1)S(1)}, bf16[2,768,128]{2,1,0:T(8,128)(2,1)S(1)}, u32[]{:S(2)}, u32[]{:S(2)}) collective-permute-start(bf16[2,768,128]{2,1,0:T(8,128)(2,1)S(1)} %collective-permute-done.7.r_8_), channel_id=1, source_target_pairs={{0,16},{16,0},{1,17},{17,1},{2,18},{18,2},{3,19},{19,3},{4,20},{20... | collective-permute-start | bytes 1179656 | tf_op jit(solution)/shard_map/ppermute | solution.py:203
  48.4 4.8 %collective-permute-done.8.r_9_ = bf16[2,768,128]{2,1,0:T(8,128)(2,1)S(1)} collective-permute-done((bf16[2,768,128]{2,1,0:T(8,128)(2,1)S(1)}, bf16[2,768,128]{2,1,0:T(8,128)(2,1)S(1)}, u32[]{:S(2)}, u32[]{:S(2)}) %collective-permute-start.8) | collective-permute-done | bytes 393248 | tf_op jit(solution)/shard_map/ppermute | solution.py:203
  53.2 3.4 %shard_map.86 = (f32[128,512]{1,0:T(8,128)S(1)}, f32[128,512]{1,0:T(8,128)S(1)}) custom-call(s32[5]{0:T(128)S(1)} %stack.30.r_0_, s32[256,2]{1,0:T(8,128)S(1)} %fusion.2.r_1_, bf16[256,1536]{1,0:T(8,128)(2,1)S(1)} %pad_maximum_fusion.r_2_, bf16[1,1536,128]{2,1,0:T(8,128)(2,1)S(1)} %copy-done, bf16[1,1536,128]{2,1,0:T(8,128)(2,1)S(1)} %copy-done.1, ...), custom_call_target="tpu_custom_call" | custom-call | flops 805306368 | bytes 3145728 | tf_op jit(solution)/shard_map/pallas_call | solution.py:18
  58.4 2.4 %collective-permute-start.15 = (bf16[1,768,128]{2,1,0:T(8,128)(2,1)S(1)}, bf16[1,768,128]{2,1,0:T(8,128)(2,1)S(1)}, u32[]{:S(2)}, u32[]{:S(2)}) collective-permute-start(bf16[1,768,128]{2,1,0:T(8,128)(2,1)S(1)} %constant_dynamic-slice_fusion), channel_id=1, source_target_pairs={{0,6},{2,4},{4,2},{6,0},{1,7},{3,5},{5,3},{7,1},{8,14},{10,12},{12... | collective-permute-start | bytes 589832 | tf_op jit(solution)/shard_map/ppermute | solution.py:186
  60.8 1.6 %collective-permute-start.10 = (bf16[128,512]{1,0:T(8,128)(2,1)S(1)}, bf16[128,512]{1,0:T(8,128)(2,1)S(1)}, u32[]{:S(2)}, u32[]{:S(2)}) collective-permute-start(bf16[128,512]{1,0:T(8,128)(2,1)S(1)} %get-tuple-element.40), channel_id=1, source_target_pairs={{0,8},{8,0},{1,9},{9,1},{2,10},{10,2},{3,11},{11,3},{4,12},{12,4},... | collective-permute-start | bytes 393224 | tf_op jit(solution)/shard_map/ppermute | solution.py:233
  62.4 5.7 %collective-permute-done.15.r_5_ = bf16[1,768,128]{2,1,0:T(8,128)(2,1)S(1)} collective-permute-done((bf16[1,768,128]{2,1,0:T(8,128)(2,1)S(1)}, bf16[1,768,128]{2,1,0:T(8,128)(2,1)S(1)}, u32[]{:S(2)}, u32[]{:S(2)}) %collective-permute-start.15) | collective-permute-done | bytes 196640 | tf_op jit(solution)/shard_map/ppermute | solution.py:186
  69.6 8.4 %collective-permute-done.17.r_7_ = bf16[1,768,128]{2,1,0:T(8,128)(2,1)} collective-permute-done((bf16[1,768,128]{2,1,0:T(8,128)(2,1)S(1)}, bf16[1,768,128]{2,1,0:T(8,128)(2,1)}, u32[]{:S(2)}, u32[]{:S(2)}) %collective-permute-start.17) | collective-permute-done | bytes 196640 | tf_op jit(solution)/shard_map/ppermute | solution.py:186
  78.0 1.5 %collective-permute-start.18 = (bf16[1,768,128]{2,1,0:T(8,128)(2,1)}, bf16[1,768,128]{2,1,0:T(8,128)(2,1)}, u32[]{:S(2)}, u32[]{:S(2)}) collective-permute-start(bf16[1,768,128]{2,1,0:T(8,128)(2,1)} %collective-permute-done.17.r_7_), channel_id=1, source_target_pairs={{0,16},{16,0},{1,17},{17,1},{2,18},{18,2},{3,19},{19,3},{4,20},{20... | collective-permute-start | bytes 589832 | tf_op jit(solution)/shard_map/ppermute | solution.py:205
  83.6 1.8 %shard_map.88 = (f32[1536,128]{1,0:T(8,128)S(1)}, bf16[1536,128]{1,0:T(8,128)(2,1)S(1)}, bf16[1536,128]{1,0:T(8,128)(2,1)S(1)}, bf16[1536,128]{1,0:T(8,128)(2,1)S(1)}) custom-call(s32[4]{0:T(128)S(1)} %pad_add_fusion.r_0_, s32[256,2]{1,0:T(8,128)S(1)} %fusion.2.r_1_, bf16[1536,256]{1,0:T(8,128)(2,1)S(1)} %copy.17.r_2_, ...), custom_call_target="tpu_custom_call" | custom-call | tf_op jit(solution)/shard_map/pallas_call | solution.py:18
  85.4 4.3 %collective-permute-done.14.r_4_ = bf16[1,1536,128]{2,1,0:T(8,128)(2,1)} collective-permute-done((bf16[1,1536,128]{2,1,0:T(8,128)(2,1)}, bf16[1,1536,128]{2,1,0:T(8,128)(2,1)}, u32[]{:S(2)}, u32[]{:S(2)}) %collective-permute-start.14) | collective-permute-done | bytes 393248 | tf_op jit(solution)/shard_map/ppermute | solution.py:186
  89.7 3.0 %shard_map.89 = (f32[128,256]{1,0:T(8,128)S(1)}, f32[128,256]{1,0:T(8,128)S(1)}) custom-call(s32[5]{0:T(128)S(1)} %stack.30.r_0_, s32[256,2]{1,0:T(8,128)S(1)} %fusion.2.r_1_, bf16[256,1536]{1,0:T(8,128)(2,1)S(1)} %get-tuple-element.30.r_2_, bf16[1,1536,128]{2,1,0:T(8,128)(2,1)} %r_3_.4, bf16[1,1536,128]{2,1,0:T(8,128)(2,1)} %collective-permute-done.14.r_4_, ...), custom_call_target="tpu_custom_call" | custom-call | flops 402653184 | bytes 1572864 | tf_op jit(solution)/shard_map/pallas_call | solution.py:18
  94.2 1.6 %collective-permute-start.20 = (bf16[128,256]{1,0:T(8,128)(2,1)S(1)}, bf16[128,256]{1,0:T(8,128)(2,1)S(1)}, u32[]{:S(2)}, u32[]{:S(2)}) collective-permute-start(bf16[128,256]{1,0:T(8,128)(2,1)S(1)} %get-tuple-element.38), channel_id=1, source_target_pairs={{0,8},{8,0},{1,9},{9,1},{2,10},{10,2},{3,11},{11,3},{4,12},{12,4},... | collective-permute-start | bytes 196616 | tf_op jit(solution)/shard_map/ppermute | solution.py:233
  95.8 2.8 %collective-permute-done.20.rest_0_ = bf16[128,256]{1,0:T(8,128)(2,1)S(1)} collective-permute-done((bf16[128,256]{1,0:T(8,128)(2,1)S(1)}, bf16[128,256]{1,0:T(8,128)(2,1)S(1)}, u32[]{:S(2)}, u32[]{:S(2)}) %collective-permute-start.20) | collective-permute-done | bytes 65568 | tf_op jit(solution)/shard_map/ppermute | solution.py:233
  100.2 2.8 %shard_map.91 = (bf16[128,1536]{1,0:T(8,128)(2,1)S(1)}, bf16[128,1536]{1,0:T(8,128)(2,1)S(1)}) custom-call(s32[5]{0:T(128)S(1)} %stack.30.r_0_, s32[256,2]{1,0:T(8,128)S(1)} %fusion.2.r_1_, bf16[256,512]{1,0:T(8,128)(2,1)S(1)} %pad_maximum_fusion.4.r_2_, bf16[1,1536,128]{2,1,0:T(8,128)(2,1)S(1)} %copy-done, bf16[1,1536,128]{2,1,0:T(8,128)(2,1)S(1)} %copy-done.1, ...), custom_call_target="tpu_custom_call" | custom-call | flops 805306368 | bytes 3145728 | tf_op jit(solution)/shard_map/pallas_call | solution.py:18
  103.2 2.3 %collective-permute-start.26 = (bf16[1536,128]{1,0:T(8,128)(2,1)S(1)}, bf16[1536,128]{1,0:T(8,128)(2,1)S(1)}, u32[]{:S(2)}, u32[]{:S(2)}) collective-permute-start(bf16[1536,128]{1,0:T(8,128)(2,1)S(1)} %get-tuple-element.29), channel_id=1, source_target_pairs={{0,6},{2,4},{4,2},{6,0},{1,7},{3,5},{5,3},{7,1},{8,14},{10,12},{12... | collective-permute-start | bytes 1179656 | tf_op jit(solution)/shard_map/ppermute | solution.py:186
  105.5 2.1 %collective-permute-start.24 = (bf16[1536,128]{1,0:T(8,128)(2,1)S(1)}, bf16[1536,128]{1,0:T(8,128)(2,1)S(1)}, u32[]{:S(2)}, u32[]{:S(2)}) collective-permute-start(bf16[1536,128]{1,0:T(8,128)(2,1)S(1)} %get-tuple-element.27), channel_id=1, source_target_pairs={{0,2},{2,0},{4,6},{6,4},{1,3},{3,1},{5,7},{7,5},{8,10},{10,8},{12,... | collective-permute-start | bytes 1179656 | tf_op jit(solution)/shard_map/ppermute | solution.py:186
  107.9 1.6 %collective-permute-start.23 = (bf16[64,3072]{1,0:T(8,128)(2,1)S(1)}, bf16[64,3072]{1,0:T(8,128)(2,1)S(1)}, u32[]{:S(2)}, u32[]{:S(2)}) collective-permute-start(bf16[64,3072]{1,0:T(8,128)(2,1)S(1)} %get-tuple-element.43), channel_id=1, source_target_pairs={{0,8},{8,0},{1,9},{9,1},{2,10},{10,2},{3,11},{11,3},{4,12},{12,4},... | collective-permute-start | bytes 1179656 | tf_op jit(solution)/shard_map/ppermute | solution.py:337
  109.4 7.7 %collective-permute-done.26 = bf16[1536,128]{1,0:T(8,128)(2,1)S(1)} collective-permute-done((bf16[1536,128]{1,0:T(8,128)(2,1)S(1)}, bf16[1536,128]{1,0:T(8,128)(2,1)S(1)}, u32[]{:S(2)}, u32[]{:S(2)}) %collective-permute-start.26) | collective-permute-done | bytes 393248 | tf_op jit(solution)/shard_map/ppermute | solution.py:186
  117.1 22.5 %collective-permute-done.25 = bf16[1536,128]{1,0:T(8,128)(2,1)S(1)} collective-permute-done((bf16[1536,128]{1,0:T(8,128)(2,1)S(1)}, bf16[1536,128]{1,0:T(8,128)(2,1)S(1)}, u32[]{:S(2)}, u32[]{:S(2)}) %collective-permute-start.25) | collective-permute-done | bytes 393248 | tf_op jit(solution)/shard_map/ppermute | solution.py:186
  (102 shorter events, 24.3 us)
Async XLA Ops:
  4.3 18.6 %collective-permute-start.5 = (bf16[2,768,128]{2,1,0:T(8,128)(2,1)S(1)}, bf16[2,768,128]{2,1,0:T(8,128)(2,1)S(1)}, u32[]{:S(2)}, u32[]{:S(2)}) collective-permute-start(bf16[2,768,128]{2,1,0:T(8,128)(2,1)S(1)} %constant_dynamic-slice_fusion.1), channel_id=1, source_target_pairs={{0,6},{2,4},{4,2},{6,0},{1,7},{3,5},{5,3},{7,1},{8,14},{10,12},{12... | collective-permute-start | bytes 1179656 | tf_op jit(solution)/shard_map/ppermute | solution.py:186
  9.4 33.6 %collective-permute-start.7 = (bf16[2,768,128]{2,1,0:T(8,128)(2,1)S(1)}, bf16[2,768,128]{2,1,0:T(8,128)(2,1)S(1)}, u32[]{:S(2)}, u32[]{:S(2)}) collective-permute-start(bf16[2,768,128]{2,1,0:T(8,128)(2,1)S(1)} %constant_dynamic-slice_fusion.1), channel_id=1, source_target_pairs={{0,4},{2,6},{4,0},{6,2},{1,5},{3,7},{5,1},{7,3},{8,12},{10,14},{12... | collective-permute-start | bytes 1179656 | tf_op jit(solution)/shard_map/ppermute | solution.py:186
  10.2 11.1 %collective-permute-start.2 = (bf16[64,3072]{1,0:T(8,128)(2,1)}, bf16[64,3072]{1,0:T(8,128)(2,1)S(1)}, u32[]{:S(2)}, u32[]{:S(2)}) collective-permute-start(bf16[64,3072]{1,0:T(8,128)(2,1)} %get-tuple-element.53), channel_id=1, source_target_pairs={{0,8},{8,0},{1,9},{9,1},{2,10},{10,2},{3,11},{11,3},{4,12},{12,4},... | collective-permute-start | bytes 1179656 | tf_op jit(solution)/shard_map/ppermute | solution.py:223
  12.3 9.1 %collective-permute-start = (bf16[64,128]{1,0:T(8,128)(2,1)S(1)}, bf16[64,128]{1,0:T(8,128)(2,1)S(1)}, u32[]{:S(2)}, u32[]{:S(2)}) collective-permute-start(bf16[64,128]{1,0:T(8,128)(2,1)S(1)} %concatenate.43), channel_id=1, source_target_pairs={{0,8},{8,0},{1,9},{9,1},{2,10},{10,2},{3,11},{11,3},{4,12},{12,4},... | collective-permute-start | bytes 49160 | tf_op jit(solution)/shard_map/ppermute | solution.py:227
  12.9 35.5 %collective-permute-start.4 = (bf16[2,1536,128]{2,1,0:T(8,128)(2,1)}, bf16[2,1536,128]{2,1,0:T(8,128)(2,1)S(1)}, u32[]{:S(2)}, u32[]{:S(2)}) collective-permute-start(bf16[2,1536,128]{2,1,0:T(8,128)(2,1)} %constant_dynamic-update-slice_fusion), channel_id=1, source_target_pairs={{0,2},{2,0},{4,6},{6,4},{1,3},{3,1},{5,7},{7,5},{8,10},{10,8},{12,... | collective-permute-start | bytes 2359304 | tf_op jit(solution)/shard_map/ppermute | solution.py:186
  21.3 24.2 %collective-permute-start.1 = (bf16[128,128]{1,0:T(8,128)(2,1)S(1)}, bf16[128,128]{1,0:T(8,128)(2,1)S(1)}, u32[]{:S(2)}, u32[]{:S(2)}) collective-permute-start(bf16[128,128]{1,0:T(8,128)(2,1)S(1)} %pad_maximum_fusion.8.info), channel_id=1, source_target_pairs={{0,1},{1,0},{2,3},{3,2},{4,5},{5,4},{6,7},{7,6},{8,9},{9,8},{10,11... | collective-permute-start | bytes 98312 | tf_op jit(solution)/shard_map/ppermute | solution.py:228
  22.4 24.7 %collective-permute-start.3 = (bf16[128,1536]{1,0:T(8,128)(2,1)}, bf16[128,1536]{1,0:T(8,128)(2,1)}, u32[]{:S(2)}, u32[]{:S(2)}) collective-permute-start(bf16[128,1536]{1,0:T(8,128)(2,1)} %get-tuple-element.51), channel_id=1, source_target_pairs={{0,1},{1,0},{2,3},{3,2},{4,5},{5,4},{6,7},{7,6},{8,9},{9,8},{10,11... | collective-permute-start | bytes 1179656 | tf_op jit(solution)/shard_map/ppermute | solution.py:224
  22.9 25.5 %collective-permute-start.6 = (bf16[2,768,128]{2,1,0:T(8,128)(2,1)S(1)}, bf16[2,768,128]{2,1,0:T(8,128)(2,1)S(1)}, u32[]{:S(2)}, u32[]{:S(2)}) collective-permute-start(bf16[2,768,128]{2,1,0:T(8,128)(2,1)S(1)} %collective-permute-done.5.r_6_), channel_id=1, source_target_pairs={{0,16},{16,0},{1,17},{17,1},{2,18},{18,2},{3,19},{19,3},{4,20},{20... | collective-permute-start | bytes 1179656 | tf_op jit(solution)/shard_map/ppermute | solution.py:203
  43.0 10.1 %collective-permute-start.8 = (bf16[2,768,128]{2,1,0:T(8,128)(2,1)S(1)}, bf16[2,768,128]{2,1,0:T(8,128)(2,1)S(1)}, u32[]{:S(2)}, u32[]{:S(2)}) collective-permute-start(bf16[2,768,128]{2,1,0:T(8,128)(2,1)S(1)} %collective-permute-done.7.r_8_), channel_id=1, source_target_pairs={{0,16},{16,0},{1,17},{17,1},{2,18},{18,2},{3,19},{19,3},{4,20},{20... | collective-permute-start | bytes 1179656 | tf_op jit(solution)/shard_map/ppermute | solution.py:203
  45.6 11.1 %collective-permute-start.11 = (bf16[64,3072]{1,0:T(8,128)(2,1)}, bf16[64,3072]{1,0:T(8,128)(2,1)S(1)}, u32[]{:S(2)}, u32[]{:S(2)}) collective-permute-start(bf16[64,3072]{1,0:T(8,128)(2,1)} %get-tuple-element.49), channel_id=1, source_target_pairs={{0,8},{8,0},{1,9},{9,1},{2,10},{10,2},{3,11},{11,3},{4,12},{12,4},... | collective-permute-start | bytes 1179656 | tf_op jit(solution)/shard_map/ppermute | solution.py:223
  56.6 4.1 %collective-permute-start.9 = (f32[128,512]{1,0:T(8,128)S(1)}, f32[128,512]{1,0:T(8,128)S(1)}, u32[]{:S(2)}, u32[]{:S(2)}) collective-permute-start(f32[128,512]{1,0:T(8,128)S(1)} %get-tuple-element.22), channel_id=1, source_target_pairs={{0,1},{1,0},{2,3},{3,2},{4,5},{5,4},{6,7},{7,6},{8,9},{9,8},{10,11... | collective-permute-start | bytes 786440 | tf_op jit(solution)/shard_map/ppermute | solution.py:232
  56.9 23.4 %collective-permute-start.12 = (bf16[128,1536]{1,0:T(8,128)(2,1)S(1)}, bf16[128,1536]{1,0:T(8,128)(2,1)S(1)}, u32[]{:S(2)}, u32[]{:S(2)}) collective-permute-start(bf16[128,1536]{1,0:T(8,128)(2,1)S(1)} %get-tuple-element.47), channel_id=1, source_target_pairs={{0,1},{1,0},{2,3},{3,2},{4,5},{5,4},{6,7},{7,6},{8,9},{9,8},{10,11... | collective-permute-start | bytes 1179656 | tf_op jit(solution)/shard_map/ppermute | solution.py:224
  58.4 9.7 %collective-permute-start.15 = (bf16[1,768,128]{2,1,0:T(8,128)(2,1)S(1)}, bf16[1,768,128]{2,1,0:T(8,128)(2,1)S(1)}, u32[]{:S(2)}, u32[]{:S(2)}) collective-permute-start(bf16[1,768,128]{2,1,0:T(8,128)(2,1)S(1)} %constant_dynamic-slice_fusion), channel_id=1, source_target_pairs={{0,6},{2,4},{4,2},{6,0},{1,7},{3,5},{5,3},{7,1},{8,14},{10,12},{12... | collective-permute-start | bytes 589832 | tf_op jit(solution)/shard_map/ppermute | solution.py:186
  60.7 17.3 %collective-permute-start.17 = (bf16[1,768,128]{2,1,0:T(8,128)(2,1)S(1)}, bf16[1,768,128]{2,1,0:T(8,128)(2,1)}, u32[]{:S(2)}, u32[]{:S(2)}) collective-permute-start(bf16[1,768,128]{2,1,0:T(8,128)(2,1)S(1)} %constant_dynamic-slice_fusion), channel_id=1, source_target_pairs={{0,4},{2,6},{4,0},{6,2},{1,5},{3,7},{5,1},{7,3},{8,12},{10,14},{12... | collective-permute-start | bytes 589832 | tf_op jit(solution)/shard_map/ppermute | solution.py:186
  60.8 18.7 %collective-permute-start.10 = (bf16[128,512]{1,0:T(8,128)(2,1)S(1)}, bf16[128,512]{1,0:T(8,128)(2,1)S(1)}, u32[]{:S(2)}, u32[]{:S(2)}) collective-permute-start(bf16[128,512]{1,0:T(8,128)(2,1)S(1)} %get-tuple-element.40), channel_id=1, source_target_pairs={{0,8},{8,0},{1,9},{9,1},{2,10},{10,2},{3,11},{11,3},{4,12},{12,4},... | collective-permute-start | bytes 393224 | tf_op jit(solution)/shard_map/ppermute | solution.py:233
  68.1 17.3 %collective-permute-start.16 = (bf16[1,768,128]{2,1,0:T(8,128)(2,1)S(1)}, bf16[1,768,128]{2,1,0:T(8,128)(2,1)}, u32[]{:S(2)}, u32[]{:S(2)}) collective-permute-start(bf16[1,768,128]{2,1,0:T(8,128)(2,1)S(1)} %collective-permute-done.15.r_5_), channel_id=1, source_target_pairs={{0,16},{16,0},{1,17},{17,1},{2,18},{18,2},{3,19},{19,3},{4,20},{20... | collective-permute-start | bytes 589832 | tf_op jit(solution)/shard_map/ppermute | solution.py:205
  78.0 7.4 %collective-permute-start.18 = (bf16[1,768,128]{2,1,0:T(8,128)(2,1)}, bf16[1,768,128]{2,1,0:T(8,128)(2,1)}, u32[]{:S(2)}, u32[]{:S(2)}) collective-permute-start(bf16[1,768,128]{2,1,0:T(8,128)(2,1)} %collective-permute-done.17.r_7_), channel_id=1, source_target_pairs={{0,16},{16,0},{1,17},{17,1},{2,18},{18,2},{3,19},{19,3},{4,20},{20... | collective-permute-start | bytes 589832 | tf_op jit(solution)/shard_map/ppermute | solution.py:205
  79.5 10.2 %collective-permute-start.14 = (bf16[1,1536,128]{2,1,0:T(8,128)(2,1)}, bf16[1,1536,128]{2,1,0:T(8,128)(2,1)}, u32[]{:S(2)}, u32[]{:S(2)}) collective-permute-start(bf16[1,1536,128]{2,1,0:T(8,128)(2,1)} %r_3_.4), channel_id=1, source_target_pairs={{0,2},{2,0},{4,6},{6,4},{1,3},{3,1},{5,7},{7,5},{8,10},{10,8},{12,... | collective-permute-start | bytes 1179656 | tf_op jit(solution)/shard_map/ppermute | solution.py:186
  94.2 4.3 %collective-permute-start.20 = (bf16[128,256]{1,0:T(8,128)(2,1)S(1)}, bf16[128,256]{1,0:T(8,128)(2,1)S(1)}, u32[]{:S(2)}, u32[]{:S(2)}) collective-permute-start(bf16[128,256]{1,0:T(8,128)(2,1)S(1)} %get-tuple-element.38), channel_id=1, source_target_pairs={{0,8},{8,0},{1,9},{9,1},{2,10},{10,2},{3,11},{11,3},{4,12},{12,4},... | collective-permute-start | bytes 196616 | tf_op jit(solution)/shard_map/ppermute | solution.py:233
  103.0 4.6 %collective-permute-start.22 = (bf16[128,1536]{1,0:T(8,128)(2,1)S(1)}, bf16[128,1536]{1,0:T(8,128)(2,1)S(1)}, u32[]{:S(2)}, u32[]{:S(2)}) collective-permute-start(bf16[128,1536]{1,0:T(8,128)(2,1)S(1)} %get-tuple-element.37), channel_id=1, source_target_pairs={{0,1},{1,0},{2,3},{3,2},{4,5},{5,4},{6,7},{7,6},{8,9},{9,8},{10,11... | collective-permute-start | bytes 1179656 | tf_op jit(solution)/shard_map/ppermute | solution.py:336
  103.2 13.9 %collective-permute-start.26 = (bf16[1536,128]{1,0:T(8,128)(2,1)S(1)}, bf16[1536,128]{1,0:T(8,128)(2,1)S(1)}, u32[]{:S(2)}, u32[]{:S(2)}) collective-permute-start(bf16[1536,128]{1,0:T(8,128)(2,1)S(1)} %get-tuple-element.29), channel_id=1, source_target_pairs={{0,6},{2,4},{4,2},{6,0},{1,7},{3,5},{5,3},{7,1},{8,14},{10,12},{12... | collective-permute-start | bytes 1179656 | tf_op jit(solution)/shard_map/ppermute | solution.py:186
  105.5 34.1 %collective-permute-start.25 = (bf16[1536,128]{1,0:T(8,128)(2,1)S(1)}, bf16[1536,128]{1,0:T(8,128)(2,1)S(1)}, u32[]{:S(2)}, u32[]{:S(2)}) collective-permute-start(bf16[1536,128]{1,0:T(8,128)(2,1)S(1)} %get-tuple-element.28), channel_id=1, source_target_pairs={{0,4},{2,6},{4,0},{6,2},{1,5},{3,7},{5,1},{7,3},{8,12},{10,14},{12... | collective-permute-start | bytes 1179656 | tf_op jit(solution)/shard_map/ppermute | solution.py:186
  105.5 34.1 %collective-permute-start.24 = (bf16[1536,128]{1,0:T(8,128)(2,1)S(1)}, bf16[1536,128]{1,0:T(8,128)(2,1)S(1)}, u32[]{:S(2)}, u32[]{:S(2)}) collective-permute-start(bf16[1536,128]{1,0:T(8,128)(2,1)S(1)} %get-tuple-element.27), channel_id=1, source_target_pairs={{0,2},{2,0},{4,6},{6,4},{1,3},{3,1},{5,7},{7,5},{8,10},{10,8},{12,... | collective-permute-start | bytes 1179656 | tf_op jit(solution)/shard_map/ppermute | solution.py:186
  107.9 32.8 %collective-permute-start.23 = (bf16[64,3072]{1,0:T(8,128)(2,1)S(1)}, bf16[64,3072]{1,0:T(8,128)(2,1)S(1)}, u32[]{:S(2)}, u32[]{:S(2)}) collective-permute-start(bf16[64,3072]{1,0:T(8,128)(2,1)S(1)} %get-tuple-element.43), channel_id=1, source_target_pairs={{0,8},{8,0},{1,9},{9,1},{2,10},{10,2},{3,11},{11,3},{4,12},{12,4},... | collective-permute-start | bytes 1179656 | tf_op jit(solution)/shard_map/ppermute | solution.py:337
  (20 other events, 146.8 us)

commit v3 on v2

--- a/solution.py
+++ b/solution.py
@@ -172,6 +172,10 @@
     return lax.optimization_barrier((value, *earlier))[0]
 
 
+def after_all(values, earlier):
+    return lax.optimization_barrier((tuple(values), tuple(earlier)))[0]
+
+
 def per_device(tokens, cotangent, expert_ids, combine, gate_weight, up_weight, down_weight):
     n = lax.axis_size("expert")
     nx, nc = lax.axis_size("fsdp"), lax.axis_size("dp")
@@ -185,24 +189,26 @@
     def partner(block, k):
         return pp(block, "expert", [(i, i ^ k) for i in range(n)])
 
-    gu_own = jnp.concatenate([gate_weight, up_weight])
-    gu_near = lax.dynamic_slice_in_dim(gu_own, g * half, half, 1)
+    gu_near = jnp.concatenate(
+        [lax.dynamic_slice_in_dim(w, g * half, half, 1) for w in (gate_weight, up_weight)]
+    )
     dn_near = lax.dynamic_slice_in_dim(down_weight, g * half, half, 1)
     far_ones = list(range(n - 1, 1, -1))
     gu, dn = {}, {}
     for k in far_ones:
         gu[k] = partner(gu_near, k)
-    gu[1] = partner(gu_own, 1)
+    near_ones = [partner(w, 1) for w in (gate_weight, up_weight)]
     for k in far_ones:
         dn[k] = partner(after(dn_near, gu[k]), k)
-    dn[1] = partner(after(down_weight, gu[1]), 1)
+    dn[1] = partner(after(down_weight, near_ones[1]), 1)
     labels = jnp.stack([e, e ^ 1] + [e ^ k for k in far_ones] + [g]).astype(jnp.int32)
-    layout = ["parts", "full"] + ["halves"] * len(far_ones)
-    gu_refs, dn_refs = [gate_weight, up_weight, gu[1]], [down_weight, dn[1]]
+    layout = ["parts", "parts"] + ["halves"] * len(far_ones)
+    gu_refs, dn_refs = [gate_weight, up_weight, *near_ones], [down_weight, dn[1]]
     for k in far_ones:
         gu_refs += [gu[k], pp(gu[k], "groups", SWAP)]
-    for k in far_ones:
-        dn_refs += [dn[k], pp(dn[k], "groups", SWAP)]
+    dn_far = [pp(dn[k], "groups", SWAP) for k in far_ones]
+    for k, block in zip(far_ones, dn_far):
+        dn_refs += [dn[k], block]
 
     tokens = after(tokens, gu_near)
     cotangent = after(cotangent, gu_near)
@@ -228,8 +234,8 @@
         info = jnp.concatenate([mine_info, pp(mine_info, "dp", SWAP)])
         blocks = 2
 
-        def reduce_rows(parts):
-            total = parts[0] + pp(parts[1], "dp", SWAP)
+        def reduce_rows(parts, *earlier):
+            total = after(parts[0], *earlier) + pp(parts[1], "dp", SWAP)
             return [total, pp(total.astype(BF), "fsdp", SWAP)]
 
         def share_rows(rows):
@@ -248,7 +254,7 @@
         mine_info = extra
         info = lax.all_gather(extra, ("fsdp", "dp"), axis=0, tiled=True)
 
-        def reduce_rows(parts):
+        def reduce_rows(parts, *_):
             return [lax.psum_scatter(parts[0], ("fsdp", "dp"), scatter_dimension=0, tiled=True)]
 
         def share_rows(rows):
@@ -278,7 +284,7 @@
             nbytes=2 * n * quarter * parts * ff,
         )
 
-    first = reduce_rows(sums(tok, gu_refs, 2))
+    first = reduce_rows(sums(tok, gu_refs, 2), *dn.values())
     m = first[0].shape[0]
     full_sums, hidden = call(
         hidden_step,
@@ -298,9 +304,11 @@
         cot_t,
         hidden,
     )
+    shares = {k: partner(pieces[k], k) for k in range(1, n) if k != 2}
+    shares[2] = partner(after(pieces[2], shares[n - 1]), 2)
     grad_down = pieces[0]
     for k in range(1, n):
-        grad_down = grad_down + partner(pieces[k], k).astype(F32)
+        grad_down = grad_down + shares[k].astype(F32)
 
     second = reduce_rows(sums(after(cot, *pieces), dn_refs, 1))
     grads = call(
@@ -334,6 +342,7 @@
             )
 
         back = join(back[0], pp(back[1], "dp", SWAP), d)
+        back = after(back, shares[1], shares[n - 1])
         grad_tokens = join(back[:own], pp(back[own:], "fsdp", SWAP), f)
     else:
         back = lax.all_to_all(

time: 142 us -> 128 us (0.901)
  waiting for transfers between devices: 85.2 us -> 67.4 us
  starting transfers between devices: 28.3 us -> 32.8 us
    ppermute x9 -> x10, waiting for transfers between devices: 67.2 us -> 56 us  [partner(): return pp(block, 'expert', [(i, i ^ k) for i in range(n)])]
    ppermute x9 -> x10, starting transfers between devices: 12.5 us -> 17.5 us  [partner(): return pp(block, 'expert', [(i, i ^ k) for i in range(n)])]
    ppermute x1, waiting for transfers between devices: 7.83 us -> 4.11 us  [per_device(): mine_info = jnp.concatenate([extra, pp(extra, 'fsdp', SWAP)])]
    ppermute x2, waiting for transfers between devices: 4.76 us -> 1.2 us  [per_device(): gu_refs += [gu[k], pp(gu[k], 'groups', SWAP)]]
    ppermute x2, waiting for transfers between devices: 2.77 us -> 5.09 us  [reduce_rows(): return [total, pp(total.astype(BF), 'fsdp', SWAP)]]
  transfers between devices with their start and end apart: 27 -> 28, of which waited for: 11 -> 12; matrix products, arithmetic and copies ran while one was open for 7% -> 8% of each run, Pallas kernels for 4% -> 7%
where the time goes in v3:
time: 128 us
  waiting for transfers between devices  67.4 us (53%)
  starting transfers between devices  32.8 us (26%)
  Pallas kernels  11.8 us (9%)
  other arithmetic  8.99 us (7%)
  local copies, waits for them, and re-layouts  5.55 us (4%)
    ppermute x10, waiting for transfers between devices, partner(): return pp(block, 'expert', [(i, i ^ k) for i in range(n)])  56 us
    ppermute x10, starting transfers between devices, partner(): return pp(block, 'expert', [(i, i ^ k) for i in range(n)])  17.5 us
    pallas_call x6, Pallas kernels, call(): pl.pallas_call(body, out_shape=outs, in_specs=specs, out_specs=jax.tree.m...  11.8 us
    ppermute x2, waiting for transfers between devices, reduce_rows(): return [total, pp(total.astype(BF), 'fsdp', SWAP)]  5.09 us
    ppermute x2, starting transfers between devices, spread(): a = jnp.concatenate([halve(a, f), pp(halve(a, 1 - f), 'fsdp', SWAP)])  4.24 us
    ppermute x1, waiting for transfers between devices, per_device(): mine_info = jnp.concatenate([extra, pp(extra, 'fsdp', SWAP)])  4.11 us
    select_n x4, other arithmetic, halve(): return jnp.where(at == 0, a[:, :m], a[:, m:])  3.34 us
    ppermute x2, starting transfers between devices, per_device(): gu_refs += [gu[k], pp(gu[k], 'groups', SWAP)]  3.04 us
  transfers between devices with their start and end apart: 28, of which 12 were waited for; matrix products, arithmetic and copies ran while one was open for 8% of the time, Pallas kernels for 7%

profile of v3, /device:TPU:0, one launch (start us, length us, event | category | flops | bytes accessed | tf_op | source)
XLA Modules:
  0.0 127.7 jit_solution(1905900961155887792)
XLA Ops:
  2.8 3.0 %collective-permute-start.2 = (bf16[64,3072]{1,0:T(8,128)(2,1)S(1)}, bf16[64,3072]{1,0:T(8,128)(2,1)S(1)}, u32[]{:S(2)}, u32[]{:S(2)}) collective-permute-start(bf16[64,3072]{1,0:T(8,128)(2,1)S(1)} %get-tuple-element.59), channel_id=1, source_target_pairs={{0,8},{8,0},{1,9},{9,1},{2,10},{10,2},{3,11},{11,3},{4,12},{12,4},... | collective-permute-start | bytes 1179656 | tf_op jit(solution)/shard_map/ppermute | solution.py:229
  7.0 1.6 %collective-permute-start.5 = (bf16[1,1536,128]{2,1,0:T(8,128)(2,1)S(1)}, bf16[1,1536,128]{2,1,0:T(8,128)(2,1)S(1)}, u32[]{:S(2)}, u32[]{:S(2)}) collective-permute-start(bf16[1,1536,128]{2,1,0:T(8,128)(2,1)S(1)} %copy-done.1), channel_id=1, source_target_pairs={{0,2},{2,0},{4,6},{6,4},{1,3},{3,1},{5,7},{7,5},{8,10},{10,8},{12,... | collective-permute-start | bytes 1179656 | tf_op jit(solution)/shard_map/ppermute | solution.py:190
  8.6 2.5 %collective-permute-start.6 = (bf16[2,768,128]{2,1,0:T(8,128)(2,1)S(1)}, bf16[2,768,128]{2,1,0:T(8,128)(2,1)S(1)}, u32[]{:S(2)}, u32[]{:S(2)}) collective-permute-start(bf16[2,768,128]{2,1,0:T(8,128)(2,1)S(1)} %pad_maximum_fusion.4), channel_id=1, source_target_pairs={{0,6},{2,4},{4,2},{6,0},{1,7},{3,5},{5,3},{7,1},{8,14},{10,12},{12... | collective-permute-start | bytes 1179656 | tf_op jit(solution)/shard_map/ppermute | solution.py:190
  11.1 4.1 %collective-permute-done = bf16[64,128]{1,0:T(8,128)(2,1)S(1)} collective-permute-done((bf16[64,128]{1,0:T(8,128)(2,1)S(1)}, bf16[64,128]{1,0:T(8,128)(2,1)S(1)}, u32[]{:S(2)}, u32[]{:S(2)}) %collective-permute-start) | collective-permute-done | bytes 16416 | tf_op jit(solution)/shard_map/ppermute | solution.py:233
  16.0 2.2 %broadcast_select_fusion.7 = (bf16[128,1536]{1,0:T(8,128)(2,1)}, bf16[128,1536]{1,0:T(8,128)(2,1)}) fusion(pred[]{:T(512)S(6)} %eq.9, bf16[64,3072]{1,0:T(8,128)(2,1)} %copy-done.19, bf16[64,3072]{1,0:T(8,128)(2,1)S(1)} %get-tuple-element.58, pred[]{:T(512)S(6)} %eq.21), kind=kLoop, calls=%fused_computation.21 | loop fusion | flops 2752512 | bytes 1572866 | tf_op jit(solution)/shard_map/jit(_where)/select_n | solution.py:226
  19.7 1.8 %collective-permute-start.4 = (bf16[1,1536,128]{2,1,0:T(8,128)(2,1)S(1)}, bf16[1,1536,128]{2,1,0:T(8,128)(2,1)S(1)}, u32[]{:S(2)}, u32[]{:S(2)}) collective-permute-start(bf16[1,1536,128]{2,1,0:T(8,128)(2,1)S(1)} %copy-done), channel_id=1, source_target_pairs={{0,2},{2,0},{4,6},{6,4},{1,3},{3,1},{5,7},{7,5},{8,10},{10,8},{12,... | collective-permute-start | bytes 1179656 | tf_op jit(solution)/shard_map/ppermute | solution.py:190
  21.5 8.1 %collective-permute-done.6.r_7_ = bf16[2,768,128]{2,1,0:T(8,128)(2,1)S(1)} collective-permute-done((bf16[2,768,128]{2,1,0:T(8,128)(2,1)S(1)}, bf16[2,768,128]{2,1,0:T(8,128)(2,1)S(1)}, u32[]{:S(2)}, u32[]{:S(2)}) %collective-permute-start.6) | collective-permute-done | bytes 393248 | tf_op jit(solution)/shard_map/ppermute | solution.py:190
  31.1 13.9 %collective-permute-done.8.r_9_ = bf16[2,768,128]{2,1,0:T(8,128)(2,1)S(1)} collective-permute-done((bf16[2,768,128]{2,1,0:T(8,128)(2,1)S(1)}, bf16[2,768,128]{2,1,0:T(8,128)(2,1)S(1)}, u32[]{:S(2)}, u32[]{:S(2)}) %collective-permute-start.8) | collective-permute-done | bytes 393248 | tf_op jit(solution)/shard_map/ppermute | solution.py:190
  45.0 1.5 %collective-permute-start.9 = (bf16[2,768,128]{2,1,0:T(8,128)(2,1)S(1)}, bf16[2,768,128]{2,1,0:T(8,128)(2,1)S(1)}, u32[]{:S(2)}, u32[]{:S(2)}) collective-permute-start(bf16[2,768,128]{2,1,0:T(8,128)(2,1)S(1)} %collective-permute-done.8.r_9_), channel_id=1, source_target_pairs={{0,16},{16,0},{1,17},{17,1},{2,18},{18,2},{3,19},{19,3},{4,20},{20... | collective-permute-start | bytes 1179656 | tf_op jit(solution)/shard_map/ppermute | solution.py:208
  49.9 2.7 %collective-permute-start.10 = (bf16[1,768,128]{2,1,0:T(8,128)(2,1)S(1)}, bf16[1,768,128]{2,1,0:T(8,128)(2,1)S(1)}, u32[]{:S(2)}, u32[]{:S(2)}) collective-permute-start(bf16[1,768,128]{2,1,0:T(8,128)(2,1)S(1)} %copy-done.20), channel_id=1, source_target_pairs={{0,6},{2,4},{4,2},{6,0},{1,7},{3,5},{5,3},{7,1},{8,14},{10,12},{12... | collective-permute-start | bytes 589832 | tf_op jit(solution)/shard_map/ppermute | solution.py:190
  54.6 3.4 %shard_map.86 = (f32[128,512]{1,0:T(8,128)S(1)}, f32[128,512]{1,0:T(8,128)S(1)}) custom-call(s32[5]{0:T(128)S(1)} %stack.30.r_0_, s32[256,2]{1,0:T(8,128)S(1)} %fusion.2.r_1_, bf16[256,1536]{1,0:T(8,128)(2,1)S(1)} %pad_maximum_fusion.r_2_, bf16[1,1536,128]{2,1,0:T(8,128)(2,1)S(1)} %copy-done, bf16[1,1536,128]{2,1,0:T(8,128)(2,1)S(1)} %copy-done.1, ...), custom_call_target="tpu_custom_call" | custom-call | flops 805306368 | bytes 3145728 | tf_op jit(solution)/shard_map/pallas_call | solution.py:18
  58.9 5.8 %collective-permute-done.10.r_5_ = bf16[1,768,128]{2,1,0:T(8,128)(2,1)S(1)} collective-permute-done((bf16[1,768,128]{2,1,0:T(8,128)(2,1)S(1)}, bf16[1,768,128]{2,1,0:T(8,128)(2,1)S(1)}, u32[]{:S(2)}, u32[]{:S(2)}) %collective-permute-start.10) | collective-permute-done | bytes 196640 | tf_op jit(solution)/shard_map/ppermute | solution.py:190
  64.6 3.9 %collective-permute-done.11.r_7_ = bf16[1,768,128]{2,1,0:T(8,128)(2,1)} collective-permute-done((bf16[1,768,128]{2,1,0:T(8,128)(2,1)S(1)}, bf16[1,768,128]{2,1,0:T(8,128)(2,1)}, u32[]{:S(2)}, u32[]{:S(2)}) %collective-permute-start.11) | collective-permute-done | bytes 196640 | tf_op jit(solution)/shard_map/ppermute | solution.py:190
  70.3 1.5 %collective-permute-start.19 = (bf16[1,768,128]{2,1,0:T(8,128)(2,1)}, bf16[1,768,128]{2,1,0:T(8,128)(2,1)}, u32[]{:S(2)}, u32[]{:S(2)}) collective-permute-start(bf16[1,768,128]{2,1,0:T(8,128)(2,1)} %collective-permute-done.11.r_7_), channel_id=1, source_target_pairs={{0,16},{16,0},{1,17},{17,1},{2,18},{18,2},{3,19},{19,3},{4,20},{20... | collective-permute-start | bytes 589832 | tf_op jit(solution)/shard_map/ppermute | solution.py:209
  71.8 1.8 %collective-permute-done.14.rest_0_ = bf16[128,512]{1,0:T(8,128)(2,1)S(1)} collective-permute-done((bf16[128,512]{1,0:T(8,128)(2,1)S(1)}, bf16[128,512]{1,0:T(8,128)(2,1)S(1)}, u32[]{:S(2)}, u32[]{:S(2)}) %collective-permute-start.14) | collective-permute-done | bytes 131104 | tf_op jit(solution)/shard_map/ppermute | solution.py:239
  77.8 1.8 %shard_map.88 = (f32[1536,128]{1,0:T(8,128)S(1)}, bf16[1536,128]{1,0:T(8,128)(2,1)S(1)}, bf16[1536,128]{1,0:T(8,128)(2,1)S(1)}, bf16[1536,128]{1,0:T(8,128)(2,1)S(1)}) custom-call(s32[4]{0:T(128)S(1)} %pad_add_fusion.r_0_, s32[256,2]{1,0:T(8,128)S(1)} %fusion.2.r_1_, bf16[1536,256]{1,0:T(8,128)(2,1)S(1)} %copy.17.r_2_, ...), custom_call_target="tpu_custom_call" | custom-call | tf_op jit(solution)/shard_map/pallas_call | solution.py:18
  79.6 2.9 %shard_map.89 = (f32[128,256]{1,0:T(8,128)S(1)}, f32[128,256]{1,0:T(8,128)S(1)}) custom-call(s32[5]{0:T(128)S(1)} %stack.30.r_0_, s32[256,2]{1,0:T(8,128)S(1)} %fusion.2.r_1_, bf16[256,1536]{1,0:T(8,128)(2,1)S(1)} %get-tuple-element.37.r_2_, bf16[1,1536,128]{2,1,0:T(8,128)(2,1)S(1)} %copy-done.11, bf16[1,1536,128]{2,1,0:T(8,128)(2,1)S(1)} %copy-done.13, ...), custom_call_target="tpu_custom_call" | custom-call | flops 402653184 | bytes 1572864 | tf_op jit(solution)/shard_map/pallas_call | solution.py:18
  85.2 3.3 %collective-permute-done.21.rest_0_ = bf16[128,256]{1,0:T(8,128)(2,1)S(1)} collective-permute-done((bf16[128,256]{1,0:T(8,128)(2,1)S(1)}, bf16[128,256]{1,0:T(8,128)(2,1)S(1)}, u32[]{:S(2)}, u32[]{:S(2)}) %collective-permute-start.21) | collective-permute-done | bytes 65568 | tf_op jit(solution)/shard_map/ppermute | solution.py:239
  88.8 2.4 %collective-permute-start.25 = (bf16[1536,128]{1,0:T(8,128)(2,1)S(1)}, bf16[1536,128]{1,0:T(8,128)(2,1)S(1)}, u32[]{:S(2)}, u32[]{:S(2)}) collective-permute-start(bf16[1536,128]{1,0:T(8,128)(2,1)S(1)} %get-tuple-element.36), channel_id=1, source_target_pairs={{0,6},{2,4},{4,2},{6,0},{1,7},{3,5},{5,3},{7,1},{8,14},{10,12},{12... | collective-permute-start | bytes 1179656 | tf_op jit(solution)/shard_map/ppermute | solution.py:190
  91.2 2.8 %shard_map.91 = (bf16[128,1536]{1,0:T(8,128)(2,1)S(1)}, bf16[128,1536]{1,0:T(8,128)(2,1)S(1)}) custom-call(s32[5]{0:T(128)S(1)} %stack.30.r_0_, s32[256,2]{1,0:T(8,128)S(1)} %fusion.2.r_1_, bf16[256,512]{1,0:T(8,128)(2,1)S(1)} %pad_maximum_fusion.5.r_2_, bf16[1,1536,128]{2,1,0:T(8,128)(2,1)S(1)} %copy-done, bf16[1,1536,128]{2,1,0:T(8,128)(2,1)S(1)} %copy-done.1, ...), custom_call_target="tpu_custom_call" | custom-call | flops 805306368 | bytes 3145728 | tf_op jit(solution)/shard_map/pallas_call | solution.py:18
  94.2 8.4 %collective-permute-done.25 = bf16[1536,128]{1,0:T(8,128)(2,1)S(1)} collective-permute-done((bf16[1536,128]{1,0:T(8,128)(2,1)S(1)}, bf16[1536,128]{1,0:T(8,128)(2,1)S(1)}, u32[]{:S(2)}, u32[]{:S(2)}) %collective-permute-start.25) | collective-permute-done | bytes 393248 | tf_op jit(solution)/shard_map/ppermute | solution.py:190
  102.6 5.5 %collective-permute-start.27 = (bf16[1536,128]{1,0:T(8,128)(2,1)S(1)}, bf16[1536,128]{1,0:T(8,128)(2,1)S(1)}, u32[]{:S(2)}, u32[]{:S(2)}) collective-permute-start(bf16[1536,128]{1,0:T(8,128)(2,1)S(1)} %get-tuple-element.43), channel_id=1, source_target_pairs={{0,4},{2,6},{4,0},{6,2},{1,5},{3,7},{5,1},{7,3},{8,12},{10,14},{12... | collective-permute-start | bytes 1179656 | tf_op jit(solution)/shard_map/ppermute | solution.py:190
  108.4 4.4 %collective-permute-done.24 = bf16[1536,128]{1,0:T(8,128)(2,1)S(1)} collective-permute-done((bf16[1536,128]{1,0:T(8,128)(2,1)S(1)}, bf16[1536,128]{1,0:T(8,128)(2,1)S(1)}, u32[]{:S(2)}, u32[]{:S(2)}) %collective-permute-start.24) | collective-permute-done | bytes 393248 | tf_op jit(solution)/shard_map/ppermute | solution.py:190
  113.9 11.7 %collective-permute-done.27 = bf16[1536,128]{1,0:T(8,128)(2,1)S(1)} collective-permute-done((bf16[1536,128]{1,0:T(8,128)(2,1)S(1)}, bf16[1536,128]{1,0:T(8,128)(2,1)S(1)}, u32[]{:S(2)}, u32[]{:S(2)}) %collective-permute-start.27) | collective-permute-done | bytes 393248 | tf_op jit(solution)/shard_map/ppermute | solution.py:190
  (116 shorter events, 25.8 us)
Async XLA Ops:
  2.8 12.5 %collective-permute-start.2 = (bf16[64,3072]{1,0:T(8,128)(2,1)S(1)}, bf16[64,3072]{1,0:T(8,128)(2,1)S(1)}, u32[]{:S(2)}, u32[]{:S(2)}) collective-permute-start(bf16[64,3072]{1,0:T(8,128)(2,1)S(1)} %get-tuple-element.59), channel_id=1, source_target_pairs={{0,8},{8,0},{1,9},{9,1},{2,10},{10,2},{3,11},{11,3},{4,12},{12,4},... | collective-permute-start | bytes 1179656 | tf_op jit(solution)/shard_map/ppermute | solution.py:229
  6.4 8.9 %collective-permute-start = (bf16[64,128]{1,0:T(8,128)(2,1)S(1)}, bf16[64,128]{1,0:T(8,128)(2,1)S(1)}, u32[]{:S(2)}, u32[]{:S(2)}) collective-permute-start(bf16[64,128]{1,0:T(8,128)(2,1)S(1)} %concatenate.43), channel_id=1, source_target_pairs={{0,8},{8,0},{1,9},{9,1},{2,10},{10,2},{3,11},{11,3},{4,12},{12,4},... | collective-permute-start | bytes 49160 | tf_op jit(solution)/shard_map/ppermute | solution.py:233
  7.0 40.3 %collective-permute-start.5 = (bf16[1,1536,128]{2,1,0:T(8,128)(2,1)S(1)}, bf16[1,1536,128]{2,1,0:T(8,128)(2,1)S(1)}, u32[]{:S(2)}, u32[]{:S(2)}) collective-permute-start(bf16[1,1536,128]{2,1,0:T(8,128)(2,1)S(1)} %copy-done.1), channel_id=1, source_target_pairs={{0,2},{2,0},{4,6},{6,4},{1,3},{3,1},{5,7},{7,5},{8,10},{10,8},{12,... | collective-permute-start | bytes 1179656 | tf_op jit(solution)/shard_map/ppermute | solution.py:190
  8.6 21.1 %collective-permute-start.6 = (bf16[2,768,128]{2,1,0:T(8,128)(2,1)S(1)}, bf16[2,768,128]{2,1,0:T(8,128)(2,1)S(1)}, u32[]{:S(2)}, u32[]{:S(2)}) collective-permute-start(bf16[2,768,128]{2,1,0:T(8,128)(2,1)S(1)} %pad_maximum_fusion.4), channel_id=1, source_target_pairs={{0,6},{2,4},{4,2},{6,0},{1,7},{3,5},{5,3},{7,1},{8,14},{10,12},{12... | collective-permute-start | bytes 1179656 | tf_op jit(solution)/shard_map/ppermute | solution.py:190
  11.0 34.0 %collective-permute-start.8 = (bf16[2,768,128]{2,1,0:T(8,128)(2,1)S(1)}, bf16[2,768,128]{2,1,0:T(8,128)(2,1)S(1)}, u32[]{:S(2)}, u32[]{:S(2)}) collective-permute-start(bf16[2,768,128]{2,1,0:T(8,128)(2,1)S(1)} %pad_maximum_fusion.4), channel_id=1, source_target_pairs={{0,4},{2,6},{4,0},{6,2},{1,5},{3,7},{5,1},{7,3},{8,12},{10,14},{12... | collective-permute-start | bytes 1179656 | tf_op jit(solution)/shard_map/ppermute | solution.py:190
  18.2 30.3 %collective-permute-start.3 = (bf16[128,1536]{1,0:T(8,128)(2,1)}, bf16[128,1536]{1,0:T(8,128)(2,1)}, u32[]{:S(2)}, u32[]{:S(2)}) collective-permute-start(bf16[128,1536]{1,0:T(8,128)(2,1)} %get-tuple-element.57), channel_id=1, source_target_pairs={{0,1},{1,0},{2,3},{3,2},{4,5},{5,4},{6,7},{7,6},{8,9},{9,8},{10,11... | collective-permute-start | bytes 1179656 | tf_op jit(solution)/shard_map/ppermute | solution.py:230
  19.7 30.2 %collective-permute-start.4 = (bf16[1,1536,128]{2,1,0:T(8,128)(2,1)S(1)}, bf16[1,1536,128]{2,1,0:T(8,128)(2,1)S(1)}, u32[]{:S(2)}, u32[]{:S(2)}) collective-permute-start(bf16[1,1536,128]{2,1,0:T(8,128)(2,1)S(1)} %copy-done), channel_id=1, source_target_pairs={{0,2},{2,0},{4,6},{6,4},{1,3},{3,1},{5,7},{7,5},{8,10},{10,8},{12,... | collective-permute-start | bytes 1179656 | tf_op jit(solution)/shard_map/ppermute | solution.py:190
  29.6 22.9 %collective-permute-start.7 = (bf16[2,768,128]{2,1,0:T(8,128)(2,1)S(1)}, bf16[2,768,128]{2,1,0:T(8,128)(2,1)S(1)}, u32[]{:S(2)}, u32[]{:S(2)}) collective-permute-start(bf16[2,768,128]{2,1,0:T(8,128)(2,1)S(1)} %collective-permute-done.6.r_7_), channel_id=1, source_target_pairs={{0,16},{16,0},{1,17},{17,1},{2,18},{18,2},{3,19},{19,3},{4,20},{20... | collective-permute-start | bytes 1179656 | tf_op jit(solution)/shard_map/ppermute | solution.py:208
  45.0 9.6 %collective-permute-start.9 = (bf16[2,768,128]{2,1,0:T(8,128)(2,1)S(1)}, bf16[2,768,128]{2,1,0:T(8,128)(2,1)S(1)}, u32[]{:S(2)}, u32[]{:S(2)}) collective-permute-start(bf16[2,768,128]{2,1,0:T(8,128)(2,1)S(1)} %collective-permute-done.8.r_9_), channel_id=1, source_target_pairs={{0,16},{16,0},{1,17},{17,1},{2,18},{18,2},{3,19},{19,3},{4,20},{20... | collective-permute-start | bytes 1179656 | tf_op jit(solution)/shard_map/ppermute | solution.py:208
  47.3 10.9 %collective-permute-start.15 = (bf16[64,3072]{1,0:T(8,128)(2,1)}, bf16[64,3072]{1,0:T(8,128)(2,1)S(1)}, u32[]{:S(2)}, u32[]{:S(2)}) collective-permute-start(bf16[64,3072]{1,0:T(8,128)(2,1)} %get-tuple-element.55), channel_id=1, source_target_pairs={{0,8},{8,0},{1,9},{9,1},{2,10},{10,2},{3,11},{11,3},{4,12},{12,4},... | collective-permute-start | bytes 1179656 | tf_op jit(solution)/shard_map/ppermute | solution.py:229
  48.6 20.0 %collective-permute-start.12 = (bf16[1,1536,128]{2,1,0:T(8,128)(2,1)}, bf16[1,1536,128]{2,1,0:T(8,128)(2,1)S(1)}, u32[]{:S(2)}, u32[]{:S(2)}) collective-permute-start(bf16[1,1536,128]{2,1,0:T(8,128)(2,1)} %r_3_.4), channel_id=1, source_target_pairs={{0,2},{2,0},{4,6},{6,4},{1,3},{3,1},{5,7},{7,5},{8,10},{10,8},{12,... | collective-permute-start | bytes 1179656 | tf_op jit(solution)/shard_map/ppermute | solution.py:190
  49.9 14.7 %collective-permute-start.10 = (bf16[1,768,128]{2,1,0:T(8,128)(2,1)S(1)}, bf16[1,768,128]{2,1,0:T(8,128)(2,1)S(1)}, u32[]{:S(2)}, u32[]{:S(2)}) collective-permute-start(bf16[1,768,128]{2,1,0:T(8,128)(2,1)S(1)} %copy-done.20), channel_id=1, source_target_pairs={{0,6},{2,4},{4,2},{6,0},{1,7},{3,5},{5,3},{7,1},{8,14},{10,12},{12... | collective-permute-start | bytes 589832 | tf_op jit(solution)/shard_map/ppermute | solution.py:190
  52.6 15.9 %collective-permute-start.11 = (bf16[1,768,128]{2,1,0:T(8,128)(2,1)S(1)}, bf16[1,768,128]{2,1,0:T(8,128)(2,1)}, u32[]{:S(2)}, u32[]{:S(2)}) collective-permute-start(bf16[1,768,128]{2,1,0:T(8,128)(2,1)S(1)} %copy-done.20), channel_id=1, source_target_pairs={{0,4},{2,6},{4,0},{6,2},{1,5},{3,7},{5,1},{7,3},{8,12},{10,14},{12... | collective-permute-start | bytes 589832 | tf_op jit(solution)/shard_map/ppermute | solution.py:190
  58.1 10.4 %collective-permute-start.13 = (f32[128,512]{1,0:T(8,128)S(1)}, f32[128,512]{1,0:T(8,128)S(1)}, u32[]{:S(2)}, u32[]{:S(2)}) collective-permute-start(f32[128,512]{1,0:T(8,128)S(1)} %get-tuple-element.29), channel_id=1, source_target_pairs={{0,1},{1,0},{2,3},{3,2},{4,5},{5,4},{6,7},{7,6},{8,9},{9,8},{10,11... | collective-permute-start | bytes 786440 | tf_op jit(solution)/shard_map/ppermute | solution.py:238
  58.3 16.1 %collective-permute-start.16 = (bf16[128,1536]{1,0:T(8,128)(2,1)S(1)}, bf16[128,1536]{1,0:T(8,128)(2,1)S(1)}, u32[]{:S(2)}, u32[]{:S(2)}) collective-permute-start(bf16[128,1536]{1,0:T(8,128)(2,1)S(1)} %get-tuple-element.53), channel_id=1, source_target_pairs={{0,1},{1,0},{2,3},{3,2},{4,5},{5,4},{6,7},{7,6},{8,9},{9,8},{10,11... | collective-permute-start | bytes 1179656 | tf_op jit(solution)/shard_map/ppermute | solution.py:230
  68.6 5.0 %collective-permute-start.14 = (bf16[128,512]{1,0:T(8,128)(2,1)S(1)}, bf16[128,512]{1,0:T(8,128)(2,1)S(1)}, u32[]{:S(2)}, u32[]{:S(2)}) collective-permute-start(bf16[128,512]{1,0:T(8,128)(2,1)S(1)} %get-tuple-element.46), channel_id=1, source_target_pairs={{0,8},{8,0},{1,9},{9,1},{2,10},{10,2},{3,11},{11,3},{4,12},{12,4},... | collective-permute-start | bytes 393224 | tf_op jit(solution)/shard_map/ppermute | solution.py:239
  69.8 9.8 %collective-permute-start.18 = (bf16[1,768,128]{2,1,0:T(8,128)(2,1)S(1)}, bf16[1,768,128]{2,1,0:T(8,128)(2,1)}, u32[]{:S(2)}, u32[]{:S(2)}) collective-permute-start(bf16[1,768,128]{2,1,0:T(8,128)(2,1)S(1)} %collective-permute-done.10.r_5_), channel_id=1, source_target_pairs={{0,16},{16,0},{1,17},{17,1},{2,18},{18,2},{3,19},{19,3},{4,20},{20... | collective-permute-start | bytes 589832 | tf_op jit(solution)/shard_map/ppermute | solution.py:209
  70.3 9.3 %collective-permute-start.19 = (bf16[1,768,128]{2,1,0:T(8,128)(2,1)}, bf16[1,768,128]{2,1,0:T(8,128)(2,1)}, u32[]{:S(2)}, u32[]{:S(2)}) collective-permute-start(bf16[1,768,128]{2,1,0:T(8,128)(2,1)} %collective-permute-done.11.r_7_), channel_id=1, source_target_pairs={{0,16},{16,0},{1,17},{17,1},{2,18},{18,2},{3,19},{19,3},{4,20},{20... | collective-permute-start | bytes 589832 | tf_op jit(solution)/shard_map/ppermute | solution.py:209
  84.1 4.4 %collective-permute-start.21 = (bf16[128,256]{1,0:T(8,128)(2,1)S(1)}, bf16[128,256]{1,0:T(8,128)(2,1)S(1)}, u32[]{:S(2)}, u32[]{:S(2)}) collective-permute-start(bf16[128,256]{1,0:T(8,128)(2,1)S(1)} %get-tuple-element.44), channel_id=1, source_target_pairs={{0,8},{8,0},{1,9},{9,1},{2,10},{10,2},{3,11},{11,3},{4,12},{12,4},... | collective-permute-start | bytes 196616 | tf_op jit(solution)/shard_map/ppermute | solution.py:239
  88.8 13.9 %collective-permute-start.25 = (bf16[1536,128]{1,0:T(8,128)(2,1)S(1)}, bf16[1536,128]{1,0:T(8,128)(2,1)S(1)}, u32[]{:S(2)}, u32[]{:S(2)}) collective-permute-start(bf16[1536,128]{1,0:T(8,128)(2,1)S(1)} %get-tuple-element.36), channel_id=1, source_target_pairs={{0,6},{2,4},{4,2},{6,0},{1,7},{3,5},{5,3},{7,1},{8,14},{10,12},{12... | collective-permute-start | bytes 1179656 | tf_op jit(solution)/shard_map/ppermute | solution.py:190
  94.0 14.2 %collective-permute-start.23 = (bf16[128,1536]{1,0:T(8,128)(2,1)S(1)}, bf16[128,1536]{1,0:T(8,128)(2,1)S(1)}, u32[]{:S(2)}, u32[]{:S(2)}) collective-permute-start(bf16[128,1536]{1,0:T(8,128)(2,1)S(1)} %get-tuple-element.41), channel_id=1, source_target_pairs={{0,1},{1,0},{2,3},{3,2},{4,5},{5,4},{6,7},{7,6},{8,9},{9,8},{10,11... | collective-permute-start | bytes 1179656 | tf_op jit(solution)/shard_map/ppermute | solution.py:344
  94.2 18.5 %collective-permute-start.24 = (bf16[1536,128]{1,0:T(8,128)(2,1)S(1)}, bf16[1536,128]{1,0:T(8,128)(2,1)S(1)}, u32[]{:S(2)}, u32[]{:S(2)}) collective-permute-start(bf16[1536,128]{1,0:T(8,128)(2,1)S(1)} %get-tuple-element.34), channel_id=1, source_target_pairs={{0,2},{2,0},{4,6},{6,4},{1,3},{3,1},{5,7},{7,5},{8,10},{10,8},{12,... | collective-permute-start | bytes 1179656 | tf_op jit(solution)/shard_map/ppermute | solution.py:190
  102.6 22.9 %collective-permute-start.27 = (bf16[1536,128]{1,0:T(8,128)(2,1)S(1)}, bf16[1536,128]{1,0:T(8,128)(2,1)S(1)}, u32[]{:S(2)}, u32[]{:S(2)}) collective-permute-start(bf16[1536,128]{1,0:T(8,128)(2,1)S(1)} %get-tuple-element.43), channel_id=1, source_target_pairs={{0,4},{2,6},{4,0},{6,2},{1,5},{3,7},{5,1},{7,3},{8,12},{10,14},{12... | collective-permute-start | bytes 1179656 | tf_op jit(solution)/shard_map/ppermute | solution.py:190
  112.8 13.8 %collective-permute-start.26 = (bf16[64,3072]{1,0:T(8,128)(2,1)S(1)}, bf16[64,3072]{1,0:T(8,128)(2,1)S(1)}, u32[]{:S(2)}, u32[]{:S(2)}) collective-permute-start(bf16[64,3072]{1,0:T(8,128)(2,1)S(1)} %get-tuple-element.49), channel_id=1, source_target_pairs={{0,8},{8,0},{1,9},{9,1},{2,10},{10,2},{3,11},{11,3},{4,12},{12,4},... | collective-permute-start | bytes 1179656 | tf_op jit(solution)/shard_map/ppermute | solution.py:346
  (27 other events, 147.9 us)

commit v4 on v2

v4 whole, which is shorter than its diff:
```python
import jax
import jax.numpy as jnp
from jax import lax
from jax.experimental import pallas as pl
from jax.experimental.pallas import tpu as pltpu
from jax.sharding import PartitionSpec as P

BF = jnp.bfloat16
F32 = jnp.float32
VMEM = pl.BlockSpec(memory_space=pltpu.VMEM)
SMEM = pl.BlockSpec(memory_space=pltpu.SMEM)
ANY = pl.BlockSpec(memory_space=pl.ANY)
SWAP = [(0, 1), (1, 0)]
PARAMS = pltpu.CompilerParams(vmem_limit_bytes=48 * 1024 * 1024)


def call(body, outs, specs, *args, scratch=(), flops=0):
    return pl.pallas_call(
        body,
        out_shape=outs,
        in_specs=specs,
        out_specs=jax.tree.map(lambda _: VMEM, outs),
        scratch_shapes=list(scratch),
        compiler_params=PARAMS,
        cost_estimate=pl.CostEstimate(flops=flops, bytes_accessed=0, transcendentals=0),
    )(*args)


def mm(left, right, dims):
    return lax.dot_general(left, right, (dims, ((), ())), preferred_element_type=F32)


def weight_copies(layout, scal, refs, held, sems):
    slots, at, sem = [], 0, 0
    rows = held.shape[1]
    half = rows // 2
    ff = 128
    parts = held.shape[2] // ff
    mine = scal[len(layout)]
    near = pl.ds(pl.multiple_of(mine * half, 16), half)
    far = pl.ds(pl.multiple_of((1 - mine) * half, 16), half)
    for s, kind in enumerate(layout):
        copies = []
        for p in range(parts):
            lanes = pl.ds(p * ff, ff)
            if kind == "parts":
                pairs = [(refs[at + p].at[0], pl.ds(0, rows))]
            elif kind == "full":
                pairs = [(refs[at].at[p], pl.ds(0, rows))]
            else:
                pairs = [(refs[at].at[p], near), (refs[at + 1].at[p], far)]
            for source, where in pairs:
                copies.append(
                    pltpu.make_async_copy(source, held.at[s, where, lanes], sems.at[sem])
                )
                sem += 1
        at += {"parts": parts, "full": 1, "halves": 2}[kind]
        slots.append(copies)
    return slots


def copy_count(layout, parts):
    return sum(parts * (2 if kind == "halves" else 1) for kind in layout)


def pick(ids, label, value, width):
    zero = jnp.zeros((), value.dtype)
    return jnp.where(ids[:, 0:1] == label, value[:, :width], zero) + jnp.where(
        ids[:, 1:2] == label, value[:, width:], zero
    )


def forward_sums(layout, outs, based, scal, ids, rows, *refs):
    held, sems = refs[-2:]
    results = refs[-2 - outs : -2]
    base = refs[:outs] if based else ()
    refs = refs[len(base) :]
    width = held.shape[2]
    slots = weight_copies(layout, scal, refs, held, sems)
    for copies in slots:
        for c in copies:
            c.start()
    total = [None, None]
    for s, copies in enumerate(slots):
        for c in copies:
            c.wait()
        value = mm(rows[...], held[s], ((1,), (0,)))
        label = scal[s]
        for k in range(2):
            picked = jnp.where(ids[:, k : k + 1] == label, value, 0.0)
            total[k] = picked if total[k] is None else total[k] + picked
    m = results[0].shape[0]
    for j, out in enumerate(results):
        for k in range(2):
            lanes = slice(k * width, (k + 1) * width)
            value = total[k][j * m : (j + 1) * m]
            out[:, lanes] = base[j][:, lanes] + value if based else value


def stacked(blocks):
    return jnp.concatenate([b[...] for b in blocks], axis=0) if len(blocks) > 1 else blocks[0][...]


def token_sums(layout, outs, scal, ids, *refs):
    grads, refs = stacked(refs[:outs]), refs[outs:]
    held, sems = refs[-2:]
    results = refs[-2 - outs : -2]
    width = held.shape[2]
    slots = weight_copies(layout, scal, refs, held, sems)
    for copies in slots:
        for c in copies:
            c.start()
    total = None
    for s, copies in enumerate(slots):
        for c in copies:
            c.wait()
        value = mm(pick(ids, scal[s], grads, width), held[s], ((1,), (1,)))
        total = value if total is None else total + value
    m = results[0].shape[0]
    for j, out in enumerate(results):
        out[...] = total[j * m : (j + 1) * m].astype(BF)


def down_products(count, scal, ids, scaled_t, *refs):
    outs = refs[-count:]
    hidden = stacked(refs[:-count])
    ff = hidden.shape[1] // 2
    for j in range(count):
        rows = pick(ids, scal[j], hidden, ff)
        outs[j][...] = mm(scaled_t[...], rows, ((1,), (0,))).astype(outs[j].dtype)


def whole_sum(part, other):
    if not other:
        return part[...]
    m = part.shape[0] // 2
    o = other[0]
    return part[...] + jnp.concatenate([o[m:, :], o[:m, :]], axis=0).astype(F32)


def slot_weight(info, k):
    low, middle, high = (
        info[:, at + k : at + k + 1].astype(F32) for at in (6, 4, 2)
    )
    return (high + middle) + low


def hidden_step(info, part, *rest):
    other, (sums, hidden) = rest[:-2], rest[-2:]
    total = whole_sum(part, other)
    sums[...] = total
    ff = total.shape[1] // 4
    for k in range(2):
        gate = total[:, 2 * k * ff : (2 * k + 1) * ff]
        up = total[:, (2 * k + 1) * ff : (2 * k + 2) * ff]
        act = gate * jax.nn.sigmoid(gate)
        hidden[:, k * ff : (k + 1) * ff] = (slot_weight(info, k) * (act * up)).astype(BF)


def grad_step(info, sums, part, *rest):
    other, grads = rest[:-1], rest[-1]
    total = whole_sum(part, other)
    ff = total.shape[1] // 2
    for k in range(2):
        gate = sums[:, 2 * k * ff : (2 * k + 1) * ff]
        up = sums[:, (2 * k + 1) * ff : (2 * k + 2) * ff]
        hidden_grad = slot_weight(info, k) * total[:, k * ff : (k + 1) * ff]
        sig = jax.nn.sigmoid(gate)
        slope = sig * (1.0 + gate * (1.0 - sig))
        grads[:, 2 * k * ff : (2 * k + 1) * ff] = (hidden_grad * up * slope).astype(BF)
        grads[:, (2 * k + 1) * ff : (2 * k + 2) * ff] = (hidden_grad * (gate * sig)).astype(BF)


def split3(value):
    high = lax.reduce_precision(value, 8, 7)
    rest = value - high
    middle = lax.reduce_precision(rest, 8, 7)
    low = rest - middle
    return [high.astype(BF), middle.astype(BF), low.astype(BF)]


def after(value, *earlier):
    return lax.optimization_barrier((value, *earlier))[0]


def after_all(values, earlier):
    return lax.optimization_barrier((tuple(values), tuple(earlier)))[0]


def near_rows(scal, gate, up, down, pair, single, sems):
    half = pair.shape[1]
    rows = pl.ds(pl.multiple_of(scal[0] * half, 16), half)
    copies = [
        pltpu.make_async_copy(source.at[0, rows], target, sems.at[i])
        for i, (source, target) in enumerate(
            ((gate, pair.at[0]), (up, pair.at[1]), (down, single.at[0]))
        )
    ]
    for c in copies:
        c.start()
    for c in copies:
        c.wait()


def per_device(tokens, cotangent, expert_ids, combine, gate_weight, up_weight, down_weight):
    n = lax.axis_size("expert")
    nx, nc = lax.axis_size("fsdp"), lax.axis_size("dp")
    g, f, e, d = (lax.axis_index(a) for a in ("groups", "fsdp", "expert", "dp"))
    own, width = tokens.shape
    quarter, ff = gate_weight.shape[1:]
    half = quarter // 2
    pp = lax.ppermute
    small = nx == 2 and nc == 2
    plane = nx * nc
    rows = plane * own
    blocks = 2 if small else 1
    mine = rows // blocks

    def partner(block, k):
        return pp(block, "expert", [(i, i ^ k) for i in range(n)])

    def region(work, *earlier):
        shapes = jax.eval_shape(work)
        return lax.cond(
            after(g, *earlier) < n * n,
            work,
            lambda: jax.tree.map(lambda s: jnp.zeros(s.shape, s.dtype), shapes),
        )

    gu_near, dn_near = call(
        near_rows,
        [jax.ShapeDtypeStruct((c, half, ff), BF) for c in (2, 1)],
        [SMEM, ANY, ANY, ANY],
        g.reshape(1).astype(jnp.int32),
        gate_weight,
        up_weight,
        down_weight,
        scratch=[pltpu.SemaphoreType.DMA((3,))],
    )
    first_one, *later_ones = range(n - 1, 1, -1)
    gu = {first_one: partner(gu_near, first_one)}
    nearest = [partner(gate_weight, 1)]

    def halve(a, at):
        m = a.shape[1] // 2
        return jnp.where(at == 0, a[:, :m], a[:, m:])

    def spread(a):
        if small:
            for axis, at in (("fsdp", f), ("dp", d)):
                a = jnp.concatenate([halve(a, at), pp(halve(a, 1 - at), axis, SWAP)])
            return a
        a = a.reshape(own, plane, quarter).transpose(1, 0, 2)
        return lax.all_to_all(a, ("fsdp", "dp"), 0, 0, tiled=True).reshape(rows, quarter)

    def spread_tokens():
        extra = jnp.concatenate(
            [expert_ids.astype(F32).astype(BF)]
            + split3(combine)
            + [jnp.zeros((own, 120), BF)],
            axis=1,
        )
        if small:
            mine_info = jnp.concatenate([extra, pp(extra, "fsdp", SWAP)])
            info = jnp.concatenate([mine_info, pp(mine_info, "dp", SWAP)])
        else:
            mine_info = extra
            info = lax.all_gather(extra, ("fsdp", "dp"), axis=0, tiled=True)
        return spread(tokens), info[:, :2].astype(jnp.int32), mine_info

    def spread_cotangent():
        cot = spread(cotangent)
        return cot, cot.T

    def reduce_rows(parts):
        if small:
            total = parts[0] + pp(parts[1], "dp", SWAP)
            return [total, pp(total.astype(BF), "fsdp", SWAP)]
        return [lax.psum_scatter(parts[0], ("fsdp", "dp"), scatter_dimension=0, tiled=True)]

    def share_rows(a):
        if small:
            return [a, pp(a, "dp", SWAP)]
        return [lax.all_gather(a, ("fsdp", "dp"), axis=0, tiled=True)]

    def held(kinds, parts):
        return [
            pltpu.VMEM((len(kinds), quarter, parts * ff), BF),
            pltpu.SemaphoreType.DMA((copy_count(kinds, parts),)),
        ]

    def sums(a, slots, parts, base=()):
        kinds = [kind for kind, _, _ in slots]
        refs = [r for _, _, rs in slots for r in rs]
        scal = jnp.stack([label for _, label, _ in slots] + [g]).astype(jnp.int32)
        return call(
            lambda *r: forward_sums(kinds, blocks, bool(base), *r),
            [jax.ShapeDtypeStruct((mine, 2 * parts * ff), F32)] * blocks,
            [SMEM, VMEM, VMEM] + [VMEM] * len(base) + [ANY] * len(refs),
            scal,
            ids,
            a,
            *base,
            *refs,
            scratch=held(kinds, parts),
        )

    tok, ids, mine_info = region(spread_tokens, gu_near)

    k = first_one
    gu[k] = after(gu[k], tok)
    far = pp(gu[k], "groups", SWAP)
    gu[later_ones[0]] = partner(after(gu_near, gu[k], nearest[0]), later_ones[0])
    nearest.append(partner(after(up_weight, nearest[0]), 1))
    cot, cot_t = region(spread_cotangent, gu[k])
    gu_slots = [
        ("parts", e, [gate_weight, up_weight]),
        ("parts", e ^ 1, nearest),
        ("halves", e ^ k, [gu[k], far]),
    ]
    dn_slots = [("parts", e, [down_weight])]
    todo, parts, dn = gu_slots, (), {}
    for i, k in enumerate(later_ones):
        gu[k] = after(gu[k], cot)
        far = pp(after(gu[k], far), "groups", SWAP)
        if i == 0:
            dn[first_one] = partner(after(dn_near, gu[k]), first_one)
            dn[1] = partner(after(down_weight, gu[k]), 1)
        dn[k] = partner(after(down_weight, gu[k]), k)
        if i + 1 < len(later_ones):
            gu[later_ones[i + 1]] = partner(after(gu_near, gu[k]), later_ones[i + 1])
        parts = region(lambda t=todo, p=parts: sums(tok, t, 2, p), gu[k])
        todo = [("halves", e ^ k, [gu[k], far])]
        gu_slots = gu_slots + todo
    dn_slots += [("parts", e ^ k, [dn[k]]) for k in [1, *later_ones]]
    parts = sums(tok, todo, 2, parts)
    first = region(lambda: reduce_rows(parts))

    m = first[0].shape[0]
    targets = jnp.stack([e ^ k for k in range(n)]).astype(jnp.int32)

    def down_step():
        dn_far = pp(dn[first_one], "groups", SWAP)
        full_sums, hidden = call(
            hidden_step,
            [jax.ShapeDtypeStruct((m, 4 * ff), F32), jax.ShapeDtypeStruct((m, 2 * ff), BF)],
            [VMEM] * (1 + len(first)),
            mine_info,
            *first,
        )
        hidden = share_rows(hidden)
        pieces = call(
            lambda *r: down_products(n, *r),
            [jax.ShapeDtypeStruct((quarter, ff), F32 if k == 0 else BF) for k in range(n)],
            [SMEM, VMEM, VMEM] + [VMEM] * len(hidden),
            targets,
            ids,
            cot_t,
            *hidden,
        )
        return full_sums, pieces, dn_far

    full_sums, pieces, dn_far = region(down_step)
    dn_slots.append(("halves", e ^ first_one, [dn[first_one], dn_far]))
    shares = [partner(pieces[k], k) for k in range(n - 1, 0, -1)]

    def token_gradient():
        second = reduce_rows(sums(cot, dn_slots, 1))
        grads = call(
            grad_step,
            jax.ShapeDtypeStruct((m, 4 * ff), BF),
            [VMEM] * (2 + len(second)),
            mine_info,
            full_sums,
            *second,
        )
        grads = share_rows(grads)
        kinds = [kind for kind, _, _ in gu_slots]
        gu_refs = [r for _, _, rs in gu_slots for r in rs]
        back = call(
            lambda *r: token_sums(kinds, blocks, *r),
            [jax.ShapeDtypeStruct((mine, quarter), BF)] * blocks,
            [SMEM, VMEM] + [VMEM] * blocks + [ANY] * len(gu_refs),
            jnp.stack([label for _, label, _ in gu_slots] + [g]).astype(jnp.int32),
            ids,
            *grads,
            *gu_refs,
            scratch=held(kinds, 2),
        )
        if small:

            def join(kept, came, at):
                return jnp.where(
                    at == 0,
                    jnp.concatenate([kept, came], axis=1),
                    jnp.concatenate([came, kept], axis=1),
                )

            back = join(back[0], pp(back[1], "dp", SWAP), d)
            return join(back[:own], pp(back[own:], "fsdp", SWAP), f)
        back = lax.all_to_all(
            back[0].reshape(plane, own, quarter), ("fsdp", "dp"), 0, 0, tiled=True
        )
        return back.transpose(1, 0, 2).reshape(own, width)

    grad_tokens = region(token_gradient, *pieces)
    grad_down = after(pieces[0], grad_tokens)
    for share in shares:
        grad_down = grad_down + share.astype(F32)
    return (grad_tokens, grad_down[None])


def solution(mesh):
    rows = P(("groups", "fsdp", "expert", "dp"), None)
    weights = P("expert", ("fsdp", "dp"), None)
    return jax.shard_map(
        per_device,
        mesh=mesh,
        in_specs=(rows, rows, rows, rows, weights, weights, weights),
        out_specs=(rows, P(("groups", "expert"), ("fsdp", "dp"), None)),
        check_vma=False,
    )
```

time: 142 us -> 111 us (0.78)
  waiting for transfers between devices: 85.2 us -> 50.6 us
  Pallas kernels: 12 us -> 19.6 us
  local copies, waits for them, and re-layouts: 6.69 us -> 1.5 us
  starting transfers between devices: 28.3 us -> 30.6 us
    ppermute x9 -> x10, waiting for transfers between devices: 67.2 us -> 4.17 us  [partner(): return pp(block, 'expert', [(i, i ^ k) for i in range(n)])]
    ppermute x14 -> x13, waiting for transfers between devices: 14 us -> 36.6 us  [the longest x4 18.8 us: spread(): a = jnp.concatenate([halve(a, at), pp(halve(a, 1 - at), axis, SWAP)])]
    pallas_call x6 -> x8, Pallas kernels: 12 us -> 19.6 us  [call(): pl.pallas_call(body, out_shape=outs, in_specs=specs, out_specs=jax.tree.m...]
    ppermute x2, waiting for transfers between devices: 2.77 us -> 6.93 us  [reduce_rows(): return [total, pp(total.astype(BF), 'fsdp', SWAP)]]
    ppermute x9 -> x10, starting transfers between devices: 12.5 us -> 16.2 us  [partner(): return pp(block, 'expert', [(i, i ^ k) for i in range(n)])]
    dynamic_slice x2 -> x0, local copies, waits for them, and re-layouts: 1.96 us -> none  [the longest x1 1.02 us: per_device(): gu_near = lax.dynamic_slice_in_dim(gu_own, g * half, half, 1)]
    ppermute x2, waiting for transfers between devices: 1.34 us -> 2.86 us  [reduce_rows(): total = parts[0] + pp(parts[1], 'dp', SWAP)]
    ppermute x14 -> x13, starting transfers between devices: 12.5 us -> 11.1 us  [the longest x4 3.19 us: spread(): a = jnp.concatenate([halve(a, at), pp(halve(a, 1 - at), axis, SWAP)])]
  transfers between devices with their start and end apart: 27 -> 27, of which waited for: 11 -> 17; matrix products, arithmetic and copies ran while one was open for 7% -> 6% of each run, Pallas kernels for 4% -> 17%
where the time goes in v4:
time: 111 us
  waiting for transfers between devices  50.6 us (46%)
  starting transfers between devices  30.6 us (28%)
  Pallas kernels  19.6 us (18%)
  other arithmetic  7.87 us (7%)
  local copies, waits for them, and re-layouts  1.5 us (1%)
    pallas_call x8, Pallas kernels, call(): pl.pallas_call(body, out_shape=outs, in_specs=specs, out_specs=jax.tree.m...  19.6 us
    ppermute x4, waiting for transfers between devices, spread(): a = jnp.concatenate([halve(a, at), pp(halve(a, 1 - at), axis, SWAP)])  18.8 us
    ppermute x10, starting transfers between devices, partner(): return pp(block, 'expert', [(i, i ^ k) for i in range(n)])  16.2 us
    ppermute x1, waiting for transfers between devices, token_gradient(): return join(back[:own], pp(back[own:], 'fsdp', SWAP), f)  9.7 us
    ppermute x2, waiting for transfers between devices, reduce_rows(): return [total, pp(total.astype(BF), 'fsdp', SWAP)]  6.93 us
    ppermute x10, waiting for transfers between devices, partner(): return pp(block, 'expert', [(i, i ^ k) for i in range(n)])  4.17 us
    ppermute x4, starting transfers between devices, spread(): a = jnp.concatenate([halve(a, at), pp(halve(a, 1 - at), axis, SWAP)])  3.19 us
    ppermute x2, starting transfers between devices, reduce_rows(): return [total, pp(total.astype(BF), 'fsdp', SWAP)]  3.11 us
  transfers between devices with their start and end apart: 27, of which 17 were waited for; matrix products, arithmetic and copies ran while one was open for 6% of the time, Pallas kernels for 17%

profile of v4, /device:TPU:0, one launch (start us, length us, event | category | flops | bytes accessed | tf_op | source)
XLA Modules:
  0.0 111.1 jit_solution(7804309918012561282)
XLA Ops:
  1.9 5.1 %collective-permute-start.15 = (bf16[2,768,128]{2,1,0:T(8,128)(2,1)S(1)}, bf16[2,768,128]{2,1,0:T(8,128)(2,1)}, u32[]{:S(2)}, u32[]{:S(2)}) collective-permute-start(bf16[2,768,128]{2,1,0:T(8,128)(2,1)S(1)} %get-tuple-element.214), channel_id=1, source_target_pairs={{0,6},{2,4},{4,2},{6,0},{1,7},{3,5},{5,3},{7,1},{8,14},{10,12},{12... | collective-permute-start | bytes 1179656 | tf_op jit(solution)/shard_map/ppermute | solution.py:220
  7.1 17.0 %conditional.6 = (bf16[256,1536]{1,0:T(8,128)(2,1)S(1)}, s32[256,2]{1,0:T(8,128)S(1)}, bf16[128,128]{1,0:T(8,128)(2,1)}) conditional(s32[]{:T(128)} %convert_element_type.50, () %tuple.67, (s32[]{:T(128)}, s32[]{:T(128)}, bf16[64,6144]{1,0:T(8,128)(2,1)S(1)}, s32[64,2]{0,1:T(2,128)S(1)}, f32[64,2]{0,1:T(2,128)S(1)}) %tuple.125), branch_computations={%region_0.0_spmd, %region_1.2_spmd} | conditional | flops 4788358 | bytes 8246522 | solution.py:224
  8.9 8.9 %collective-permute-done.2 = bf16[64,3072]{1,0:T(8,128)(2,1)S(1)} collective-permute-done((bf16[64,3072]{1,0:T(8,128)(2,1)S(1)}, bf16[64,3072]{1,0:T(8,128)(2,1)S(1)}, u32[]{:S(2)}, u32[]{:S(2)}) %collective-permute-start.2) | collective-permute-done | bytes 393248 | tf_op jit(solution)/shard_map/cond/branch_1_fun/ppermute | solution.py:251
  19.7 2.2 %collective-permute-done.4 = bf16[64,128]{1,0:T(8,128)(2,1)S(1)} collective-permute-done((bf16[64,128]{1,0:T(8,128)(2,1)S(1)}, bf16[64,128]{1,0:T(8,128)(2,1)S(1)}, u32[]{:S(2)}, u32[]{:S(2)}) %collective-permute-start.4) | collective-permute-done | bytes 16416 | tf_op jit(solution)/shard_map/cond/branch_1_fun/ppermute | solution.py:264
  28.6 14.5 %conditional.7 = (bf16[256,1536]{1,0:T(8,128)(2,1)}, bf16[1536,256]{0,1:T(8,128)(2,1)S(1)}) conditional(s32[]{:T(128)} %convert_element_type.51, () %tuple.73, (s32[]{:T(128)}, s32[]{:T(128)}, bf16[64,6144]{1,0:T(8,128)(2,1)}) %tuple.74), branch_computations={%region_2.3_spmd, %region_3.4_spmd} | conditional | flops 6291462 | bytes 9437344 | solution.py:224
  28.6 1.9 %broadcast_select_fusion.6 = (bf16[64,3072]{1,0:T(8,128)(2,1)S(1)}, bf16[64,3072]{1,0:T(8,128)(2,1)}) fusion(pred[]{:T(512)S(6)} %eq.25, bf16[64,6144]{1,0:T(8,128)(2,1)} %get-tuple-element.246, pred[]{:T(512)S(6)} %eq.26), kind=kLoop, calls=%fused_computation.26 | loop fusion | flops 393216 | bytes 1572866 | tf_op jit(solution)/shard_map/cond/branch_1_fun/jit(_where)/select_n | solution.py:246
  32.0 8.2 %collective-permute-done.13 = bf16[64,3072]{1,0:T(8,128)(2,1)S(1)} collective-permute-done((bf16[64,3072]{1,0:T(8,128)(2,1)}, bf16[64,3072]{1,0:T(8,128)(2,1)S(1)}, u32[]{:S(2)}, u32[]{:S(2)}) %collective-permute-start.13) | collective-permute-done | bytes 393248 | tf_op jit(solution)/shard_map/cond/branch_1_fun/ppermute | solution.py:251
  43.1 2.0 %collective-permute-done.17.r_5_ = bf16[2,768,128]{2,1,0:T(8,128)(2,1)S(1)} collective-permute-done((bf16[2,768,128]{2,1,0:T(8,128)(2,1)S(1)}, bf16[2,768,128]{2,1,0:T(8,128)(2,1)S(1)}, u32[]{:S(2)}, u32[]{:S(2)}) %collective-permute-start.17) | collective-permute-done | bytes 393248 | tf_op jit(solution)/shard_map/ppermute | solution.py:220
  47.9 3.3 %collective-permute-start.23 = (bf16[1,1536,128]{2,1,0:T(8,128)(2,1)}, bf16[1,1536,128]{2,1,0:T(8,128)(2,1)}, u32[]{:S(2)}, u32[]{:S(2)}) collective-permute-start(bf16[1,1536,128]{2,1,0:T(8,128)(2,1)} %down.1), channel_id=1, source_target_pairs={{0,4},{2,6},{4,0},{6,2},{1,5},{3,7},{5,1},{7,3},{8,12},{10,14},{12... | collective-permute-start | bytes 1179656 | tf_op jit(solution)/shard_map/ppermute | solution.py:220
  51.2 3.8 %conditional.8 = ((f32[128,512]{1,0:T(8,128)S(1)}, f32[128,512]{1,0:T(8,128)})) conditional(s32[]{:T(128)} %convert_element_type.52, () %tuple.77, (s32[]{:T(128)}, s32[]{:T(128)}, s32[]{:T(128)}, s32[]{:T(128)}, s32[256,2]{1,0:T(8,128)S(1)}, /*index=5*/bf16[256,1536]{1,0:T(8,128)(2,1)S(1)}, bf16[1,1536,128]{2,1,0:T(8,128)(2,1)S(1)}, ...), branch_computations={%region_4.5_spmd, %region_5.6_spmd} | conditional | flops 12 | bytes 524320 | solution.py:224
  51.3 3.7 %branch_1_fun.6 = (f32[128,512]{1,0:T(8,128)S(1)}, f32[128,512]{1,0:T(8,128)}) custom-call(s32[4]{0:T(128)S(1)} %pad_add_fusion.r_0_, s32[256,2]{1,0:T(8,128)S(1)} %get-tuple-element.124.r_1_, bf16[256,1536]{1,0:T(8,128)(2,1)S(1)} %get-tuple-element.125.r_2_, bf16[1,1536,128]{2,1,0:T(8,128)(2,1)S(1)} %get-tuple-element.126.r_3_, ...), custom_call_target="tpu_custom_call" | custom-call | tf_op jit(solution)/shard_map/cond/branch_1_fun/pallas_call | solution.py:18
  55.6 2.4 %shard_map.91 = (f32[128,512]{1,0:T(8,128)S(1)}, f32[128,512]{1,0:T(8,128)S(1)}) custom-call(s32[2]{0:T(128)S(1)} %pad_add_fusion.1.r_0_, s32[256,2]{1,0:T(8,128)S(1)} %get-tuple-element.211.r_1_, bf16[256,1536]{1,0:T(8,128)(2,1)S(1)} %get-tuple-element.212.r_2_, f32[128,512]{1,0:T(8,128)S(1)} %get-tuple-element.220.r_3_, ...), custom_call_target="tpu_custom_call" | custom-call | tf_op jit(solution)/shard_map/pallas_call | solution.py:18
  58.1 7.4 %conditional.9 = (f32[128,512]{1,0:T(8,128)S(1)}, bf16[128,512]{1,0:T(8,128)(2,1)}) conditional(s32[]{:T(128)} %convert_element_type.49, () %tuple.69, (f32[128,512]{1,0:T(8,128)S(1)}, f32[128,512]{1,0:T(8,128)S(1)}) %tuple.81), branch_computations={%region_6.7_spmd, %region_7.8_spmd} | conditional | flops 131072 | bytes 2490464 | solution.py:224
  61.3 4.2 %collective-permute-done.7 = bf16[128,512]{1,0:T(8,128)(2,1)} collective-permute-done((bf16[128,512]{1,0:T(8,128)(2,1)S(1)}, bf16[128,512]{1,0:T(8,128)(2,1)}, u32[]{:S(2)}, u32[]{:S(2)}) %collective-permute-start.7) | collective-permute-done | bytes 131104 | tf_op jit(solution)/shard_map/cond/branch_1_fun/ppermute | solution.py:278
  66.1 7.2 %conditional.10 = (f32[128,512]{1,0:T(8,128)}, f32[1536,128]{1,0:T(8,128)}, bf16[1536,128]{1,0:T(8,128)(2,1)}, bf16[1536,128]{1,0:T(8,128)(2,1)}, bf16[1536,128]...) conditional(s32[]{:T(128)} %convert_element_type.49, () %tuple.65, (bf16[128,128]{1,0:T(8,128)(2,1)}, ...), branch_computations={%region_8.9_spmd, %region_9.10_spmd} | conditional | bytes 2621568 | solution.py:224
  67.6 1.7 %branch_1_fun.7 = (f32[128,512]{1,0:T(8,128)}, bf16[128,256]{1,0:T(8,128)(2,1)S(1)}) custom-call(bf16[128,128]{1,0:T(8,128)(2,1)} %get-tuple-element.134.info, f32[128,512]{1,0:T(8,128)S(1)} %get-tuple-element.135.part, bf16[128,512]{1,0:T(8,128)(2,1)} %get-tuple-element.136.rest_0_), custom_call_target="tpu_custom_call" | custom-call | tf_op jit(solution)/shard_map/cond/branch_1_fun/pallas_call | solution.py:18
  70.6 2.7 %branch_1_fun.8 = (f32[1536,128]{1,0:T(8,128)}, bf16[1536,128]{1,0:T(8,128)(2,1)}, bf16[1536,128]{1,0:T(8,128)(2,1)}, bf16[1536,128]{1,0:T(8,128)(2,1)}) custom-call(s32[4]{0:T(128)S(1)} %get-tuple-element.138.r_0_, s32[256,2]{1,0:T(8,128)S(1)} %get-tuple-element.139.r_1_, bf16[1536,256]{1,0:T(8,128)(2,1)S(1)} %copy.19.r_2_, ...), custom_call_target="tpu_custom_call" | custom-call | tf_op jit(solution)/shard_map/cond/branch_1_fun/pallas_call | solution.py:18
  74.8 2.9 %collective-permute-start.26 = (bf16[1536,128]{1,0:T(8,128)(2,1)}, bf16[1536,128]{1,0:T(8,128)(2,1)}, u32[]{:S(2)}, u32[]{:S(2)}) collective-permute-start(bf16[1536,128]{1,0:T(8,128)(2,1)} %get-tuple-element.231), channel_id=1, source_target_pairs={{0,2},{2,0},{4,6},{6,4},{1,3},{3,1},{5,7},{7,5},{8,10},{10,8},{12,... | collective-permute-start | bytes 1179656 | tf_op jit(solution)/shard_map/ppermute | solution.py:220
  77.7 29.5 %conditional.11 = (bf16[64,6144]{1,0:T(8,128)(2,1)}) conditional(s32[]{:T(128)} %convert_element_type.53, () %tuple.85, (s32[]{:T(128)}, s32[]{:T(128)}, s32[]{:T(128)}, s32[]{:T(128)}, s32[]{:T(128)}, /*index=5*/s32[]{:T(128)}, s32[]{:T(128)}, s32[256,2]{1,0:T(8,128)S(1)}, bf16[256,1536]{1,0:T(8,128)(2,1)}, bf16[1,1536,128]{2,1,0:T(8,128)(2,1)S(1)}, ...), branch_computations={%region_10.11_spmd, %region_11.12_spmd} | conditional | flops 7143426 | bytes 9634100 | solution.py:224
  77.8 3.4 %branch_1_fun.9 = (f32[128,256]{1,0:T(8,128)S(1)}, f32[128,256]{1,0:T(8,128)S(1)}) custom-call(s32[5]{0:T(128)S(1)} %stack.60.r_0_, s32[256,2]{1,0:T(8,128)S(1)} %get-tuple-element.154.r_1_, bf16[256,1536]{1,0:T(8,128)(2,1)} %get-tuple-element.157.r_2_, bf16[1,1536,128]{2,1,0:T(8,128)(2,1)S(1)} %get-tuple-element.158.r_3_, ...), custom_call_target="tpu_custom_call" | custom-call | tf_op jit(solution)/shard_map/cond/branch_1_fun/pallas_call | solution.py:18
  84.2 2.8 %collective-permute-done.9.rest_0_ = bf16[128,256]{1,0:T(8,128)(2,1)S(1)} collective-permute-done((bf16[128,256]{1,0:T(8,128)(2,1)S(1)}, bf16[128,256]{1,0:T(8,128)(2,1)S(1)}, u32[]{:S(2)}, u32[]{:S(2)}) %collective-permute-start.9) | collective-permute-done | bytes 65568 | tf_op jit(solution)/shard_map/cond/branch_1_fun/ppermute | solution.py:278
  89.6 3.3 %branch_1_fun.11 = (bf16[128,1536]{1,0:T(8,128)(2,1)S(1)}, bf16[128,1536]{1,0:T(8,128)(2,1)S(1)}) custom-call(s32[5]{0:T(128)S(1)} %stack.56.r_0_, s32[256,2]{1,0:T(8,128)S(1)} %get-tuple-element.154.r_1_, bf16[128,512]{1,0:T(8,128)(2,1)S(1)} %branch_1_fun.10.r_2_, bf16[128,512]{1,0:T(8,128)(2,1)S(1)} %collective-permute-done.10.r_3_, ...), custom_call_target="tpu_custom_call" | custom-call | tf_op jit(solution)/shard_map/cond/branch_1_fun/pallas_call | solution.py:18
  96.5 9.7 %collective-permute-done.12 = bf16[64,3072]{1,0:T(8,128)(2,1)S(1)} collective-permute-done((bf16[64,3072]{1,0:T(8,128)(2,1)S(1)}, bf16[64,3072]{1,0:T(8,128)(2,1)S(1)}, u32[]{:S(2)}, u32[]{:S(2)}) %collective-permute-start.12) | collective-permute-done | bytes 393248 | tf_op jit(solution)/shard_map/cond/branch_1_fun/ppermute | solution.py:400
  108.7 2.4 %add_bitcast_fusion = f32[1,1536,128]{2,1,0:T(8,128)} fusion(bf16[1536,128]{1,0:T(8,128)(2,1)} %collective-permute-done.26, bf16[1536,128]{1,0:T(8,128)(2,1)} %collective-permute-done.25, f32[1536,128]{1,0:T(8,128)} %get-tuple-element.238, bf16[1536,128]{1,0:T(8,128)(2,1)S(1)} %collective-permute-done.24), kind=kLoop, calls=%fused_computation.31 | loop fusion | flops 1179648 | bytes 2752512 | tf_op jit(solution)/shard_map/broadcast_in_dim | solution.py:410
  (85 shorter events, 39.3 us)
Async XLA Ops:
  1.9 22.2 %collective-permute-start.15 = (bf16[2,768,128]{2,1,0:T(8,128)(2,1)S(1)}, bf16[2,768,128]{2,1,0:T(8,128)(2,1)}, u32[]{:S(2)}, u32[]{:S(2)}) collective-permute-start(bf16[2,768,128]{2,1,0:T(8,128)(2,1)S(1)} %get-tuple-element.214), channel_id=1, source_target_pairs={{0,6},{2,4},{4,2},{6,0},{1,7},{3,5},{5,3},{7,1},{8,14},{10,12},{12... | collective-permute-start | bytes 1179656 | tf_op jit(solution)/shard_map/ppermute | solution.py:220
  7.0 17.7 %collective-permute-start.16 = (bf16[1,1536,128]{2,1,0:T(8,128)(2,1)S(1)}, bf16[1,1536,128]{2,1,0:T(8,128)(2,1)}, u32[]{:S(2)}, u32[]{:S(2)}) collective-permute-start(bf16[1,1536,128]{2,1,0:T(8,128)(2,1)S(1)} %copy-done), channel_id=1, source_target_pairs={{0,2},{2,0},{4,6},{6,4},{1,3},{3,1},{5,7},{7,5},{8,10},{10,8},{12,... | collective-permute-start | bytes 1179656 | tf_op jit(solution)/shard_map/ppermute | solution.py:220
  7.2 10.6 %collective-permute-start.2 = (bf16[64,3072]{1,0:T(8,128)(2,1)S(1)}, bf16[64,3072]{1,0:T(8,128)(2,1)S(1)}, u32[]{:S(2)}, u32[]{:S(2)}) collective-permute-start(bf16[64,3072]{1,0:T(8,128)(2,1)S(1)} %get-tuple-element.273), channel_id=1, source_target_pairs={{0,8},{8,0},{1,9},{9,1},{2,10},{10,2},{3,11},{11,3},{4,12},{12,4},... | collective-permute-start | bytes 1179656 | tf_op jit(solution)/shard_map/cond/branch_1_fun/ppermute | solution.py:251
  17.9 6.1 %collective-permute-start.3 = (bf16[128,1536]{1,0:T(8,128)(2,1)S(1)}, bf16[128,1536]{1,0:T(8,128)(2,1)S(1)}, u32[]{:S(2)}, u32[]{:S(2)}) collective-permute-start(bf16[128,1536]{1,0:T(8,128)(2,1)S(1)} %get-tuple-element.271), channel_id=1, source_target_pairs={{0,1},{1,0},{2,3},{3,2},{4,5},{5,4},{6,7},{7,6},{8,9},{9,8},{10,11... | collective-permute-start | bytes 1179656 | tf_op jit(solution)/shard_map/cond/branch_1_fun/ppermute | solution.py:251
  18.1 3.8 %collective-permute-start.4 = (bf16[64,128]{1,0:T(8,128)(2,1)S(1)}, bf16[64,128]{1,0:T(8,128)(2,1)S(1)}, u32[]{:S(2)}, u32[]{:S(2)}) collective-permute-start(bf16[64,128]{1,0:T(8,128)(2,1)S(1)} %concatenate.25), channel_id=1, source_target_pairs={{0,8},{8,0},{1,9},{9,1},{2,10},{10,2},{3,11},{11,3},{4,12},{12,4},... | collective-permute-start | bytes 49160 | tf_op jit(solution)/shard_map/cond/branch_1_fun/ppermute | solution.py:264
  22.6 1.4 %collective-permute-start.5 = (bf16[128,128]{1,0:T(8,128)(2,1)}, bf16[128,128]{1,0:T(8,128)(2,1)S(1)}, u32[]{:S(2)}, u32[]{:S(2)}) collective-permute-start(bf16[128,128]{1,0:T(8,128)(2,1)} %pad_maximum_fusion.4), channel_id=1, source_target_pairs={{0,1},{1,0},{2,3},{3,2},{4,5},{5,4},{6,7},{7,6},{8,9},{9,8},{10,11... | collective-permute-start | bytes 98312 | tf_op jit(solution)/shard_map/cond/branch_1_fun/ppermute | solution.py:265
  24.8 20.4 %collective-permute-start.17 = (bf16[2,768,128]{2,1,0:T(8,128)(2,1)S(1)}, bf16[2,768,128]{2,1,0:T(8,128)(2,1)S(1)}, u32[]{:S(2)}, u32[]{:S(2)}) collective-permute-start(bf16[2,768,128]{2,1,0:T(8,128)(2,1)S(1)} %get-tuple-element.214), channel_id=1, source_target_pairs={{0,4},{2,6},{4,0},{6,2},{1,5},{3,7},{5,1},{7,3},{8,12},{10,14},{12... | collective-permute-start | bytes 1179656 | tf_op jit(solution)/shard_map/ppermute | solution.py:220
  25.4 19.7 %collective-permute-start.19 = (bf16[2,768,128]{2,1,0:T(8,128)(2,1)}, bf16[2,768,128]{2,1,0:T(8,128)(2,1)}, u32[]{:S(2)}, u32[]{:S(2)}) collective-permute-start(bf16[2,768,128]{2,1,0:T(8,128)(2,1)} %collective-permute-done.15), channel_id=1, source_target_pairs={{0,16},{16,0},{1,17},{17,1},{2,18},{18,2},{3,19},{19,3},{4,20},{20... | collective-permute-start | bytes 1179656 | tf_op jit(solution)/shard_map/ppermute | solution.py:312
  26.9 24.3 %collective-permute-start.18 = (bf16[1,1536,128]{2,1,0:T(8,128)(2,1)S(1)}, bf16[1,1536,128]{2,1,0:T(8,128)(2,1)}, u32[]{:S(2)}, u32[]{:S(2)}) collective-permute-start(bf16[1,1536,128]{2,1,0:T(8,128)(2,1)S(1)} %copy-done.1), channel_id=1, source_target_pairs={{0,2},{2,0},{4,6},{6,4},{1,3},{3,1},{5,7},{7,5},{8,10},{10,8},{12,... | collective-permute-start | bytes 1179656 | tf_op jit(solution)/shard_map/ppermute | solution.py:220
  30.5 9.7 %collective-permute-start.13 = (bf16[64,3072]{1,0:T(8,128)(2,1)}, bf16[64,3072]{1,0:T(8,128)(2,1)S(1)}, u32[]{:S(2)}, u32[]{:S(2)}) collective-permute-start(bf16[64,3072]{1,0:T(8,128)(2,1)} %get-tuple-element.280), channel_id=1, source_target_pairs={{0,8},{8,0},{1,9},{9,1},{2,10},{10,2},{3,11},{11,3},{4,12},{12,4},... | collective-permute-start | bytes 1179656 | tf_op jit(solution)/shard_map/cond/branch_1_fun/ppermute | solution.py:251
  40.4 1.8 %collective-permute-start.14 = (bf16[128,1536]{1,0:T(8,128)(2,1)S(1)}, bf16[128,1536]{1,0:T(8,128)(2,1)S(1)}, u32[]{:S(2)}, u32[]{:S(2)}) collective-permute-start(bf16[128,1536]{1,0:T(8,128)(2,1)S(1)} %get-tuple-element.278), channel_id=1, source_target_pairs={{0,1},{1,0},{2,3},{3,2},{4,5},{5,4},{6,7},{7,6},{8,9},{9,8},{10,11... | collective-permute-start | bytes 1179656 | tf_op jit(solution)/shard_map/cond/branch_1_fun/ppermute | solution.py:251
  45.1 10.5 %collective-permute-start.20 = (bf16[2,768,128]{2,1,0:T(8,128)(2,1)S(1)}, bf16[2,768,128]{2,1,0:T(8,128)(2,1)}, u32[]{:S(2)}, u32[]{:S(2)}) collective-permute-start(bf16[2,768,128]{2,1,0:T(8,128)(2,1)S(1)} %collective-permute-done.17.r_5_), channel_id=1, source_target_pairs={{0,16},{16,0},{1,17},{17,1},{2,18},{18,2},{3,19},{19,3},{4,20},{20... | collective-permute-start | bytes 1179656 | tf_op jit(solution)/shard_map/ppermute | solution.py:325
  46.7 18.8 %collective-permute-start.21 = (bf16[1,768,128]{2,1,0:T(8,128)(2,1)S(1)}, bf16[1,768,128]{2,1,0:T(8,128)(2,1)S(1)}, u32[]{:S(2)}, u32[]{:S(2)}) collective-permute-start(bf16[1,768,128]{2,1,0:T(8,128)(2,1)S(1)} %get-tuple-element.229), channel_id=1, source_target_pairs={{0,6},{2,4},{4,2},{6,0},{1,7},{3,5},{5,3},{7,1},{8,14},{10,12},{12... | collective-permute-start | bytes 589832 | tf_op jit(solution)/shard_map/ppermute | solution.py:220
  47.9 29.8 %collective-permute-start.22 = (bf16[1,1536,128]{2,1,0:T(8,128)(2,1)}, bf16[1,1536,128]{2,1,0:T(8,128)(2,1)}, u32[]{:S(2)}, u32[]{:S(2)}) collective-permute-start(bf16[1,1536,128]{2,1,0:T(8,128)(2,1)} %down.1), channel_id=1, source_target_pairs={{0,2},{2,0},{4,6},{6,4},{1,3},{3,1},{5,7},{7,5},{8,10},{10,8},{12,... | collective-permute-start | bytes 1179656 | tf_op jit(solution)/shard_map/ppermute | solution.py:220
  47.9 29.8 %collective-permute-start.23 = (bf16[1,1536,128]{2,1,0:T(8,128)(2,1)}, bf16[1,1536,128]{2,1,0:T(8,128)(2,1)}, u32[]{:S(2)}, u32[]{:S(2)}) collective-permute-start(bf16[1,1536,128]{2,1,0:T(8,128)(2,1)} %down.1), channel_id=1, source_target_pairs={{0,4},{2,6},{4,0},{6,2},{1,5},{3,7},{5,1},{7,3},{8,12},{10,14},{12... | collective-permute-start | bytes 1179656 | tf_op jit(solution)/shard_map/ppermute | solution.py:220
  58.1 1.6 %collective-permute-start.6 = (f32[128,512]{1,0:T(8,128)S(1)}, f32[128,512]{1,0:T(8,128)S(1)}, u32[]{:S(2)}, u32[]{:S(2)}) collective-permute-start(f32[128,512]{1,0:T(8,128)S(1)} %get-tuple-element.133), channel_id=1, source_target_pairs={{0,1},{1,0},{2,3},{3,2},{4,5},{5,4},{6,7},{7,6},{8,9},{9,8},{10,11... | collective-permute-start | bytes 786440 | tf_op jit(solution)/shard_map/cond/branch_1_fun/ppermute | solution.py:277
  59.7 5.7 %collective-permute-start.7 = (bf16[128,512]{1,0:T(8,128)(2,1)S(1)}, bf16[128,512]{1,0:T(8,128)(2,1)}, u32[]{:S(2)}, u32[]{:S(2)}) collective-permute-start(bf16[128,512]{1,0:T(8,128)(2,1)S(1)} %get-tuple-element.266), channel_id=1, source_target_pairs={{0,8},{8,0},{1,9},{9,1},{2,10},{10,2},{3,11},{11,3},{4,12},{12,4},... | collective-permute-start | bytes 393224 | tf_op jit(solution)/shard_map/cond/branch_1_fun/ppermute | solution.py:278
  66.1 7.2 %collective-permute-start.1 = (bf16[1,768,128]{2,1,0:T(8,128)(2,1)}, bf16[1,768,128]{2,1,0:T(8,128)(2,1)}, u32[]{:S(2)}, u32[]{:S(2)}) collective-permute-start(bf16[1,768,128]{2,1,0:T(8,128)(2,1)} %get-tuple-element.146), channel_id=1, source_target_pairs={{0,16},{16,0},{1,17},{17,1},{2,18},{18,2},{3,19},{19,3},{4,20},{20... | collective-permute-start | bytes 589832 | tf_op jit(solution)/shard_map/cond/branch_1_fun/ppermute | solution.py:343
  73.3 33.9 %collective-permute-start.24 = (bf16[1536,128]{1,0:T(8,128)(2,1)}, bf16[1536,128]{1,0:T(8,128)(2,1)S(1)}, u32[]{:S(2)}, u32[]{:S(2)}) collective-permute-start(bf16[1536,128]{1,0:T(8,128)(2,1)} %get-tuple-element.233), channel_id=1, source_target_pairs={{0,6},{2,4},{4,2},{6,0},{1,7},{3,5},{5,3},{7,1},{8,14},{10,12},{12... | collective-permute-start | bytes 1179656 | tf_op jit(solution)/shard_map/ppermute | solution.py:220
  74.8 33.9 %collective-permute-start.25 = (bf16[1536,128]{1,0:T(8,128)(2,1)}, bf16[1536,128]{1,0:T(8,128)(2,1)}, u32[]{:S(2)}, u32[]{:S(2)}) collective-permute-start(bf16[1536,128]{1,0:T(8,128)(2,1)} %get-tuple-element.232), channel_id=1, source_target_pairs={{0,4},{2,6},{4,0},{6,2},{1,5},{3,7},{5,1},{7,3},{8,12},{10,14},{12... | collective-permute-start | bytes 1179656 | tf_op jit(solution)/shard_map/ppermute | solution.py:220
  74.8 33.9 %collective-permute-start.26 = (bf16[1536,128]{1,0:T(8,128)(2,1)}, bf16[1536,128]{1,0:T(8,128)(2,1)}, u32[]{:S(2)}, u32[]{:S(2)}) collective-permute-start(bf16[1536,128]{1,0:T(8,128)(2,1)} %get-tuple-element.231), channel_id=1, source_target_pairs={{0,2},{2,0},{4,6},{6,4},{1,3},{3,1},{5,7},{7,5},{8,10},{10,8},{12,... | collective-permute-start | bytes 1179656 | tf_op jit(solution)/shard_map/ppermute | solution.py:220
  82.7 4.3 %collective-permute-start.9 = (bf16[128,256]{1,0:T(8,128)(2,1)S(1)}, bf16[128,256]{1,0:T(8,128)(2,1)S(1)}, u32[]{:S(2)}, u32[]{:S(2)}) collective-permute-start(bf16[128,256]{1,0:T(8,128)(2,1)S(1)} %get-tuple-element.268), channel_id=1, source_target_pairs={{0,8},{8,0},{1,9},{9,1},{2,10},{10,2},{3,11},{11,3},{4,12},{12,4},... | collective-permute-start | bytes 196616 | tf_op jit(solution)/shard_map/cond/branch_1_fun/ppermute | solution.py:278
  92.9 1.8 %collective-permute-start.11 = (bf16[128,1536]{1,0:T(8,128)(2,1)S(1)}, bf16[128,1536]{1,0:T(8,128)(2,1)S(1)}, u32[]{:S(2)}, u32[]{:S(2)}) collective-permute-start(bf16[128,1536]{1,0:T(8,128)(2,1)S(1)} %get-tuple-element.174), channel_id=1, source_target_pairs={{0,1},{1,0},{2,3},{3,2},{4,5},{5,4},{6,7},{7,6},{8,9},{9,8},{10,11... | collective-permute-start | bytes 1179656 | tf_op jit(solution)/shard_map/cond/branch_1_fun/ppermute | solution.py:399
  94.9 11.2 %collective-permute-start.12 = (bf16[64,3072]{1,0:T(8,128)(2,1)S(1)}, bf16[64,3072]{1,0:T(8,128)(2,1)S(1)}, u32[]{:S(2)}, u32[]{:S(2)}) collective-permute-start(bf16[64,3072]{1,0:T(8,128)(2,1)S(1)} %get-tuple-element.282), channel_id=1, source_target_pairs={{0,8},{8,0},{1,9},{9,1},{2,10},{10,2},{3,11},{11,3},{4,12},{12,4},... | collective-permute-start | bytes 1179656 | tf_op jit(solution)/shard_map/cond/branch_1_fun/ppermute | solution.py:400
  (10 other events, 61.8 us)

commit v5 on v4

v5 whole, which is shorter than its diff:
```python
import jax
import jax.numpy as jnp
from jax import lax
from jax.experimental import pallas as pl
from jax.experimental.pallas import tpu as pltpu
from jax.sharding import PartitionSpec as P

BF = jnp.bfloat16
F32 = jnp.float32
VMEM = pl.BlockSpec(memory_space=pltpu.VMEM)
SMEM = pl.BlockSpec(memory_space=pltpu.SMEM)
ANY = pl.BlockSpec(memory_space=pl.ANY)
FF = 128
SWAP = [(0, 1), (1, 0)]
PARAMS = pltpu.CompilerParams(vmem_limit_bytes=48 * 1024 * 1024)


def call(body, outs, specs, *args, scratch=(), flops=0):
    return pl.pallas_call(
        body,
        out_shape=outs,
        in_specs=specs,
        out_specs=jax.tree.map(lambda _: VMEM, outs),
        scratch_shapes=list(scratch),
        compiler_params=PARAMS,
        cost_estimate=pl.CostEstimate(flops=flops, bytes_accessed=0, transcendentals=0),
    )(*args)


def mm(left, right, dims):
    return lax.dot_general(left, right, (dims, ((), ())), preferred_element_type=F32)


def weight_copies(layout, scal, refs, held, sems):
    slots, at, sem = [], 0, 0
    rows = held.shape[0]
    half = rows // 2
    parts = held.shape[1] // (len(layout) * FF)
    mine = scal[len(layout)]
    near = pl.ds(pl.multiple_of(mine * half, 16), half)
    far = pl.ds(pl.multiple_of((1 - mine) * half, 16), half)
    for s, kind in enumerate(layout):
        copies = []
        for p in range(parts):
            lanes = pl.ds((s * parts + p) * FF, FF)
            if kind == "parts":
                pairs = [(refs[at + p].at[0], pl.ds(0, rows))]
            else:
                pairs = [(refs[at].at[p], near), (refs[at + 1].at[p], far)]
            for source, where in pairs:
                copies.append(pltpu.make_async_copy(source, held.at[where, lanes], sems.at[sem]))
                sem += 1
        at += parts if kind == "parts" else 2
        slots.append(copies)
    for copies in slots:
        for c in copies:
            c.start()
    return slots


def copy_count(layout, parts):
    return sum(parts if kind == "parts" else 2 * parts for kind in layout)


def pick(ids, label, pair):
    zero = jnp.zeros((), pair[0].dtype)
    return jnp.where(ids[:, 0:1] == label, pair[0], zero) + jnp.where(
        ids[:, 1:2] == label, pair[1], zero
    )


def forward_sums(layout, outs, scal, ids, rows, *refs):
    held, sems = refs[-2:]
    results = refs[-2 - outs : -2]
    width = held.shape[1] // len(layout)
    copied = sum(1 if kind == "parts" and width == FF else 2 for kind in layout)
    base, refs = refs[: len(refs) - 2 - outs - copied], refs[-2 - outs - copied :]
    total = [0.0, 0.0]
    for s, copies in enumerate(weight_copies(layout, scal, refs, held, sems)):
        for c in copies:
            c.wait()
        value = mm(rows[...], held[:, s * width : (s + 1) * width], ((1,), (0,)))
        for k in range(2):
            total[k] = total[k] + jnp.where(ids[:, k : k + 1] == scal[s], value, 0.0)
    m = results[0].shape[0]
    for j, out in enumerate(results):
        for k in range(2):
            lanes = slice(k * width, (k + 1) * width)
            value = total[k][j * m : (j + 1) * m]
            out[:, lanes] = base[j][:, lanes] + value if base else value


def full_sums(part, *others):
    if not others:
        return part[...]
    (other,) = others
    m = other.shape[0] // 2
    return part[...] + jnp.concatenate([other[m:, :], other[:m, :]], axis=0).astype(F32)


def slot_weight(info, k):
    low, middle, high = (info[:, at + k : at + k + 1].astype(F32) for at in (6, 4, 2))
    return (high + middle) + low


def gate_and_up(total, k):
    ff = total.shape[1] // 4
    return total[:, 2 * k * ff : (2 * k + 1) * ff], total[:, (2 * k + 1) * ff : (2 * k + 2) * ff]


def hidden_step(info, *refs):
    total, hidden = full_sums(*refs[:-1]), refs[-1]
    for k in range(2):
        gate, up = gate_and_up(total, k)
        act = gate * jax.nn.sigmoid(gate)
        ff = gate.shape[1]
        hidden[:, k * ff : (k + 1) * ff] = (slot_weight(info, k) * (act * up)).astype(BF)


def grad_step(given, info, *refs):
    total, down, grads = full_sums(*refs[:given]), full_sums(*refs[given:-1]), refs[-1]
    for k in range(2):
        gate, up = gate_and_up(total, k)
        ff = gate.shape[1]
        hidden_grad = slot_weight(info, k) * down[:, k * ff : (k + 1) * ff]
        sig = jax.nn.sigmoid(gate)
        slope = sig * (1.0 + gate * (1.0 - sig))
        at = 2 * k * ff
        grads[:, at : at + ff] = (hidden_grad * up * slope).astype(BF)
        grads[:, at + ff : at + 2 * ff] = (hidden_grad * (gate * sig)).astype(BF)


def stacked(blocks):
    return jnp.concatenate([b[...] for b in blocks], axis=0) if len(blocks) > 1 else blocks[0][...]


def pairs_of(blocks):
    both = stacked(blocks)
    width = both.shape[1] // 2
    return both[:, :width], both[:, width:]


def down_products(count, scal, ids, scaled_t, *refs):
    outs, rows = refs[-count - 1 : -1], refs[-1]
    ff = outs[0].shape[1]

    @pl.when(pl.program_id(0) == 0)
    def _():
        hidden = pairs_of(refs[: -count - 1])
        for j in range(count):
            rows[:, j * ff : (j + 1) * ff] = pick(ids, scal[j], hidden)

    value = mm(scaled_t[...], rows[...], ((1,), (0,)))
    for j in range(count):
        outs[j][...] = value[:, j * ff : (j + 1) * ff].astype(outs[j].dtype)


def token_sums(layout, given, outs, scal, ids, *refs):
    held, sems = refs[-2:]
    results = refs[-2 - outs : -2]
    slots = weight_copies(layout, scal, refs[given:], held, sems)
    grads = pairs_of(refs[:given])
    rows = jnp.concatenate([pick(ids, scal[s], grads) for s in range(len(layout))], axis=1)
    for copies in slots:
        for c in copies:
            c.wait()
    m = results[0].shape[0]
    width = held.shape[0]
    step = width // 3 if width % 384 == 0 else width
    for at in range(0, width, step):
        value = mm(rows, held[at : at + step, :], ((1,), (1,))).astype(BF)
        for j, out in enumerate(results):
            out[:, at : at + step] = value[j * m : (j + 1) * m]


def pack(count, tail, scal, *refs):
    blocks, apart, (sent, kept) = refs[:count], refs[count:-2], refs[-2:]
    half = sent.shape[1] - tail
    m = blocks[0].shape[0]
    for v in range(2):

        @pl.when(scal[0] == v)
        def _():
            for j, block in enumerate(blocks):
                rows = slice(j * m, (j + 1) * m)
                kept[rows, :half] = block[:, v * half : (v + 1) * half]
                sent[rows, :half] = block[:, (1 - v) * half : (2 - v) * half]
                if tail:
                    rest = apart[j][...] if apart else block[:, 2 * half :]
                    kept[rows, half:] = rest
                    sent[rows, half:] = rest


def turn(block, out):
    out[...] = block[...].T


def place_columns(scal, *refs):
    out = refs[-1]
    width = refs[0].shape[1]
    for j, block in enumerate(refs[:-1]):
        out[:, pl.ds(pl.multiple_of(scal[j] * width, 128), width)] = block[...]


def split3(value):
    high = lax.reduce_precision(value, 8, 7)
    rest = value - high
    middle = lax.reduce_precision(rest, 8, 7)
    low = rest - middle
    return [high.astype(BF), middle.astype(BF), low.astype(BF)]


def after(value, *earlier):
    return lax.optimization_barrier((value, *earlier))[0]


def after_all(values, earlier):
    return lax.optimization_barrier((tuple(values), tuple(earlier)))[0]


def near_rows(scal, gate, up, down, pair, single, sems):
    half = pair.shape[1]
    rows = pl.ds(pl.multiple_of(scal[0] * half, 16), half)
    copies = [
        pltpu.make_async_copy(source.at[0, rows], target, sems.at[i])
        for i, (source, target) in enumerate(
            ((gate, pair.at[0]), (up, pair.at[1]), (down, single.at[0]))
        )
    ]
    for c in copies:
        c.start()
    for c in copies:
        c.wait()


def per_device(tokens, cotangent, expert_ids, combine, gate_weight, up_weight, down_weight):
    n = lax.axis_size("expert")
    nx, nc = lax.axis_size("fsdp"), lax.axis_size("dp")
    g, f, e, d = (lax.axis_index(a) for a in ("groups", "fsdp", "expert", "dp"))
    own, width = tokens.shape
    quarter, ff = gate_weight.shape[1:]
    half = quarter // 2
    pp = lax.ppermute
    small = nx == 2 and nc == 2
    plane = nx * nc
    rows = plane * own
    blocks = 2 if small else 1
    m = rows // blocks

    def partner(block, k):
        return pp(block, "expert", [(i, i ^ k) for i in range(n)])

    def region(work, *earlier):
        shapes = jax.eval_shape(work)
        return lax.cond(
            after(g, *earlier) < n * n,
            work,
            lambda: jax.tree.map(lambda s: jnp.zeros(s.shape, s.dtype), shapes),
        )

    gu_near, dn_near = call(
        near_rows,
        [jax.ShapeDtypeStruct((c, half, ff), BF) for c in (2, 1)],
        [SMEM, ANY, ANY, ANY],
        g.reshape(1).astype(jnp.int32),
        gate_weight,
        up_weight,
        down_weight,
        scratch=[pltpu.SemaphoreType.DMA((3,))],
    )
    first_one, *later_ones = range(n - 1, 1, -1)
    gu = {first_one: partner(gu_near, first_one)}
    nearest = [partner(gate_weight, 1)]

    def swap_columns(blocks, axis, at, tail):
        m, w = blocks[0].shape
        apart = tail and blocks[1].shape[1] == tail
        w, count = (w, 1) if apart else (w - tail, len(blocks))
        shape = jax.ShapeDtypeStruct((count * m, w // 2 + tail), BF)
        sent, kept = call(
            lambda *r: pack(count, tail, *r),
            [shape] * 2,
            [SMEM] + [VMEM] * len(blocks),
            at.reshape(1).astype(jnp.int32),
            *blocks,
        )
        return [kept, pp(sent, axis, SWAP)]

    def spread(a, extra=None):
        if small:
            tail = 0 if extra is None else extra.shape[1]
            a = [a] if extra is None else [a, extra]
            return swap_columns(swap_columns(a, "fsdp", f, tail), "dp", d, tail)
        a = a.reshape(own, plane, quarter).transpose(1, 0, 2)
        return [lax.all_to_all(a, ("fsdp", "dp"), 0, 0, tiled=True).reshape(rows, quarter)]

    def spread_tokens():
        extra = jnp.concatenate(
            [expert_ids.astype(F32).astype(BF)]
            + split3(combine)
            + [jnp.zeros((own, 120), BF)],
            axis=1,
        )
        if small:
            kept, came = spread(tokens, extra)
            mine_info = kept[:, quarter:]
            info = jnp.concatenate([mine_info, came[:, quarter:]])
            tok = jnp.concatenate([kept[:, :quarter], came[:, :quarter]])
        else:
            mine_info = extra
            info = lax.all_gather(extra, ("fsdp", "dp"), axis=0, tiled=True)
            (tok,) = spread(tokens)
        return tok, info[:, :2].astype(jnp.int32), mine_info

    def spread_cotangent():
        return jnp.concatenate(spread(cotangent))

    def turned():
        return call(turn, jax.ShapeDtypeStruct((quarter, rows), BF), [VMEM], cot)

    def reduce_rows(parts):
        if small:
            total = parts[0] + pp(parts[1], "dp", SWAP)
            return [total, pp(total.astype(BF), "fsdp", SWAP)]
        return [lax.psum_scatter(parts[0], ("fsdp", "dp"), scatter_dimension=0, tiled=True)]

    def share_rows(a):
        if small:
            return [a, pp(a, "dp", SWAP)]
        return [lax.all_gather(a, ("fsdp", "dp"), axis=0, tiled=True)]

    def held(kinds, parts):
        return [
            pltpu.VMEM((quarter, len(kinds) * parts * ff), BF),
            pltpu.SemaphoreType.DMA((copy_count(kinds, parts),)),
        ]

    def sums(a, slots, parts, base=()):
        kinds = [kind for kind, _, _ in slots]
        refs = [r for _, _, rs in slots for r in rs]
        scal = jnp.stack([label for _, label, _ in slots] + [g]).astype(jnp.int32)
        return call(
            lambda *r: forward_sums(kinds, blocks, *r),
            [jax.ShapeDtypeStruct((m, 2 * parts * ff), F32)] * blocks,
            [SMEM, VMEM, VMEM] + [VMEM] * len(base) + [ANY] * len(refs),
            scal,
            ids,
            a,
            *base,
            *refs,
            scratch=held(kinds, parts),
        )

    tok, ids, mine_info = region(spread_tokens, gu_near)

    k = first_one
    gu[k] = after(gu[k], tok)
    far = pp(gu[k], "groups", SWAP)
    gu[later_ones[0]] = partner(after(gu_near, gu[k], nearest[0]), later_ones[0])
    nearest.append(partner(after(up_weight, nearest[0]), 1))
    cot = region(spread_cotangent, gu[k])
    gu_slots = [
        ("parts", e, [gate_weight, up_weight]),
        ("parts", e ^ 1, nearest),
        ("halves", e ^ k, [gu[k], far]),
    ]
    dn_slots = [("parts", e, [down_weight])]
    dn = {}
    for i, k in enumerate(later_ones):
        gu[k] = after(gu[k], cot)
        far = pp(after(gu[k], far), "groups", SWAP)
        if i == 0:
            dn[first_one] = partner(after(dn_near, gu[k]), first_one)
            dn[1] = partner(after(down_weight, gu[k]), 1)
        dn[k] = partner(after(down_weight, gu[k]), k)
        if i + 1 < len(later_ones):
            gu[later_ones[i + 1]] = partner(after(gu_near, gu[k]), later_ones[i + 1])
        if i == 0:
            parts, cot_t = region(lambda: (sums(tok, gu_slots, 2), turned()), gu[k])
        else:
            parts = region(lambda t=todo, p=parts: sums(tok, t, 2, p), gu[k])
        todo = [("halves", e ^ k, [gu[k], far])]
        gu_slots = gu_slots + todo
    dn_slots += [("parts", e ^ k, [dn[k]]) for k in [1, *later_ones]]
    parts = sums(tok, todo, 2, parts)
    first = region(lambda: reduce_rows(parts))

    targets = jnp.stack([e ^ k for k in range(n)]).astype(jnp.int32)

    def down_step():
        dn_far = pp(dn[first_one], "groups", SWAP)
        hidden = call(
            hidden_step,
            jax.ShapeDtypeStruct((first[0].shape[0], 2 * ff), BF),
            [VMEM] * (1 + len(first)),
            mine_info,
            *first,
        )
        hidden = share_rows(hidden)
        steps = 3 if quarter % 48 == 0 and small else 1
        whole = [pl.BlockSpec(a.shape, lambda i: (0, 0)) for a in hidden]
        pieces = pl.pallas_call(
            lambda *r: down_products(n, *r),
            grid=(steps,),
            out_shape=[
                jax.ShapeDtypeStruct((quarter, ff), F32 if k == 0 else BF) for k in range(n)
            ],
            in_specs=[
                SMEM,
                pl.BlockSpec((rows, 2), lambda i: (0, 0)),
                pl.BlockSpec((quarter // steps, rows), lambda i: (i, 0)),
                *whole,
            ],
            out_specs=[pl.BlockSpec((quarter // steps, ff), lambda i: (i, 0))] * n,
            scratch_shapes=[pltpu.VMEM((rows, n * ff), BF)],
            compiler_params=PARAMS,
            cost_estimate=pl.CostEstimate(flops=0, bytes_accessed=0, transcendentals=0),
        )(targets, ids, cot_t, *hidden)
        return pieces, dn_far

    pieces, dn_far = region(down_step)
    dn_slots.append(("halves", e ^ first_one, [dn[first_one], dn_far]))
    shares = [partner(pieces[k], k) for k in range(n - 1, 0, -1)]

    def token_gradient():
        second = reduce_rows(sums(cot, dn_slots, 1))
        grads = call(
            lambda *r: grad_step(len(first), *r),
            jax.ShapeDtypeStruct((first[0].shape[0], 4 * ff), BF),
            [VMEM] * (1 + 2 * len(first)),
            mine_info,
            *first,
            *second,
        )
        grads = share_rows(grads)
        kinds = [kind for kind, _, _ in gu_slots]
        gu_refs = [r for _, _, rs in gu_slots for r in rs]
        pieces_out = plane if small else 1
        back = call(
            lambda *r: token_sums(kinds, len(grads), pieces_out, *r),
            [jax.ShapeDtypeStruct((rows // pieces_out, quarter), BF)] * pieces_out,
            [SMEM, VMEM] + [VMEM] * len(grads) + [ANY] * len(gu_refs),
            jnp.stack([label for _, label, _ in gu_slots] + [g]).astype(jnp.int32),
            ids,
            *grads,
            *gu_refs,
            scratch=held(kinds, 2),
        )
        if small:
            across = pp(back[1], "fsdp", SWAP)
            beside = pp(back[2], "dp", SWAP)
            aslant = pp(
                after(back[3], beside), ("fsdp", "dp"), [(i, 3 - i) for i in range(4)]
            )
            at = 2 * f + d
            return call(
                place_columns,
                jax.ShapeDtypeStruct((own, width), BF),
                [SMEM] + [VMEM] * 4,
                jnp.stack([at, at ^ 2, at ^ 1, at ^ 3]).astype(jnp.int32),
                back[0],
                across,
                beside,
                aslant,
            )
        back = lax.all_to_all(
            back[0].reshape(plane, own, quarter), ("fsdp", "dp"), 0, 0, tiled=True
        )
        return back.transpose(1, 0, 2).reshape(own, width)

    grad_tokens = region(token_gradient, *pieces)
    grad_down = after(pieces[0], grad_tokens)
    for share in shares:
        grad_down = grad_down + share.astype(F32)
    return (grad_tokens, grad_down[None])


def solution(mesh):
    rows = P(("groups", "fsdp", "expert", "dp"), None)
    weights = P("expert", ("fsdp", "dp"), None)
    return jax.shard_map(
        per_device,
        mesh=mesh,
        in_specs=(rows, rows, rows, rows, weights, weights, weights),
        out_specs=(rows, P(("groups", "expert"), ("fsdp", "dp"), None)),
        check_vma=False,
    )
```

time: 111 us -> 111 us (level)
  other arithmetic: 7.87 us -> 3.77 us
  waiting for transfers between devices: 50.6 us -> 52.7 us
  Pallas kernels: 19.6 us -> 21.5 us
    ppermute x10, waiting for transfers between devices: 4.17 us -> 10.6 us  [partner(): return pp(block, 'expert', [(i, i ^ k) for i in range(n)])]
    ppermute x8 -> x7, waiting for transfers between devices: 33.8 us -> 28 us  [the longest x4 19.8 us: swap_columns(): return [kept, pp(sent, axis, SWAP)]]
    select_n x6 -> x0, other arithmetic: 3.49 us -> none  [the longest x4 2.23 us: halve(): return jnp.where(at == 0, a[:, :m], a[:, m:])]
    pallas_call x0 -> x1, Pallas kernels: none -> 3.16 us  [down_step(): pl.pallas_call(lambda *r: down_products(n, *r), grid=(steps,), out_shape=...]
    concatenate x3 -> x2, other arithmetic: 1.6 us -> 0.1 us  [the longest x1 0.05 us: spread_tokens(): tok = jnp.concatenate([kept[:, :quarter], came[:, :quarter]])]
    pallas_call x8 -> x13, Pallas kernels: 19.6 us -> 18.3 us  [call(): pl.pallas_call(body, out_shape=outs, in_specs=specs, out_specs=jax.tree.m...]
    ppermute x1, waiting for transfers between devices: 0.64 us -> 1.88 us  [per_device(): far = pp(after(gu[k], far), 'groups', SWAP)]
    ppermute x8 -> x7, starting transfers between devices: 6.49 us -> 5.98 us  [the longest x4 3.24 us: swap_columns(): return [kept, pp(sent, axis, SWAP)]]
  transfers between devices with their start and end apart: 27 -> 26, of which waited for: 17 -> 16; matrix products, arithmetic and copies ran while one was open for 6% -> 2% of each run, Pallas kernels for 17% -> 18%
where the time goes in v5:
time: 111 us; the launch traced here: 110 us
  waiting for transfers between devices  52.7 us (47%)
  starting transfers between devices  30 us (27%)
  Pallas kernels  21.5 us (19%)
  other arithmetic  3.77 us (3%)
  local copies, waits for them, and re-layouts  1.18 us (1%)
    ppermute x4, waiting for transfers between devices, swap_columns(): return [kept, pp(sent, axis, SWAP)]  19.8 us
    pallas_call x13, Pallas kernels, call(): pl.pallas_call(body, out_shape=outs, in_specs=specs, out_specs=jax.tree.m...  18.3 us
    ppermute x10, starting transfers between devices, partner(): return pp(block, 'expert', [(i, i ^ k) for i in range(n)])  16.2 us
    ppermute x10, waiting for transfers between devices, partner(): return pp(block, 'expert', [(i, i ^ k) for i in range(n)])  10.6 us
    ppermute x2, waiting for transfers between devices, reduce_rows(): return [total, pp(total.astype(BF), 'fsdp', SWAP)]  6.94 us
    ppermute x1, waiting for transfers between devices, token_gradient(): across = pp(back[1], 'fsdp', SWAP)  5.13 us
    ppermute x4, starting transfers between devices, swap_columns(): return [kept, pp(sent, axis, SWAP)]  3.24 us
    pallas_call x1, Pallas kernels, down_step(): pl.pallas_call(lambda *r: down_products(n, *r), grid=(steps,), out_shape=...  3.16 us
  transfers between devices with their start and end apart: 26, of which 16 were waited for; matrix products, arithmetic and copies ran while one was open for 2% of the time, Pallas kernels for 18%

profile of v5, /device:TPU:0, one launch (start us, length us, event | category | flops | bytes accessed | tf_op | source)
XLA Modules:
  0.0 110.2 jit_solution(1071079337809278083)
XLA Ops:
  1.9 5.1 %collective-permute-start.14 = (bf16[2,768,128]{2,1,0:T(8,128)(2,1)S(1)}, bf16[2,768,128]{2,1,0:T(8,128)(2,1)S(1)}, u32[]{:S(2)}, u32[]{:S(2)}) collective-permute-start(bf16[2,768,128]{2,1,0:T(8,128)(2,1)S(1)} %get-tuple-element.232), channel_id=1, source_target_pairs={{0,6},{2,4},{4,2},{6,0},{1,7},{3,5},{5,3},{7,1},{8,14},{10,12},{12... | collective-permute-start | bytes 1179656 | tf_op jit(solution)/shard_map/ppermute | solution.py:251
  7.0 15.3 %conditional.6 = (bf16[256,1536]{1,0:T(8,128)(2,1)S(1)}, s32[256,2]{1,0:T(8,128)S(1)}, bf16[128,128]{1,0:T(8,128)(2,1)}) conditional(s32[]{:T(128)} %convert_element_type.50, () %tuple.67, (s32[]{:T(128)}, s32[]{:T(128)}, s32[64,2]{0,1:T(2,128)S(1)}, f32[64,2]{0,1:T(2,128)S(1)}, bf16[64,6144]{1,0:T(8,128)(2,1)}) %tuple.114), branch_computations={%region_0.0_spmd, %region_1.0_spmd} | conditional | flops 1576064 | bytes 6739050 | solution.py:255
  10.1 9.4 %collective-permute-done.2.r_2_ = bf16[64,3200]{1,0:T(8,128)(2,1)S(1)} collective-permute-done((bf16[64,3200]{1,0:T(8,128)(2,1)S(1)}, bf16[64,3200]{1,0:T(8,128)(2,1)S(1)}, u32[]{:S(2)}, u32[]{:S(2)}) %collective-permute-start.2) | collective-permute-done | bytes 409632 | tf_op jit(solution)/shard_map/cond/branch_1_fun/ppermute | solution.py:287
  22.4 2.4 %collective-permute-done.15 = bf16[1,1536,128]{2,1,0:T(8,128)(2,1)} collective-permute-done((bf16[1,1536,128]{2,1,0:T(8,128)(2,1)S(1)}, bf16[1,1536,128]{2,1,0:T(8,128)(2,1)}, u32[]{:S(2)}, u32[]{:S(2)}) %collective-permute-start.15) | collective-permute-done | bytes 393248 | tf_op jit(solution)/shard_map/ppermute | solution.py:251
  28.5 12.2 %conditional.7 = (bf16[256,1536]{1,0:T(8,128)(2,1)S(1)}) conditional(s32[]{:T(128)} %convert_element_type.51, () %tuple.73, (s32[]{:T(128)}, s32[]{:T(128)}, bf16[64,6144]{1,0:T(8,128)(2,1)}) %tuple.74), branch_computations={%region_2.0_spmd, %region_3.0_spmd} | conditional | flops 1572864 | bytes 4718680 | solution.py:255
  31.3 7.5 %collective-permute-done.4.r_2_ = bf16[64,3072]{1,0:T(8,128)(2,1)S(1)} collective-permute-done((bf16[64,3072]{1,0:T(8,128)(2,1)S(1)}, bf16[64,3072]{1,0:T(8,128)(2,1)S(1)}, u32[]{:S(2)}, u32[]{:S(2)}) %collective-permute-start.4) | collective-permute-done | bytes 393248 | tf_op jit(solution)/shard_map/cond/branch_1_fun/ppermute | solution.py:287
  40.7 4.6 %collective-permute-done.16.r_5_ = bf16[2,768,128]{2,1,0:T(8,128)(2,1)} collective-permute-done((bf16[2,768,128]{2,1,0:T(8,128)(2,1)S(1)}, bf16[2,768,128]{2,1,0:T(8,128)(2,1)}, u32[]{:S(2)}, u32[]{:S(2)}) %collective-permute-start.16) | collective-permute-done | bytes 393248 | tf_op jit(solution)/shard_map/ppermute | solution.py:251
  47.5 3.7 %collective-permute-start.22 = (bf16[1,1536,128]{2,1,0:T(8,128)(2,1)}, bf16[1,1536,128]{2,1,0:T(8,128)(2,1)}, u32[]{:S(2)}, u32[]{:S(2)}) collective-permute-start(bf16[1,1536,128]{2,1,0:T(8,128)(2,1)} %down.1), channel_id=1, source_target_pairs={{0,4},{2,6},{4,0},{6,2},{1,5},{3,7},{5,1},{7,3},{8,12},{10,14},{12... | collective-permute-start | bytes 1179656 | tf_op jit(solution)/shard_map/ppermute | solution.py:251
  51.3 3.3 %conditional.8 = (f32[128,512]{1,0:T(8,128)S(1)}, f32[128,512]{1,0:T(8,128)S(1)}, bf16[1536,256]{1,0:T(8,128)(2,1)S(1)}) conditional(s32[]{:T(128)} %convert_element_type.52, () %tuple.77, (s32[]{:T(128)}, s32[]{:T(128)}, s32[]{:T(128)}, s32[]{:T(128)}, s32[256,2]{1,0:T(8,128)S(1)}, /*index=5*/bf16[256,1536]{1,0:T(8,128)(2,1)S(1)}, ...), branch_computations={%region_4.0_spmd, %region_5.0_spmd} | conditional | flops 12 | bytes 1310754 | solution.py:255
  51.3 3.0 %branch_1_fun.16 = (f32[128,512]{1,0:T(8,128)S(1)}, f32[128,512]{1,0:T(8,128)S(1)}) custom-call(s32[4]{0:T(128)S(1)} %pad_add_fusion.r_0_, s32[256,2]{1,0:T(8,128)S(1)} %get-tuple-element.139.r_1_, bf16[256,1536]{1,0:T(8,128)(2,1)S(1)} %get-tuple-element.140.r_2_, bf16[1,1536,128]{2,1,0:T(8,128)(2,1)S(1)} %get-tuple-element.141.r_3_, ...), custom_call_target="tpu_custom_call" | custom-call | tf_op jit(solution)/shard_map/cond/branch_1_fun/pallas_call | solution.py:19
  56.5 2.2 %shard_map.91 = (f32[128,512]{1,0:T(8,128)S(1)}, f32[128,512]{1,0:T(8,128)S(1)}) custom-call(s32[2]{0:T(128)S(1)} %pad_add_fusion.2.r_0_, s32[256,2]{1,0:T(8,128)S(1)} %get-tuple-element.229.r_1_, bf16[256,1536]{1,0:T(8,128)(2,1)S(1)} %get-tuple-element.230.r_2_, f32[128,512]{1,0:T(8,128)S(1)} %get-tuple-element.237.r_3_, ...), custom_call_target="tpu_custom_call" | custom-call | tf_op jit(solution)/shard_map/pallas_call | solution.py:19
  58.7 7.4 %conditional.9 = (f32[128,512]{1,0:T(8,128)S(1)}, bf16[128,512]{1,0:T(8,128)(2,1)}) conditional(s32[]{:T(128)} %convert_element_type.49, () %tuple.69, (f32[128,512]{1,0:T(8,128)S(1)}, f32[128,512]{1,0:T(8,128)S(1)}) %tuple.81), branch_computations={%region_6.0_spmd, %region_7.0_spmd} | conditional | flops 131072 | bytes 2490464 | solution.py:255
  61.9 4.2 %collective-permute-done.7 = bf16[128,512]{1,0:T(8,128)(2,1)} collective-permute-done((bf16[128,512]{1,0:T(8,128)(2,1)S(1)}, bf16[128,512]{1,0:T(8,128)(2,1)}, u32[]{:S(2)}, u32[]{:S(2)}) %collective-permute-start.7) | collective-permute-done | bytes 131104 | tf_op jit(solution)/shard_map/cond/branch_1_fun/ppermute | solution.py:324
  66.0 7.1 %conditional.10 = (f32[1536,128]{1,0:T(8,128)}, bf16[1536,128]{1,0:T(8,128)(2,1)}, bf16[1536,128]{1,0:T(8,128)(2,1)}, bf16[1536,128]{1,0:T(8,128)(2,1)}, bf16[1,768,128]{2,1,0:T(8,128)(2,1)}) conditional(s32[]{:T(128)} %convert_element_type.49, () %tuple.65, (bf16[128,128]{1,0:T(8,128)(2,1)}, f32[128,512]{1,0:T(8,128)S(1)}, ...), branch_computations={%region_8.0_spmd, %region_9.0_spmd} | conditional | bytes 2162740 | solution.py:255
  70.0 3.2 %branch_1_fun.19 = (f32[1536,128]{1,0:T(8,128)}, bf16[1536,128]{1,0:T(8,128)(2,1)}, bf16[1536,128]{1,0:T(8,128)(2,1)}, bf16[1536,128]{1,0:T(8,128)(2,1)}) custom-call(s32[4]{0:T(128)S(1)} %get-tuple-element.152.r_0_, s32[256,2]{1,0:T(8,128)S(1)} %get-tuple-element.153.r_1_, bf16[1536,256]{1,0:T(8,128)(2,1)S(1)} %get-tuple-element.154.r_2_, ...), custom_call_target="tpu_custom_call" | custom-call | tf_op jit(solution)/shard_map/cond/branch_1_fun/pallas_call | solution.py:402
  73.3 4.3 %collective-permute-start.25 = (bf16[1536,128]{1,0:T(8,128)(2,1)}, bf16[1536,128]{1,0:T(8,128)(2,1)}, u32[]{:S(2)}, u32[]{:S(2)}) collective-permute-start(bf16[1536,128]{1,0:T(8,128)(2,1)} %get-tuple-element.248), channel_id=1, source_target_pairs={{0,2},{2,0},{4,6},{6,4},{1,3},{3,1},{5,7},{7,5},{8,10},{10,8},{12,... | collective-permute-start | bytes 1179656 | tf_op jit(solution)/shard_map/ppermute | solution.py:251
  77.6 26.4 %conditional.11 = (bf16[64,6144]{1,0:T(8,128)(2,1)S(1)}) conditional(s32[]{:T(128)} %convert_element_type.53, () %tuple.85, (s32[]{:T(128)}, s32[]{:T(128)}, s32[]{:T(128)}, s32[]{:T(128)}, s32[]{:T(128)}, /*index=5*/s32[]{:T(128)}, s32[]{:T(128)}, s32[256,2]{1,0:T(8,128)S(1)}, bf16[256,1536]{1,0:T(8,128)(2,1)S(1)}, ...), branch_computations={%region_10.0_spmd, %region_11.0_spmd} | conditional | flops 65553 | bytes 4129188 | solution.py:255
  77.7 3.0 %branch_1_fun.20 = (f32[128,256]{1,0:T(8,128)S(1)}, f32[128,256]{1,0:T(8,128)S(1)}) custom-call(s32[5]{0:T(128)S(1)} %stack.75.r_0_, s32[256,2]{1,0:T(8,128)S(1)} %get-tuple-element.170.r_1_, bf16[256,1536]{1,0:T(8,128)(2,1)S(1)} %get-tuple-element.174.r_2_, bf16[1,1536,128]{2,1,0:T(8,128)(2,1)} %get-tuple-element.175.r_3_, ...), custom_call_target="tpu_custom_call" | custom-call | tf_op jit(solution)/shard_map/cond/branch_1_fun/pallas_call | solution.py:19
  83.7 2.8 %collective-permute-done.9.r_4_ = bf16[128,256]{1,0:T(8,128)(2,1)S(1)} collective-permute-done((bf16[128,256]{1,0:T(8,128)(2,1)S(1)}, bf16[128,256]{1,0:T(8,128)(2,1)S(1)}, u32[]{:S(2)}, u32[]{:S(2)}) %collective-permute-start.9) | collective-permute-done | bytes 65568 | tf_op jit(solution)/shard_map/cond/branch_1_fun/ppermute | solution.py:324
  89.0 3.4 %branch_1_fun.22 = (bf16[64,1536]{1,0:T(8,128)(2,1)S(1)}, bf16[64,1536]{1,0:T(8,128)(2,1)S(1)}, bf16[64,1536]{1,0:T(8,128)(2,1)S(1)}, bf16[64,1536]{1,0:T(8,128)(2,1)S(1)}) custom-call(s32[5]{0:T(128)S(1)} %stack.71.r_0_, s32[256,2]{1,0:T(8,128)S(1)} %get-tuple-element.170.r_1_, bf16[128,512]{1,0:T(8,128)(2,1)S(1)} %branch_1_fun.21.r_2_, ...), custom_call_target="tpu_custom_call" | custom-call | tf_op jit(solution)/shard_map/cond/branch_1_fun/pallas_call | solution.py:19
  95.3 5.1 %collective-permute-done.11.refs_1_ = bf16[64,1536]{1,0:T(8,128)(2,1)S(1)} collective-permute-done((bf16[64,1536]{1,0:T(8,128)(2,1)S(1)}, bf16[64,1536]{1,0:T(8,128)(2,1)S(1)}, u32[]{:S(2)}, u32[]{:S(2)}) %collective-permute-start.11) | collective-permute-done | bytes 196640 | tf_op jit(solution)/shard_map/cond/branch_1_fun/ppermute | solution.py:450
  100.4 3.1 %collective-permute-done.13.refs_3_ = bf16[64,1536]{1,0:T(8,128)(2,1)S(1)} collective-permute-done((bf16[64,1536]{1,0:T(8,128)(2,1)S(1)}, bf16[64,1536]{1,0:T(8,128)(2,1)S(1)}, u32[]{:S(2)}, u32[]{:S(2)}) %collective-permute-start.13) | collective-permute-done | bytes 196640 | tf_op jit(solution)/shard_map/cond/branch_1_fun/ppermute | solution.py:452
  104.1 3.6 %collective-permute-done.24 = bf16[1536,128]{1,0:T(8,128)(2,1)} collective-permute-done((bf16[1536,128]{1,0:T(8,128)(2,1)}, bf16[1536,128]{1,0:T(8,128)(2,1)}, u32[]{:S(2)}, u32[]{:S(2)}) %collective-permute-start.24) | collective-permute-done | bytes 393248 | tf_op jit(solution)/shard_map/ppermute | solution.py:251
  107.7 2.5 %add_bitcast_fusion = f32[1,1536,128]{2,1,0:T(8,128)} fusion(bf16[1536,128]{1,0:T(8,128)(2,1)} %collective-permute-done.25, bf16[1536,128]{1,0:T(8,128)(2,1)} %collective-permute-done.24, f32[1536,128]{1,0:T(8,128)} %get-tuple-element.254, bf16[1536,128]{1,0:T(8,128)(2,1)} %collective-permute-done.23), kind=kLoop, calls=%fused_computation.12 | loop fusion | flops 1179648 | bytes 2752512 | tf_op jit(solution)/shard_map/broadcast_in_dim | solution.py:475
  (88 shorter events, 36.2 us)
Async XLA Ops:
  1.9 20.5 %collective-permute-start.14 = (bf16[2,768,128]{2,1,0:T(8,128)(2,1)S(1)}, bf16[2,768,128]{2,1,0:T(8,128)(2,1)S(1)}, u32[]{:S(2)}, u32[]{:S(2)}) collective-permute-start(bf16[2,768,128]{2,1,0:T(8,128)(2,1)S(1)} %get-tuple-element.232), channel_id=1, source_target_pairs={{0,6},{2,4},{4,2},{6,0},{1,7},{3,5},{5,3},{7,1},{8,14},{10,12},{12... | collective-permute-start | bytes 1179656 | tf_op jit(solution)/shard_map/ppermute | solution.py:251
  7.0 17.7 %collective-permute-start.15 = (bf16[1,1536,128]{2,1,0:T(8,128)(2,1)S(1)}, bf16[1,1536,128]{2,1,0:T(8,128)(2,1)}, u32[]{:S(2)}, u32[]{:S(2)}) collective-permute-start(bf16[1,1536,128]{2,1,0:T(8,128)(2,1)S(1)} %copy-done), channel_id=1, source_target_pairs={{0,2},{2,0},{4,6},{6,4},{1,3},{3,1},{5,7},{7,5},{8,10},{10,8},{12,... | collective-permute-start | bytes 1179656 | tf_op jit(solution)/shard_map/ppermute | solution.py:251
  8.6 11.0 %collective-permute-start.2 = (bf16[64,3200]{1,0:T(8,128)(2,1)S(1)}, bf16[64,3200]{1,0:T(8,128)(2,1)S(1)}, u32[]{:S(2)}, u32[]{:S(2)}) collective-permute-start(bf16[64,3200]{1,0:T(8,128)(2,1)S(1)} %get-tuple-element.125), channel_id=1, source_target_pairs={{0,8},{8,0},{1,9},{9,1},{2,10},{10,2},{3,11},{11,3},{4,12},{12,4},... | collective-permute-start | bytes 1228808 | tf_op jit(solution)/shard_map/cond/branch_1_fun/ppermute | solution.py:287
  19.6 1.8 %collective-permute-start.3 = (bf16[128,1664]{1,0:T(8,128)(2,1)S(1)}, bf16[128,1664]{1,0:T(8,128)(2,1)S(1)}, u32[]{:S(2)}, u32[]{:S(2)}) collective-permute-start(bf16[128,1664]{1,0:T(8,128)(2,1)S(1)} %get-tuple-element.127), channel_id=1, source_target_pairs={{0,1},{1,0},{2,3},{3,2},{4,5},{5,4},{6,7},{7,6},{8,9},{9,8},{10,11... | collective-permute-start | bytes 1277960 | tf_op jit(solution)/shard_map/cond/branch_1_fun/ppermute | solution.py:287
  24.7 20.6 %collective-permute-start.16 = (bf16[2,768,128]{2,1,0:T(8,128)(2,1)S(1)}, bf16[2,768,128]{2,1,0:T(8,128)(2,1)}, u32[]{:S(2)}, u32[]{:S(2)}) collective-permute-start(bf16[2,768,128]{2,1,0:T(8,128)(2,1)S(1)} %get-tuple-element.232), channel_id=1, source_target_pairs={{0,4},{2,6},{4,0},{6,2},{1,5},{3,7},{5,1},{7,3},{8,12},{10,14},{12... | collective-permute-start | bytes 1179656 | tf_op jit(solution)/shard_map/ppermute | solution.py:251
  25.3 20.0 %collective-permute-start.18 = (bf16[2,768,128]{2,1,0:T(8,128)(2,1)S(1)}, bf16[2,768,128]{2,1,0:T(8,128)(2,1)}, u32[]{:S(2)}, u32[]{:S(2)}) collective-permute-start(bf16[2,768,128]{2,1,0:T(8,128)(2,1)S(1)} %collective-permute-done.14), channel_id=1, source_target_pairs={{0,16},{16,0},{1,17},{17,1},{2,18},{18,2},{3,19},{19,3},{4,20},{20... | collective-permute-start | bytes 1179656 | tf_op jit(solution)/shard_map/ppermute | solution.py:358
  26.8 24.5 %collective-permute-start.17 = (bf16[1,1536,128]{2,1,0:T(8,128)(2,1)S(1)}, bf16[1,1536,128]{2,1,0:T(8,128)(2,1)}, u32[]{:S(2)}, u32[]{:S(2)}) collective-permute-start(bf16[1,1536,128]{2,1,0:T(8,128)(2,1)S(1)} %copy-done.1), channel_id=1, source_target_pairs={{0,2},{2,0},{4,6},{6,4},{1,3},{3,1},{5,7},{7,5},{8,10},{10,8},{12,... | collective-permute-start | bytes 1179656 | tf_op jit(solution)/shard_map/ppermute | solution.py:251
  29.7 9.0 %collective-permute-start.4 = (bf16[64,3072]{1,0:T(8,128)(2,1)S(1)}, bf16[64,3072]{1,0:T(8,128)(2,1)S(1)}, u32[]{:S(2)}, u32[]{:S(2)}) collective-permute-start(bf16[64,3072]{1,0:T(8,128)(2,1)S(1)} %get-tuple-element.132), channel_id=1, source_target_pairs={{0,8},{8,0},{1,9},{9,1},{2,10},{10,2},{3,11},{11,3},{4,12},{12,4},... | collective-permute-start | bytes 1179656 | tf_op jit(solution)/shard_map/cond/branch_1_fun/ppermute | solution.py:287
  38.8 1.8 %collective-permute-start.5 = (bf16[128,1536]{1,0:T(8,128)(2,1)S(1)}, bf16[128,1536]{1,0:T(8,128)(2,1)S(1)}, u32[]{:S(2)}, u32[]{:S(2)}) collective-permute-start(bf16[128,1536]{1,0:T(8,128)(2,1)S(1)} %get-tuple-element.134), channel_id=1, source_target_pairs={{0,1},{1,0},{2,3},{3,2},{4,5},{5,4},{6,7},{7,6},{8,9},{9,8},{10,11... | collective-permute-start | bytes 1179656 | tf_op jit(solution)/shard_map/cond/branch_1_fun/ppermute | solution.py:287
  45.3 11.2 %collective-permute-start.19 = (bf16[2,768,128]{2,1,0:T(8,128)(2,1)}, bf16[2,768,128]{2,1,0:T(8,128)(2,1)}, u32[]{:S(2)}, u32[]{:S(2)}) collective-permute-start(bf16[2,768,128]{2,1,0:T(8,128)(2,1)} %collective-permute-done.16.r_5_), channel_id=1, source_target_pairs={{0,16},{16,0},{1,17},{17,1},{2,18},{18,2},{3,19},{19,3},{4,20},{20... | collective-permute-start | bytes 1179656 | tf_op jit(solution)/shard_map/ppermute | solution.py:371
  46.7 19.3 %collective-permute-start.20 = (bf16[1,768,128]{2,1,0:T(8,128)(2,1)S(1)}, bf16[1,768,128]{2,1,0:T(8,128)(2,1)}, u32[]{:S(2)}, u32[]{:S(2)}) collective-permute-start(bf16[1,768,128]{2,1,0:T(8,128)(2,1)S(1)} %get-tuple-element.246), channel_id=1, source_target_pairs={{0,6},{2,4},{4,2},{6,0},{1,7},{3,5},{5,3},{7,1},{8,14},{10,12},{12... | collective-permute-start | bytes 589832 | tf_op jit(solution)/shard_map/ppermute | solution.py:251
  47.5 30.1 %collective-permute-start.21 = (bf16[1,1536,128]{2,1,0:T(8,128)(2,1)}, bf16[1,1536,128]{2,1,0:T(8,128)(2,1)}, u32[]{:S(2)}, u32[]{:S(2)}) collective-permute-start(bf16[1,1536,128]{2,1,0:T(8,128)(2,1)} %down.1), channel_id=1, source_target_pairs={{0,2},{2,0},{4,6},{6,4},{1,3},{3,1},{5,7},{7,5},{8,10},{10,8},{12,... | collective-permute-start | bytes 1179656 | tf_op jit(solution)/shard_map/ppermute | solution.py:251
  47.5 30.1 %collective-permute-start.22 = (bf16[1,1536,128]{2,1,0:T(8,128)(2,1)}, bf16[1,1536,128]{2,1,0:T(8,128)(2,1)}, u32[]{:S(2)}, u32[]{:S(2)}) collective-permute-start(bf16[1,1536,128]{2,1,0:T(8,128)(2,1)} %down.1), channel_id=1, source_target_pairs={{0,4},{2,6},{4,0},{6,2},{1,5},{3,7},{5,1},{7,3},{8,12},{10,14},{12... | collective-permute-start | bytes 1179656 | tf_op jit(solution)/shard_map/ppermute | solution.py:251
  58.7 1.6 %collective-permute-start.6 = (f32[128,512]{1,0:T(8,128)S(1)}, f32[128,512]{1,0:T(8,128)S(1)}, u32[]{:S(2)}, u32[]{:S(2)}) collective-permute-start(f32[128,512]{1,0:T(8,128)S(1)} %get-tuple-element.151), channel_id=1, source_target_pairs={{0,1},{1,0},{2,3},{3,2},{4,5},{5,4},{6,7},{7,6},{8,9},{9,8},{10,11... | collective-permute-start | bytes 786440 | tf_op jit(solution)/shard_map/cond/branch_1_fun/ppermute | solution.py:323
  60.3 5.7 %collective-permute-start.7 = (bf16[128,512]{1,0:T(8,128)(2,1)S(1)}, bf16[128,512]{1,0:T(8,128)(2,1)}, u32[]{:S(2)}, u32[]{:S(2)}) collective-permute-start(bf16[128,512]{1,0:T(8,128)(2,1)S(1)} %get-tuple-element.268), channel_id=1, source_target_pairs={{0,8},{8,0},{1,9},{9,1},{2,10},{10,2},{3,11},{11,3},{4,12},{12,4},... | collective-permute-start | bytes 393224 | tf_op jit(solution)/shard_map/cond/branch_1_fun/ppermute | solution.py:324
  66.1 7.1 %collective-permute-start.1 = (bf16[1,768,128]{2,1,0:T(8,128)(2,1)}, bf16[1,768,128]{2,1,0:T(8,128)(2,1)}, u32[]{:S(2)}, u32[]{:S(2)}) collective-permute-start(bf16[1,768,128]{2,1,0:T(8,128)(2,1)} %get-tuple-element.162), channel_id=1, source_target_pairs={{0,16},{16,0},{1,17},{17,1},{2,18},{18,2},{3,19},{19,3},{4,20},{20... | collective-permute-start | bytes 589832 | tf_op jit(solution)/shard_map/cond/branch_1_fun/ppermute | solution.py:391
  73.2 30.9 %collective-permute-start.23 = (bf16[1536,128]{1,0:T(8,128)(2,1)}, bf16[1536,128]{1,0:T(8,128)(2,1)}, u32[]{:S(2)}, u32[]{:S(2)}) collective-permute-start(bf16[1536,128]{1,0:T(8,128)(2,1)} %get-tuple-element.250), channel_id=1, source_target_pairs={{0,6},{2,4},{4,2},{6,0},{1,7},{3,5},{5,3},{7,1},{8,14},{10,12},{12... | collective-permute-start | bytes 1179656 | tf_op jit(solution)/shard_map/ppermute | solution.py:251
  73.2 34.5 %collective-permute-start.24 = (bf16[1536,128]{1,0:T(8,128)(2,1)}, bf16[1536,128]{1,0:T(8,128)(2,1)}, u32[]{:S(2)}, u32[]{:S(2)}) collective-permute-start(bf16[1536,128]{1,0:T(8,128)(2,1)} %get-tuple-element.249), channel_id=1, source_target_pairs={{0,4},{2,6},{4,0},{6,2},{1,5},{3,7},{5,1},{7,3},{8,12},{10,14},{12... | collective-permute-start | bytes 1179656 | tf_op jit(solution)/shard_map/ppermute | solution.py:251
  73.3 34.4 %collective-permute-start.25 = (bf16[1536,128]{1,0:T(8,128)(2,1)}, bf16[1536,128]{1,0:T(8,128)(2,1)}, u32[]{:S(2)}, u32[]{:S(2)}) collective-permute-start(bf16[1536,128]{1,0:T(8,128)(2,1)} %get-tuple-element.248), channel_id=1, source_target_pairs={{0,2},{2,0},{4,6},{6,4},{1,3},{3,1},{5,7},{7,5},{8,10},{10,8},{12,... | collective-permute-start | bytes 1179656 | tf_op jit(solution)/shard_map/ppermute | solution.py:251
  82.2 4.3 %collective-permute-start.9 = (bf16[128,256]{1,0:T(8,128)(2,1)S(1)}, bf16[128,256]{1,0:T(8,128)(2,1)S(1)}, u32[]{:S(2)}, u32[]{:S(2)}) collective-permute-start(bf16[128,256]{1,0:T(8,128)(2,1)S(1)} %get-tuple-element.270), channel_id=1, source_target_pairs={{0,8},{8,0},{1,9},{9,1},{2,10},{10,2},{3,11},{11,3},{4,12},{12,4},... | collective-permute-start | bytes 196616 | tf_op jit(solution)/shard_map/cond/branch_1_fun/ppermute | solution.py:324
  87.6 1.4 %collective-permute-start.10 = (bf16[128,512]{1,0:T(8,128)(2,1)S(1)}, bf16[128,512]{1,0:T(8,128)(2,1)S(1)}, u32[]{:S(2)}, u32[]{:S(2)}) collective-permute-start(bf16[128,512]{1,0:T(8,128)(2,1)S(1)} %branch_1_fun.21.r_2_), channel_id=1, source_target_pairs={{0,1},{1,0},{2,3},{3,2},{4,5},{5,4},{6,7},{7,6},{8,9},{9,8},{10,11... | collective-permute-start | bytes 393224 | tf_op jit(solution)/shard_map/cond/branch_1_fun/ppermute | solution.py:329
  92.4 1.7 %collective-permute-start.12 = (bf16[64,1536]{1,0:T(8,128)(2,1)S(1)}, bf16[64,1536]{1,0:T(8,128)(2,1)S(1)}, u32[]{:S(2)}, u32[]{:S(2)}) collective-permute-start(bf16[64,1536]{1,0:T(8,128)(2,1)S(1)} %get-tuple-element.192), channel_id=1, source_target_pairs={{0,1},{1,0},{2,3},{3,2},{4,5},{5,4},{6,7},{7,6},{8,9},{9,8},{10,11... | collective-permute-start | bytes 589832 | tf_op jit(solution)/shard_map/cond/branch_1_fun/ppermute | solution.py:451
  92.7 7.7 %collective-permute-start.11 = (bf16[64,1536]{1,0:T(8,128)(2,1)S(1)}, bf16[64,1536]{1,0:T(8,128)(2,1)S(1)}, u32[]{:S(2)}, u32[]{:S(2)}) collective-permute-start(bf16[64,1536]{1,0:T(8,128)(2,1)S(1)} %get-tuple-element.191), channel_id=1, source_target_pairs={{0,8},{8,0},{1,9},{9,1},{2,10},{10,2},{3,11},{11,3},{4,12},{12,4},... | collective-permute-start | bytes 589832 | tf_op jit(solution)/shard_map/cond/branch_1_fun/ppermute | solution.py:450
  94.2 9.3 %collective-permute-start.13 = (bf16[64,1536]{1,0:T(8,128)(2,1)S(1)}, bf16[64,1536]{1,0:T(8,128)(2,1)S(1)}, u32[]{:S(2)}, u32[]{:S(2)}) collective-permute-start(bf16[64,1536]{1,0:T(8,128)(2,1)S(1)} %get-tuple-element.194), channel_id=1, source_target_pairs={{0,9},{1,8},{8,1},{9,0},{2,11},{3,10},{10,3},{11,2},{4,13},{5,12},... | collective-permute-start | bytes 589832 | tf_op jit(solution)/shard_map/cond/branch_1_fun/ppermute | solution.py:452
  (11 other events, 99.7 us)

commit v6 on v5

--- a/solution.py
+++ b/solution.py
@@ -356,7 +356,7 @@
     k = first_one
     gu[k] = after(gu[k], tok)
     far = pp(gu[k], "groups", SWAP)
-    gu[later_ones[0]] = partner(after(gu_near, gu[k], nearest[0]), later_ones[0])
+    gu[later_ones[0]] = partner(after(gu_near, gu[k]), later_ones[0])
     nearest.append(partner(after(up_weight, nearest[0]), 1))
     cot = region(spread_cotangent, gu[k])
     gu_slots = [
@@ -397,7 +397,7 @@
             *first,
         )
         hidden = share_rows(hidden)
-        steps = 3 if quarter % 48 == 0 and small else 1
+        steps = 1
         whole = [pl.BlockSpec(a.shape, lambda i: (0, 0)) for a in hidden]
         pieces = pl.pallas_call(
             lambda *r: down_products(n, *r),

time: 111 us -> 108 us (0.973)
  waiting for transfers between devices: 52.7 us -> 49.8 us
    ppermute x10, waiting for transfers between devices: 10.6 us -> 7.75 us  [partner(): return pp(block, 'expert', [(i, i ^ k) for i in range(n)])]
  transfers between devices with their start and end apart: 26 -> 26, of which waited for: 16 -> 15; matrix products, arithmetic and copies ran while one was open for 2% -> 2% of each run, Pallas kernels for 18% -> 19%
where the time goes in v6:
time: 108 us
  waiting for transfers between devices  49.8 us (46%)
  starting transfers between devices  30.6 us (28%)
  Pallas kernels  21.2 us (20%)
  other arithmetic  3.77 us (3%)
  local copies, waits for them, and re-layouts  1.18 us (1%)
    ppermute x4, waiting for transfers between devices, swap_columns(): return [kept, pp(sent, axis, SWAP)]  20.3 us
    pallas_call x13, Pallas kernels, call(): pl.pallas_call(body, out_shape=outs, in_specs=specs, out_specs=jax.tree.m...  18.3 us
    ppermute x10, starting transfers between devices, partner(): return pp(block, 'expert', [(i, i ^ k) for i in range(n)])  16.8 us
    ppermute x10, waiting for transfers between devices, partner(): return pp(block, 'expert', [(i, i ^ k) for i in range(n)])  7.75 us
    ppermute x2, waiting for transfers between devices, reduce_rows(): return [total, pp(total.astype(BF), 'fsdp', SWAP)]  6.94 us
    ppermute x1, waiting for transfers between devices, token_gradient(): across = pp(back[1], 'fsdp', SWAP)  5.13 us
    ppermute x4, starting transfers between devices, swap_columns(): return [kept, pp(sent, axis, SWAP)]  3.24 us
    ppermute x2, starting transfers between devices, reduce_rows(): return [total, pp(total.astype(BF), 'fsdp', SWAP)]  3.1 us
  transfers between devices with their start and end apart: 26, of which 15 were waited for; matrix products, arithmetic and copies ran while one was open for 2% of the time, Pallas kernels for 19%

profile of v6, /device:TPU:0, one launch (start us, length us, event | category | flops | bytes accessed | tf_op | source)
XLA Modules:
  0.0 107.6 jit_solution(7109812306322854995)
XLA Ops:
  1.9 5.1 %collective-permute-start.14 = (bf16[2,768,128]{2,1,0:T(8,128)(2,1)S(1)}, bf16[2,768,128]{2,1,0:T(8,128)(2,1)S(1)}, u32[]{:S(2)}, u32[]{:S(2)}) collective-permute-start(bf16[2,768,128]{2,1,0:T(8,128)(2,1)S(1)} %get-tuple-element.232), channel_id=1, source_target_pairs={{0,6},{2,4},{4,2},{6,0},{1,7},{3,5},{5,3},{7,1},{8,14},{10,12},{12... | collective-permute-start | bytes 1179656 | tf_op jit(solution)/shard_map/ppermute | solution.py:251
  7.0 15.3 %conditional.6 = (bf16[256,1536]{1,0:T(8,128)(2,1)S(1)}, s32[256,2]{1,0:T(8,128)S(1)}, bf16[128,128]{1,0:T(8,128)(2,1)}) conditional(s32[]{:T(128)} %convert_element_type.50, () %tuple.67, (s32[]{:T(128)}, s32[]{:T(128)}, s32[64,2]{0,1:T(2,128)S(1)}, f32[64,2]{0,1:T(2,128)S(1)}, bf16[64,6144]{1,0:T(8,128)(2,1)}) %tuple.114), branch_computations={%region_0.0_spmd, %region_1.0_spmd} | conditional | flops 1576064 | bytes 6739050 | solution.py:255
  10.1 9.4 %collective-permute-done.2.r_2_ = bf16[64,3200]{1,0:T(8,128)(2,1)S(1)} collective-permute-done((bf16[64,3200]{1,0:T(8,128)(2,1)S(1)}, bf16[64,3200]{1,0:T(8,128)(2,1)S(1)}, u32[]{:S(2)}, u32[]{:S(2)}) %collective-permute-start.2) | collective-permute-done | bytes 409632 | tf_op jit(solution)/shard_map/cond/branch_1_fun/ppermute | solution.py:287
  22.4 2.9 %collective-permute-start.15 = (bf16[2,768,128]{2,1,0:T(8,128)(2,1)S(1)}, bf16[2,768,128]{2,1,0:T(8,128)(2,1)}, u32[]{:S(2)}, u32[]{:S(2)}) collective-permute-start(bf16[2,768,128]{2,1,0:T(8,128)(2,1)S(1)} %get-tuple-element.232), channel_id=1, source_target_pairs={{0,4},{2,6},{4,0},{6,2},{1,5},{3,7},{5,1},{7,3},{8,12},{10,14},{12... | collective-permute-start | bytes 1179656 | tf_op jit(solution)/shard_map/ppermute | solution.py:251
  26.8 12.7 %conditional.7 = (bf16[256,1536]{1,0:T(8,128)(2,1)S(1)}) conditional(s32[]{:T(128)} %convert_element_type.51, () %tuple.73, (s32[]{:T(128)}, s32[]{:T(128)}, bf16[64,6144]{1,0:T(8,128)(2,1)}) %tuple.74), branch_computations={%region_2.0_spmd, %region_3.0_spmd} | conditional | flops 1572864 | bytes 4718680 | solution.py:255
  29.5 8.1 %collective-permute-done.4.r_2_ = bf16[64,3072]{1,0:T(8,128)(2,1)S(1)} collective-permute-done((bf16[64,3072]{1,0:T(8,128)(2,1)S(1)}, bf16[64,3072]{1,0:T(8,128)(2,1)S(1)}, u32[]{:S(2)}, u32[]{:S(2)}) %collective-permute-start.4) | collective-permute-done | bytes 393248 | tf_op jit(solution)/shard_map/cond/branch_1_fun/ppermute | solution.py:287
  39.5 3.6 %collective-permute-done.15.r_5_ = bf16[2,768,128]{2,1,0:T(8,128)(2,1)} collective-permute-done((bf16[2,768,128]{2,1,0:T(8,128)(2,1)S(1)}, bf16[2,768,128]{2,1,0:T(8,128)(2,1)}, u32[]{:S(2)}, u32[]{:S(2)}) %collective-permute-start.15) | collective-permute-done | bytes 393248 | tf_op jit(solution)/shard_map/ppermute | solution.py:251
  46.3 2.9 %collective-permute-start.22 = (bf16[1,1536,128]{2,1,0:T(8,128)(2,1)}, bf16[1,1536,128]{2,1,0:T(8,128)(2,1)}, u32[]{:S(2)}, u32[]{:S(2)}) collective-permute-start(bf16[1,1536,128]{2,1,0:T(8,128)(2,1)} %down.1), channel_id=1, source_target_pairs={{0,4},{2,6},{4,0},{6,2},{1,5},{3,7},{5,1},{7,3},{8,12},{10,14},{12... | collective-permute-start | bytes 1179656 | tf_op jit(solution)/shard_map/ppermute | solution.py:251
  49.1 3.3 %conditional.8 = (f32[128,512]{1,0:T(8,128)S(1)}, f32[128,512]{1,0:T(8,128)S(1)}, bf16[1536,256]{1,0:T(8,128)(2,1)S(1)}) conditional(s32[]{:T(128)} %convert_element_type.52, () %tuple.77, (s32[]{:T(128)}, s32[]{:T(128)}, s32[]{:T(128)}, s32[]{:T(128)}, s32[256,2]{1,0:T(8,128)S(1)}, /*index=5*/bf16[256,1536]{1,0:T(8,128)(2,1)S(1)}, ...), branch_computations={%region_4.0_spmd, %region_5.0_spmd} | conditional | flops 12 | bytes 1310754 | solution.py:255
  49.2 3.0 %branch_1_fun.16 = (f32[128,512]{1,0:T(8,128)S(1)}, f32[128,512]{1,0:T(8,128)S(1)}) custom-call(s32[4]{0:T(128)S(1)} %pad_add_fusion.r_0_, s32[256,2]{1,0:T(8,128)S(1)} %get-tuple-element.139.r_1_, bf16[256,1536]{1,0:T(8,128)(2,1)S(1)} %get-tuple-element.140.r_2_, bf16[1,1536,128]{2,1,0:T(8,128)(2,1)S(1)} %get-tuple-element.141.r_3_, ...), custom_call_target="tpu_custom_call" | custom-call | tf_op jit(solution)/shard_map/cond/branch_1_fun/pallas_call | solution.py:19
  53.7 2.2 %shard_map.91 = (f32[128,512]{1,0:T(8,128)S(1)}, f32[128,512]{1,0:T(8,128)S(1)}) custom-call(s32[2]{0:T(128)S(1)} %pad_add_fusion.2.r_0_, s32[256,2]{1,0:T(8,128)S(1)} %get-tuple-element.229.r_1_, bf16[256,1536]{1,0:T(8,128)(2,1)S(1)} %get-tuple-element.230.r_2_, f32[128,512]{1,0:T(8,128)S(1)} %get-tuple-element.237.r_3_, ...), custom_call_target="tpu_custom_call" | custom-call | tf_op jit(solution)/shard_map/pallas_call | solution.py:19
  55.9 7.4 %conditional.9 = (f32[128,512]{1,0:T(8,128)S(1)}, bf16[128,512]{1,0:T(8,128)(2,1)}) conditional(s32[]{:T(128)} %convert_element_type.49, () %tuple.69, (f32[128,512]{1,0:T(8,128)S(1)}, f32[128,512]{1,0:T(8,128)S(1)}) %tuple.81), branch_computations={%region_6.0_spmd, %region_7.0_spmd} | conditional | flops 131072 | bytes 2490464 | solution.py:255
  59.1 4.2 %collective-permute-done.7 = bf16[128,512]{1,0:T(8,128)(2,1)} collective-permute-done((bf16[128,512]{1,0:T(8,128)(2,1)S(1)}, bf16[128,512]{1,0:T(8,128)(2,1)}, u32[]{:S(2)}, u32[]{:S(2)}) %collective-permute-start.7) | collective-permute-done | bytes 131104 | tf_op jit(solution)/shard_map/cond/branch_1_fun/ppermute | solution.py:324
  63.3 6.9 %conditional.10 = (f32[1536,128]{1,0:T(8,128)}, bf16[1536,128]{1,0:T(8,128)(2,1)}, bf16[1536,128]{1,0:T(8,128)(2,1)}, bf16[1536,128]{1,0:T(8,128)(2,1)}, bf16[1,768,128]{2,1,0:T(8,128)(2,1)}) conditional(s32[]{:T(128)} %convert_element_type.49, () %tuple.65, (bf16[128,128]{1,0:T(8,128)(2,1)}, f32[128,512]{1,0:T(8,128)S(1)}, ...), branch_computations={%region_8.0_spmd, %region_9.0_spmd} | conditional | bytes 2162740 | solution.py:255
  67.3 2.9 %branch_1_fun.19 = (f32[1536,128]{1,0:T(8,128)}, bf16[1536,128]{1,0:T(8,128)(2,1)}, bf16[1536,128]{1,0:T(8,128)(2,1)}, bf16[1536,128]{1,0:T(8,128)(2,1)}) custom-call(s32[4]{0:T(128)S(1)} %get-tuple-element.152.r_0_, s32[256,2]{1,0:T(8,128)S(1)} %get-tuple-element.153.r_1_, bf16[1536,256]{1,0:T(8,128)(2,1)S(1)} %get-tuple-element.154.r_2_, ...), custom_call_target="tpu_custom_call" | custom-call | tf_op jit(solution)/shard_map/cond/branch_1_fun/pallas_call | solution.py:402
  71.8 2.7 %collective-permute-start.25 = (bf16[1536,128]{1,0:T(8,128)(2,1)}, bf16[1536,128]{1,0:T(8,128)(2,1)}, u32[]{:S(2)}, u32[]{:S(2)}) collective-permute-start(bf16[1536,128]{1,0:T(8,128)(2,1)} %get-tuple-element.248), channel_id=1, source_target_pairs={{0,2},{2,0},{4,6},{6,4},{1,3},{3,1},{5,7},{7,5},{8,10},{10,8},{12,... | collective-permute-start | bytes 1179656 | tf_op jit(solution)/shard_map/ppermute | solution.py:251
  74.5 26.4 %conditional.11 = (bf16[64,6144]{1,0:T(8,128)(2,1)S(1)}) conditional(s32[]{:T(128)} %convert_element_type.53, () %tuple.85, (s32[]{:T(128)}, s32[]{:T(128)}, s32[]{:T(128)}, s32[]{:T(128)}, s32[]{:T(128)}, /*index=5*/s32[]{:T(128)}, s32[]{:T(128)}, s32[256,2]{1,0:T(8,128)S(1)}, bf16[256,1536]{1,0:T(8,128)(2,1)S(1)}, ...), branch_computations={%region_10.0_spmd, %region_11.0_spmd} | conditional | flops 65553 | bytes 4129188 | solution.py:255
  74.6 3.0 %branch_1_fun.20 = (f32[128,256]{1,0:T(8,128)S(1)}, f32[128,256]{1,0:T(8,128)S(1)}) custom-call(s32[5]{0:T(128)S(1)} %stack.75.r_0_, s32[256,2]{1,0:T(8,128)S(1)} %get-tuple-element.170.r_1_, bf16[256,1536]{1,0:T(8,128)(2,1)S(1)} %get-tuple-element.174.r_2_, bf16[1,1536,128]{2,1,0:T(8,128)(2,1)} %get-tuple-element.175.r_3_, ...), custom_call_target="tpu_custom_call" | custom-call | tf_op jit(solution)/shard_map/cond/branch_1_fun/pallas_call | solution.py:19
  80.6 2.8 %collective-permute-done.9.r_4_ = bf16[128,256]{1,0:T(8,128)(2,1)S(1)} collective-permute-done((bf16[128,256]{1,0:T(8,128)(2,1)S(1)}, bf16[128,256]{1,0:T(8,128)(2,1)S(1)}, u32[]{:S(2)}, u32[]{:S(2)}) %collective-permute-start.9) | collective-permute-done | bytes 65568 | tf_op jit(solution)/shard_map/cond/branch_1_fun/ppermute | solution.py:324
  86.0 3.4 %branch_1_fun.22 = (bf16[64,1536]{1,0:T(8,128)(2,1)S(1)}, bf16[64,1536]{1,0:T(8,128)(2,1)S(1)}, bf16[64,1536]{1,0:T(8,128)(2,1)S(1)}, bf16[64,1536]{1,0:T(8,128)(2,1)S(1)}) custom-call(s32[5]{0:T(128)S(1)} %stack.71.r_0_, s32[256,2]{1,0:T(8,128)S(1)} %get-tuple-element.170.r_1_, bf16[128,512]{1,0:T(8,128)(2,1)S(1)} %branch_1_fun.21.r_2_, ...), custom_call_target="tpu_custom_call" | custom-call | tf_op jit(solution)/shard_map/cond/branch_1_fun/pallas_call | solution.py:19
  92.2 5.1 %collective-permute-done.11.refs_1_ = bf16[64,1536]{1,0:T(8,128)(2,1)S(1)} collective-permute-done((bf16[64,1536]{1,0:T(8,128)(2,1)S(1)}, bf16[64,1536]{1,0:T(8,128)(2,1)S(1)}, u32[]{:S(2)}, u32[]{:S(2)}) %collective-permute-start.11) | collective-permute-done | bytes 196640 | tf_op jit(solution)/shard_map/cond/branch_1_fun/ppermute | solution.py:450
  97.3 3.1 %collective-permute-done.13.refs_3_ = bf16[64,1536]{1,0:T(8,128)(2,1)S(1)} collective-permute-done((bf16[64,1536]{1,0:T(8,128)(2,1)S(1)}, bf16[64,1536]{1,0:T(8,128)(2,1)S(1)}, u32[]{:S(2)}, u32[]{:S(2)}) %collective-permute-start.13) | collective-permute-done | bytes 196640 | tf_op jit(solution)/shard_map/cond/branch_1_fun/ppermute | solution.py:452
  101.0 4.1 %collective-permute-done.24 = bf16[1536,128]{1,0:T(8,128)(2,1)} collective-permute-done((bf16[1536,128]{1,0:T(8,128)(2,1)}, bf16[1536,128]{1,0:T(8,128)(2,1)}, u32[]{:S(2)}, u32[]{:S(2)}) %collective-permute-start.24) | collective-permute-done | bytes 393248 | tf_op jit(solution)/shard_map/ppermute | solution.py:251
  105.1 2.5 %add_bitcast_fusion = f32[1,1536,128]{2,1,0:T(8,128)} fusion(bf16[1536,128]{1,0:T(8,128)(2,1)} %collective-permute-done.25, bf16[1536,128]{1,0:T(8,128)(2,1)} %collective-permute-done.24, f32[1536,128]{1,0:T(8,128)} %get-tuple-element.254, bf16[1536,128]{1,0:T(8,128)(2,1)} %collective-permute-done.23), kind=kLoop, calls=%fused_computation.12 | loop fusion | flops 1179648 | bytes 2752512 | tf_op jit(solution)/shard_map/broadcast_in_dim | solution.py:475
  (88 shorter events, 35.8 us)
Async XLA Ops:
  1.9 20.5 %collective-permute-start.14 = (bf16[2,768,128]{2,1,0:T(8,128)(2,1)S(1)}, bf16[2,768,128]{2,1,0:T(8,128)(2,1)S(1)}, u32[]{:S(2)}, u32[]{:S(2)}) collective-permute-start(bf16[2,768,128]{2,1,0:T(8,128)(2,1)S(1)} %get-tuple-element.232), channel_id=1, source_target_pairs={{0,6},{2,4},{4,2},{6,0},{1,7},{3,5},{5,3},{7,1},{8,14},{10,12},{12... | collective-permute-start | bytes 1179656 | tf_op jit(solution)/shard_map/ppermute | solution.py:251
  7.0 19.8 %collective-permute-start.16 = (bf16[1,1536,128]{2,1,0:T(8,128)(2,1)S(1)}, bf16[1,1536,128]{2,1,0:T(8,128)(2,1)}, u32[]{:S(2)}, u32[]{:S(2)}) collective-permute-start(bf16[1,1536,128]{2,1,0:T(8,128)(2,1)S(1)} %copy-done), channel_id=1, source_target_pairs={{0,2},{2,0},{4,6},{6,4},{1,3},{3,1},{5,7},{7,5},{8,10},{10,8},{12,... | collective-permute-start | bytes 1179656 | tf_op jit(solution)/shard_map/ppermute | solution.py:251
  8.6 11.0 %collective-permute-start.2 = (bf16[64,3200]{1,0:T(8,128)(2,1)S(1)}, bf16[64,3200]{1,0:T(8,128)(2,1)S(1)}, u32[]{:S(2)}, u32[]{:S(2)}) collective-permute-start(bf16[64,3200]{1,0:T(8,128)(2,1)S(1)} %get-tuple-element.125), channel_id=1, source_target_pairs={{0,8},{8,0},{1,9},{9,1},{2,10},{10,2},{3,11},{11,3},{4,12},{12,4},... | collective-permute-start | bytes 1228808 | tf_op jit(solution)/shard_map/cond/branch_1_fun/ppermute | solution.py:287
  19.6 1.8 %collective-permute-start.3 = (bf16[128,1664]{1,0:T(8,128)(2,1)S(1)}, bf16[128,1664]{1,0:T(8,128)(2,1)S(1)}, u32[]{:S(2)}, u32[]{:S(2)}) collective-permute-start(bf16[128,1664]{1,0:T(8,128)(2,1)S(1)} %get-tuple-element.127), channel_id=1, source_target_pairs={{0,1},{1,0},{2,3},{3,2},{4,5},{5,4},{6,7},{7,6},{8,9},{9,8},{10,11... | collective-permute-start | bytes 1277960 | tf_op jit(solution)/shard_map/cond/branch_1_fun/ppermute | solution.py:287
  22.4 20.8 %collective-permute-start.15 = (bf16[2,768,128]{2,1,0:T(8,128)(2,1)S(1)}, bf16[2,768,128]{2,1,0:T(8,128)(2,1)}, u32[]{:S(2)}, u32[]{:S(2)}) collective-permute-start(bf16[2,768,128]{2,1,0:T(8,128)(2,1)S(1)} %get-tuple-element.232), channel_id=1, source_target_pairs={{0,4},{2,6},{4,0},{6,2},{1,5},{3,7},{5,1},{7,3},{8,12},{10,14},{12... | collective-permute-start | bytes 1179656 | tf_op jit(solution)/shard_map/ppermute | solution.py:251
  25.2 17.9 %collective-permute-start.18 = (bf16[2,768,128]{2,1,0:T(8,128)(2,1)S(1)}, bf16[2,768,128]{2,1,0:T(8,128)(2,1)}, u32[]{:S(2)}, u32[]{:S(2)}) collective-permute-start(bf16[2,768,128]{2,1,0:T(8,128)(2,1)S(1)} %collective-permute-done.14), channel_id=1, source_target_pairs={{0,16},{16,0},{1,17},{17,1},{2,18},{18,2},{3,19},{19,3},{4,20},{20... | collective-permute-start | bytes 1179656 | tf_op jit(solution)/shard_map/ppermute | solution.py:358
  26.8 22.3 %collective-permute-start.17 = (bf16[1,1536,128]{2,1,0:T(8,128)(2,1)S(1)}, bf16[1,1536,128]{2,1,0:T(8,128)(2,1)}, u32[]{:S(2)}, u32[]{:S(2)}) collective-permute-start(bf16[1,1536,128]{2,1,0:T(8,128)(2,1)S(1)} %copy-done.1), channel_id=1, source_target_pairs={{0,2},{2,0},{4,6},{6,4},{1,3},{3,1},{5,7},{7,5},{8,10},{10,8},{12,... | collective-permute-start | bytes 1179656 | tf_op jit(solution)/shard_map/ppermute | solution.py:251
  28.0 9.6 %collective-permute-start.4 = (bf16[64,3072]{1,0:T(8,128)(2,1)S(1)}, bf16[64,3072]{1,0:T(8,128)(2,1)S(1)}, u32[]{:S(2)}, u32[]{:S(2)}) collective-permute-start(bf16[64,3072]{1,0:T(8,128)(2,1)S(1)} %get-tuple-element.132), channel_id=1, source_target_pairs={{0,8},{8,0},{1,9},{9,1},{2,10},{10,2},{3,11},{11,3},{4,12},{12,4},... | collective-permute-start | bytes 1179656 | tf_op jit(solution)/shard_map/cond/branch_1_fun/ppermute | solution.py:287
  37.7 1.8 %collective-permute-start.5 = (bf16[128,1536]{1,0:T(8,128)(2,1)S(1)}, bf16[128,1536]{1,0:T(8,128)(2,1)S(1)}, u32[]{:S(2)}, u32[]{:S(2)}) collective-permute-start(bf16[128,1536]{1,0:T(8,128)(2,1)S(1)} %get-tuple-element.134), channel_id=1, source_target_pairs={{0,1},{1,0},{2,3},{3,2},{4,5},{5,4},{6,7},{7,6},{8,9},{9,8},{10,11... | collective-permute-start | bytes 1179656 | tf_op jit(solution)/shard_map/cond/branch_1_fun/ppermute | solution.py:287
  43.1 10.6 %collective-permute-start.19 = (bf16[2,768,128]{2,1,0:T(8,128)(2,1)}, bf16[2,768,128]{2,1,0:T(8,128)(2,1)}, u32[]{:S(2)}, u32[]{:S(2)}) collective-permute-start(bf16[2,768,128]{2,1,0:T(8,128)(2,1)} %collective-permute-done.15.r_5_), channel_id=1, source_target_pairs={{0,16},{16,0},{1,17},{17,1},{2,18},{18,2},{3,19},{19,3},{4,20},{20... | collective-permute-start | bytes 1179656 | tf_op jit(solution)/shard_map/ppermute | solution.py:371
  44.6 18.7 %collective-permute-start.20 = (bf16[1,768,128]{2,1,0:T(8,128)(2,1)S(1)}, bf16[1,768,128]{2,1,0:T(8,128)(2,1)}, u32[]{:S(2)}, u32[]{:S(2)}) collective-permute-start(bf16[1,768,128]{2,1,0:T(8,128)(2,1)S(1)} %get-tuple-element.246), channel_id=1, source_target_pairs={{0,6},{2,4},{4,2},{6,0},{1,7},{3,5},{5,3},{7,1},{8,14},{10,12},{12... | collective-permute-start | bytes 589832 | tf_op jit(solution)/shard_map/ppermute | solution.py:251
  46.2 28.3 %collective-permute-start.21 = (bf16[1,1536,128]{2,1,0:T(8,128)(2,1)}, bf16[1,1536,128]{2,1,0:T(8,128)(2,1)}, u32[]{:S(2)}, u32[]{:S(2)}) collective-permute-start(bf16[1,1536,128]{2,1,0:T(8,128)(2,1)} %down.1), channel_id=1, source_target_pairs={{0,2},{2,0},{4,6},{6,4},{1,3},{3,1},{5,7},{7,5},{8,10},{10,8},{12,... | collective-permute-start | bytes 1179656 | tf_op jit(solution)/shard_map/ppermute | solution.py:251
  46.3 28.3 %collective-permute-start.22 = (bf16[1,1536,128]{2,1,0:T(8,128)(2,1)}, bf16[1,1536,128]{2,1,0:T(8,128)(2,1)}, u32[]{:S(2)}, u32[]{:S(2)}) collective-permute-start(bf16[1,1536,128]{2,1,0:T(8,128)(2,1)} %down.1), channel_id=1, source_target_pairs={{0,4},{2,6},{4,0},{6,2},{1,5},{3,7},{5,1},{7,3},{8,12},{10,14},{12... | collective-permute-start | bytes 1179656 | tf_op jit(solution)/shard_map/ppermute | solution.py:251
  55.9 1.6 %collective-permute-start.6 = (f32[128,512]{1,0:T(8,128)S(1)}, f32[128,512]{1,0:T(8,128)S(1)}, u32[]{:S(2)}, u32[]{:S(2)}) collective-permute-start(f32[128,512]{1,0:T(8,128)S(1)} %get-tuple-element.151), channel_id=1, source_target_pairs={{0,1},{1,0},{2,3},{3,2},{4,5},{5,4},{6,7},{7,6},{8,9},{9,8},{10,11... | collective-permute-start | bytes 786440 | tf_op jit(solution)/shard_map/cond/branch_1_fun/ppermute | solution.py:323
  57.6 5.7 %collective-permute-start.7 = (bf16[128,512]{1,0:T(8,128)(2,1)S(1)}, bf16[128,512]{1,0:T(8,128)(2,1)}, u32[]{:S(2)}, u32[]{:S(2)}) collective-permute-start(bf16[128,512]{1,0:T(8,128)(2,1)S(1)} %get-tuple-element.268), channel_id=1, source_target_pairs={{0,8},{8,0},{1,9},{9,1},{2,10},{10,2},{3,11},{11,3},{4,12},{12,4},... | collective-permute-start | bytes 393224 | tf_op jit(solution)/shard_map/cond/branch_1_fun/ppermute | solution.py:324
  63.3 6.9 %collective-permute-start.1 = (bf16[1,768,128]{2,1,0:T(8,128)(2,1)}, bf16[1,768,128]{2,1,0:T(8,128)(2,1)}, u32[]{:S(2)}, u32[]{:S(2)}) collective-permute-start(bf16[1,768,128]{2,1,0:T(8,128)(2,1)} %get-tuple-element.162), channel_id=1, source_target_pairs={{0,16},{16,0},{1,17},{17,1},{2,18},{18,2},{3,19},{19,3},{4,20},{20... | collective-permute-start | bytes 589832 | tf_op jit(solution)/shard_map/cond/branch_1_fun/ppermute | solution.py:391
  70.1 30.9 %collective-permute-start.23 = (bf16[1536,128]{1,0:T(8,128)(2,1)}, bf16[1536,128]{1,0:T(8,128)(2,1)}, u32[]{:S(2)}, u32[]{:S(2)}) collective-permute-start(bf16[1536,128]{1,0:T(8,128)(2,1)} %get-tuple-element.250), channel_id=1, source_target_pairs={{0,6},{2,4},{4,2},{6,0},{1,7},{3,5},{5,3},{7,1},{8,14},{10,12},{12... | collective-permute-start | bytes 1179656 | tf_op jit(solution)/shard_map/ppermute | solution.py:251
  71.8 33.3 %collective-permute-start.24 = (bf16[1536,128]{1,0:T(8,128)(2,1)}, bf16[1536,128]{1,0:T(8,128)(2,1)}, u32[]{:S(2)}, u32[]{:S(2)}) collective-permute-start(bf16[1536,128]{1,0:T(8,128)(2,1)} %get-tuple-element.249), channel_id=1, source_target_pairs={{0,4},{2,6},{4,0},{6,2},{1,5},{3,7},{5,1},{7,3},{8,12},{10,14},{12... | collective-permute-start | bytes 1179656 | tf_op jit(solution)/shard_map/ppermute | solution.py:251
  71.8 33.3 %collective-permute-start.25 = (bf16[1536,128]{1,0:T(8,128)(2,1)}, bf16[1536,128]{1,0:T(8,128)(2,1)}, u32[]{:S(2)}, u32[]{:S(2)}) collective-permute-start(bf16[1536,128]{1,0:T(8,128)(2,1)} %get-tuple-element.248), channel_id=1, source_target_pairs={{0,2},{2,0},{4,6},{6,4},{1,3},{3,1},{5,7},{7,5},{8,10},{10,8},{12,... | collective-permute-start | bytes 1179656 | tf_op jit(solution)/shard_map/ppermute | solution.py:251
  77.7 1.4 %collective-permute-start.8 = (f32[128,256]{1,0:T(8,128)S(1)}, f32[128,256]{1,0:T(8,128)S(1)}, u32[]{:S(2)}, u32[]{:S(2)}) collective-permute-start(f32[128,256]{1,0:T(8,128)S(1)} %get-tuple-element.181), channel_id=1, source_target_pairs={{0,1},{1,0},{2,3},{3,2},{4,5},{5,4},{6,7},{7,6},{8,9},{9,8},{10,11... | collective-permute-start | bytes 393224 | tf_op jit(solution)/shard_map/cond/branch_1_fun/ppermute | solution.py:323
  79.1 4.3 %collective-permute-start.9 = (bf16[128,256]{1,0:T(8,128)(2,1)S(1)}, bf16[128,256]{1,0:T(8,128)(2,1)S(1)}, u32[]{:S(2)}, u32[]{:S(2)}) collective-permute-start(bf16[128,256]{1,0:T(8,128)(2,1)S(1)} %get-tuple-element.270), channel_id=1, source_target_pairs={{0,8},{8,0},{1,9},{9,1},{2,10},{10,2},{3,11},{11,3},{4,12},{12,4},... | collective-permute-start | bytes 196616 | tf_op jit(solution)/shard_map/cond/branch_1_fun/ppermute | solution.py:324
  89.4 1.7 %collective-permute-start.12 = (bf16[64,1536]{1,0:T(8,128)(2,1)S(1)}, bf16[64,1536]{1,0:T(8,128)(2,1)S(1)}, u32[]{:S(2)}, u32[]{:S(2)}) collective-permute-start(bf16[64,1536]{1,0:T(8,128)(2,1)S(1)} %get-tuple-element.192), channel_id=1, source_target_pairs={{0,1},{1,0},{2,3},{3,2},{4,5},{5,4},{6,7},{7,6},{8,9},{9,8},{10,11... | collective-permute-start | bytes 589832 | tf_op jit(solution)/shard_map/cond/branch_1_fun/ppermute | solution.py:451
  89.6 7.7 %collective-permute-start.11 = (bf16[64,1536]{1,0:T(8,128)(2,1)S(1)}, bf16[64,1536]{1,0:T(8,128)(2,1)S(1)}, u32[]{:S(2)}, u32[]{:S(2)}) collective-permute-start(bf16[64,1536]{1,0:T(8,128)(2,1)S(1)} %get-tuple-element.191), channel_id=1, source_target_pairs={{0,8},{8,0},{1,9},{9,1},{2,10},{10,2},{3,11},{11,3},{4,12},{12,4},... | collective-permute-start | bytes 589832 | tf_op jit(solution)/shard_map/cond/branch_1_fun/ppermute | solution.py:450
  91.1 9.3 %collective-permute-start.13 = (bf16[64,1536]{1,0:T(8,128)(2,1)S(1)}, bf16[64,1536]{1,0:T(8,128)(2,1)S(1)}, u32[]{:S(2)}, u32[]{:S(2)}) collective-permute-start(bf16[64,1536]{1,0:T(8,128)(2,1)S(1)} %get-tuple-element.194), channel_id=1, source_target_pairs={{0,9},{1,8},{8,1},{9,0},{2,11},{3,10},{10,3},{11,2},{4,13},{5,12},... | collective-permute-start | bytes 589832 | tf_op jit(solution)/shard_map/cond/branch_1_fun/ppermute | solution.py:452
  (11 other events, 97.1 us)

commit v7 on v6

--- a/solution.py
+++ b/solution.py
@@ -383,11 +383,11 @@
         gu_slots = gu_slots + todo
     dn_slots += [("parts", e ^ k, [dn[k]]) for k in [1, *later_ones]]
     parts = sums(tok, todo, 2, parts)
-    first = region(lambda: reduce_rows(parts))
 
     targets = jnp.stack([e ^ k for k in range(n)]).astype(jnp.int32)
 
     def down_step():
+        first = reduce_rows(parts)
         dn_far = pp(dn[first_one], "groups", SWAP)
         hidden = call(
             hidden_step,
@@ -416,9 +416,9 @@
             compiler_params=PARAMS,
             cost_estimate=pl.CostEstimate(flops=0, bytes_accessed=0, transcendentals=0),
         )(targets, ids, cot_t, *hidden)
-        return pieces, dn_far
-
-    pieces, dn_far = region(down_step)
+        return pieces, dn_far, first
+
+    pieces, dn_far, first = region(down_step)
     dn_slots.append(("halves", e ^ first_one, [dn[first_one], dn_far]))
     shares = [partner(pieces[k], k) for k in range(n - 1, 0, -1)]
 

time: 108 us -> 107 us (level)
  waiting for transfers between devices: 49.8 us -> 48.4 us
  starting transfers between devices: 30.6 us -> 31.8 us
    ppermute x2, waiting for transfers between devices: 6.94 us -> 5.41 us  [reduce_rows(): return [total, pp(total.astype(BF), 'fsdp', SWAP)]]
    ppermute x10, starting transfers between devices: 16.8 us -> 17.9 us  [partner(): return pp(block, 'expert', [(i, i ^ k) for i in range(n)])]
  transfers between devices with their start and end apart: 26 -> 26, of which waited for: 15 -> 15; matrix products, arithmetic and copies ran while one was open for 2% -> 3% of each run, Pallas kernels for 19% -> 18%
where the time goes in v7:
time: 107 us
  waiting for transfers between devices  48.4 us (45%)
  starting transfers between devices  31.8 us (30%)
  Pallas kernels  20.3 us (19%)
  other arithmetic  4.38 us (4%)
  local copies, waits for them, and re-layouts  1.2 us (1%)
    ppermute x4, waiting for transfers between devices, swap_columns(): return [kept, pp(sent, axis, SWAP)]  20.3 us
    ppermute x10, starting transfers between devices, partner(): return pp(block, 'expert', [(i, i ^ k) for i in range(n)])  17.9 us
    pallas_call x13, Pallas kernels, call(): pl.pallas_call(body, out_shape=outs, in_specs=specs, out_specs=jax.tree.m...  17.4 us
    ppermute x10, waiting for transfers between devices, partner(): return pp(block, 'expert', [(i, i ^ k) for i in range(n)])  8.59 us
    ppermute x2, waiting for transfers between devices, reduce_rows(): return [total, pp(total.astype(BF), 'fsdp', SWAP)]  5.41 us
    ppermute x1, waiting for transfers between devices, token_gradient(): across = pp(back[1], 'fsdp', SWAP)  5.12 us
    ppermute x4, starting transfers between devices, swap_columns(): return [kept, pp(sent, axis, SWAP)]  3.25 us
    ppermute x1, waiting for transfers between devices, token_gradient(): pp(after(back[3], beside), ('fsdp', 'dp'), [(i, 3 - i) for i in range(4)])  3.08 us
  transfers between devices with their start and end apart: 26, of which 15 were waited for; matrix products, arithmetic and copies ran while one was open for 3% of the time, Pallas kernels for 18%

profile of v7, /device:TPU:0, one launch (start us, length us, event | category | flops | bytes accessed | tf_op | source)
XLA Modules:
  0.0 107.1 jit_solution(3540780657435087271)
XLA Ops:
  1.9 5.1 %collective-permute-start.14 = (bf16[2,768,128]{2,1,0:T(8,128)(2,1)S(1)}, bf16[2,768,128]{2,1,0:T(8,128)(2,1)S(1)}, u32[]{:S(2)}, u32[]{:S(2)}) collective-permute-start(bf16[2,768,128]{2,1,0:T(8,128)(2,1)S(1)} %get-tuple-element.225), channel_id=1, source_target_pairs={{0,6},{2,4},{4,2},{6,0},{1,7},{3,5},{5,3},{7,1},{8,14},{10,12},{12... | collective-permute-start | bytes 1179656 | tf_op jit(solution)/shard_map/ppermute | solution.py:251
  7.1 14.2 %conditional.5 = (bf16[256,1536]{1,0:T(8,128)(2,1)S(1)}, s32[256,2]{1,0:T(8,128)S(1)}, bf16[128,128]{1,0:T(8,128)(2,1)}) conditional(s32[]{:T(128)} %convert_element_type.49, () %tuple.59, (s32[]{:T(128)}, s32[]{:T(128)}, s32[64,2]{0,1:T(2,128)S(1)}, f32[64,2]{0,1:T(2,128)S(1)}, bf16[64,6144]{1,0:T(8,128)(2,1)S(1)}) %tuple.102), branch_computations={%region_0.0_spmd, %region_1.0_spmd} | conditional | flops 1576064 | bytes 6739050 | solution.py:255
  9.1 9.4 %collective-permute-done.r_2_ = bf16[64,3200]{1,0:T(8,128)(2,1)S(1)} collective-permute-done((bf16[64,3200]{1,0:T(8,128)(2,1)S(1)}, bf16[64,3200]{1,0:T(8,128)(2,1)S(1)}, u32[]{:S(2)}, u32[]{:S(2)}) %collective-permute-start) | collective-permute-done | bytes 409632 | tf_op jit(solution)/shard_map/cond/branch_1_fun/ppermute | solution.py:287
  21.3 4.0 %collective-permute-start.15 = (bf16[2,768,128]{2,1,0:T(8,128)(2,1)S(1)}, bf16[2,768,128]{2,1,0:T(8,128)(2,1)}, u32[]{:S(2)}, u32[]{:S(2)}) collective-permute-start(bf16[2,768,128]{2,1,0:T(8,128)(2,1)S(1)} %get-tuple-element.225), channel_id=1, source_target_pairs={{0,4},{2,6},{4,0},{6,2},{1,5},{3,7},{5,1},{7,3},{8,12},{10,14},{12... | collective-permute-start | bytes 1179656 | tf_op jit(solution)/shard_map/ppermute | solution.py:251
  26.8 12.7 %conditional.6 = (bf16[256,1536]{1,0:T(8,128)(2,1)S(1)}) conditional(s32[]{:T(128)} %convert_element_type.50, () %tuple.64, (s32[]{:T(128)}, s32[]{:T(128)}, bf16[64,6144]{1,0:T(8,128)(2,1)}) %tuple.65), branch_computations={%region_2.0_spmd, %region_3.0_spmd} | conditional | flops 1572864 | bytes 4718680 | solution.py:255
  29.6 8.0 %collective-permute-done.2.r_2_ = bf16[64,3072]{1,0:T(8,128)(2,1)S(1)} collective-permute-done((bf16[64,3072]{1,0:T(8,128)(2,1)S(1)}, bf16[64,3072]{1,0:T(8,128)(2,1)S(1)}, u32[]{:S(2)}, u32[]{:S(2)}) %collective-permute-start.2) | collective-permute-done | bytes 393248 | tf_op jit(solution)/shard_map/cond/branch_1_fun/ppermute | solution.py:287
  37.8 1.7 %collective-permute-done.3 = bf16[128,1536]{1,0:T(8,128)(2,1)S(1)} collective-permute-done((bf16[128,1536]{1,0:T(8,128)(2,1)S(1)}, bf16[128,1536]{1,0:T(8,128)(2,1)S(1)}, u32[]{:S(2)}, u32[]{:S(2)}) %collective-permute-start.3) | collective-permute-done | bytes 393248 | tf_op jit(solution)/shard_map/cond/branch_1_fun/ppermute | solution.py:287
  39.5 2.7 %collective-permute-done.15.r_5_ = bf16[2,768,128]{2,1,0:T(8,128)(2,1)} collective-permute-done((bf16[2,768,128]{2,1,0:T(8,128)(2,1)S(1)}, bf16[2,768,128]{2,1,0:T(8,128)(2,1)}, u32[]{:S(2)}, u32[]{:S(2)}) %collective-permute-start.15) | collective-permute-done | bytes 393248 | tf_op jit(solution)/shard_map/ppermute | solution.py:251
  45.4 2.9 %collective-permute-start.22 = (bf16[1,1536,128]{2,1,0:T(8,128)(2,1)}, bf16[1,1536,128]{2,1,0:T(8,128)(2,1)}, u32[]{:S(2)}, u32[]{:S(2)}) collective-permute-start(bf16[1,1536,128]{2,1,0:T(8,128)(2,1)} %down.1), channel_id=1, source_target_pairs={{0,4},{2,6},{4,0},{6,2},{1,5},{3,7},{5,1},{7,3},{8,12},{10,14},{12... | collective-permute-start | bytes 1179656 | tf_op jit(solution)/shard_map/ppermute | solution.py:251
  48.4 3.3 %conditional.7 = (f32[128,512]{1,0:T(8,128)S(1)}, f32[128,512]{1,0:T(8,128)S(1)}, bf16[1536,256]{1,0:T(8,128)(2,1)S(1)}) conditional(s32[]{:T(128)} %convert_element_type.51, () %tuple.68, (s32[]{:T(128)}, s32[]{:T(128)}, s32[]{:T(128)}, s32[]{:T(128)}, s32[256,2]{1,0:T(8,128)S(1)}, /*index=5*/bf16[256,1536]{1,0:T(8,128)(2,1)S(1)}, ...), branch_computations={%region_4.0_spmd, %region_5.0_spmd} | conditional | flops 12 | bytes 1310754 | solution.py:255
  48.4 3.0 %branch_1_fun.16 = (f32[128,512]{1,0:T(8,128)S(1)}, f32[128,512]{1,0:T(8,128)S(1)}) custom-call(s32[4]{0:T(128)S(1)} %pad_add_fusion.r_0_, s32[256,2]{1,0:T(8,128)S(1)} %get-tuple-element.135.r_1_, bf16[256,1536]{1,0:T(8,128)(2,1)S(1)} %get-tuple-element.136.r_2_, bf16[1,1536,128]{2,1,0:T(8,128)(2,1)S(1)} %get-tuple-element.137.r_3_, ...), custom_call_target="tpu_custom_call" | custom-call | tf_op jit(solution)/shard_map/cond/branch_1_fun/pallas_call | solution.py:19
  52.3 2.2 %shard_map.91 = (f32[128,512]{1,0:T(8,128)S(1)}, f32[128,512]{1,0:T(8,128)S(1)}) custom-call(s32[2]{0:T(128)S(1)} %pad_add_fusion.2.r_0_, s32[256,2]{1,0:T(8,128)S(1)} %get-tuple-element.222.r_1_, bf16[256,1536]{1,0:T(8,128)(2,1)S(1)} %get-tuple-element.223.r_2_, f32[128,512]{1,0:T(8,128)S(1)} %get-tuple-element.230.r_3_, ...), custom_call_target="tpu_custom_call" | custom-call | tf_op jit(solution)/shard_map/pallas_call | solution.py:19
  54.5 13.4 %conditional.8 = (f32[1536,128]{1,0:T(8,128)}, bf16[1536,128]{1,0:T(8,128)(2,1)}, bf16[1536,128]{1,0:T(8,128)(2,1)}, bf16[1536,128]{1,0:T(8,128)(2,1)}, bf16[1,7...) conditional(s32[]{:T(128)} %convert_element_type.48, () %tuple.57, ...), branch_computations={%region_6.0_spmd, %region_7.0_spmd} | conditional | flops 131072 | bytes 3539160 | solution.py:255
  59.8 2.6 %collective-permute-done.5.refs_1_ = bf16[128,512]{1,0:T(8,128)(2,1)} collective-permute-done((bf16[128,512]{1,0:T(8,128)(2,1)S(1)}, bf16[128,512]{1,0:T(8,128)(2,1)}, u32[]{:S(2)}, u32[]{:S(2)}) %collective-permute-start.5) | collective-permute-done | bytes 131104 | tf_op jit(solution)/shard_map/cond/branch_1_fun/ppermute | solution.py:324
  65.0 2.9 %branch_1_fun.19 = (f32[1536,128]{1,0:T(8,128)}, bf16[1536,128]{1,0:T(8,128)(2,1)}, bf16[1536,128]{1,0:T(8,128)(2,1)}, bf16[1536,128]{1,0:T(8,128)(2,1)}) custom-call(s32[4]{0:T(128)S(1)} %get-tuple-element.146.r_0_, s32[256,2]{1,0:T(8,128)S(1)} %get-tuple-element.147.r_1_, bf16[1536,256]{1,0:T(8,128)(2,1)S(1)} %get-tuple-element.148.r_2_, ...), custom_call_target="tpu_custom_call" | custom-call | tf_op jit(solution)/shard_map/cond/branch_1_fun/pallas_call | solution.py:402
  69.9 2.4 %collective-permute-start.25 = (bf16[1536,128]{1,0:T(8,128)(2,1)}, bf16[1536,128]{1,0:T(8,128)(2,1)}, u32[]{:S(2)}, u32[]{:S(2)}) collective-permute-start(bf16[1536,128]{1,0:T(8,128)(2,1)} %get-tuple-element.240), channel_id=1, source_target_pairs={{0,2},{2,0},{4,6},{6,4},{1,3},{3,1},{5,7},{7,5},{8,10},{10,8},{12,... | collective-permute-start | bytes 1179656 | tf_op jit(solution)/shard_map/ppermute | solution.py:251
  72.3 26.5 %conditional.9 = (bf16[64,6144]{1,0:T(8,128)(2,1)S(1)}) conditional(s32[]{:T(128)} %convert_element_type.52, () %tuple.75, (s32[]{:T(128)}, s32[]{:T(128)}, s32[]{:T(128)}, s32[]{:T(128)}, s32[]{:T(128)}, /*index=5*/s32[]{:T(128)}, s32[]{:T(128)}, s32[256,2]{1,0:T(8,128)S(1)}, bf16[256,1536]{1,0:T(8,128)(2,1)S(1)}, bf16[1,1536,128]{2,1,0:T(8,128)(2,1)}, ...), branch_computations={%region_8.0_spmd, %region_9.0_spmd} | conditional | flops 65553 | bytes 4129188 | solution.py:255
  72.4 3.0 %branch_1_fun.20 = (f32[128,256]{1,0:T(8,128)S(1)}, f32[128,256]{1,0:T(8,128)S(1)}) custom-call(s32[5]{0:T(128)S(1)} %stack.76.r_0_, s32[256,2]{1,0:T(8,128)S(1)} %get-tuple-element.164.r_1_, bf16[256,1536]{1,0:T(8,128)(2,1)S(1)} %get-tuple-element.168.r_2_, bf16[1,1536,128]{2,1,0:T(8,128)(2,1)} %get-tuple-element.169.r_3_, ...), custom_call_target="tpu_custom_call" | custom-call | tf_op jit(solution)/shard_map/cond/branch_1_fun/pallas_call | solution.py:19
  78.4 2.8 %collective-permute-done.9.r_4_ = bf16[128,256]{1,0:T(8,128)(2,1)S(1)} collective-permute-done((bf16[128,256]{1,0:T(8,128)(2,1)S(1)}, bf16[128,256]{1,0:T(8,128)(2,1)S(1)}, u32[]{:S(2)}, u32[]{:S(2)}) %collective-permute-start.9) | collective-permute-done | bytes 65568 | tf_op jit(solution)/shard_map/cond/branch_1_fun/ppermute | solution.py:324
  83.8 3.4 %branch_1_fun.22 = (bf16[64,1536]{1,0:T(8,128)(2,1)S(1)}, bf16[64,1536]{1,0:T(8,128)(2,1)S(1)}, bf16[64,1536]{1,0:T(8,128)(2,1)S(1)}, bf16[64,1536]{1,0:T(8,128)(2,1)S(1)}) custom-call(s32[5]{0:T(128)S(1)} %stack.72.r_0_, s32[256,2]{1,0:T(8,128)S(1)} %get-tuple-element.164.r_1_, bf16[128,512]{1,0:T(8,128)(2,1)S(1)} %branch_1_fun.21.r_2_, ...), custom_call_target="tpu_custom_call" | custom-call | tf_op jit(solution)/shard_map/cond/branch_1_fun/pallas_call | solution.py:19
  90.0 5.1 %collective-permute-done.11.refs_1_ = bf16[64,1536]{1,0:T(8,128)(2,1)S(1)} collective-permute-done((bf16[64,1536]{1,0:T(8,128)(2,1)S(1)}, bf16[64,1536]{1,0:T(8,128)(2,1)S(1)}, u32[]{:S(2)}, u32[]{:S(2)}) %collective-permute-start.11) | collective-permute-done | bytes 196640 | tf_op jit(solution)/shard_map/cond/branch_1_fun/ppermute | solution.py:450
  95.1 3.1 %collective-permute-done.13.refs_3_ = bf16[64,1536]{1,0:T(8,128)(2,1)S(1)} collective-permute-done((bf16[64,1536]{1,0:T(8,128)(2,1)S(1)}, bf16[64,1536]{1,0:T(8,128)(2,1)S(1)}, u32[]{:S(2)}, u32[]{:S(2)}) %collective-permute-start.13) | collective-permute-done | bytes 196640 | tf_op jit(solution)/shard_map/cond/branch_1_fun/ppermute | solution.py:452
  98.8 5.8 %collective-permute-done.24 = bf16[1536,128]{1,0:T(8,128)(2,1)} collective-permute-done((bf16[1536,128]{1,0:T(8,128)(2,1)}, bf16[1536,128]{1,0:T(8,128)(2,1)}, u32[]{:S(2)}, u32[]{:S(2)}) %collective-permute-start.24) | collective-permute-done | bytes 393248 | tf_op jit(solution)/shard_map/ppermute | solution.py:251
  104.6 2.4 %add_bitcast_fusion = f32[1,1536,128]{2,1,0:T(8,128)} fusion(bf16[1536,128]{1,0:T(8,128)(2,1)} %collective-permute-done.25, bf16[1536,128]{1,0:T(8,128)(2,1)} %collective-permute-done.24, f32[1536,128]{1,0:T(8,128)} %get-tuple-element.248, bf16[1536,128]{1,0:T(8,128)(2,1)S(1)} %collective-permute-done.23), kind=kLoop, calls=%fused_computation.12 | loop fusion | flops 1179648 | bytes 2752512 | tf_op jit(solution)/shard_map/broadcast_in_dim | solution.py:475
  (85 shorter events, 33.4 us)
Async XLA Ops:
  1.9 19.4 %collective-permute-start.14 = (bf16[2,768,128]{2,1,0:T(8,128)(2,1)S(1)}, bf16[2,768,128]{2,1,0:T(8,128)(2,1)S(1)}, u32[]{:S(2)}, u32[]{:S(2)}) collective-permute-start(bf16[2,768,128]{2,1,0:T(8,128)(2,1)S(1)} %get-tuple-element.225), channel_id=1, source_target_pairs={{0,6},{2,4},{4,2},{6,0},{1,7},{3,5},{5,3},{7,1},{8,14},{10,12},{12... | collective-permute-start | bytes 1179656 | tf_op jit(solution)/shard_map/ppermute | solution.py:251
  7.0 19.8 %collective-permute-start.16 = (bf16[1,1536,128]{2,1,0:T(8,128)(2,1)S(1)}, bf16[1,1536,128]{2,1,0:T(8,128)(2,1)}, u32[]{:S(2)}, u32[]{:S(2)}) collective-permute-start(bf16[1,1536,128]{2,1,0:T(8,128)(2,1)S(1)} %copy-done), channel_id=1, source_target_pairs={{0,2},{2,0},{4,6},{6,4},{1,3},{3,1},{5,7},{7,5},{8,10},{10,8},{12,... | collective-permute-start | bytes 1179656 | tf_op jit(solution)/shard_map/ppermute | solution.py:251
  7.5 11.0 %collective-permute-start = (bf16[64,3200]{1,0:T(8,128)(2,1)S(1)}, bf16[64,3200]{1,0:T(8,128)(2,1)S(1)}, u32[]{:S(2)}, u32[]{:S(2)}) collective-permute-start(bf16[64,3200]{1,0:T(8,128)(2,1)S(1)} %get-tuple-element.121), channel_id=1, source_target_pairs={{0,8},{8,0},{1,9},{9,1},{2,10},{10,2},{3,11},{11,3},{4,12},{12,4},... | collective-permute-start | bytes 1228808 | tf_op jit(solution)/shard_map/cond/branch_1_fun/ppermute | solution.py:287
  18.6 1.8 %collective-permute-start.1 = (bf16[128,1664]{1,0:T(8,128)(2,1)S(1)}, bf16[128,1664]{1,0:T(8,128)(2,1)S(1)}, u32[]{:S(2)}, u32[]{:S(2)}) collective-permute-start(bf16[128,1664]{1,0:T(8,128)(2,1)S(1)} %get-tuple-element.123), channel_id=1, source_target_pairs={{0,1},{1,0},{2,3},{3,2},{4,5},{5,4},{6,7},{7,6},{8,9},{9,8},{10,11... | collective-permute-start | bytes 1277960 | tf_op jit(solution)/shard_map/cond/branch_1_fun/ppermute | solution.py:287
  21.3 21.0 %collective-permute-start.15 = (bf16[2,768,128]{2,1,0:T(8,128)(2,1)S(1)}, bf16[2,768,128]{2,1,0:T(8,128)(2,1)}, u32[]{:S(2)}, u32[]{:S(2)}) collective-permute-start(bf16[2,768,128]{2,1,0:T(8,128)(2,1)S(1)} %get-tuple-element.225), channel_id=1, source_target_pairs={{0,4},{2,6},{4,0},{6,2},{1,5},{3,7},{5,1},{7,3},{8,12},{10,14},{12... | collective-permute-start | bytes 1179656 | tf_op jit(solution)/shard_map/ppermute | solution.py:251
  25.3 17.0 %collective-permute-start.18 = (bf16[2,768,128]{2,1,0:T(8,128)(2,1)S(1)}, bf16[2,768,128]{2,1,0:T(8,128)(2,1)}, u32[]{:S(2)}, u32[]{:S(2)}) collective-permute-start(bf16[2,768,128]{2,1,0:T(8,128)(2,1)S(1)} %collective-permute-done.14), channel_id=1, source_target_pairs={{0,16},{16,0},{1,17},{17,1},{2,18},{18,2},{3,19},{19,3},{4,20},{20... | collective-permute-start | bytes 1179656 | tf_op jit(solution)/shard_map/ppermute | solution.py:358
  26.8 21.5 %collective-permute-start.17 = (bf16[1,1536,128]{2,1,0:T(8,128)(2,1)S(1)}, bf16[1,1536,128]{2,1,0:T(8,128)(2,1)}, u32[]{:S(2)}, u32[]{:S(2)}) collective-permute-start(bf16[1,1536,128]{2,1,0:T(8,128)(2,1)S(1)} %copy-done.1), channel_id=1, source_target_pairs={{0,2},{2,0},{4,6},{6,4},{1,3},{3,1},{5,7},{7,5},{8,10},{10,8},{12,... | collective-permute-start | bytes 1179656 | tf_op jit(solution)/shard_map/ppermute | solution.py:251
  28.0 9.6 %collective-permute-start.2 = (bf16[64,3072]{1,0:T(8,128)(2,1)S(1)}, bf16[64,3072]{1,0:T(8,128)(2,1)S(1)}, u32[]{:S(2)}, u32[]{:S(2)}) collective-permute-start(bf16[64,3072]{1,0:T(8,128)(2,1)S(1)} %get-tuple-element.128), channel_id=1, source_target_pairs={{0,8},{8,0},{1,9},{9,1},{2,10},{10,2},{3,11},{11,3},{4,12},{12,4},... | collective-permute-start | bytes 1179656 | tf_op jit(solution)/shard_map/cond/branch_1_fun/ppermute | solution.py:287
  37.7 1.8 %collective-permute-start.3 = (bf16[128,1536]{1,0:T(8,128)(2,1)S(1)}, bf16[128,1536]{1,0:T(8,128)(2,1)S(1)}, u32[]{:S(2)}, u32[]{:S(2)}) collective-permute-start(bf16[128,1536]{1,0:T(8,128)(2,1)S(1)} %get-tuple-element.130), channel_id=1, source_target_pairs={{0,1},{1,0},{2,3},{3,2},{4,5},{5,4},{6,7},{7,6},{8,9},{9,8},{10,11... | collective-permute-start | bytes 1179656 | tf_op jit(solution)/shard_map/cond/branch_1_fun/ppermute | solution.py:287
  42.3 10.0 %collective-permute-start.19 = (bf16[2,768,128]{2,1,0:T(8,128)(2,1)}, bf16[2,768,128]{2,1,0:T(8,128)(2,1)}, u32[]{:S(2)}, u32[]{:S(2)}) collective-permute-start(bf16[2,768,128]{2,1,0:T(8,128)(2,1)} %collective-permute-done.15.r_5_), channel_id=1, source_target_pairs={{0,16},{16,0},{1,17},{17,1},{2,18},{18,2},{3,19},{19,3},{4,20},{20... | collective-permute-start | bytes 1179656 | tf_op jit(solution)/shard_map/ppermute | solution.py:371
  43.8 10.6 %collective-permute-start.20 = (bf16[1,768,128]{2,1,0:T(8,128)(2,1)S(1)}, bf16[1,768,128]{2,1,0:T(8,128)(2,1)}, u32[]{:S(2)}, u32[]{:S(2)}) collective-permute-start(bf16[1,768,128]{2,1,0:T(8,128)(2,1)S(1)} %get-tuple-element.238), channel_id=1, source_target_pairs={{0,6},{2,4},{4,2},{6,0},{1,7},{3,5},{5,3},{7,1},{8,14},{10,12},{12... | collective-permute-start | bytes 589832 | tf_op jit(solution)/shard_map/ppermute | solution.py:251
  45.4 26.9 %collective-permute-start.21 = (bf16[1,1536,128]{2,1,0:T(8,128)(2,1)}, bf16[1,1536,128]{2,1,0:T(8,128)(2,1)}, u32[]{:S(2)}, u32[]{:S(2)}) collective-permute-start(bf16[1,1536,128]{2,1,0:T(8,128)(2,1)} %down.1), channel_id=1, source_target_pairs={{0,2},{2,0},{4,6},{6,4},{1,3},{3,1},{5,7},{7,5},{8,10},{10,8},{12,... | collective-permute-start | bytes 1179656 | tf_op jit(solution)/shard_map/ppermute | solution.py:251
  45.4 26.8 %collective-permute-start.22 = (bf16[1,1536,128]{2,1,0:T(8,128)(2,1)}, bf16[1,1536,128]{2,1,0:T(8,128)(2,1)}, u32[]{:S(2)}, u32[]{:S(2)}) collective-permute-start(bf16[1,1536,128]{2,1,0:T(8,128)(2,1)} %down.1), channel_id=1, source_target_pairs={{0,4},{2,6},{4,0},{6,2},{1,5},{3,7},{5,1},{7,3},{8,12},{10,14},{12... | collective-permute-start | bytes 1179656 | tf_op jit(solution)/shard_map/ppermute | solution.py:251
  54.5 1.6 %collective-permute-start.4 = (f32[128,512]{1,0:T(8,128)S(1)}, f32[128,512]{1,0:T(8,128)S(1)}, u32[]{:S(2)}, u32[]{:S(2)}) collective-permute-start(f32[128,512]{1,0:T(8,128)S(1)} %get-tuple-element.151), channel_id=1, source_target_pairs={{0,1},{1,0},{2,3},{3,2},{4,5},{5,4},{6,7},{7,6},{8,9},{9,8},{10,11... | collective-permute-start | bytes 786440 | tf_op jit(solution)/shard_map/cond/branch_1_fun/ppermute | solution.py:323
  56.8 5.6 %collective-permute-start.5 = (bf16[128,512]{1,0:T(8,128)(2,1)S(1)}, bf16[128,512]{1,0:T(8,128)(2,1)}, u32[]{:S(2)}, u32[]{:S(2)}) collective-permute-start(bf16[128,512]{1,0:T(8,128)(2,1)S(1)} %get-tuple-element.262), channel_id=1, source_target_pairs={{0,8},{8,0},{1,9},{9,1},{2,10},{10,2},{3,11},{11,3},{4,12},{12,4},... | collective-permute-start | bytes 393224 | tf_op jit(solution)/shard_map/cond/branch_1_fun/ppermute | solution.py:324
  58.3 9.6 %collective-permute-start.7 = (bf16[1,768,128]{2,1,0:T(8,128)(2,1)}, bf16[1,768,128]{2,1,0:T(8,128)(2,1)}, u32[]{:S(2)}, u32[]{:S(2)}) collective-permute-start(bf16[1,768,128]{2,1,0:T(8,128)(2,1)} %get-tuple-element.156), channel_id=1, source_target_pairs={{0,16},{16,0},{1,17},{17,1},{2,18},{18,2},{3,19},{19,3},{4,20},{20... | collective-permute-start | bytes 589832 | tf_op jit(solution)/shard_map/cond/branch_1_fun/ppermute | solution.py:391
  67.9 30.9 %collective-permute-start.23 = (bf16[1536,128]{1,0:T(8,128)(2,1)}, bf16[1536,128]{1,0:T(8,128)(2,1)S(1)}, u32[]{:S(2)}, u32[]{:S(2)}) collective-permute-start(bf16[1536,128]{1,0:T(8,128)(2,1)} %get-tuple-element.242), channel_id=1, source_target_pairs={{0,6},{2,4},{4,2},{6,0},{1,7},{3,5},{5,3},{7,1},{8,14},{10,12},{12... | collective-permute-start | bytes 1179656 | tf_op jit(solution)/shard_map/ppermute | solution.py:251
  69.3 35.3 %collective-permute-start.24 = (bf16[1536,128]{1,0:T(8,128)(2,1)}, bf16[1536,128]{1,0:T(8,128)(2,1)}, u32[]{:S(2)}, u32[]{:S(2)}) collective-permute-start(bf16[1536,128]{1,0:T(8,128)(2,1)} %get-tuple-element.241), channel_id=1, source_target_pairs={{0,4},{2,6},{4,0},{6,2},{1,5},{3,7},{5,1},{7,3},{8,12},{10,14},{12... | collective-permute-start | bytes 1179656 | tf_op jit(solution)/shard_map/ppermute | solution.py:251
  69.9 34.7 %collective-permute-start.25 = (bf16[1536,128]{1,0:T(8,128)(2,1)}, bf16[1536,128]{1,0:T(8,128)(2,1)}, u32[]{:S(2)}, u32[]{:S(2)}) collective-permute-start(bf16[1536,128]{1,0:T(8,128)(2,1)} %get-tuple-element.240), channel_id=1, source_target_pairs={{0,2},{2,0},{4,6},{6,4},{1,3},{3,1},{5,7},{7,5},{8,10},{10,8},{12,... | collective-permute-start | bytes 1179656 | tf_op jit(solution)/shard_map/ppermute | solution.py:251
  75.4 1.4 %collective-permute-start.8 = (f32[128,256]{1,0:T(8,128)S(1)}, f32[128,256]{1,0:T(8,128)S(1)}, u32[]{:S(2)}, u32[]{:S(2)}) collective-permute-start(f32[128,256]{1,0:T(8,128)S(1)} %get-tuple-element.175), channel_id=1, source_target_pairs={{0,1},{1,0},{2,3},{3,2},{4,5},{5,4},{6,7},{7,6},{8,9},{9,8},{10,11... | collective-permute-start | bytes 393224 | tf_op jit(solution)/shard_map/cond/branch_1_fun/ppermute | solution.py:323
  76.8 4.3 %collective-permute-start.9 = (bf16[128,256]{1,0:T(8,128)(2,1)S(1)}, bf16[128,256]{1,0:T(8,128)(2,1)S(1)}, u32[]{:S(2)}, u32[]{:S(2)}) collective-permute-start(bf16[128,256]{1,0:T(8,128)(2,1)S(1)} %get-tuple-element.264), channel_id=1, source_target_pairs={{0,8},{8,0},{1,9},{9,1},{2,10},{10,2},{3,11},{11,3},{4,12},{12,4},... | collective-permute-start | bytes 196616 | tf_op jit(solution)/shard_map/cond/branch_1_fun/ppermute | solution.py:324
  87.2 1.7 %collective-permute-start.12 = (bf16[64,1536]{1,0:T(8,128)(2,1)S(1)}, bf16[64,1536]{1,0:T(8,128)(2,1)S(1)}, u32[]{:S(2)}, u32[]{:S(2)}) collective-permute-start(bf16[64,1536]{1,0:T(8,128)(2,1)S(1)} %get-tuple-element.186), channel_id=1, source_target_pairs={{0,1},{1,0},{2,3},{3,2},{4,5},{5,4},{6,7},{7,6},{8,9},{9,8},{10,11... | collective-permute-start | bytes 589832 | tf_op jit(solution)/shard_map/cond/branch_1_fun/ppermute | solution.py:451
  87.4 7.7 %collective-permute-start.11 = (bf16[64,1536]{1,0:T(8,128)(2,1)S(1)}, bf16[64,1536]{1,0:T(8,128)(2,1)S(1)}, u32[]{:S(2)}, u32[]{:S(2)}) collective-permute-start(bf16[64,1536]{1,0:T(8,128)(2,1)S(1)} %get-tuple-element.185), channel_id=1, source_target_pairs={{0,8},{8,0},{1,9},{9,1},{2,10},{10,2},{3,11},{11,3},{4,12},{12,4},... | collective-permute-start | bytes 589832 | tf_op jit(solution)/shard_map/cond/branch_1_fun/ppermute | solution.py:450
  88.9 9.3 %collective-permute-start.13 = (bf16[64,1536]{1,0:T(8,128)(2,1)S(1)}, bf16[64,1536]{1,0:T(8,128)(2,1)S(1)}, u32[]{:S(2)}, u32[]{:S(2)}) collective-permute-start(bf16[64,1536]{1,0:T(8,128)(2,1)S(1)} %get-tuple-element.188), channel_id=1, source_target_pairs={{0,9},{1,8},{8,1},{9,0},{2,11},{3,10},{10,3},{11,2},{4,13},{5,12},... | collective-permute-start | bytes 589832 | tf_op jit(solution)/shard_map/cond/branch_1_fun/ppermute | solution.py:452
  (10 other events, 101.2 us)

commit v8 on v7

--- a/solution.py
+++ b/solution.py
@@ -403,7 +403,7 @@
             lambda *r: down_products(n, *r),
             grid=(steps,),
             out_shape=[
-                jax.ShapeDtypeStruct((quarter, ff), F32 if k == 0 else BF) for k in range(n)
+                jax.ShapeDtypeStruct((quarter, ff), BF) for k in range(n)
             ],
             in_specs=[
                 SMEM,
@@ -469,7 +469,7 @@
         return back.transpose(1, 0, 2).reshape(own, width)
 
     grad_tokens = region(token_gradient, *pieces)
-    grad_down = after(pieces[0], grad_tokens)
+    grad_down = after(pieces[0], grad_tokens).astype(F32)
     for share in shares:
         grad_down = grad_down + share.astype(F32)
     return (grad_tokens, grad_down[None])

time: 107 us -> 107 us (level)
  no operation moved by 1% of the time
where the time goes in v8:
time: 107 us
  waiting for transfers between devices  48.4 us (45%)
  starting transfers between devices  31.8 us (30%)
  Pallas kernels  20 us (19%)
  other arithmetic  4.26 us (4%)
  local copies, waits for them, and re-layouts  1.2 us (1%)
    ppermute x4, waiting for transfers between devices, swap_columns(): return [kept, pp(sent, axis, SWAP)]  20.3 us
    ppermute x10, starting transfers between devices, partner(): return pp(block, 'expert', [(i, i ^ k) for i in range(n)])  17.9 us
    pallas_call x13, Pallas kernels, call(): pl.pallas_call(body, out_shape=outs, in_specs=specs, out_specs=jax.tree.m...  17.4 us
    ppermute x10, waiting for transfers between devices, partner(): return pp(block, 'expert', [(i, i ^ k) for i in range(n)])  8.6 us
    ppermute x2, waiting for transfers between devices, reduce_rows(): return [total, pp(total.astype(BF), 'fsdp', SWAP)]  5.41 us
    ppermute x1, waiting for transfers between devices, token_gradient(): across = pp(back[1], 'fsdp', SWAP)  5.12 us
    ppermute x4, starting transfers between devices, swap_columns(): return [kept, pp(sent, axis, SWAP)]  3.25 us
    ppermute x1, waiting for transfers between devices, token_gradient(): pp(after(back[3], beside), ('fsdp', 'dp'), [(i, 3 - i) for i in range(4)])  3.08 us
  transfers between devices with their start and end apart: 26, of which 15 were waited for; matrix products, arithmetic and copies ran while one was open for 3% of the time, Pallas kernels for 18%

profile of v8, /device:TPU:0, one launch (start us, length us, event | category | flops | bytes accessed | tf_op | source)
XLA Modules:
  0.0 106.7 jit_solution(17892283728593169563)
XLA Ops:
  1.9 5.1 %collective-permute-start.14 = (bf16[2,768,128]{2,1,0:T(8,128)(2,1)S(1)}, bf16[2,768,128]{2,1,0:T(8,128)(2,1)S(1)}, u32[]{:S(2)}, u32[]{:S(2)}) collective-permute-start(bf16[2,768,128]{2,1,0:T(8,128)(2,1)S(1)} %get-tuple-element.225), channel_id=1, source_target_pairs={{0,6},{2,4},{4,2},{6,0},{1,7},{3,5},{5,3},{7,1},{8,14},{10,12},{12... | collective-permute-start | bytes 1179656 | tf_op jit(solution)/shard_map/ppermute | solution.py:251
  7.1 14.2 %conditional.5 = (bf16[256,1536]{1,0:T(8,128)(2,1)S(1)}, s32[256,2]{1,0:T(8,128)S(1)}, bf16[128,128]{1,0:T(8,128)(2,1)}) conditional(s32[]{:T(128)} %convert_element_type.52, () %tuple.59, (s32[]{:T(128)}, s32[]{:T(128)}, s32[64,2]{0,1:T(2,128)S(1)}, f32[64,2]{0,1:T(2,128)S(1)}, bf16[64,6144]{1,0:T(8,128)(2,1)S(1)}) %tuple.102), branch_computations={%region_0.0_spmd, %region_1.0_spmd} | conditional | flops 1576064 | bytes 6739050 | solution.py:255
  9.1 9.4 %collective-permute-done.r_2_ = bf16[64,3200]{1,0:T(8,128)(2,1)S(1)} collective-permute-done((bf16[64,3200]{1,0:T(8,128)(2,1)S(1)}, bf16[64,3200]{1,0:T(8,128)(2,1)S(1)}, u32[]{:S(2)}, u32[]{:S(2)}) %collective-permute-start) | collective-permute-done | bytes 409632 | tf_op jit(solution)/shard_map/cond/branch_1_fun/ppermute | solution.py:287
  21.3 4.0 %collective-permute-start.15 = (bf16[2,768,128]{2,1,0:T(8,128)(2,1)S(1)}, bf16[2,768,128]{2,1,0:T(8,128)(2,1)}, u32[]{:S(2)}, u32[]{:S(2)}) collective-permute-start(bf16[2,768,128]{2,1,0:T(8,128)(2,1)S(1)} %get-tuple-element.225), channel_id=1, source_target_pairs={{0,4},{2,6},{4,0},{6,2},{1,5},{3,7},{5,1},{7,3},{8,12},{10,14},{12... | collective-permute-start | bytes 1179656 | tf_op jit(solution)/shard_map/ppermute | solution.py:251
  26.8 12.7 %conditional.6 = (bf16[256,1536]{1,0:T(8,128)(2,1)S(1)}) conditional(s32[]{:T(128)} %convert_element_type.53, () %tuple.64, (s32[]{:T(128)}, s32[]{:T(128)}, bf16[64,6144]{1,0:T(8,128)(2,1)}) %tuple.65), branch_computations={%region_2.0_spmd, %region_3.0_spmd} | conditional | flops 1572864 | bytes 4718680 | solution.py:255
  29.6 8.0 %collective-permute-done.2.r_2_ = bf16[64,3072]{1,0:T(8,128)(2,1)S(1)} collective-permute-done((bf16[64,3072]{1,0:T(8,128)(2,1)S(1)}, bf16[64,3072]{1,0:T(8,128)(2,1)S(1)}, u32[]{:S(2)}, u32[]{:S(2)}) %collective-permute-start.2) | collective-permute-done | bytes 393248 | tf_op jit(solution)/shard_map/cond/branch_1_fun/ppermute | solution.py:287
  37.8 1.7 %collective-permute-done.3 = bf16[128,1536]{1,0:T(8,128)(2,1)S(1)} collective-permute-done((bf16[128,1536]{1,0:T(8,128)(2,1)S(1)}, bf16[128,1536]{1,0:T(8,128)(2,1)S(1)}, u32[]{:S(2)}, u32[]{:S(2)}) %collective-permute-start.3) | collective-permute-done | bytes 393248 | tf_op jit(solution)/shard_map/cond/branch_1_fun/ppermute | solution.py:287
  39.5 2.7 %collective-permute-done.15.r_5_ = bf16[2,768,128]{2,1,0:T(8,128)(2,1)} collective-permute-done((bf16[2,768,128]{2,1,0:T(8,128)(2,1)S(1)}, bf16[2,768,128]{2,1,0:T(8,128)(2,1)}, u32[]{:S(2)}, u32[]{:S(2)}) %collective-permute-start.15) | collective-permute-done | bytes 393248 | tf_op jit(solution)/shard_map/ppermute | solution.py:251
  45.4 2.9 %collective-permute-start.22 = (bf16[1,1536,128]{2,1,0:T(8,128)(2,1)}, bf16[1,1536,128]{2,1,0:T(8,128)(2,1)}, u32[]{:S(2)}, u32[]{:S(2)}) collective-permute-start(bf16[1,1536,128]{2,1,0:T(8,128)(2,1)} %down.1), channel_id=1, source_target_pairs={{0,4},{2,6},{4,0},{6,2},{1,5},{3,7},{5,1},{7,3},{8,12},{10,14},{12... | collective-permute-start | bytes 1179656 | tf_op jit(solution)/shard_map/ppermute | solution.py:251
  48.4 3.3 %conditional.7 = (f32[128,512]{1,0:T(8,128)S(1)}, f32[128,512]{1,0:T(8,128)S(1)}, bf16[1536,256]{1,0:T(8,128)(2,1)S(1)}) conditional(s32[]{:T(128)} %convert_element_type.54, () %tuple.68, (s32[]{:T(128)}, s32[]{:T(128)}, s32[]{:T(128)}, s32[]{:T(128)}, s32[256,2]{1,0:T(8,128)S(1)}, /*index=5*/bf16[256,1536]{1,0:T(8,128)(2,1)S(1)}, ...), branch_computations={%region_4.0_spmd, %region_5.0_spmd} | conditional | flops 12 | bytes 1310754 | solution.py:255
  48.4 3.0 %branch_1_fun.16 = (f32[128,512]{1,0:T(8,128)S(1)}, f32[128,512]{1,0:T(8,128)S(1)}) custom-call(s32[4]{0:T(128)S(1)} %pad_add_fusion.r_0_, s32[256,2]{1,0:T(8,128)S(1)} %get-tuple-element.135.r_1_, bf16[256,1536]{1,0:T(8,128)(2,1)S(1)} %get-tuple-element.136.r_2_, bf16[1,1536,128]{2,1,0:T(8,128)(2,1)S(1)} %get-tuple-element.137.r_3_, ...), custom_call_target="tpu_custom_call" | custom-call | tf_op jit(solution)/shard_map/cond/branch_1_fun/pallas_call | solution.py:19
  52.3 2.2 %shard_map.91 = (f32[128,512]{1,0:T(8,128)S(1)}, f32[128,512]{1,0:T(8,128)S(1)}) custom-call(s32[2]{0:T(128)S(1)} %pad_add_fusion.2.r_0_, s32[256,2]{1,0:T(8,128)S(1)} %get-tuple-element.222.r_1_, bf16[256,1536]{1,0:T(8,128)(2,1)S(1)} %get-tuple-element.223.r_2_, f32[128,512]{1,0:T(8,128)S(1)} %get-tuple-element.230.r_3_, ...), custom_call_target="tpu_custom_call" | custom-call | tf_op jit(solution)/shard_map/pallas_call | solution.py:19
  54.5 13.1 %conditional.8 = (bf16[1536,128]{1,0:T(8,128)(2,1)S(1)}, bf16[1536,128]{1,0:T(8,128)(2,1)}, bf16[1536,128]{1,0:T(8,128)(2,1)}, bf16[1536,128]{1,0:T(8,128)(2,1)}...) conditional(s32[]{:T(128)} %convert_element_type.51, () %tuple.57, ...), branch_computations={%region_6.0_spmd, %region_7.0_spmd} | conditional | flops 131072 | bytes 3539160 | solution.py:255
  59.8 2.6 %collective-permute-done.5.refs_1_ = bf16[128,512]{1,0:T(8,128)(2,1)} collective-permute-done((bf16[128,512]{1,0:T(8,128)(2,1)S(1)}, bf16[128,512]{1,0:T(8,128)(2,1)}, u32[]{:S(2)}, u32[]{:S(2)}) %collective-permute-start.5) | collective-permute-done | bytes 131104 | tf_op jit(solution)/shard_map/cond/branch_1_fun/ppermute | solution.py:324
  65.0 2.6 %branch_1_fun.19 = (bf16[1536,128]{1,0:T(8,128)(2,1)S(1)}, bf16[1536,128]{1,0:T(8,128)(2,1)}, bf16[1536,128]{1,0:T(8,128)(2,1)}, bf16[1536,128]{1,0:T(8,128)(2,1)}) custom-call(s32[4]{0:T(128)S(1)} %get-tuple-element.146.r_0_, s32[256,2]{1,0:T(8,128)S(1)} %get-tuple-element.147.r_1_, bf16[1536,256]{1,0:T(8,128)(2,1)S(1)} %get-tuple-element.148.r_2_, ...), custom_call_target="tpu_custom_call" | custom-call | tf_op jit(solution)/shard_map/cond/branch_1_fun/pallas_call | solution.py:402
  69.6 2.4 %collective-permute-start.25 = (bf16[1536,128]{1,0:T(8,128)(2,1)}, bf16[1536,128]{1,0:T(8,128)(2,1)}, u32[]{:S(2)}, u32[]{:S(2)}) collective-permute-start(bf16[1536,128]{1,0:T(8,128)(2,1)} %get-tuple-element.240), channel_id=1, source_target_pairs={{0,2},{2,0},{4,6},{6,4},{1,3},{3,1},{5,7},{7,5},{8,10},{10,8},{12,... | collective-permute-start | bytes 1179656 | tf_op jit(solution)/shard_map/ppermute | solution.py:251
  72.0 26.5 %conditional.9 = (bf16[64,6144]{1,0:T(8,128)(2,1)S(1)}) conditional(s32[]{:T(128)} %convert_element_type.55, () %tuple.75, (s32[]{:T(128)}, s32[]{:T(128)}, s32[]{:T(128)}, s32[]{:T(128)}, s32[]{:T(128)}, /*index=5*/s32[]{:T(128)}, s32[]{:T(128)}, s32[256,2]{1,0:T(8,128)S(1)}, bf16[256,1536]{1,0:T(8,128)(2,1)S(1)}, bf16[1,1536,128]{2,1,0:T(8,128)(2,1)}, ...), branch_computations={%region_8.0_spmd, %region_9.0_spmd} | conditional | flops 65553 | bytes 4129188 | solution.py:255
  72.1 3.0 %branch_1_fun.20 = (f32[128,256]{1,0:T(8,128)S(1)}, f32[128,256]{1,0:T(8,128)S(1)}) custom-call(s32[5]{0:T(128)S(1)} %stack.76.r_0_, s32[256,2]{1,0:T(8,128)S(1)} %get-tuple-element.164.r_1_, bf16[256,1536]{1,0:T(8,128)(2,1)S(1)} %get-tuple-element.168.r_2_, bf16[1,1536,128]{2,1,0:T(8,128)(2,1)} %get-tuple-element.169.r_3_, ...), custom_call_target="tpu_custom_call" | custom-call | tf_op jit(solution)/shard_map/cond/branch_1_fun/pallas_call | solution.py:19
  78.1 2.8 %collective-permute-done.9.r_4_ = bf16[128,256]{1,0:T(8,128)(2,1)S(1)} collective-permute-done((bf16[128,256]{1,0:T(8,128)(2,1)S(1)}, bf16[128,256]{1,0:T(8,128)(2,1)S(1)}, u32[]{:S(2)}, u32[]{:S(2)}) %collective-permute-start.9) | collective-permute-done | bytes 65568 | tf_op jit(solution)/shard_map/cond/branch_1_fun/ppermute | solution.py:324
  83.5 3.4 %branch_1_fun.22 = (bf16[64,1536]{1,0:T(8,128)(2,1)S(1)}, bf16[64,1536]{1,0:T(8,128)(2,1)S(1)}, bf16[64,1536]{1,0:T(8,128)(2,1)S(1)}, bf16[64,1536]{1,0:T(8,128)(2,1)S(1)}) custom-call(s32[5]{0:T(128)S(1)} %stack.72.r_0_, s32[256,2]{1,0:T(8,128)S(1)} %get-tuple-element.164.r_1_, bf16[128,512]{1,0:T(8,128)(2,1)S(1)} %branch_1_fun.21.r_2_, ...), custom_call_target="tpu_custom_call" | custom-call | tf_op jit(solution)/shard_map/cond/branch_1_fun/pallas_call | solution.py:19
  89.7 5.1 %collective-permute-done.11.refs_1_ = bf16[64,1536]{1,0:T(8,128)(2,1)S(1)} collective-permute-done((bf16[64,1536]{1,0:T(8,128)(2,1)S(1)}, bf16[64,1536]{1,0:T(8,128)(2,1)S(1)}, u32[]{:S(2)}, u32[]{:S(2)}) %collective-permute-start.11) | collective-permute-done | bytes 196640 | tf_op jit(solution)/shard_map/cond/branch_1_fun/ppermute | solution.py:450
  94.8 3.1 %collective-permute-done.13.refs_3_ = bf16[64,1536]{1,0:T(8,128)(2,1)S(1)} collective-permute-done((bf16[64,1536]{1,0:T(8,128)(2,1)S(1)}, bf16[64,1536]{1,0:T(8,128)(2,1)S(1)}, u32[]{:S(2)}, u32[]{:S(2)}) %collective-permute-start.13) | collective-permute-done | bytes 196640 | tf_op jit(solution)/shard_map/cond/branch_1_fun/ppermute | solution.py:452
  98.6 5.8 %collective-permute-done.24 = bf16[1536,128]{1,0:T(8,128)(2,1)} collective-permute-done((bf16[1536,128]{1,0:T(8,128)(2,1)}, bf16[1536,128]{1,0:T(8,128)(2,1)}, u32[]{:S(2)}, u32[]{:S(2)}) %collective-permute-start.24) | collective-permute-done | bytes 393248 | tf_op jit(solution)/shard_map/ppermute | solution.py:251
  104.4 2.3 %add_bitcast_fusion = f32[1,1536,128]{2,1,0:T(8,128)} fusion(bf16[1536,128]{1,0:T(8,128)(2,1)} %collective-permute-done.25, bf16[1536,128]{1,0:T(8,128)(2,1)} %collective-permute-done.24, bf16[1536,128]{1,0:T(8,128)(2,1)} %collective-permute-done.23, bf16[1536,128]{1,0:T(8,128)(2,1)S(1)} %get-tuple-element.248), kind=kLoop, calls=%fused_computation.12 | loop fusion | flops 1376256 | bytes 2359296 | tf_op jit(solution)/shard_map/broadcast_in_dim | solution.py:475
  (85 shorter events, 33.4 us)
Async XLA Ops:
  1.9 19.4 %collective-permute-start.14 = (bf16[2,768,128]{2,1,0:T(8,128)(2,1)S(1)}, bf16[2,768,128]{2,1,0:T(8,128)(2,1)S(1)}, u32[]{:S(2)}, u32[]{:S(2)}) collective-permute-start(bf16[2,768,128]{2,1,0:T(8,128)(2,1)S(1)} %get-tuple-element.225), channel_id=1, source_target_pairs={{0,6},{2,4},{4,2},{6,0},{1,7},{3,5},{5,3},{7,1},{8,14},{10,12},{12... | collective-permute-start | bytes 1179656 | tf_op jit(solution)/shard_map/ppermute | solution.py:251
  7.0 19.8 %collective-permute-start.16 = (bf16[1,1536,128]{2,1,0:T(8,128)(2,1)S(1)}, bf16[1,1536,128]{2,1,0:T(8,128)(2,1)}, u32[]{:S(2)}, u32[]{:S(2)}) collective-permute-start(bf16[1,1536,128]{2,1,0:T(8,128)(2,1)S(1)} %copy-done), channel_id=1, source_target_pairs={{0,2},{2,0},{4,6},{6,4},{1,3},{3,1},{5,7},{7,5},{8,10},{10,8},{12,... | collective-permute-start | bytes 1179656 | tf_op jit(solution)/shard_map/ppermute | solution.py:251
  7.5 11.0 %collective-permute-start = (bf16[64,3200]{1,0:T(8,128)(2,1)S(1)}, bf16[64,3200]{1,0:T(8,128)(2,1)S(1)}, u32[]{:S(2)}, u32[]{:S(2)}) collective-permute-start(bf16[64,3200]{1,0:T(8,128)(2,1)S(1)} %get-tuple-element.121), channel_id=1, source_target_pairs={{0,8},{8,0},{1,9},{9,1},{2,10},{10,2},{3,11},{11,3},{4,12},{12,4},... | collective-permute-start | bytes 1228808 | tf_op jit(solution)/shard_map/cond/branch_1_fun/ppermute | solution.py:287
  18.6 1.8 %collective-permute-start.1 = (bf16[128,1664]{1,0:T(8,128)(2,1)S(1)}, bf16[128,1664]{1,0:T(8,128)(2,1)S(1)}, u32[]{:S(2)}, u32[]{:S(2)}) collective-permute-start(bf16[128,1664]{1,0:T(8,128)(2,1)S(1)} %get-tuple-element.123), channel_id=1, source_target_pairs={{0,1},{1,0},{2,3},{3,2},{4,5},{5,4},{6,7},{7,6},{8,9},{9,8},{10,11... | collective-permute-start | bytes 1277960 | tf_op jit(solution)/shard_map/cond/branch_1_fun/ppermute | solution.py:287
  21.3 21.0 %collective-permute-start.15 = (bf16[2,768,128]{2,1,0:T(8,128)(2,1)S(1)}, bf16[2,768,128]{2,1,0:T(8,128)(2,1)}, u32[]{:S(2)}, u32[]{:S(2)}) collective-permute-start(bf16[2,768,128]{2,1,0:T(8,128)(2,1)S(1)} %get-tuple-element.225), channel_id=1, source_target_pairs={{0,4},{2,6},{4,0},{6,2},{1,5},{3,7},{5,1},{7,3},{8,12},{10,14},{12... | collective-permute-start | bytes 1179656 | tf_op jit(solution)/shard_map/ppermute | solution.py:251
  25.3 17.0 %collective-permute-start.18 = (bf16[2,768,128]{2,1,0:T(8,128)(2,1)S(1)}, bf16[2,768,128]{2,1,0:T(8,128)(2,1)}, u32[]{:S(2)}, u32[]{:S(2)}) collective-permute-start(bf16[2,768,128]{2,1,0:T(8,128)(2,1)S(1)} %collective-permute-done.14), channel_id=1, source_target_pairs={{0,16},{16,0},{1,17},{17,1},{2,18},{18,2},{3,19},{19,3},{4,20},{20... | collective-permute-start | bytes 1179656 | tf_op jit(solution)/shard_map/ppermute | solution.py:358
  26.8 21.5 %collective-permute-start.17 = (bf16[1,1536,128]{2,1,0:T(8,128)(2,1)S(1)}, bf16[1,1536,128]{2,1,0:T(8,128)(2,1)}, u32[]{:S(2)}, u32[]{:S(2)}) collective-permute-start(bf16[1,1536,128]{2,1,0:T(8,128)(2,1)S(1)} %copy-done.1), channel_id=1, source_target_pairs={{0,2},{2,0},{4,6},{6,4},{1,3},{3,1},{5,7},{7,5},{8,10},{10,8},{12,... | collective-permute-start | bytes 1179656 | tf_op jit(solution)/shard_map/ppermute | solution.py:251
  28.0 9.6 %collective-permute-start.2 = (bf16[64,3072]{1,0:T(8,128)(2,1)S(1)}, bf16[64,3072]{1,0:T(8,128)(2,1)S(1)}, u32[]{:S(2)}, u32[]{:S(2)}) collective-permute-start(bf16[64,3072]{1,0:T(8,128)(2,1)S(1)} %get-tuple-element.128), channel_id=1, source_target_pairs={{0,8},{8,0},{1,9},{9,1},{2,10},{10,2},{3,11},{11,3},{4,12},{12,4},... | collective-permute-start | bytes 1179656 | tf_op jit(solution)/shard_map/cond/branch_1_fun/ppermute | solution.py:287
  37.7 1.8 %collective-permute-start.3 = (bf16[128,1536]{1,0:T(8,128)(2,1)S(1)}, bf16[128,1536]{1,0:T(8,128)(2,1)S(1)}, u32[]{:S(2)}, u32[]{:S(2)}) collective-permute-start(bf16[128,1536]{1,0:T(8,128)(2,1)S(1)} %get-tuple-element.130), channel_id=1, source_target_pairs={{0,1},{1,0},{2,3},{3,2},{4,5},{5,4},{6,7},{7,6},{8,9},{9,8},{10,11... | collective-permute-start | bytes 1179656 | tf_op jit(solution)/shard_map/cond/branch_1_fun/ppermute | solution.py:287
  42.3 10.0 %collective-permute-start.19 = (bf16[2,768,128]{2,1,0:T(8,128)(2,1)}, bf16[2,768,128]{2,1,0:T(8,128)(2,1)}, u32[]{:S(2)}, u32[]{:S(2)}) collective-permute-start(bf16[2,768,128]{2,1,0:T(8,128)(2,1)} %collective-permute-done.15.r_5_), channel_id=1, source_target_pairs={{0,16},{16,0},{1,17},{17,1},{2,18},{18,2},{3,19},{19,3},{4,20},{20... | collective-permute-start | bytes 1179656 | tf_op jit(solution)/shard_map/ppermute | solution.py:371
  43.8 10.6 %collective-permute-start.20 = (bf16[1,768,128]{2,1,0:T(8,128)(2,1)S(1)}, bf16[1,768,128]{2,1,0:T(8,128)(2,1)}, u32[]{:S(2)}, u32[]{:S(2)}) collective-permute-start(bf16[1,768,128]{2,1,0:T(8,128)(2,1)S(1)} %get-tuple-element.238), channel_id=1, source_target_pairs={{0,6},{2,4},{4,2},{6,0},{1,7},{3,5},{5,3},{7,1},{8,14},{10,12},{12... | collective-permute-start | bytes 589832 | tf_op jit(solution)/shard_map/ppermute | solution.py:251
  45.4 26.6 %collective-permute-start.21 = (bf16[1,1536,128]{2,1,0:T(8,128)(2,1)}, bf16[1,1536,128]{2,1,0:T(8,128)(2,1)}, u32[]{:S(2)}, u32[]{:S(2)}) collective-permute-start(bf16[1,1536,128]{2,1,0:T(8,128)(2,1)} %down.1), channel_id=1, source_target_pairs={{0,2},{2,0},{4,6},{6,4},{1,3},{3,1},{5,7},{7,5},{8,10},{10,8},{12,... | collective-permute-start | bytes 1179656 | tf_op jit(solution)/shard_map/ppermute | solution.py:251
  45.4 26.6 %collective-permute-start.22 = (bf16[1,1536,128]{2,1,0:T(8,128)(2,1)}, bf16[1,1536,128]{2,1,0:T(8,128)(2,1)}, u32[]{:S(2)}, u32[]{:S(2)}) collective-permute-start(bf16[1,1536,128]{2,1,0:T(8,128)(2,1)} %down.1), channel_id=1, source_target_pairs={{0,4},{2,6},{4,0},{6,2},{1,5},{3,7},{5,1},{7,3},{8,12},{10,14},{12... | collective-permute-start | bytes 1179656 | tf_op jit(solution)/shard_map/ppermute | solution.py:251
  54.5 1.6 %collective-permute-start.4 = (f32[128,512]{1,0:T(8,128)S(1)}, f32[128,512]{1,0:T(8,128)S(1)}, u32[]{:S(2)}, u32[]{:S(2)}) collective-permute-start(f32[128,512]{1,0:T(8,128)S(1)} %get-tuple-element.151), channel_id=1, source_target_pairs={{0,1},{1,0},{2,3},{3,2},{4,5},{5,4},{6,7},{7,6},{8,9},{9,8},{10,11... | collective-permute-start | bytes 786440 | tf_op jit(solution)/shard_map/cond/branch_1_fun/ppermute | solution.py:323
  56.8 5.6 %collective-permute-start.5 = (bf16[128,512]{1,0:T(8,128)(2,1)S(1)}, bf16[128,512]{1,0:T(8,128)(2,1)}, u32[]{:S(2)}, u32[]{:S(2)}) collective-permute-start(bf16[128,512]{1,0:T(8,128)(2,1)S(1)} %get-tuple-element.262), channel_id=1, source_target_pairs={{0,8},{8,0},{1,9},{9,1},{2,10},{10,2},{3,11},{11,3},{4,12},{12,4},... | collective-permute-start | bytes 393224 | tf_op jit(solution)/shard_map/cond/branch_1_fun/ppermute | solution.py:324
  58.3 9.3 %collective-permute-start.7 = (bf16[1,768,128]{2,1,0:T(8,128)(2,1)}, bf16[1,768,128]{2,1,0:T(8,128)(2,1)}, u32[]{:S(2)}, u32[]{:S(2)}) collective-permute-start(bf16[1,768,128]{2,1,0:T(8,128)(2,1)} %get-tuple-element.156), channel_id=1, source_target_pairs={{0,16},{16,0},{1,17},{17,1},{2,18},{18,2},{3,19},{19,3},{4,20},{20... | collective-permute-start | bytes 589832 | tf_op jit(solution)/shard_map/cond/branch_1_fun/ppermute | solution.py:391
  67.6 30.9 %collective-permute-start.23 = (bf16[1536,128]{1,0:T(8,128)(2,1)}, bf16[1536,128]{1,0:T(8,128)(2,1)}, u32[]{:S(2)}, u32[]{:S(2)}) collective-permute-start(bf16[1536,128]{1,0:T(8,128)(2,1)} %get-tuple-element.242), channel_id=1, source_target_pairs={{0,6},{2,4},{4,2},{6,0},{1,7},{3,5},{5,3},{7,1},{8,14},{10,12},{12... | collective-permute-start | bytes 1179656 | tf_op jit(solution)/shard_map/ppermute | solution.py:251
  69.1 35.3 %collective-permute-start.24 = (bf16[1536,128]{1,0:T(8,128)(2,1)}, bf16[1536,128]{1,0:T(8,128)(2,1)}, u32[]{:S(2)}, u32[]{:S(2)}) collective-permute-start(bf16[1536,128]{1,0:T(8,128)(2,1)} %get-tuple-element.241), channel_id=1, source_target_pairs={{0,4},{2,6},{4,0},{6,2},{1,5},{3,7},{5,1},{7,3},{8,12},{10,14},{12... | collective-permute-start | bytes 1179656 | tf_op jit(solution)/shard_map/ppermute | solution.py:251
  69.6 34.7 %collective-permute-start.25 = (bf16[1536,128]{1,0:T(8,128)(2,1)}, bf16[1536,128]{1,0:T(8,128)(2,1)}, u32[]{:S(2)}, u32[]{:S(2)}) collective-permute-start(bf16[1536,128]{1,0:T(8,128)(2,1)} %get-tuple-element.240), channel_id=1, source_target_pairs={{0,2},{2,0},{4,6},{6,4},{1,3},{3,1},{5,7},{7,5},{8,10},{10,8},{12,... | collective-permute-start | bytes 1179656 | tf_op jit(solution)/shard_map/ppermute | solution.py:251
  75.1 1.4 %collective-permute-start.8 = (f32[128,256]{1,0:T(8,128)S(1)}, f32[128,256]{1,0:T(8,128)S(1)}, u32[]{:S(2)}, u32[]{:S(2)}) collective-permute-start(f32[128,256]{1,0:T(8,128)S(1)} %get-tuple-element.175), channel_id=1, source_target_pairs={{0,1},{1,0},{2,3},{3,2},{4,5},{5,4},{6,7},{7,6},{8,9},{9,8},{10,11... | collective-permute-start | bytes 393224 | tf_op jit(solution)/shard_map/cond/branch_1_fun/ppermute | solution.py:323
  76.6 4.3 %collective-permute-start.9 = (bf16[128,256]{1,0:T(8,128)(2,1)S(1)}, bf16[128,256]{1,0:T(8,128)(2,1)S(1)}, u32[]{:S(2)}, u32[]{:S(2)}) collective-permute-start(bf16[128,256]{1,0:T(8,128)(2,1)S(1)} %get-tuple-element.264), channel_id=1, source_target_pairs={{0,8},{8,0},{1,9},{9,1},{2,10},{10,2},{3,11},{11,3},{4,12},{12,4},... | collective-permute-start | bytes 196616 | tf_op jit(solution)/shard_map/cond/branch_1_fun/ppermute | solution.py:324
  86.9 1.7 %collective-permute-start.12 = (bf16[64,1536]{1,0:T(8,128)(2,1)S(1)}, bf16[64,1536]{1,0:T(8,128)(2,1)S(1)}, u32[]{:S(2)}, u32[]{:S(2)}) collective-permute-start(bf16[64,1536]{1,0:T(8,128)(2,1)S(1)} %get-tuple-element.186), channel_id=1, source_target_pairs={{0,1},{1,0},{2,3},{3,2},{4,5},{5,4},{6,7},{7,6},{8,9},{9,8},{10,11... | collective-permute-start | bytes 589832 | tf_op jit(solution)/shard_map/cond/branch_1_fun/ppermute | solution.py:451
  87.1 7.7 %collective-permute-start.11 = (bf16[64,1536]{1,0:T(8,128)(2,1)S(1)}, bf16[64,1536]{1,0:T(8,128)(2,1)S(1)}, u32[]{:S(2)}, u32[]{:S(2)}) collective-permute-start(bf16[64,1536]{1,0:T(8,128)(2,1)S(1)} %get-tuple-element.185), channel_id=1, source_target_pairs={{0,8},{8,0},{1,9},{9,1},{2,10},{10,2},{3,11},{11,3},{4,12},{12,4},... | collective-permute-start | bytes 589832 | tf_op jit(solution)/shard_map/cond/branch_1_fun/ppermute | solution.py:450
  88.6 9.3 %collective-permute-start.13 = (bf16[64,1536]{1,0:T(8,128)(2,1)S(1)}, bf16[64,1536]{1,0:T(8,128)(2,1)S(1)}, u32[]{:S(2)}, u32[]{:S(2)}) collective-permute-start(bf16[64,1536]{1,0:T(8,128)(2,1)S(1)} %get-tuple-element.188), channel_id=1, source_target_pairs={{0,9},{1,8},{8,1},{9,0},{2,11},{3,10},{10,3},{11,2},{4,13},{5,12},... | collective-permute-start | bytes 589832 | tf_op jit(solution)/shard_map/cond/branch_1_fun/ppermute | solution.py:452
  (10 other events, 100.9 us)

commit v9 on v8

--- a/solution.py
+++ b/solution.py
@@ -420,7 +420,7 @@
 
     pieces, dn_far, first = region(down_step)
     dn_slots.append(("halves", e ^ first_one, [dn[first_one], dn_far]))
-    shares = [partner(pieces[k], k) for k in range(n - 1, 0, -1)]
+    shares = [partner(pieces[k], k) for k in [*range(2, n), 1]]
 
     def token_gradient():
         second = reduce_rows(sums(cot, dn_slots, 1))

time: 107 us -> 106 us (level)
  the two profiles are of different devices: /device:TPU:0 before, /device:TPU:11 now
where the time goes in v9:
time: 106 us; the launch traced here: 105 us
  waiting for transfers between devices  50.7 us (48%)
  starting transfers between devices  28.3 us (27%)
  Pallas kernels  20 us (19%)
  other arithmetic  4.26 us (4%)
  local copies, waits for them, and re-layouts  1.19 us (1%)
    ppermute x4, waiting for transfers between devices, swap_columns(): return [kept, pp(sent, axis, SWAP)]  19.7 us
    pallas_call x13, Pallas kernels, call(): pl.pallas_call(body, out_shape=outs, in_specs=specs, out_specs=jax.tree.m...  17.4 us
    ppermute x10, starting transfers between devices, partner(): return pp(block, 'expert', [(i, i ^ k) for i in range(n)])  12.6 us
    ppermute x10, waiting for transfers between devices, partner(): return pp(block, 'expert', [(i, i ^ k) for i in range(n)])  7.13 us
    ppermute x2, waiting for transfers between devices, reduce_rows(): return [total, pp(total.astype(BF), 'fsdp', SWAP)]  7.11 us
    ppermute x4, starting transfers between devices, swap_columns(): return [kept, pp(sent, axis, SWAP)]  6.05 us
    ppermute x1, waiting for transfers between devices, token_gradient(): pp(after(back[3], beside), ('fsdp', 'dp'), [(i, 3 - i) for i in range(4)])  4.78 us
    ppermute x1, waiting for transfers between devices, token_gradient(): across = pp(back[1], 'fsdp', SWAP)  4.58 us
  transfers between devices with their start and end apart: 26, of which 17 were waited for; matrix products, arithmetic and copies ran while one was open for 3% of the time, Pallas kernels for 18%

profile of v9, /device:TPU:11, one launch (start us, length us, event | category | flops | bytes accessed | tf_op | source)
XLA Modules:
  0.0 105.4 jit_solution(12557519336359943788)
XLA Ops:
  3.3 2.2 %collective-permute-start.16 = (bf16[1,1536,128]{2,1,0:T(8,128)(2,1)S(1)}, bf16[1,1536,128]{2,1,0:T(8,128)(2,1)}, u32[]{:S(2)}, u32[]{:S(2)}) collective-permute-start(bf16[1,1536,128]{2,1,0:T(8,128)(2,1)S(1)} %copy-done), channel_id=1, source_target_pairs={{0,2},{2,0},{4,6},{6,4},{1,3},{3,1},{5,7},{7,5},{8,10},{10,8},{12,... | collective-permute-start | bytes 1179656 | tf_op jit(solution)/shard_map/ppermute | solution.py:251
  5.5 14.8 %conditional.5 = (bf16[256,1536]{1,0:T(8,128)(2,1)S(1)}, s32[256,2]{1,0:T(8,128)S(1)}, bf16[128,128]{1,0:T(8,128)(2,1)}) conditional(s32[]{:T(128)} %convert_element_type.52, () %tuple.59, (s32[]{:T(128)}, s32[]{:T(128)}, s32[64,2]{0,1:T(2,128)S(1)}, f32[64,2]{0,1:T(2,128)S(1)}, bf16[64,6144]{1,0:T(8,128)(2,1)S(1)}) %tuple.102), branch_computations={%region_0.0_spmd, %region_1.0_spmd} | conditional | flops 1576064 | bytes 6739050 | solution.py:255
  6.2 9.5 %collective-permute-done.r_2_ = bf16[64,3200]{1,0:T(8,128)(2,1)S(1)} collective-permute-done((bf16[64,3200]{1,0:T(8,128)(2,1)S(1)}, bf16[64,3200]{1,0:T(8,128)(2,1)S(1)}, u32[]{:S(2)}, u32[]{:S(2)}) %collective-permute-start) | collective-permute-done | bytes 409632 | tf_op jit(solution)/shard_map/cond/branch_1_fun/ppermute | solution.py:287
  15.8 2.2 %collective-permute-start.1 = (bf16[128,1664]{1,0:T(8,128)(2,1)S(1)}, bf16[128,1664]{1,0:T(8,128)(2,1)S(1)}, u32[]{:S(2)}, u32[]{:S(2)}) collective-permute-start(bf16[128,1664]{1,0:T(8,128)(2,1)S(1)} %get-tuple-element.123), channel_id=1, source_target_pairs={{0,1},{1,0},{2,3},{3,2},{4,5},{5,4},{6,7},{7,6},{8,9},{9,8},{10,11... | collective-permute-start | bytes 1277960 | tf_op jit(solution)/shard_map/cond/branch_1_fun/ppermute | solution.py:287
  22.6 1.6 %collective-permute-start.17 = (bf16[1,1536,128]{2,1,0:T(8,128)(2,1)S(1)}, bf16[1,1536,128]{2,1,0:T(8,128)(2,1)}, u32[]{:S(2)}, u32[]{:S(2)}) collective-permute-start(bf16[1,1536,128]{2,1,0:T(8,128)(2,1)S(1)} %copy-done.1), channel_id=1, source_target_pairs={{0,2},{2,0},{4,6},{6,4},{1,3},{3,1},{5,7},{7,5},{8,10},{10,8},{12,... | collective-permute-start | bytes 1179656 | tf_op jit(solution)/shard_map/ppermute | solution.py:251
  24.2 14.3 %conditional.6 = (bf16[256,1536]{1,0:T(8,128)(2,1)S(1)}) conditional(s32[]{:T(128)} %convert_element_type.53, () %tuple.64, (s32[]{:T(128)}, s32[]{:T(128)}, bf16[64,6144]{1,0:T(8,128)(2,1)}) %tuple.65), branch_computations={%region_2.0_spmd, %region_3.0_spmd} | conditional | flops 1572864 | bytes 4718680 | solution.py:255
  25.7 8.2 %collective-permute-done.2.r_2_ = bf16[64,3072]{1,0:T(8,128)(2,1)S(1)} collective-permute-done((bf16[64,3072]{1,0:T(8,128)(2,1)S(1)}, bf16[64,3072]{1,0:T(8,128)(2,1)S(1)}, u32[]{:S(2)}, u32[]{:S(2)}) %collective-permute-start.2) | collective-permute-done | bytes 393248 | tf_op jit(solution)/shard_map/cond/branch_1_fun/ppermute | solution.py:287
  34.0 3.2 %collective-permute-start.3 = (bf16[128,1536]{1,0:T(8,128)(2,1)S(1)}, bf16[128,1536]{1,0:T(8,128)(2,1)S(1)}, u32[]{:S(2)}, u32[]{:S(2)}) collective-permute-start(bf16[128,1536]{1,0:T(8,128)(2,1)S(1)} %get-tuple-element.130), channel_id=1, source_target_pairs={{0,1},{1,0},{2,3},{3,2},{4,5},{5,4},{6,7},{7,6},{8,9},{9,8},{10,11... | collective-permute-start | bytes 1179656 | tf_op jit(solution)/shard_map/cond/branch_1_fun/ppermute | solution.py:287
  39.5 2.9 %collective-permute-start.21 = (bf16[1,1536,128]{2,1,0:T(8,128)(2,1)}, bf16[1,1536,128]{2,1,0:T(8,128)(2,1)}, u32[]{:S(2)}, u32[]{:S(2)}) collective-permute-start(bf16[1,1536,128]{2,1,0:T(8,128)(2,1)} %down.1), channel_id=1, source_target_pairs={{0,2},{2,0},{4,6},{6,4},{1,3},{3,1},{5,7},{7,5},{8,10},{10,8},{12,... | collective-permute-start | bytes 1179656 | tf_op jit(solution)/shard_map/ppermute | solution.py:251
  43.4 3.3 %conditional.7 = (f32[128,512]{1,0:T(8,128)S(1)}, f32[128,512]{1,0:T(8,128)S(1)}, bf16[1536,256]{1,0:T(8,128)(2,1)S(1)}) conditional(s32[]{:T(128)} %convert_element_type.54, () %tuple.68, (s32[]{:T(128)}, s32[]{:T(128)}, s32[]{:T(128)}, s32[]{:T(128)}, s32[256,2]{1,0:T(8,128)S(1)}, /*index=5*/bf16[256,1536]{1,0:T(8,128)(2,1)S(1)}, ...), branch_computations={%region_4.0_spmd, %region_5.0_spmd} | conditional | flops 12 | bytes 1310754 | solution.py:255
  43.5 3.0 %branch_1_fun.16 = (f32[128,512]{1,0:T(8,128)S(1)}, f32[128,512]{1,0:T(8,128)S(1)}) custom-call(s32[4]{0:T(128)S(1)} %pad_add_fusion.r_0_, s32[256,2]{1,0:T(8,128)S(1)} %get-tuple-element.135.r_1_, bf16[256,1536]{1,0:T(8,128)(2,1)S(1)} %get-tuple-element.136.r_2_, bf16[1,1536,128]{2,1,0:T(8,128)(2,1)S(1)} %get-tuple-element.137.r_3_, ...), custom_call_target="tpu_custom_call" | custom-call | tf_op jit(solution)/shard_map/cond/branch_1_fun/pallas_call | solution.py:19
  46.7 2.6 %collective-permute-done.19.r_6_ = bf16[2,768,128]{2,1,0:T(8,128)(2,1)} collective-permute-done((bf16[2,768,128]{2,1,0:T(8,128)(2,1)}, bf16[2,768,128]{2,1,0:T(8,128)(2,1)}, u32[]{:S(2)}, u32[]{:S(2)}) %collective-permute-start.19) | collective-permute-done | bytes 393248 | tf_op jit(solution)/shard_map/ppermute | solution.py:371
  49.3 2.2 %shard_map.91 = (f32[128,512]{1,0:T(8,128)S(1)}, f32[128,512]{1,0:T(8,128)S(1)}) custom-call(s32[2]{0:T(128)S(1)} %pad_add_fusion.2.r_0_, s32[256,2]{1,0:T(8,128)S(1)} %get-tuple-element.222.r_1_, bf16[256,1536]{1,0:T(8,128)(2,1)S(1)} %get-tuple-element.223.r_2_, f32[128,512]{1,0:T(8,128)S(1)} %get-tuple-element.230.r_3_, ...), custom_call_target="tpu_custom_call" | custom-call | tf_op jit(solution)/shard_map/pallas_call | solution.py:19
  51.5 14.0 %conditional.8 = (bf16[1536,128]{1,0:T(8,128)(2,1)S(1)}, bf16[1536,128]{1,0:T(8,128)(2,1)}, bf16[1536,128]{1,0:T(8,128)(2,1)}, bf16[1536,128]{1,0:T(8,128)(2,1)}...) conditional(s32[]{:T(128)} %convert_element_type.51, () %tuple.57, ...), branch_computations={%region_6.0_spmd, %region_7.0_spmd} | conditional | flops 131072 | bytes 3539160 | solution.py:255
  55.6 3.9 %collective-permute-done.5.refs_1_ = bf16[128,512]{1,0:T(8,128)(2,1)} collective-permute-done((bf16[128,512]{1,0:T(8,128)(2,1)S(1)}, bf16[128,512]{1,0:T(8,128)(2,1)}, u32[]{:S(2)}, u32[]{:S(2)}) %collective-permute-start.5) | collective-permute-done | bytes 131104 | tf_op jit(solution)/shard_map/cond/branch_1_fun/ppermute | solution.py:324
  62.8 2.6 %branch_1_fun.19 = (bf16[1536,128]{1,0:T(8,128)(2,1)S(1)}, bf16[1536,128]{1,0:T(8,128)(2,1)}, bf16[1536,128]{1,0:T(8,128)(2,1)}, bf16[1536,128]{1,0:T(8,128)(2,1)}) custom-call(s32[4]{0:T(128)S(1)} %get-tuple-element.146.r_0_, s32[256,2]{1,0:T(8,128)S(1)} %get-tuple-element.147.r_1_, bf16[1536,256]{1,0:T(8,128)(2,1)S(1)} %get-tuple-element.148.r_2_, ...), custom_call_target="tpu_custom_call" | custom-call | tf_op jit(solution)/shard_map/cond/branch_1_fun/pallas_call | solution.py:402
  69.0 28.0 %conditional.9 = (bf16[64,6144]{1,0:T(8,128)(2,1)S(1)}) conditional(s32[]{:T(128)} %convert_element_type.55, () %tuple.75, (s32[]{:T(128)}, s32[]{:T(128)}, s32[]{:T(128)}, s32[]{:T(128)}, s32[]{:T(128)}, /*index=5*/s32[]{:T(128)}, s32[]{:T(128)}, s32[256,2]{1,0:T(8,128)S(1)}, bf16[256,1536]{1,0:T(8,128)(2,1)S(1)}, bf16[1,1536,128]{2,1,0:T(8,128)(2,1)}, ...), branch_computations={%region_8.0_spmd, %region_9.0_spmd} | conditional | flops 65553 | bytes 4129188 | solution.py:255
  69.1 3.0 %branch_1_fun.20 = (f32[128,256]{1,0:T(8,128)S(1)}, f32[128,256]{1,0:T(8,128)S(1)}) custom-call(s32[5]{0:T(128)S(1)} %stack.76.r_0_, s32[256,2]{1,0:T(8,128)S(1)} %get-tuple-element.164.r_1_, bf16[256,1536]{1,0:T(8,128)(2,1)S(1)} %get-tuple-element.168.r_2_, bf16[1,1536,128]{2,1,0:T(8,128)(2,1)} %get-tuple-element.169.r_3_, ...), custom_call_target="tpu_custom_call" | custom-call | tf_op jit(solution)/shard_map/cond/branch_1_fun/pallas_call | solution.py:19
  74.7 3.3 %collective-permute-done.9.r_4_ = bf16[128,256]{1,0:T(8,128)(2,1)S(1)} collective-permute-done((bf16[128,256]{1,0:T(8,128)(2,1)S(1)}, bf16[128,256]{1,0:T(8,128)(2,1)S(1)}, u32[]{:S(2)}, u32[]{:S(2)}) %collective-permute-start.9) | collective-permute-done | bytes 65568 | tf_op jit(solution)/shard_map/cond/branch_1_fun/ppermute | solution.py:324
  81.3 3.4 %branch_1_fun.22 = (bf16[64,1536]{1,0:T(8,128)(2,1)S(1)}, bf16[64,1536]{1,0:T(8,128)(2,1)S(1)}, bf16[64,1536]{1,0:T(8,128)(2,1)S(1)}, bf16[64,1536]{1,0:T(8,128)(2,1)S(1)}) custom-call(s32[5]{0:T(128)S(1)} %stack.72.r_0_, s32[256,2]{1,0:T(8,128)S(1)} %get-tuple-element.164.r_1_, bf16[128,512]{1,0:T(8,128)(2,1)S(1)} %branch_1_fun.21.r_2_, ...), custom_call_target="tpu_custom_call" | custom-call | tf_op jit(solution)/shard_map/cond/branch_1_fun/pallas_call | solution.py:19
  87.0 4.6 %collective-permute-done.11.refs_1_ = bf16[64,1536]{1,0:T(8,128)(2,1)S(1)} collective-permute-done((bf16[64,1536]{1,0:T(8,128)(2,1)S(1)}, bf16[64,1536]{1,0:T(8,128)(2,1)S(1)}, u32[]{:S(2)}, u32[]{:S(2)}) %collective-permute-start.11) | collective-permute-done | bytes 196640 | tf_op jit(solution)/shard_map/cond/branch_1_fun/ppermute | solution.py:450
  91.6 4.8 %collective-permute-done.13.refs_3_ = bf16[64,1536]{1,0:T(8,128)(2,1)S(1)} collective-permute-done((bf16[64,1536]{1,0:T(8,128)(2,1)S(1)}, bf16[64,1536]{1,0:T(8,128)(2,1)S(1)}, u32[]{:S(2)}, u32[]{:S(2)}) %collective-permute-start.13) | collective-permute-done | bytes 196640 | tf_op jit(solution)/shard_map/cond/branch_1_fun/ppermute | solution.py:452
  97.0 6.0 %collective-permute-done.24 = bf16[1536,128]{1,0:T(8,128)(2,1)} collective-permute-done((bf16[1536,128]{1,0:T(8,128)(2,1)}, bf16[1536,128]{1,0:T(8,128)(2,1)}, u32[]{:S(2)}, u32[]{:S(2)}) %collective-permute-start.24) | collective-permute-done | bytes 393248 | tf_op jit(solution)/shard_map/ppermute | solution.py:251
  103.1 2.3 %add_bitcast_fusion = f32[1,1536,128]{2,1,0:T(8,128)} fusion(bf16[1536,128]{1,0:T(8,128)(2,1)} %collective-permute-done.25, bf16[1536,128]{1,0:T(8,128)(2,1)} %collective-permute-done.24, bf16[1536,128]{1,0:T(8,128)(2,1)} %collective-permute-done.23, bf16[1536,128]{1,0:T(8,128)(2,1)S(1)} %get-tuple-element.248), kind=kLoop, calls=%fused_computation.12 | loop fusion | flops 1376256 | bytes 2359296 | tf_op jit(solution)/shard_map/broadcast_in_dim | solution.py:475
  (85 shorter events, 33.2 us)
Async XLA Ops:
  1.9 18.8 %collective-permute-start.14 = (bf16[2,768,128]{2,1,0:T(8,128)(2,1)S(1)}, bf16[2,768,128]{2,1,0:T(8,128)(2,1)S(1)}, u32[]{:S(2)}, u32[]{:S(2)}) collective-permute-start(bf16[2,768,128]{2,1,0:T(8,128)(2,1)S(1)} %get-tuple-element.225), channel_id=1, source_target_pairs={{0,6},{2,4},{4,2},{6,0},{1,7},{3,5},{5,3},{7,1},{8,14},{10,12},{12... | collective-permute-start | bytes 1179656 | tf_op jit(solution)/shard_map/ppermute | solution.py:251
  3.3 19.3 %collective-permute-start.16 = (bf16[1,1536,128]{2,1,0:T(8,128)(2,1)S(1)}, bf16[1,1536,128]{2,1,0:T(8,128)(2,1)}, u32[]{:S(2)}, u32[]{:S(2)}) collective-permute-start(bf16[1,1536,128]{2,1,0:T(8,128)(2,1)S(1)} %copy-done), channel_id=1, source_target_pairs={{0,2},{2,0},{4,6},{6,4},{1,3},{3,1},{5,7},{7,5},{8,10},{10,8},{12,... | collective-permute-start | bytes 1179656 | tf_op jit(solution)/shard_map/ppermute | solution.py:251
  5.9 9.8 %collective-permute-start = (bf16[64,3200]{1,0:T(8,128)(2,1)S(1)}, bf16[64,3200]{1,0:T(8,128)(2,1)S(1)}, u32[]{:S(2)}, u32[]{:S(2)}) collective-permute-start(bf16[64,3200]{1,0:T(8,128)(2,1)S(1)} %get-tuple-element.121), channel_id=1, source_target_pairs={{0,8},{8,0},{1,9},{9,1},{2,10},{10,2},{3,11},{11,3},{4,12},{12,4},... | collective-permute-start | bytes 1228808 | tf_op jit(solution)/shard_map/cond/branch_1_fun/ppermute | solution.py:287
  15.8 3.6 %collective-permute-start.1 = (bf16[128,1664]{1,0:T(8,128)(2,1)S(1)}, bf16[128,1664]{1,0:T(8,128)(2,1)S(1)}, u32[]{:S(2)}, u32[]{:S(2)}) collective-permute-start(bf16[128,1664]{1,0:T(8,128)(2,1)S(1)} %get-tuple-element.123), channel_id=1, source_target_pairs={{0,1},{1,0},{2,3},{3,2},{4,5},{5,4},{6,7},{7,6},{8,9},{9,8},{10,11... | collective-permute-start | bytes 1277960 | tf_op jit(solution)/shard_map/cond/branch_1_fun/ppermute | solution.py:287
  20.7 17.9 %collective-permute-start.15 = (bf16[2,768,128]{2,1,0:T(8,128)(2,1)S(1)}, bf16[2,768,128]{2,1,0:T(8,128)(2,1)}, u32[]{:S(2)}, u32[]{:S(2)}) collective-permute-start(bf16[2,768,128]{2,1,0:T(8,128)(2,1)S(1)} %get-tuple-element.225), channel_id=1, source_target_pairs={{0,4},{2,6},{4,0},{6,2},{1,5},{3,7},{5,1},{7,3},{8,12},{10,14},{12... | collective-permute-start | bytes 1179656 | tf_op jit(solution)/shard_map/ppermute | solution.py:251
  20.7 17.9 %collective-permute-start.18 = (bf16[2,768,128]{2,1,0:T(8,128)(2,1)S(1)}, bf16[2,768,128]{2,1,0:T(8,128)(2,1)}, u32[]{:S(2)}, u32[]{:S(2)}) collective-permute-start(bf16[2,768,128]{2,1,0:T(8,128)(2,1)S(1)} %collective-permute-done.14), channel_id=1, source_target_pairs={{0,16},{16,0},{1,17},{17,1},{2,18},{18,2},{3,19},{19,3},{4,20},{20... | collective-permute-start | bytes 1179656 | tf_op jit(solution)/shard_map/ppermute | solution.py:358
  22.6 20.8 %collective-permute-start.17 = (bf16[1,1536,128]{2,1,0:T(8,128)(2,1)S(1)}, bf16[1,1536,128]{2,1,0:T(8,128)(2,1)}, u32[]{:S(2)}, u32[]{:S(2)}) collective-permute-start(bf16[1,1536,128]{2,1,0:T(8,128)(2,1)S(1)} %copy-done.1), channel_id=1, source_target_pairs={{0,2},{2,0},{4,6},{6,4},{1,3},{3,1},{5,7},{7,5},{8,10},{10,8},{12,... | collective-permute-start | bytes 1179656 | tf_op jit(solution)/shard_map/ppermute | solution.py:251
  25.4 8.5 %collective-permute-start.2 = (bf16[64,3072]{1,0:T(8,128)(2,1)S(1)}, bf16[64,3072]{1,0:T(8,128)(2,1)S(1)}, u32[]{:S(2)}, u32[]{:S(2)}) collective-permute-start(bf16[64,3072]{1,0:T(8,128)(2,1)S(1)} %get-tuple-element.128), channel_id=1, source_target_pairs={{0,8},{8,0},{1,9},{9,1},{2,10},{10,2},{3,11},{11,3},{4,12},{12,4},... | collective-permute-start | bytes 1179656 | tf_op jit(solution)/shard_map/cond/branch_1_fun/ppermute | solution.py:287
  34.0 4.5 %collective-permute-start.3 = (bf16[128,1536]{1,0:T(8,128)(2,1)S(1)}, bf16[128,1536]{1,0:T(8,128)(2,1)S(1)}, u32[]{:S(2)}, u32[]{:S(2)}) collective-permute-start(bf16[128,1536]{1,0:T(8,128)(2,1)S(1)} %get-tuple-element.130), channel_id=1, source_target_pairs={{0,1},{1,0},{2,3},{3,2},{4,5},{5,4},{6,7},{7,6},{8,9},{9,8},{10,11... | collective-permute-start | bytes 1179656 | tf_op jit(solution)/shard_map/cond/branch_1_fun/ppermute | solution.py:287
  38.6 10.7 %collective-permute-start.19 = (bf16[2,768,128]{2,1,0:T(8,128)(2,1)}, bf16[2,768,128]{2,1,0:T(8,128)(2,1)}, u32[]{:S(2)}, u32[]{:S(2)}) collective-permute-start(bf16[2,768,128]{2,1,0:T(8,128)(2,1)} %collective-permute-done.15.r_5_), channel_id=1, source_target_pairs={{0,16},{16,0},{1,17},{17,1},{2,18},{18,2},{3,19},{19,3},{4,20},{20... | collective-permute-start | bytes 1179656 | tf_op jit(solution)/shard_map/ppermute | solution.py:371
  39.3 12.1 %collective-permute-start.20 = (bf16[1,768,128]{2,1,0:T(8,128)(2,1)S(1)}, bf16[1,768,128]{2,1,0:T(8,128)(2,1)}, u32[]{:S(2)}, u32[]{:S(2)}) collective-permute-start(bf16[1,768,128]{2,1,0:T(8,128)(2,1)S(1)} %get-tuple-element.238), channel_id=1, source_target_pairs={{0,6},{2,4},{4,2},{6,0},{1,7},{3,5},{5,3},{7,1},{8,14},{10,12},{12... | collective-permute-start | bytes 589832 | tf_op jit(solution)/shard_map/ppermute | solution.py:251
  39.5 29.5 %collective-permute-start.21 = (bf16[1,1536,128]{2,1,0:T(8,128)(2,1)}, bf16[1,1536,128]{2,1,0:T(8,128)(2,1)}, u32[]{:S(2)}, u32[]{:S(2)}) collective-permute-start(bf16[1,1536,128]{2,1,0:T(8,128)(2,1)} %down.1), channel_id=1, source_target_pairs={{0,2},{2,0},{4,6},{6,4},{1,3},{3,1},{5,7},{7,5},{8,10},{10,8},{12,... | collective-permute-start | bytes 1179656 | tf_op jit(solution)/shard_map/ppermute | solution.py:251
  42.3 26.7 %collective-permute-start.22 = (bf16[1,1536,128]{2,1,0:T(8,128)(2,1)}, bf16[1,1536,128]{2,1,0:T(8,128)(2,1)}, u32[]{:S(2)}, u32[]{:S(2)}) collective-permute-start(bf16[1,1536,128]{2,1,0:T(8,128)(2,1)} %down.1), channel_id=1, source_target_pairs={{0,4},{2,6},{4,0},{6,2},{1,5},{3,7},{5,1},{7,3},{8,12},{10,14},{12... | collective-permute-start | bytes 1179656 | tf_op jit(solution)/shard_map/ppermute | solution.py:251
  51.5 2.4 %collective-permute-start.4 = (f32[128,512]{1,0:T(8,128)S(1)}, f32[128,512]{1,0:T(8,128)S(1)}, u32[]{:S(2)}, u32[]{:S(2)}) collective-permute-start(f32[128,512]{1,0:T(8,128)S(1)} %get-tuple-element.151), channel_id=1, source_target_pairs={{0,1},{1,0},{2,3},{3,2},{4,5},{5,4},{6,7},{7,6},{8,9},{9,8},{10,11... | collective-permute-start | bytes 786440 | tf_op jit(solution)/shard_map/cond/branch_1_fun/ppermute | solution.py:323
  54.7 4.8 %collective-permute-start.5 = (bf16[128,512]{1,0:T(8,128)(2,1)S(1)}, bf16[128,512]{1,0:T(8,128)(2,1)}, u32[]{:S(2)}, u32[]{:S(2)}) collective-permute-start(bf16[128,512]{1,0:T(8,128)(2,1)S(1)} %get-tuple-element.262), channel_id=1, source_target_pairs={{0,8},{8,0},{1,9},{9,1},{2,10},{10,2},{3,11},{11,3},{4,12},{12,4},... | collective-permute-start | bytes 393224 | tf_op jit(solution)/shard_map/cond/branch_1_fun/ppermute | solution.py:324
  54.9 10.5 %collective-permute-start.7 = (bf16[1,768,128]{2,1,0:T(8,128)(2,1)}, bf16[1,768,128]{2,1,0:T(8,128)(2,1)}, u32[]{:S(2)}, u32[]{:S(2)}) collective-permute-start(bf16[1,768,128]{2,1,0:T(8,128)(2,1)} %get-tuple-element.156), channel_id=1, source_target_pairs={{0,16},{16,0},{1,17},{17,1},{2,18},{18,2},{3,19},{19,3},{4,20},{20... | collective-permute-start | bytes 589832 | tf_op jit(solution)/shard_map/cond/branch_1_fun/ppermute | solution.py:391
  60.7 2.2 %collective-permute-start.6 = (bf16[128,256]{1,0:T(8,128)(2,1)S(1)}, bf16[128,256]{1,0:T(8,128)(2,1)S(1)}, u32[]{:S(2)}, u32[]{:S(2)}) collective-permute-start(bf16[128,256]{1,0:T(8,128)(2,1)S(1)} %branch_1_fun.18.r_3_), channel_id=1, source_target_pairs={{0,1},{1,0},{2,3},{3,2},{4,5},{5,4},{6,7},{7,6},{8,9},{9,8},{10,11... | collective-permute-start | bytes 196616 | tf_op jit(solution)/shard_map/cond/branch_1_fun/ppermute | solution.py:329
  65.5 31.6 %collective-permute-start.23 = (bf16[1536,128]{1,0:T(8,128)(2,1)}, bf16[1536,128]{1,0:T(8,128)(2,1)}, u32[]{:S(2)}, u32[]{:S(2)}) collective-permute-start(bf16[1536,128]{1,0:T(8,128)(2,1)} %get-tuple-element.241), channel_id=1, source_target_pairs={{0,4},{2,6},{4,0},{6,2},{1,5},{3,7},{5,1},{7,3},{8,12},{10,14},{12... | collective-permute-start | bytes 1179656 | tf_op jit(solution)/shard_map/ppermute | solution.py:251
  66.6 36.4 %collective-permute-start.24 = (bf16[1536,128]{1,0:T(8,128)(2,1)}, bf16[1536,128]{1,0:T(8,128)(2,1)}, u32[]{:S(2)}, u32[]{:S(2)}) collective-permute-start(bf16[1536,128]{1,0:T(8,128)(2,1)} %get-tuple-element.242), channel_id=1, source_target_pairs={{0,6},{2,4},{4,2},{6,0},{1,7},{3,5},{5,3},{7,1},{8,14},{10,12},{12... | collective-permute-start | bytes 1179656 | tf_op jit(solution)/shard_map/ppermute | solution.py:251
  67.8 35.2 %collective-permute-start.25 = (bf16[1536,128]{1,0:T(8,128)(2,1)}, bf16[1536,128]{1,0:T(8,128)(2,1)}, u32[]{:S(2)}, u32[]{:S(2)}) collective-permute-start(bf16[1536,128]{1,0:T(8,128)(2,1)} %get-tuple-element.240), channel_id=1, source_target_pairs={{0,2},{2,0},{4,6},{6,4},{1,3},{3,1},{5,7},{7,5},{8,10},{10,8},{12,... | collective-permute-start | bytes 1179656 | tf_op jit(solution)/shard_map/ppermute | solution.py:251
  72.1 2.2 %collective-permute-start.8 = (f32[128,256]{1,0:T(8,128)S(1)}, f32[128,256]{1,0:T(8,128)S(1)}, u32[]{:S(2)}, u32[]{:S(2)}) collective-permute-start(f32[128,256]{1,0:T(8,128)S(1)} %get-tuple-element.175), channel_id=1, source_target_pairs={{0,1},{1,0},{2,3},{3,2},{4,5},{5,4},{6,7},{7,6},{8,9},{9,8},{10,11... | collective-permute-start | bytes 393224 | tf_op jit(solution)/shard_map/cond/branch_1_fun/ppermute | solution.py:323
  74.4 3.6 %collective-permute-start.9 = (bf16[128,256]{1,0:T(8,128)(2,1)S(1)}, bf16[128,256]{1,0:T(8,128)(2,1)S(1)}, u32[]{:S(2)}, u32[]{:S(2)}) collective-permute-start(bf16[128,256]{1,0:T(8,128)(2,1)S(1)} %get-tuple-element.264), channel_id=1, source_target_pairs={{0,8},{8,0},{1,9},{9,1},{2,10},{10,2},{3,11},{11,3},{4,12},{12,4},... | collective-permute-start | bytes 196616 | tf_op jit(solution)/shard_map/cond/branch_1_fun/ppermute | solution.py:324
  85.2 6.5 %collective-permute-start.11 = (bf16[64,1536]{1,0:T(8,128)(2,1)S(1)}, bf16[64,1536]{1,0:T(8,128)(2,1)S(1)}, u32[]{:S(2)}, u32[]{:S(2)}) collective-permute-start(bf16[64,1536]{1,0:T(8,128)(2,1)S(1)} %get-tuple-element.185), channel_id=1, source_target_pairs={{0,8},{8,0},{1,9},{9,1},{2,10},{10,2},{3,11},{11,3},{4,12},{12,4},... | collective-permute-start | bytes 589832 | tf_op jit(solution)/shard_map/cond/branch_1_fun/ppermute | solution.py:450
  86.3 10.2 %collective-permute-start.13 = (bf16[64,1536]{1,0:T(8,128)(2,1)S(1)}, bf16[64,1536]{1,0:T(8,128)(2,1)S(1)}, u32[]{:S(2)}, u32[]{:S(2)}) collective-permute-start(bf16[64,1536]{1,0:T(8,128)(2,1)S(1)} %get-tuple-element.188), channel_id=1, source_target_pairs={{0,9},{1,8},{8,1},{9,0},{2,11},{3,10},{10,3},{11,2},{4,13},{5,12},... | collective-permute-start | bytes 589832 | tf_op jit(solution)/shard_map/cond/branch_1_fun/ppermute | solution.py:452
  (10 other events, 86.5 us)

commit v10 on v9

--- a/solution.py
+++ b/solution.py
@@ -200,6 +200,13 @@
     width = refs[0].shape[1]
     for j, block in enumerate(refs[:-1]):
         out[:, pl.ds(pl.multiple_of(scal[j] * width, 128), width)] = block[...]
+
+
+def add_up(*refs):
+    total = refs[0][...].astype(F32)
+    for block in refs[1:-1]:
+        total = total + block[...].astype(F32)
+    refs[-1][...] = total
 
 
 def split3(value):
@@ -469,9 +476,13 @@
         return back.transpose(1, 0, 2).reshape(own, width)
 
     grad_tokens = region(token_gradient, *pieces)
-    grad_down = after(pieces[0], grad_tokens).astype(F32)
-    for share in shares:
-        grad_down = grad_down + share.astype(F32)
+    grad_down = call(
+        add_up,
+        jax.ShapeDtypeStruct((quarter, ff), F32),
+        [VMEM] * n,
+        after(pieces[0], grad_tokens),
+        *shares,
+    )
     return (grad_tokens, grad_down[None])
 
 

time: 106 us -> 105 us (level)
  other arithmetic: 4.26 us -> 1.97 us
  Pallas kernels: 20 us -> 22 us
  waiting for transfers between devices: 50.7 us -> 49.4 us
    broadcast_in_dim x1 -> x0, other arithmetic: 2.29 us -> none  [per_device(): return (grad_tokens, grad_down[None])]
    pallas_call x13 -> x14, Pallas kernels: 17.4 us -> 19.5 us  [call(): pl.pallas_call(body, out_shape=outs, in_specs=specs, out_specs=jax.tree.m...]
    ppermute x10, waiting for transfers between devices: 7.13 us -> 6.05 us  [partner(): return pp(block, 'expert', [(i, i ^ k) for i in range(n)])]
  transfers between devices with their start and end apart: 26 -> 26, of which waited for: 17 -> 17; matrix products, arithmetic and copies ran while one was open for 3% -> 3% of each run, Pallas kernels for 18% -> 19%
where the time goes in v10:
time: 105 us
  waiting for transfers between devices  49.4 us (47%)
  starting transfers between devices  28.4 us (27%)
  Pallas kernels  22 us (21%)
  other arithmetic  1.97 us (2%)
  local copies, waits for them, and re-layouts  1.93 us (2%)
    ppermute x4, waiting for transfers between devices, swap_columns(): return [kept, pp(sent, axis, SWAP)]  19.7 us
    pallas_call x14, Pallas kernels, call(): pl.pallas_call(body, out_shape=outs, in_specs=specs, out_specs=jax.tree.m...  19.5 us
    ppermute x10, starting transfers between devices, partner(): return pp(block, 'expert', [(i, i ^ k) for i in range(n)])  12.6 us
    ppermute x2, waiting for transfers between devices, reduce_rows(): return [total, pp(total.astype(BF), 'fsdp', SWAP)]  7 us
    ppermute x10, waiting for transfers between devices, partner(): return pp(block, 'expert', [(i, i ^ k) for i in range(n)])  6.05 us
    ppermute x4, starting transfers between devices, swap_columns(): return [kept, pp(sent, axis, SWAP)]  6.05 us
    ppermute x1, waiting for transfers between devices, token_gradient(): pp(after(back[3], beside), ('fsdp', 'dp'), [(i, 3 - i) for i in range(4)])  4.78 us
    ppermute x1, waiting for transfers between devices, token_gradient(): across = pp(back[1], 'fsdp', SWAP)  4.48 us
  transfers between devices with their start and end apart: 26, of which 17 were waited for; matrix products, arithmetic and copies ran while one was open for 3% of the time, Pallas kernels for 19%

profile of v10, /device:TPU:11, one launch (start us, length us, event | category | flops | bytes accessed | tf_op | source)
XLA Modules:
  0.0 104.6 jit_solution(658851470437284537)
XLA Ops:
  3.3 2.2 %collective-permute-start.16 = (bf16[1,1536,128]{2,1,0:T(8,128)(2,1)S(1)}, bf16[1,1536,128]{2,1,0:T(8,128)(2,1)}, u32[]{:S(2)}, u32[]{:S(2)}) collective-permute-start(bf16[1,1536,128]{2,1,0:T(8,128)(2,1)S(1)} %copy-done), channel_id=1, source_target_pairs={{0,2},{2,0},{4,6},{6,4},{1,3},{3,1},{5,7},{7,5},{8,10},{10,8},{12,... | collective-permute-start | bytes 1179656 | tf_op jit(solution)/shard_map/ppermute | solution.py:258
  5.5 14.8 %conditional.5 = (bf16[256,1536]{1,0:T(8,128)(2,1)S(1)}, s32[256,2]{1,0:T(8,128)S(1)}, bf16[128,128]{1,0:T(8,128)(2,1)}) conditional(s32[]{:T(128)} %convert_element_type.40, () %tuple.59, (s32[]{:T(128)}, s32[]{:T(128)}, s32[64,2]{0,1:T(2,128)S(1)}, f32[64,2]{0,1:T(2,128)S(1)}, bf16[64,6144]{1,0:T(8,128)(2,1)S(1)}) %tuple.102), branch_computations={%region_0.0_spmd, %region_1.0_spmd} | conditional | flops 1576064 | bytes 6739050 | solution.py:262
  6.2 9.5 %collective-permute-done.r_2_ = bf16[64,3200]{1,0:T(8,128)(2,1)S(1)} collective-permute-done((bf16[64,3200]{1,0:T(8,128)(2,1)S(1)}, bf16[64,3200]{1,0:T(8,128)(2,1)S(1)}, u32[]{:S(2)}, u32[]{:S(2)}) %collective-permute-start) | collective-permute-done | bytes 409632 | tf_op jit(solution)/shard_map/cond/branch_1_fun/ppermute | solution.py:294
  15.8 2.2 %collective-permute-start.1 = (bf16[128,1664]{1,0:T(8,128)(2,1)S(1)}, bf16[128,1664]{1,0:T(8,128)(2,1)S(1)}, u32[]{:S(2)}, u32[]{:S(2)}) collective-permute-start(bf16[128,1664]{1,0:T(8,128)(2,1)S(1)} %get-tuple-element.123), channel_id=1, source_target_pairs={{0,1},{1,0},{2,3},{3,2},{4,5},{5,4},{6,7},{7,6},{8,9},{9,8},{10,11... | collective-permute-start | bytes 1277960 | tf_op jit(solution)/shard_map/cond/branch_1_fun/ppermute | solution.py:294
  22.6 1.6 %collective-permute-start.17 = (bf16[1,1536,128]{2,1,0:T(8,128)(2,1)S(1)}, bf16[1,1536,128]{2,1,0:T(8,128)(2,1)}, u32[]{:S(2)}, u32[]{:S(2)}) collective-permute-start(bf16[1,1536,128]{2,1,0:T(8,128)(2,1)S(1)} %copy-done.3), channel_id=1, source_target_pairs={{0,2},{2,0},{4,6},{6,4},{1,3},{3,1},{5,7},{7,5},{8,10},{10,8},{12,... | collective-permute-start | bytes 1179656 | tf_op jit(solution)/shard_map/ppermute | solution.py:258
  24.2 14.3 %conditional.6 = (bf16[256,1536]{1,0:T(8,128)(2,1)S(1)}) conditional(s32[]{:T(128)} %convert_element_type.41, () %tuple.64, (s32[]{:T(128)}, s32[]{:T(128)}, bf16[64,6144]{1,0:T(8,128)(2,1)}) %tuple.65), branch_computations={%region_2.0_spmd, %region_3.0_spmd} | conditional | flops 1572864 | bytes 4718680 | solution.py:262
  25.7 8.2 %collective-permute-done.2.r_2_ = bf16[64,3072]{1,0:T(8,128)(2,1)S(1)} collective-permute-done((bf16[64,3072]{1,0:T(8,128)(2,1)S(1)}, bf16[64,3072]{1,0:T(8,128)(2,1)S(1)}, u32[]{:S(2)}, u32[]{:S(2)}) %collective-permute-start.2) | collective-permute-done | bytes 393248 | tf_op jit(solution)/shard_map/cond/branch_1_fun/ppermute | solution.py:294
  34.0 3.2 %collective-permute-start.3 = (bf16[128,1536]{1,0:T(8,128)(2,1)S(1)}, bf16[128,1536]{1,0:T(8,128)(2,1)S(1)}, u32[]{:S(2)}, u32[]{:S(2)}) collective-permute-start(bf16[128,1536]{1,0:T(8,128)(2,1)S(1)} %get-tuple-element.130), channel_id=1, source_target_pairs={{0,1},{1,0},{2,3},{3,2},{4,5},{5,4},{6,7},{7,6},{8,9},{9,8},{10,11... | collective-permute-start | bytes 1179656 | tf_op jit(solution)/shard_map/cond/branch_1_fun/ppermute | solution.py:294
  39.5 2.9 %collective-permute-start.21 = (bf16[1,1536,128]{2,1,0:T(8,128)(2,1)}, bf16[1,1536,128]{2,1,0:T(8,128)(2,1)}, u32[]{:S(2)}, u32[]{:S(2)}) collective-permute-start(bf16[1,1536,128]{2,1,0:T(8,128)(2,1)} %down.1), channel_id=1, source_target_pairs={{0,2},{2,0},{4,6},{6,4},{1,3},{3,1},{5,7},{7,5},{8,10},{10,8},{12,... | collective-permute-start | bytes 1179656 | tf_op jit(solution)/shard_map/ppermute | solution.py:258
  43.4 3.3 %conditional.7 = (f32[128,512]{1,0:T(8,128)S(1)}, f32[128,512]{1,0:T(8,128)S(1)}, bf16[1536,256]{1,0:T(8,128)(2,1)S(1)}) conditional(s32[]{:T(128)} %convert_element_type.42, () %tuple.68, (s32[]{:T(128)}, s32[]{:T(128)}, s32[]{:T(128)}, s32[]{:T(128)}, s32[256,2]{1,0:T(8,128)S(1)}, /*index=5*/bf16[256,1536]{1,0:T(8,128)(2,1)S(1)}, ...), branch_computations={%region_4.0_spmd, %region_5.0_spmd} | conditional | flops 12 | bytes 1310754 | solution.py:262
  43.5 3.0 %branch_1_fun.16 = (f32[128,512]{1,0:T(8,128)S(1)}, f32[128,512]{1,0:T(8,128)S(1)}) custom-call(s32[4]{0:T(128)S(1)} %pad_add_fusion.r_0_, s32[256,2]{1,0:T(8,128)S(1)} %get-tuple-element.135.r_1_, bf16[256,1536]{1,0:T(8,128)(2,1)S(1)} %get-tuple-element.136.r_2_, bf16[1,1536,128]{2,1,0:T(8,128)(2,1)S(1)} %get-tuple-element.137.r_3_, ...), custom_call_target="tpu_custom_call" | custom-call | tf_op jit(solution)/shard_map/cond/branch_1_fun/pallas_call | solution.py:19
  46.7 2.6 %collective-permute-done.19.r_6_ = bf16[2,768,128]{2,1,0:T(8,128)(2,1)} collective-permute-done((bf16[2,768,128]{2,1,0:T(8,128)(2,1)}, bf16[2,768,128]{2,1,0:T(8,128)(2,1)}, u32[]{:S(2)}, u32[]{:S(2)}) %collective-permute-start.19) | collective-permute-done | bytes 393248 | tf_op jit(solution)/shard_map/ppermute | solution.py:378
  49.3 2.2 %shard_map.91 = (f32[128,512]{1,0:T(8,128)S(1)}, f32[128,512]{1,0:T(8,128)S(1)}) custom-call(s32[2]{0:T(128)S(1)} %pad_add_fusion.2.r_0_, s32[256,2]{1,0:T(8,128)S(1)} %get-tuple-element.222.r_1_, bf16[256,1536]{1,0:T(8,128)(2,1)S(1)} %get-tuple-element.223.r_2_, f32[128,512]{1,0:T(8,128)S(1)} %get-tuple-element.230.r_3_, ...), custom_call_target="tpu_custom_call" | custom-call | tf_op jit(solution)/shard_map/pallas_call | solution.py:19
  51.5 13.9 %conditional.8 = (bf16[1536,128]{1,0:T(8,128)(2,1)S(1)}, bf16[1536,128]{1,0:T(8,128)(2,1)S(1)}, bf16[1536,128]{1,0:T(8,128)(2,1)}, bf16[1536,128]{1,0:T(8,128)(2...) conditional(s32[]{:T(128)} %convert_element_type.39, () %tuple.57, ...), branch_computations={%region_6.0_spmd, %region_7.0_spmd} | conditional | flops 131072 | bytes 3539160 | solution.py:262
  55.6 3.9 %collective-permute-done.5.refs_1_ = bf16[128,512]{1,0:T(8,128)(2,1)} collective-permute-done((bf16[128,512]{1,0:T(8,128)(2,1)S(1)}, bf16[128,512]{1,0:T(8,128)(2,1)}, u32[]{:S(2)}, u32[]{:S(2)}) %collective-permute-start.5) | collective-permute-done | bytes 131104 | tf_op jit(solution)/shard_map/cond/branch_1_fun/ppermute | solution.py:331
  62.8 2.5 %branch_1_fun.19 = (bf16[1536,128]{1,0:T(8,128)(2,1)S(1)}, bf16[1536,128]{1,0:T(8,128)(2,1)S(1)}, bf16[1536,128]{1,0:T(8,128)(2,1)}, bf16[1536,128]{1,0:T(8,128)(2,1)}) custom-call(s32[4]{0:T(128)S(1)} %get-tuple-element.146.r_0_, s32[256,2]{1,0:T(8,128)S(1)} %get-tuple-element.147.r_1_, bf16[1536,256]{1,0:T(8,128)(2,1)S(1)} %get-tuple-element.148.r_2_, ...), custom_call_target="tpu_custom_call" | custom-call | tf_op jit(solution)/shard_map/cond/branch_1_fun/pallas_call | solution.py:409
  69.6 29.0 %conditional.9 = (bf16[64,6144]{1,0:T(8,128)(2,1)}) conditional(s32[]{:T(128)} %convert_element_type.43, () %tuple.75, (s32[]{:T(128)}, s32[]{:T(128)}, s32[]{:T(128)}, s32[]{:T(128)}, s32[]{:T(128)}, /*index=5*/s32[]{:T(128)}, s32[]{:T(128)}, s32[256,2]{1,0:T(8,128)S(1)}, bf16[256,1536]{1,0:T(8,128)(2,1)S(1)}, bf16[1,1536,128]{2,1,0:T(8,128)(2,1)}, ...), branch_computations={%region_8.0_spmd, %region_9.0_spmd} | conditional | flops 65553 | bytes 10420756 | solution.py:262
  69.7 3.0 %branch_1_fun.20 = (f32[128,256]{1,0:T(8,128)S(1)}, f32[128,256]{1,0:T(8,128)S(1)}) custom-call(s32[5]{0:T(128)S(1)} %stack.76.r_0_, s32[256,2]{1,0:T(8,128)S(1)} %get-tuple-element.164.r_1_, bf16[256,1536]{1,0:T(8,128)(2,1)S(1)} %get-tuple-element.168.r_2_, bf16[1,1536,128]{2,1,0:T(8,128)(2,1)} %get-tuple-element.169.r_3_, ...), custom_call_target="tpu_custom_call" | custom-call | tf_op jit(solution)/shard_map/cond/branch_1_fun/pallas_call | solution.py:19
  75.4 3.1 %collective-permute-done.9.r_4_ = bf16[128,256]{1,0:T(8,128)(2,1)S(1)} collective-permute-done((bf16[128,256]{1,0:T(8,128)(2,1)S(1)}, bf16[128,256]{1,0:T(8,128)(2,1)S(1)}, u32[]{:S(2)}, u32[]{:S(2)}) %collective-permute-start.9) | collective-permute-done | bytes 65568 | tf_op jit(solution)/shard_map/cond/branch_1_fun/ppermute | solution.py:331
  82.0 3.5 %branch_1_fun.22 = (bf16[64,1536]{1,0:T(8,128)(2,1)S(1)}, bf16[64,1536]{1,0:T(8,128)(2,1)S(1)}, bf16[64,1536]{1,0:T(8,128)(2,1)S(1)}, bf16[64,1536]{1,0:T(8,128)(2,1)S(1)}) custom-call(s32[5]{0:T(128)S(1)} %stack.72.r_0_, s32[256,2]{1,0:T(8,128)S(1)} %get-tuple-element.164.r_1_, bf16[128,512]{1,0:T(8,128)(2,1)S(1)} %branch_1_fun.21.r_2_, ...), custom_call_target="tpu_custom_call" | custom-call | tf_op jit(solution)/shard_map/cond/branch_1_fun/pallas_call | solution.py:19
  87.9 4.5 %collective-permute-done.11.refs_1_ = bf16[64,1536]{1,0:T(8,128)(2,1)S(1)} collective-permute-done((bf16[64,1536]{1,0:T(8,128)(2,1)S(1)}, bf16[64,1536]{1,0:T(8,128)(2,1)S(1)}, u32[]{:S(2)}, u32[]{:S(2)}) %collective-permute-start.11) | collective-permute-done | bytes 196640 | tf_op jit(solution)/shard_map/cond/branch_1_fun/ppermute | solution.py:457
  92.4 4.8 %collective-permute-done.13.refs_3_ = bf16[64,1536]{1,0:T(8,128)(2,1)S(1)} collective-permute-done((bf16[64,1536]{1,0:T(8,128)(2,1)S(1)}, bf16[64,1536]{1,0:T(8,128)(2,1)S(1)}, u32[]{:S(2)}, u32[]{:S(2)}) %collective-permute-start.13) | collective-permute-done | bytes 196640 | tf_op jit(solution)/shard_map/cond/branch_1_fun/ppermute | solution.py:459
  97.1 1.5 %branch_1_fun.23 = bf16[64,6144]{1,0:T(8,128)(2,1)} custom-call(s32[4]{0:T(128)S(1)} %pad_add_fusion.1.scal, bf16[64,1536]{1,0:T(8,128)(2,1)S(1)} %get-tuple-element.184.refs_0_, bf16[64,1536]{1,0:T(8,128)(2,1)S(1)} %collective-permute-done.11.refs_1_, bf16[64,1536]{1,0:T(8,128)(2,1)S(1)} %collective-permute-done.12.refs_2_, ...), custom_call_target="tpu_custom_call" | custom-call | tf_op jit(solution)/shard_map/cond/branch_1_fun/pallas_call | solution.py:19
  98.6 4.9 %collective-permute-done.24.refs_2_ = bf16[1536,128]{1,0:T(8,128)(2,1)S(1)} collective-permute-done((bf16[1536,128]{1,0:T(8,128)(2,1)}, bf16[1536,128]{1,0:T(8,128)(2,1)S(1)}, u32[]{:S(2)}, u32[]{:S(2)}) %collective-permute-start.24) | collective-permute-done | bytes 393248 | tf_op jit(solution)/shard_map/ppermute | solution.py:258
  (95 shorter events, 34.5 us)
Async XLA Ops:
  1.9 18.8 %collective-permute-start.14 = (bf16[2,768,128]{2,1,0:T(8,128)(2,1)S(1)}, bf16[2,768,128]{2,1,0:T(8,128)(2,1)S(1)}, u32[]{:S(2)}, u32[]{:S(2)}) collective-permute-start(bf16[2,768,128]{2,1,0:T(8,128)(2,1)S(1)} %get-tuple-element.225), channel_id=1, source_target_pairs={{0,6},{2,4},{4,2},{6,0},{1,7},{3,5},{5,3},{7,1},{8,14},{10,12},{12... | collective-permute-start | bytes 1179656 | tf_op jit(solution)/shard_map/ppermute | solution.py:258
  3.3 19.3 %collective-permute-start.16 = (bf16[1,1536,128]{2,1,0:T(8,128)(2,1)S(1)}, bf16[1,1536,128]{2,1,0:T(8,128)(2,1)}, u32[]{:S(2)}, u32[]{:S(2)}) collective-permute-start(bf16[1,1536,128]{2,1,0:T(8,128)(2,1)S(1)} %copy-done), channel_id=1, source_target_pairs={{0,2},{2,0},{4,6},{6,4},{1,3},{3,1},{5,7},{7,5},{8,10},{10,8},{12,... | collective-permute-start | bytes 1179656 | tf_op jit(solution)/shard_map/ppermute | solution.py:258
  5.9 9.8 %collective-permute-start = (bf16[64,3200]{1,0:T(8,128)(2,1)S(1)}, bf16[64,3200]{1,0:T(8,128)(2,1)S(1)}, u32[]{:S(2)}, u32[]{:S(2)}) collective-permute-start(bf16[64,3200]{1,0:T(8,128)(2,1)S(1)} %get-tuple-element.121), channel_id=1, source_target_pairs={{0,8},{8,0},{1,9},{9,1},{2,10},{10,2},{3,11},{11,3},{4,12},{12,4},... | collective-permute-start | bytes 1228808 | tf_op jit(solution)/shard_map/cond/branch_1_fun/ppermute | solution.py:294
  15.8 3.6 %collective-permute-start.1 = (bf16[128,1664]{1,0:T(8,128)(2,1)S(1)}, bf16[128,1664]{1,0:T(8,128)(2,1)S(1)}, u32[]{:S(2)}, u32[]{:S(2)}) collective-permute-start(bf16[128,1664]{1,0:T(8,128)(2,1)S(1)} %get-tuple-element.123), channel_id=1, source_target_pairs={{0,1},{1,0},{2,3},{3,2},{4,5},{5,4},{6,7},{7,6},{8,9},{9,8},{10,11... | collective-permute-start | bytes 1277960 | tf_op jit(solution)/shard_map/cond/branch_1_fun/ppermute | solution.py:294
  20.7 17.9 %collective-permute-start.15 = (bf16[2,768,128]{2,1,0:T(8,128)(2,1)S(1)}, bf16[2,768,128]{2,1,0:T(8,128)(2,1)}, u32[]{:S(2)}, u32[]{:S(2)}) collective-permute-start(bf16[2,768,128]{2,1,0:T(8,128)(2,1)S(1)} %get-tuple-element.225), channel_id=1, source_target_pairs={{0,4},{2,6},{4,0},{6,2},{1,5},{3,7},{5,1},{7,3},{8,12},{10,14},{12... | collective-permute-start | bytes 1179656 | tf_op jit(solution)/shard_map/ppermute | solution.py:258
  20.7 17.9 %collective-permute-start.18 = (bf16[2,768,128]{2,1,0:T(8,128)(2,1)S(1)}, bf16[2,768,128]{2,1,0:T(8,128)(2,1)}, u32[]{:S(2)}, u32[]{:S(2)}) collective-permute-start(bf16[2,768,128]{2,1,0:T(8,128)(2,1)S(1)} %collective-permute-done.14), channel_id=1, source_target_pairs={{0,16},{16,0},{1,17},{17,1},{2,18},{18,2},{3,19},{19,3},{4,20},{20... | collective-permute-start | bytes 1179656 | tf_op jit(solution)/shard_map/ppermute | solution.py:365
  22.6 20.8 %collective-permute-start.17 = (bf16[1,1536,128]{2,1,0:T(8,128)(2,1)S(1)}, bf16[1,1536,128]{2,1,0:T(8,128)(2,1)}, u32[]{:S(2)}, u32[]{:S(2)}) collective-permute-start(bf16[1,1536,128]{2,1,0:T(8,128)(2,1)S(1)} %copy-done.3), channel_id=1, source_target_pairs={{0,2},{2,0},{4,6},{6,4},{1,3},{3,1},{5,7},{7,5},{8,10},{10,8},{12,... | collective-permute-start | bytes 1179656 | tf_op jit(solution)/shard_map/ppermute | solution.py:258
  25.4 8.5 %collective-permute-start.2 = (bf16[64,3072]{1,0:T(8,128)(2,1)S(1)}, bf16[64,3072]{1,0:T(8,128)(2,1)S(1)}, u32[]{:S(2)}, u32[]{:S(2)}) collective-permute-start(bf16[64,3072]{1,0:T(8,128)(2,1)S(1)} %get-tuple-element.128), channel_id=1, source_target_pairs={{0,8},{8,0},{1,9},{9,1},{2,10},{10,2},{3,11},{11,3},{4,12},{12,4},... | collective-permute-start | bytes 1179656 | tf_op jit(solution)/shard_map/cond/branch_1_fun/ppermute | solution.py:294
  34.0 4.5 %collective-permute-start.3 = (bf16[128,1536]{1,0:T(8,128)(2,1)S(1)}, bf16[128,1536]{1,0:T(8,128)(2,1)S(1)}, u32[]{:S(2)}, u32[]{:S(2)}) collective-permute-start(bf16[128,1536]{1,0:T(8,128)(2,1)S(1)} %get-tuple-element.130), channel_id=1, source_target_pairs={{0,1},{1,0},{2,3},{3,2},{4,5},{5,4},{6,7},{7,6},{8,9},{9,8},{10,11... | collective-permute-start | bytes 1179656 | tf_op jit(solution)/shard_map/cond/branch_1_fun/ppermute | solution.py:294
  38.6 10.7 %collective-permute-start.19 = (bf16[2,768,128]{2,1,0:T(8,128)(2,1)}, bf16[2,768,128]{2,1,0:T(8,128)(2,1)}, u32[]{:S(2)}, u32[]{:S(2)}) collective-permute-start(bf16[2,768,128]{2,1,0:T(8,128)(2,1)} %collective-permute-done.15.r_5_), channel_id=1, source_target_pairs={{0,16},{16,0},{1,17},{17,1},{2,18},{18,2},{3,19},{19,3},{4,20},{20... | collective-permute-start | bytes 1179656 | tf_op jit(solution)/shard_map/ppermute | solution.py:378
  39.3 12.1 %collective-permute-start.20 = (bf16[1,768,128]{2,1,0:T(8,128)(2,1)S(1)}, bf16[1,768,128]{2,1,0:T(8,128)(2,1)}, u32[]{:S(2)}, u32[]{:S(2)}) collective-permute-start(bf16[1,768,128]{2,1,0:T(8,128)(2,1)S(1)} %get-tuple-element.238), channel_id=1, source_target_pairs={{0,6},{2,4},{4,2},{6,0},{1,7},{3,5},{5,3},{7,1},{8,14},{10,12},{12... | collective-permute-start | bytes 589832 | tf_op jit(solution)/shard_map/ppermute | solution.py:258
  39.5 30.1 %collective-permute-start.21 = (bf16[1,1536,128]{2,1,0:T(8,128)(2,1)}, bf16[1,1536,128]{2,1,0:T(8,128)(2,1)}, u32[]{:S(2)}, u32[]{:S(2)}) collective-permute-start(bf16[1,1536,128]{2,1,0:T(8,128)(2,1)} %down.1), channel_id=1, source_target_pairs={{0,2},{2,0},{4,6},{6,4},{1,3},{3,1},{5,7},{7,5},{8,10},{10,8},{12,... | collective-permute-start | bytes 1179656 | tf_op jit(solution)/shard_map/ppermute | solution.py:258
  42.3 27.3 %collective-permute-start.22 = (bf16[1,1536,128]{2,1,0:T(8,128)(2,1)}, bf16[1,1536,128]{2,1,0:T(8,128)(2,1)}, u32[]{:S(2)}, u32[]{:S(2)}) collective-permute-start(bf16[1,1536,128]{2,1,0:T(8,128)(2,1)} %down.1), channel_id=1, source_target_pairs={{0,4},{2,6},{4,0},{6,2},{1,5},{3,7},{5,1},{7,3},{8,12},{10,14},{12... | collective-permute-start | bytes 1179656 | tf_op jit(solution)/shard_map/ppermute | solution.py:258
  51.5 2.4 %collective-permute-start.4 = (f32[128,512]{1,0:T(8,128)S(1)}, f32[128,512]{1,0:T(8,128)S(1)}, u32[]{:S(2)}, u32[]{:S(2)}) collective-permute-start(f32[128,512]{1,0:T(8,128)S(1)} %get-tuple-element.151), channel_id=1, source_target_pairs={{0,1},{1,0},{2,3},{3,2},{4,5},{5,4},{6,7},{7,6},{8,9},{9,8},{10,11... | collective-permute-start | bytes 786440 | tf_op jit(solution)/shard_map/cond/branch_1_fun/ppermute | solution.py:330
  54.7 4.8 %collective-permute-start.5 = (bf16[128,512]{1,0:T(8,128)(2,1)S(1)}, bf16[128,512]{1,0:T(8,128)(2,1)}, u32[]{:S(2)}, u32[]{:S(2)}) collective-permute-start(bf16[128,512]{1,0:T(8,128)(2,1)S(1)} %get-tuple-element.262), channel_id=1, source_target_pairs={{0,8},{8,0},{1,9},{9,1},{2,10},{10,2},{3,11},{11,3},{4,12},{12,4},... | collective-permute-start | bytes 393224 | tf_op jit(solution)/shard_map/cond/branch_1_fun/ppermute | solution.py:331
  54.9 10.4 %collective-permute-start.7 = (bf16[1,768,128]{2,1,0:T(8,128)(2,1)}, bf16[1,768,128]{2,1,0:T(8,128)(2,1)}, u32[]{:S(2)}, u32[]{:S(2)}) collective-permute-start(bf16[1,768,128]{2,1,0:T(8,128)(2,1)} %get-tuple-element.156), channel_id=1, source_target_pairs={{0,16},{16,0},{1,17},{17,1},{2,18},{18,2},{3,19},{19,3},{4,20},{20... | collective-permute-start | bytes 589832 | tf_op jit(solution)/shard_map/cond/branch_1_fun/ppermute | solution.py:398
  66.1 32.6 %collective-permute-start.23 = (bf16[1536,128]{1,0:T(8,128)(2,1)}, bf16[1536,128]{1,0:T(8,128)(2,1)S(1)}, u32[]{:S(2)}, u32[]{:S(2)}) collective-permute-start(bf16[1536,128]{1,0:T(8,128)(2,1)} %get-tuple-element.241), channel_id=1, source_target_pairs={{0,4},{2,6},{4,0},{6,2},{1,5},{3,7},{5,1},{7,3},{8,12},{10,14},{12... | collective-permute-start | bytes 1179656 | tf_op jit(solution)/shard_map/ppermute | solution.py:258
  67.3 36.3 %collective-permute-start.24 = (bf16[1536,128]{1,0:T(8,128)(2,1)}, bf16[1536,128]{1,0:T(8,128)(2,1)S(1)}, u32[]{:S(2)}, u32[]{:S(2)}) collective-permute-start(bf16[1536,128]{1,0:T(8,128)(2,1)} %get-tuple-element.242), channel_id=1, source_target_pairs={{0,6},{2,4},{4,2},{6,0},{1,7},{3,5},{5,3},{7,1},{8,14},{10,12},{12... | collective-permute-start | bytes 1179656 | tf_op jit(solution)/shard_map/ppermute | solution.py:258
  68.4 35.1 %collective-permute-start.25 = (bf16[1536,128]{1,0:T(8,128)(2,1)}, bf16[1536,128]{1,0:T(8,128)(2,1)S(1)}, u32[]{:S(2)}, u32[]{:S(2)}) collective-permute-start(bf16[1536,128]{1,0:T(8,128)(2,1)} %copy-done.10), channel_id=1, source_target_pairs={{0,2},{2,0},{4,6},{6,4},{1,3},{3,1},{5,7},{7,5},{8,10},{10,8},{12,... | collective-permute-start | bytes 1179656 | tf_op jit(solution)/shard_map/ppermute | solution.py:258
  72.8 2.2 %collective-permute-start.8 = (f32[128,256]{1,0:T(8,128)S(1)}, f32[128,256]{1,0:T(8,128)S(1)}, u32[]{:S(2)}, u32[]{:S(2)}) collective-permute-start(f32[128,256]{1,0:T(8,128)S(1)} %get-tuple-element.175), channel_id=1, source_target_pairs={{0,1},{1,0},{2,3},{3,2},{4,5},{5,4},{6,7},{7,6},{8,9},{9,8},{10,11... | collective-permute-start | bytes 393224 | tf_op jit(solution)/shard_map/cond/branch_1_fun/ppermute | solution.py:330
  75.1 3.5 %collective-permute-start.9 = (bf16[128,256]{1,0:T(8,128)(2,1)S(1)}, bf16[128,256]{1,0:T(8,128)(2,1)S(1)}, u32[]{:S(2)}, u32[]{:S(2)}) collective-permute-start(bf16[128,256]{1,0:T(8,128)(2,1)S(1)} %get-tuple-element.264), channel_id=1, source_target_pairs={{0,8},{8,0},{1,9},{9,1},{2,10},{10,2},{3,11},{11,3},{4,12},{12,4},... | collective-permute-start | bytes 196616 | tf_op jit(solution)/shard_map/cond/branch_1_fun/ppermute | solution.py:331
  79.7 2.3 %collective-permute-start.10 = (bf16[128,512]{1,0:T(8,128)(2,1)S(1)}, bf16[128,512]{1,0:T(8,128)(2,1)S(1)}, u32[]{:S(2)}, u32[]{:S(2)}) collective-permute-start(bf16[128,512]{1,0:T(8,128)(2,1)S(1)} %branch_1_fun.21.r_2_), channel_id=1, source_target_pairs={{0,1},{1,0},{2,3},{3,2},{4,5},{5,4},{6,7},{7,6},{8,9},{9,8},{10,11... | collective-permute-start | bytes 393224 | tf_op jit(solution)/shard_map/cond/branch_1_fun/ppermute | solution.py:336
  86.0 6.4 %collective-permute-start.11 = (bf16[64,1536]{1,0:T(8,128)(2,1)S(1)}, bf16[64,1536]{1,0:T(8,128)(2,1)S(1)}, u32[]{:S(2)}, u32[]{:S(2)}) collective-permute-start(bf16[64,1536]{1,0:T(8,128)(2,1)S(1)} %get-tuple-element.185), channel_id=1, source_target_pairs={{0,8},{8,0},{1,9},{9,1},{2,10},{10,2},{3,11},{11,3},{4,12},{12,4},... | collective-permute-start | bytes 589832 | tf_op jit(solution)/shard_map/cond/branch_1_fun/ppermute | solution.py:457
  87.1 10.1 %collective-permute-start.13 = (bf16[64,1536]{1,0:T(8,128)(2,1)S(1)}, bf16[64,1536]{1,0:T(8,128)(2,1)S(1)}, u32[]{:S(2)}, u32[]{:S(2)}) collective-permute-start(bf16[64,1536]{1,0:T(8,128)(2,1)S(1)} %get-tuple-element.188), channel_id=1, source_target_pairs={{0,9},{1,8},{8,1},{9,0},{2,11},{3,10},{10,3},{11,2},{4,13},{5,12},... | collective-permute-start | bytes 589832 | tf_op jit(solution)/shard_map/cond/branch_1_fun/ppermute | solution.py:459
  (15 other events, 121.2 us)
